TPU v7x, 32 devices: a whole 2x2x4 slice. The times are simulated.
32 devices in a mesh: dp: 4 (over z), context: 2 (over y), experts: 4 (over x, core).
Axes of the slice: x: 2, y: 2, z: 4, core: 2. Of those that a mesh axis runs over, the one named last changes fastest.
Arguments:
- tokens: bfloat16 [12288, 768], P(('dp', 'context', 'experts')), may hold values from -6 to 6
- cotangent: bfloat16 [12288, 768], P(('dp', 'context', 'experts')), may hold values from -6 to 6
- routes: int32 [12288, 2], P(('dp', 'context', 'experts')), may hold values from 0 to 15, all different within a row; in each aligned block of 384 rows (0 to 383, 384 to 767, ...) at most 66 rows name the same one
- prompt_ids: int32 [64], P(('dp', 'context', 'experts')), may hold values from 0 to 1, as said below
- attn_gain: bfloat16 [768], P('dp'), may hold values from 0.5 to 1.5
- query_weight: bfloat16 [768, 768], P('dp'), may hold values from -0.21875 to 0.21875
- key_weight: bfloat16 [768, 768], P('dp'), may hold values from -0.21875 to 0.21875
- value_weight: bfloat16 [768, 768], P('dp'), may hold values from -0.21875 to 0.21875
- output_weight: bfloat16 [768, 768], P('dp'), may hold values from -2.5 to 2.5
- ffn_gain: bfloat16 [768], P('dp'), may hold values from 0.5 to 1.5
- router_weight: bfloat16 [768, 16], P('dp'), may hold values from -0.15625 to 0.15625
- shared_gate: bfloat16 [768, 2048], P('dp'), may hold values from -0.21875 to 0.21875
- shared_up: bfloat16 [768, 2048], P('dp'), may hold values from -0.21875 to 0.21875
- shared_down: bfloat16 [2048, 768], P('dp'), may hold values from -0.125 to 0.125
- expert_gate: bfloat16 [16, 768, 2048], P('experts'), may hold values from -0.21875 to 0.21875
- expert_up_weight: bfloat16 [16, 768, 2048], P('experts'), may hold values from -0.21875 to 0.21875
- expert_down: bfloat16 [16, 2048, 768], P('experts'), may hold values from -1.5 to 1.5
Outputs:
- layer_out: bfloat16 [12288, 768], P(('dp', 'context', 'experts'))
- grad_tokens: float32 [12288, 768], P(('dp', 'context', 'experts'))
- grad_attn_gain: float32 [768], P('dp')
- grad_query: float32 [768, 768], P('dp')
- grad_key: float32 [768, 768], P('dp')
- grad_value: float32 [768, 768], P('dp')
- grad_output: float32 [768, 768], P('dp')
- grad_ffn_gain: float32 [768], P('dp')
- grad_router: float32 [768, 16], P('dp')
- grad_shared_gate: float32 [768, 2048], P('dp')
- grad_shared_up: float32 [768, 2048], P('dp')
- grad_shared_down: float32 [2048, 768], P('dp')
- grad_expert_gate: float32 [16, 768, 2048], P('experts', None, ('dp', 'context'))
- grad_expert_up: float32 [16, 768, 2048], P('experts', None, ('dp', 'context'))
- grad_expert_down: float32 [16, 2048, 768], P('experts', ('dp', 'context'))
Inputs may be any that keep to these rules, and one draw needn't show every extreme that they name: `routes`: among the 768 choices of the rows of one device, each expert is named at most 66 times; a row names 2 different experts. `prompt_ids`: in every block some continuation follows the prompt of another block of its group.
All inputs are finite; a program needn't handle non-finite values.
Results may differ from a plain program's by a relative error of at most 0.022.
Values may be sent and summed in bfloat16 or wider, within the bound.
No kernel may reach another device: no remote copies, remote signals or barrier semaphores. Data moves between devices by JAX's collectives and lax.ppermute only.
A program may use at most 256 MiB of HBM per device.

v0:
```python
import jax
import jax.numpy as jnp
from jax import lax
from jax.sharding import PartitionSpec as P

D = 768
HEADS = 12
HD = 64
EXPERTS = 16
TOPK = 2
PROMPT = 256
CONT = 2
CLEN = 64
TOK_DEV = 384
CAP = 66


EPS = 1e-06


def rotary_tables(tok_rows):
    row_ids = jnp.arange(tok_rows)
    position = jnp.where(row_ids < PROMPT, row_ids, PROMPT + (row_ids - PROMPT) % CLEN).astype(
        jnp.float32
    )
    frequency = 10000.0 ** (-2.0 * jnp.arange(HD // 2).astype(jnp.float32) / HD)
    angles = position[:, None] * frequency[None, :]
    return (jnp.cos(angles), jnp.sin(angles))


def rotate(values_in, cos_table, sin_table):
    shaped = values_in.reshape(values_in.shape[:-1] + (HEADS, HD))
    lower_half = shaped[..., : HD // 2]
    upper_half = shaped[..., HD // 2 :]
    cos_part = cos_table[:, None, :]
    sin_part = sin_table[:, None, :]
    turned = jnp.concatenate(
        [
            lower_half * cos_part - upper_half * sin_part,
            upper_half * cos_part + lower_half * sin_part,
        ],
        -1,
    )
    return turned.reshape(values_in.shape)


def key_mask(context_index, prompt_pick, contexts):
    row_ids = jnp.arange(TOK_DEV)[:, None]
    col_ids = jnp.arange(contexts * PROMPT + CONT * CLEN)[None, :]
    prompt_row = row_ids < PROMPT
    cont_row = (row_ids - PROMPT) // CLEN
    within_row = (row_ids - PROMPT) % CLEN
    owner = jnp.sum(
        prompt_pick[None, :] * (jnp.arange(CONT)[None, :] == cont_row), -1, keepdims=True
    )
    target = jnp.where(prompt_row, context_index, owner)
    prompt_keys = col_ids < contexts * PROMPT
    prompt_ok = (
        prompt_keys
        & (col_ids // PROMPT == target)
        & (jnp.logical_not(prompt_row) | (col_ids % PROMPT <= row_ids))
    )
    offset = col_ids - contexts * PROMPT
    cont_ok = (
        jnp.logical_not(prompt_keys)
        & jnp.logical_not(prompt_row)
        & (offset // CLEN == cont_row)
        & (offset % CLEN <= within_row)
    )
    return prompt_ok | cont_ok


def inner_rows(left, right):
    return lax.dot_general(
        left, right, (((0,), (0,)), ((), ())), preferred_element_type=jnp.float32
    )


def times_transposed(left, right):
    return lax.dot_general(
        left, right, (((1,), (1,)), ((), ())), preferred_element_type=jnp.float32
    )


def swish_derivative(pre_act):
    sigma = jax.nn.sigmoid(pre_act)
    return sigma * (1.0 + pre_act * (1.0 - sigma))


def body(
    tokens,
    cotangent,
    routes,
    prompt_ids,
    attn_gain,
    query_weight,
    key_weight,
    value_weight,
    output_weight,
    ffn_gain,
    router_weight,
    shared_gate,
    shared_up,
    shared_down,
    expert_gate,
    expert_up_weight,
    expert_down,
):
    contexts = lax.axis_size("context")
    context_here = lax.axis_index("context")
    gain_one, w_query, w_key, w_value, w_out, gain_two, w_router, w_sgate, w_sup, w_sdown = (
        lax.all_gather(attn_gain, "dp", axis=0, tiled=True),
        lax.all_gather(query_weight, "dp", axis=0, tiled=True),
        lax.all_gather(key_weight, "dp", axis=0, tiled=True),
        lax.all_gather(value_weight, "dp", axis=0, tiled=True),
        lax.all_gather(output_weight, "dp", axis=0, tiled=True),
        lax.all_gather(ffn_gain, "dp", axis=0, tiled=True),
        lax.all_gather(router_weight, "dp", axis=0, tiled=True),
        lax.all_gather(shared_gate, "dp", axis=0, tiled=True),
        lax.all_gather(shared_up, "dp", axis=0, tiled=True),
        lax.all_gather(shared_down, "dp", axis=0, tiled=True),
    )
    cos_table, sin_table = rotary_tables(TOK_DEV)
    inputs = tokens.astype(jnp.float32)
    inv_rms1 = lax.rsqrt(jnp.mean(inputs * inputs, -1, keepdims=True) + EPS)
    normed1 = inputs * inv_rms1
    gain1_f = gain_one.astype(jnp.float32)
    hidden1 = (normed1 * gain1_f).astype(jnp.bfloat16)
    query_f = jnp.dot(hidden1, w_query, preferred_element_type=jnp.float32)
    key_f = jnp.dot(hidden1, w_key, preferred_element_type=jnp.float32)
    value_f = jnp.dot(hidden1, w_value, preferred_element_type=jnp.float32)
    query_b = rotate(query_f, cos_table, sin_table).astype(jnp.bfloat16)
    key_b = rotate(key_f, cos_table, sin_table).astype(jnp.bfloat16)
    value_b = value_f.astype(jnp.bfloat16)
    prompt_keys, prompt_values = (
        lax.all_gather(key_b[:PROMPT], "context", axis=0, tiled=True),
        lax.all_gather(value_b[:PROMPT], "context", axis=0, tiled=True),
    )
    keys_h = jnp.concatenate([prompt_keys, key_b[PROMPT:]], 0).reshape(-1, HEADS, HD)
    values_h = jnp.concatenate([prompt_values, value_b[PROMPT:]], 0).reshape(-1, HEADS, HD)
    query_h = query_b.reshape(TOK_DEV, HEADS, HD)
    allowed = key_mask(context_here, prompt_ids, contexts)
    scores = jnp.where(
        allowed[None],
        0.125 * jnp.einsum("qhd,khd->hqk", query_h, keys_h, preferred_element_type=jnp.float32),
        -1e30,
    )
    row_max = jnp.max(scores, -1, keepdims=True)
    exp_scores = jnp.exp(scores - row_max)
    row_total = jnp.sum(exp_scores, -1, keepdims=True)
    log_total = row_max + jnp.log(row_total)
    attn_probs = (exp_scores / row_total).astype(jnp.bfloat16)
    attended = (
        jnp.einsum("hqk,khd->qhd", attn_probs, values_h, preferred_element_type=jnp.float32)
        .reshape(TOK_DEV, D)
        .astype(jnp.bfloat16)
    )
    resid = inputs + jnp.dot(attended, w_out, preferred_element_type=jnp.float32)
    inv_rms2 = lax.rsqrt(jnp.mean(resid * resid, -1, keepdims=True) + EPS)
    normed2 = resid * inv_rms2
    gain2_f = gain_two.astype(jnp.float32)
    hidden2 = (normed2 * gain2_f).astype(jnp.bfloat16)
    logits = jnp.dot(hidden2, w_router, preferred_element_type=jnp.float32)
    route_probs = jax.nn.softmax(logits, -1)
    route_hot = (routes[:, :, None] == jnp.arange(EXPERTS)[None, None, :]).astype(jnp.float32)
    gate_vals = jnp.sum(route_probs[:, None, :] * route_hot, -1)
    shared_gpre = jnp.dot(hidden2, w_sgate, preferred_element_type=jnp.float32)
    shared_upre = jnp.dot(hidden2, w_sup, preferred_element_type=jnp.float32)
    shared_act = (jax.nn.silu(shared_gpre) * shared_upre).astype(jnp.bfloat16)
    shared_res = jnp.dot(shared_act, w_sdown, preferred_element_type=jnp.float32)
    flat_route = routes.reshape(-1)
    flat_hot = (flat_route[:, None] == jnp.arange(EXPERTS)[None, :]).astype(jnp.int32)
    slot_ids = jnp.sum((jnp.cumsum(flat_hot, 0) - flat_hot) * flat_hot, -1)
    slot_index = flat_route * CAP + slot_ids
    send_rows = jnp.repeat(hidden2, TOPK, axis=0)
    outgoing = (
        jnp.zeros((EXPERTS * CAP, D), jnp.bfloat16)
        .at[slot_index]
        .set(send_rows)
        .reshape(EXPERTS, CAP, D)
    )
    received_rows = lax.all_to_all(outgoing, "experts", split_axis=0, concat_axis=1, tiled=True)
    expert_gate_preact = jnp.einsum(
        "mgx,mxp->mgp", received_rows, expert_gate, preferred_element_type=jnp.float32
    )
    expert_up_preact = jnp.einsum(
        "mgx,mxp->mgp", received_rows, expert_up_weight, preferred_element_type=jnp.float32
    )
    expert_activation = (jax.nn.silu(expert_gate_preact) * expert_up_preact).astype(jnp.bfloat16)
    expert_res = jnp.einsum(
        "erf,efd->erd", expert_activation, expert_down, preferred_element_type=jnp.float32
    ).astype(jnp.bfloat16)
    returned = lax.all_to_all(
        expert_res, "experts", split_axis=1, concat_axis=0, tiled=True
    ).reshape(EXPERTS * CAP, D)
    picked = returned[slot_index].astype(jnp.float32).reshape(TOK_DEV, TOPK, D)
    moe_out = jnp.sum(gate_vals[:, :, None] * picked, 1)
    layer_out = (resid + shared_res + moe_out).astype(jnp.bfloat16)
    gain_one, w_query, w_key, w_value, w_out, gain_two, w_router, w_sgate, w_sup, w_sdown = (
        lax.all_gather(attn_gain, "dp", axis=0, tiled=True),
        lax.all_gather(query_weight, "dp", axis=0, tiled=True),
        lax.all_gather(key_weight, "dp", axis=0, tiled=True),
        lax.all_gather(value_weight, "dp", axis=0, tiled=True),
        lax.all_gather(output_weight, "dp", axis=0, tiled=True),
        lax.all_gather(ffn_gain, "dp", axis=0, tiled=True),
        lax.all_gather(router_weight, "dp", axis=0, tiled=True),
        lax.all_gather(shared_gate, "dp", axis=0, tiled=True),
        lax.all_gather(shared_up, "dp", axis=0, tiled=True),
        lax.all_gather(shared_down, "dp", axis=0, tiled=True),
    )
    gain1_f = gain_one.astype(jnp.float32)
    gain2_f = gain_two.astype(jnp.float32)
    grad_total = cotangent.astype(jnp.float32)
    grad_gates = jnp.sum(grad_total[:, None, :] * picked, -1)
    grad_picked = (
        (gate_vals[:, :, None] * grad_total[:, None, :])
        .astype(jnp.bfloat16)
        .reshape(TOK_DEV * TOPK, D)
    )
    grad_back = (
        jnp.zeros((EXPERTS * CAP, D), jnp.bfloat16)
        .at[slot_index]
        .set(grad_picked)
        .reshape(EXPERTS, CAP, D)
    )
    grad_arrived = lax.all_to_all(grad_back, "experts", split_axis=0, concat_axis=1, tiled=True)
    grad_expert_activation = jnp.einsum(
        "erd,efd->erf", grad_arrived, expert_down, preferred_element_type=jnp.float32
    )
    grad_expert_gate_preact = (
        grad_expert_activation * expert_up_preact * swish_derivative(expert_gate_preact)
    ).astype(jnp.bfloat16)
    grad_expert_up_preact = (grad_expert_activation * jax.nn.silu(expert_gate_preact)).astype(
        jnp.bfloat16
    )
    expert_grad_down = jnp.einsum(
        "erf,erd->edf", expert_activation, grad_arrived, preferred_element_type=jnp.float32
    )
    expert_grad_gate = jnp.einsum(
        "xvb,xva->xba", received_rows, grad_expert_gate_preact, preferred_element_type=jnp.float32
    )
    expert_grad_up = jnp.einsum(
        "xvb,xva->xba", received_rows, grad_expert_up_preact, preferred_element_type=jnp.float32
    )
    grad_einputs = jnp.einsum(
        "cgj,clj->cgl", grad_expert_gate_preact, expert_gate, preferred_element_type=jnp.float32
    )
    grad_einputs = (
        grad_einputs
        + jnp.einsum(
            "cgj,clj->cgl",
            grad_expert_up_preact,
            expert_up_weight,
            preferred_element_type=jnp.float32,
        )
    ).astype(jnp.bfloat16)
    grad_returned = lax.all_to_all(
        grad_einputs, "experts", split_axis=1, concat_axis=0, tiled=True
    ).reshape(EXPERTS * CAP, D)
    grad_moe_in = jnp.sum(
        grad_returned[slot_index].astype(jnp.float32).reshape(TOK_DEV, TOPK, D), 1
    )
    grad_rprobs = jnp.sum(grad_gates[:, :, None] * route_hot, 1)
    grad_logits = (
        route_probs * (grad_rprobs - jnp.sum(route_probs * grad_rprobs, -1, keepdims=True))
    ).astype(jnp.bfloat16)
    grad_router_local = inner_rows(hidden2, grad_logits)
    grad_total_b = grad_total.astype(jnp.bfloat16)
    grad_sdown = inner_rows(shared_act, grad_total_b)
    grad_sact = times_transposed(grad_total_b, w_sdown)
    grad_sgpre = (grad_sact * shared_upre * swish_derivative(shared_gpre)).astype(jnp.bfloat16)
    grad_supre = (grad_sact * jax.nn.silu(shared_gpre)).astype(jnp.bfloat16)
    grad_sgate = inner_rows(hidden2, grad_sgpre)
    grad_sup = inner_rows(hidden2, grad_supre)
    grad_hidden2 = (
        grad_moe_in
        + times_transposed(grad_logits, w_router)
        + times_transposed(grad_sgpre, w_sgate)
        + times_transposed(grad_supre, w_sup)
    )
    grad_gain2 = jnp.sum(grad_hidden2 * normed2, 0)
    grad_normed2 = grad_hidden2 * gain2_f
    grad_resid = (
        inv_rms2 * (grad_normed2 - normed2 * jnp.mean(grad_normed2 * normed2, -1, keepdims=True))
        + grad_total
    )
    grad_branch = grad_resid.astype(jnp.bfloat16)
    grad_wout = inner_rows(attended, grad_branch)
    grad_attended = (
        times_transposed(grad_branch, w_out).astype(jnp.bfloat16).reshape(TOK_DEV, HEADS, HD)
    )
    scores_again = jnp.where(
        allowed[None],
        0.125 * jnp.einsum("qhd,khd->hqk", query_h, keys_h, preferred_element_type=jnp.float32),
        -1e30,
    )
    probs_f = jnp.exp(scores_again - log_total)
    probs_b = probs_f.astype(jnp.bfloat16)
    grad_pattn = jnp.einsum(
        "qhd,khd->hqk", grad_attended, values_h, preferred_element_type=jnp.float32
    )
    grad_scores = (
        probs_f * (grad_pattn - jnp.sum(probs_f * grad_pattn, -1, keepdims=True))
    ).astype(jnp.bfloat16)
    grad_query = 0.125 * jnp.einsum(
        "hqk,khd->qhd", grad_scores, keys_h, preferred_element_type=jnp.float32
    ).reshape(TOK_DEV, D)
    grad_keys = 0.125 * jnp.einsum(
        "hqk,qhd->khd", grad_scores, query_h, preferred_element_type=jnp.float32
    ).reshape(-1, D)
    grad_values = jnp.einsum(
        "hqk,qhd->khd", probs_b, grad_attended, preferred_element_type=jnp.float32
    ).reshape(-1, D)
    prompt_span = contexts * PROMPT
    grad_pkeys, grad_pvalues = (
        lax.psum_scatter(
            grad_keys[:prompt_span].astype(jnp.bfloat16), "context", scatter_dimension=0, tiled=True
        ).astype(jnp.float32),
        lax.psum_scatter(
            grad_values[:prompt_span].astype(jnp.bfloat16),
            "context",
            scatter_dimension=0,
            tiled=True,
        ).astype(jnp.float32),
    )
    grad_key_all = jnp.concatenate([grad_pkeys, grad_keys[prompt_span:]], 0)
    grad_value_all = jnp.concatenate([grad_pvalues, grad_values[prompt_span:]], 0)
    grad_qpre = rotate(grad_query, cos_table, -sin_table).astype(jnp.bfloat16)
    grad_kpre = rotate(grad_key_all, cos_table, -sin_table).astype(jnp.bfloat16)
    grad_vpre = grad_value_all.astype(jnp.bfloat16)
    grad_wquery = inner_rows(hidden1, grad_qpre)
    grad_wkey = inner_rows(hidden1, grad_kpre)
    grad_wvalue = inner_rows(hidden1, grad_vpre)
    grad_hidden1 = (
        times_transposed(grad_qpre, w_query)
        + times_transposed(grad_kpre, w_key)
        + times_transposed(grad_vpre, w_value)
    )
    grad_gain1 = jnp.sum(grad_hidden1 * normed1, 0)
    grad_normed1 = grad_hidden1 * gain1_f
    grad_inputs = (
        inv_rms1 * (grad_normed1 - normed1 * jnp.mean(grad_normed1 * normed1, -1, keepdims=True))
        + grad_resid
    )
    shares = (
        lax.psum_scatter(
            grad_gain1.astype(jnp.bfloat16), "dp", scatter_dimension=0, tiled=True
        ).astype(jnp.float32),
        lax.psum_scatter(
            grad_wquery.astype(jnp.bfloat16), "dp", scatter_dimension=0, tiled=True
        ).astype(jnp.float32),
        lax.psum_scatter(
            grad_wkey.astype(jnp.bfloat16), "dp", scatter_dimension=0, tiled=True
        ).astype(jnp.float32),
        lax.psum_scatter(
            grad_wvalue.astype(jnp.bfloat16), "dp", scatter_dimension=0, tiled=True
        ).astype(jnp.float32),
        lax.psum_scatter(
            grad_wout.astype(jnp.bfloat16), "dp", scatter_dimension=0, tiled=True
        ).astype(jnp.float32),
        lax.psum_scatter(
            grad_gain2.astype(jnp.bfloat16), "dp", scatter_dimension=0, tiled=True
        ).astype(jnp.float32),
        lax.psum_scatter(
            grad_router_local.astype(jnp.bfloat16), "dp", scatter_dimension=0, tiled=True
        ).astype(jnp.float32),
        lax.psum_scatter(
            grad_sgate.astype(jnp.bfloat16), "dp", scatter_dimension=0, tiled=True
        ).astype(jnp.float32),
        lax.psum_scatter(
            grad_sup.astype(jnp.bfloat16), "dp", scatter_dimension=0, tiled=True
        ).astype(jnp.float32),
        lax.psum_scatter(
            grad_sdown.astype(jnp.bfloat16), "dp", scatter_dimension=0, tiled=True
        ).astype(jnp.float32),
    )
    totals = (
        lax.psum(shares[0].astype(jnp.bfloat16), ("context", "experts")).astype(jnp.float32),
        lax.psum(shares[1].astype(jnp.bfloat16), ("context", "experts")).astype(jnp.float32),
        lax.psum(shares[2].astype(jnp.bfloat16), ("context", "experts")).astype(jnp.float32),
        lax.psum(shares[3].astype(jnp.bfloat16), ("context", "experts")).astype(jnp.float32),
        lax.psum(shares[4].astype(jnp.bfloat16), ("context", "experts")).astype(jnp.float32),
        lax.psum(shares[5].astype(jnp.bfloat16), ("context", "experts")).astype(jnp.float32),
        lax.psum(shares[6].astype(jnp.bfloat16), ("context", "experts")).astype(jnp.float32),
        lax.psum(shares[7].astype(jnp.bfloat16), ("context", "experts")).astype(jnp.float32),
        lax.psum(shares[8].astype(jnp.bfloat16), ("context", "experts")).astype(jnp.float32),
        lax.psum(shares[9].astype(jnp.bfloat16), ("context", "experts")).astype(jnp.float32),
    )
    summed_gate, summed_up, summed_down = (
        lax.psum_scatter(
            expert_grad_gate.astype(jnp.bfloat16),
            ("dp", "context"),
            scatter_dimension=2,
            tiled=True,
        ).astype(jnp.float32),
        lax.psum_scatter(
            expert_grad_up.astype(jnp.bfloat16), ("dp", "context"), scatter_dimension=2, tiled=True
        ).astype(jnp.float32),
        lax.psum_scatter(
            expert_grad_down.astype(jnp.bfloat16),
            ("dp", "context"),
            scatter_dimension=2,
            tiled=True,
        ).astype(jnp.float32),
    )
    summed_down = jnp.transpose(summed_down, (0, 2, 1))
    return (
        layer_out,
        grad_inputs,
        totals[0],
        totals[1],
        totals[2],
        totals[3],
        totals[4],
        totals[5],
        totals[6],
        totals[7],
        totals[8],
        totals[9],
        summed_gate,
        summed_up,
        summed_down,
    )


def solution(mesh):
    return jax.shard_map(
        body,
        mesh=mesh,
        in_specs=(
            P(("dp", "context", "experts"), None),
            P(("dp", "context", "experts"), None),
            P(("dp", "context", "experts"), None),
            P(("dp", "context", "experts")),
            P("dp"),
            P("dp", None),
            P("dp", None),
            P("dp", None),
            P("dp", None),
            P("dp"),
            P("dp", None),
            P("dp", None),
            P("dp", None),
            P("dp", None),
            P("experts", None, None),
            P("experts", None, None),
            P("experts", None, None),
        ),
        out_specs=(
            P(("dp", "context", "experts"), None),
            P(("dp", "context", "experts"), None),
            P("dp"),
            P("dp", None),
            P("dp", None),
            P("dp", None),
            P("dp", None),
            P("dp"),
            P("dp", None),
            P("dp", None),
            P("dp", None),
            P("dp", None),
            P("experts", None, ("dp", "context")),
            P("experts", None, ("dp", "context")),
            P("experts", ("dp", "context"), None),
        ),
        check_vma=False,
    )
```

profile of v0, /device:TPU:0, one launch (start us, length us, event | category | flops | bytes accessed | tf_op | source)
XLA Modules:
  0.0 1475.5 jit_solution(697850950132666756)
XLA Ops:
  15.9 13.7 all-reduce.7
  32.2 10.9 all-gather.9.cloned.1.call-done
  45.8 28.3 %all-gather.11.cloned.1.call-done = bf16[768,768]{1,0:T(8,128)(2,1)} async-done(((bf16[192,768]{1,0:T(8,128)(2,1)}), bf16[768,768]{1,0:T(8,128)(2,1)}) %all-gather.11.cloned.1.call-update) | async-done | bytes 1179664 | tf_op jit(solution)/shard_map/all_gather | solution.py:113
  76.3 29.0 %all-gather.13.cloned.1.call-done = bf16[768,768]{1,0:T(8,128)(2,1)} async-done(((bf16[192,768]{1,0:T(8,128)(2,1)}), bf16[768,768]{1,0:T(8,128)(2,1)}) %all-gather.13.cloned.1.call-update) | async-done | bytes 1179664 | tf_op jit(solution)/shard_map/all_gather | solution.py:114
  110.1 10.9 all_gather.48
  121.8 11.0 all_gather.51
  135.4 2.9 fusion
  139.6 4.9 fusion.26
  148.7 3.7 reshape.665
  152.4 7.5 scatter_custom_fusion
  162.5 4.5 all-to-all-start
  169.8 4.1 mul.536
  173.9 13.7 all-gather
  189.1 10.0 scatter_custom_fusion.1
  200.5 4.6 all-to-all-start.2
  207.4 11.5 fusion.41
  218.9 5.8 fusion.39
  224.8 2.6 all-to-all-done.2
  229.5 21.4 %multiply_convert_fusion.1 = (bf16[4,264,2048]{2,1,0:T(8,128)(2,1)}, bf16[4,264,2048]{2,1,0:T(8,128)(2,1)}, bf16[4,264,2048]{2,1,0:T(8,128)(2,1)}) fusion(f32[4,264,2048]{2,1,0:T(8,128)} %fusion.41, f32[4,264,2048]{2,1,0:T(8,128)} %fusion.39, bf16[4,2048,768]{2,1,0:T(8,128)(2,1)} %param.33, bf16[4,264,768]{2,0,1:T(4,128)(2,1)S(1)} %bitcast.150), kind=kOutput, calls=%fused_computation.12 | convolution fusion | flops 3354329088 | bytes 44482560 | tf_op jit(solution)/shard_map/erd,efd->erf/dot_general | solution.py:227
  250.9 9.4 convolution_convert_fusion.6
  262.1 4.0 all-to-all-start.1
  266.0 11.4 fusion.99
  277.4 11.5 add_convert_fusion
  288.9 3.2 copy.142
  292.2 4.4 all-to-all-start.3
  302.7 3.4 gather_fusion
  306.1 3.7 reshape.643
  309.8 7.4 all-to-all-done.3
  317.3 2.9 copy.143
  321.8 3.4 gather_fusion.1
  325.2 3.8 reshape.644
  329.0 6.6 multiply_reduce_fusion.1
  335.7 5.6 reduce_sum.164
  341.4 5.0 fusion.100
  346.4 4.9 fusion.98
  351.4 6.8 multiply_convert_fusion.5
  366.6 10.3 multiply_reduce_fusion
  376.9 4.4 multiply_convert_fusion
  385.6 7.5 fusion.22
  398.8 5.8 fusion.19
  411.8 9.7 reduce-scatter.18.cloned.1.call-done
  421.5 3.0 convolution_convert_fusion.8
  424.6 4.9 convolution_convert_fusion.5
  429.6 4.9 convolution_convert_fusion.4
  435.6 4.9 convolution_convert_fusion.3
  442.3 10.6 reduce-scatter.26.cloned.1.call-done
  452.9 30.2 %reduce-scatter.20.cloned.1.call-done = bf16[192,768]{1,0:T(8,128)(2,1)} async-done(((bf16[768,768]{1,0:T(8,128)(2,1)}), bf16[192,768]{1,0:T(8,128)(2,1)}) %reduce-scatter.20.cloned.1.call-update) | async-done | bytes 294928 | tf_op jit(solution)/shard_map/reduce_scatter | solution.py:349
  483.1 30.1 %reduce-scatter.22.cloned.1.call-done = bf16[192,768]{1,0:T(8,128)(2,1)} async-done(((bf16[768,768]{1,0:T(8,128)(2,1)}), bf16[192,768]{1,0:T(8,128)(2,1)}) %reduce-scatter.22.cloned.1.call-update) | async-done | bytes 294928 | tf_op jit(solution)/shard_map/reduce_scatter | solution.py:352
  513.2 30.2 %reduce-scatter.24.cloned.1.call-done = bf16[192,768]{1,0:T(8,128)(2,1)} async-done(((bf16[768,768]{1,0:T(8,128)(2,1)}), bf16[192,768]{1,0:T(8,128)(2,1)}) %reduce-scatter.24.cloned.1.call-update) | async-done | bytes 294928 | tf_op jit(solution)/shard_map/reduce_scatter | solution.py:355
  543.4 61.8 %reduce-scatter.28.cloned.1.call-done = bf16[192,2048]{1,0:T(8,128)(2,1)} async-done(((bf16[768,2048]{1,0:T(8,128)(2,1)}), bf16[192,2048]{1,0:T(8,128)(2,1)}) %reduce-scatter.28.cloned.1.call-update) | async-done | bytes 786448 | tf_op jit(solution)/shard_map/reduce_scatter | solution.py:367
  605.2 63.0 %reduce-scatter.30.cloned.1.call-done = bf16[192,2048]{1,0:T(8,128)(2,1)} async-done(((bf16[768,2048]{1,0:T(8,128)(2,1)}), bf16[192,2048]{1,0:T(8,128)(2,1)}) %reduce-scatter.30.cloned.1.call-update) | async-done | bytes 786448 | tf_op jit(solution)/shard_map/reduce_scatter | solution.py:370
  668.2 63.0 %reduce-scatter.32.cloned.1.call-done = bf16[512,768]{1,0:T(8,128)(2,1)} async-done(((bf16[2048,768]{1,0:T(8,128)(2,1)}), bf16[512,768]{1,0:T(8,128)(2,1)}) %reduce-scatter.32.cloned.1.call-update) | async-done | bytes 786448 | tf_op jit(solution)/shard_map/reduce_scatter | solution.py:373
  732.7 12.1 convolution_convert_fusion
  746.3 12.1 convolution_convert_fusion.2
  758.4 12.0 convolution_convert_fusion.1
  772.7 5.1 fusion.27
  781.8 10.5 all-reduce.6
  792.4 12.7 all-reduce.4
  808.2 23.2 %all-reduce.10.cloned.1.call-done = (bf16[192,768]{1,0:T(8,128)(2,1)}, bf16[192,768]{1,0:T(8,128)(2,1)}, bf16[192,768]{1,0:T(8,128)(2,1)}, bf16[192,768]{1,0:T(8...) async-done(((bf16[192,768]{1,0:T(8,128)(2,1)}, bf16[192,768]{1,0:T(8,128)(2,1)}, bf16[192,768]{1,0:T(8,128)(2,1)}, ...) | async-done | bytes 3538960 | tf_op jit(solution)/shard_map/psum | solution.py:379
  840.8 202.6 %reduce-scatter.38.cloned.1.call-done = bf16[4,768,256]{2,1,0:T(8,128)(2,1)} async-done(((bf16[4,768,2048]{2,1,0:T(8,128)(2,1)}), bf16[4,768,256]{2,1,0:T(8,128)(2,1)}) %reduce-scatter.38.cloned.1.call-update) | async-done | bytes 1572880 | tf_op jit(solution)/shard_map/reduce_scatter | solution.py:399
  1047.4 206.7 %reduce-scatter.34.cloned.1.call-done = bf16[4,768,256]{2,1,0:T(8,128)(2,1)} async-done(((bf16[4,768,2048]{2,1,0:T(8,128)(2,1)}), bf16[4,768,256]{2,1,0:T(8,128)(2,1)}) %reduce-scatter.34.cloned.1.call-update) | async-done | bytes 1572880 | tf_op jit(solution)/shard_map/reduce_scatter | solution.py:390
  1254.1 3.3 convert_element_type.364
  1257.5 207.6 %reduce-scatter.36.cloned.1.call-done = bf16[4,768,256]{2,1,0:T(8,128)(2,1)} async-done(((bf16[4,768,2048]{2,1,0:T(8,128)(2,1)}), bf16[4,768,256]{2,1,0:T(8,128)(2,1)}) %reduce-scatter.36.cloned.1.call-update) | async-done | bytes 1572880 | tf_op jit(solution)/shard_map/reduce_scatter | solution.py:396
  1465.1 3.3 convert_element_type.366
  (331 shorter events, 104.2 us)
Async XLA Ops:
  7.2 35.8 %all-gather.9.cloned.1.call-start = ((), (), s32[]{:S(2)}) async-start(), calls=%async_computation.17 | async-start | bytes 1474560 | tf_op jit(solution)/shard_map/all_gather | solution.py:115
  7.9 66.2 %all-gather.11.cloned.1.call-start = ((), (), s32[]{:S(2)}) async-start(), calls=%async_computation.18 | async-start | bytes 1474560 | tf_op jit(solution)/shard_map/all_gather | solution.py:113
  8.7 96.6 %all-gather.13.cloned.1.call-start = ((), (), s32[]{:S(2)}) async-start(), calls=%async_computation.19 | async-start | bytes 1474560 | tf_op jit(solution)/shard_map/all_gather | solution.py:114
  9.4 4.7 copy-start.65
  9.4 6.0 copy-start.71
  9.4 6.2 copy-start.72
  9.4 20.2 %copy-start.8 = (bf16[384,768]{1,0:T(8,128)(2,1)S(1)}, bf16[384,768]{1,0:T(8,128)(2,1)}, u32[]{:S(2)}) copy-start(bf16[384,768]{1,0:T(8,128)(2,1)} %param.17) | copy-start | bytes 1769476
  9.5 135.1 %all-gather.15.cloned.1.call-start = ((), (), s32[]{:S(2)}) async-start(), calls=%async_computation.20 | async-start | bytes 1474560 | tf_op jit(solution)/shard_map/all_gather | solution.py:116
  10.0 20.5 %copy-start.66 = (s32[2]{0:T(128)S(1)}, s32[2]{0:T(128)}, u32[]{:S(2)}) copy-start(s32[2]{0:T(128)} %param.20) | copy-start | bytes 28
  10.0 331.3 %all-gather.21.cloned.1.call-start = ((), (), s32[]{:S(2)}) async-start(), calls=%async_computation.23 | async-start | bytes 3932160 | tf_op jit(solution)/shard_map/all_gather | solution.py:121
  10.6 335.8 %all-gather.19.cloned.1.call-start = ((), (), s32[]{:S(2)}) async-start(), calls=%async_computation.22 | async-start | bytes 3932160 | tf_op jit(solution)/shard_map/all_gather | solution.py:120
  29.6 75.7 %copy-start.57 = (f32[768]{0:T(1024)}, f32[768]{0:T(1024)S(1)}, u32[]{:S(2)}) copy-start(f32[768]{0:T(1024)S(1)} %convert_element_type.305) | copy-start | bytes 9220
  29.8 75.5 %copy-start.60 = (f32[384]{0:T(512)}, f32[384]{0:T(512)S(1)}, u32[]{:S(2)}) copy-start(f32[384]{0:T(512)S(1)} %add_rsqrt_fusion.1) | copy-start | bytes 4612
  31.5 76.0 %copy-start.46 = (f32[384,32]{0,1:T(8,128)}, f32[384,32]{0,1:T(8,128)S(1)}, u32[]{:S(2)}) copy-start(f32[384,32]{0,1:T(8,128)S(1)} %get-tuple-element.130) | copy-start | bytes 147460
  32.1 106.2 %copy-start.14 = (pred[384,640]{1,0:T(8,128)(4,1)}, pred[384,640]{1,0:T(8,128)(4,1)S(1)}, u32[]{:S(2)}) copy-start(pred[384,640]{1,0:T(8,128)(4,1)S(1)} %fusion.45) | copy-start | bytes 737284
  108.5 24.3 %copy-start.26 = (bf16[384,12,32]{0,2,1:T(8,128)(2,1)}, bf16[384,12,32]{0,2,1:T(8,128)(2,1)S(1)}, u32[]{:S(2)}) copy-start(bf16[384,12,32]{0,2,1:T(8,128)(2,1)S(1)} %get-tuple-element.120) | copy-start | bytes 884740
  108.6 12.5 slice-start.7
  121.1 11.6 copy-start.44
  121.7 16.6 %copy-start.25 = (bf16[640,768]{0,1:T(8,128)(2,1)}, bf16[640,768]{0,1:T(8,128)(2,1)S(1)}, u32[]{:S(2)}) copy-start(bf16[640,768]{0,1:T(8,128)(2,1)S(1)} %copy.123) | copy-start | bytes 2949124
  121.8 11.1 copy-start.28
  135.3 4.3 copy-start
  146.8 216.6 %copy-start.6 = (f32[384,768]{1,0:T(8,128)}, f32[384,768]{1,0:T(8,128)S(1)}, u32[]{:S(2)}) copy-start(f32[384,768]{1,0:T(8,128)S(1)} %get-tuple-element.136) | copy-start | bytes 3538948
  147.0 40.7 %copy-start.9 = (bf16[384,768]{1,0:T(8,128)(2,1)}, bf16[384,768]{1,0:T(8,128)(2,1)S(1)}, u32[]{:S(2)}) copy-start(bf16[384,768]{1,0:T(8,128)(2,1)S(1)} %multiply_convert_fusion.9) | copy-start | bytes 1769476
  162.5 5.3 copy-start.16
  162.5 38.0 %all-to-all-start = ((bf16[16,66,768]{2,1,0:T(8,128)(2,1)}), bf16[16,66,768]{2,1,0:T(8,128)(2,1)}, u32[]{:S(2)}, u32[]{:S(2)}) async-start(bf16[16,66,768]{2,1,0:T(8,128)(2,1)} %reshape.637), calls=%async_computation | async-start | bytes 3538944 | tf_op jit(solution)/shard_map/all_to_all | solution.py:182
  167.0 184.3 %all-gather.17.cloned.1.call-start = ((), (), s32[]{:S(2)}) async-start(), calls=%async_computation.21 | async-start | bytes 3932160 | tf_op jit(solution)/shard_map/all_gather | solution.py:119
  169.8 4.1 copy-start.64
  200.5 26.9 %all-to-all-start.2 = ((bf16[16,66,768]{2,1,0:T(8,128)(2,1)}), bf16[16,66,768]{2,1,0:T(8,128)(2,1)}, u32[]{:S(2)}, u32[]{:S(2)}) async-start(bf16[16,66,768]{2,1,0:T(8,128)(2,1)} %reshape.639), calls=%async_computation.2 | async-start | bytes 3538944 | tf_op jit(solution)/shard_map/all_to_all | solution.py:226
  205.1 13.8 slice-start.3
  207.4 11.5 copy-start.4
  207.4 11.5 slice-start.4
  207.4 11.5 slice-start.5
  229.5 21.4 %copy-start.36 = (bf16[4,4,66,768]{3,1,2,0:T(4,128)(2,1)}, bf16[4,4,66,768]{3,1,2,0:T(4,128)(2,1)S(1)}, u32[]{:S(2)}) copy-start(bf16[4,4,66,768]{3,1,2,0:T(4,128)(2,1)S(1)} %copy.155) | copy-start | bytes 4866052
  262.1 30.1 %all-to-all-start.1 = ((bf16[4,264,768]{2,0,1:T(4,128)(2,1)}), bf16[4,264,768]{2,0,1:T(4,128)(2,1)S(1)}, u32[]{:S(2)}, u32[]{:S(2)}) async-start(bf16[4,264,768]{2,0,1:T(4,128)(2,1)} %copy.136), calls=%async_computation.1 | async-start | bytes 3244032 | tf_op jit(solution)/shard_map/all_to_all | solution.py:193
  292.2 25.1 %all-to-all-start.3 = ((bf16[4,264,768]{2,0,1:T(4,128)(2,1)}), bf16[4,264,768]{2,0,1:T(4,128)(2,1)}, u32[]{:S(2)}, u32[]{:S(2)}) async-start(bf16[4,264,768]{2,0,1:T(4,128)(2,1)} %copy.142), calls=%async_computation.3 | async-start | bytes 3244032 | tf_op jit(solution)/shard_map/all_to_all | solution.py:257
  296.6 108.0 %reduce-scatter.16.cloned.1.call-start = ((), (), s32[]{:S(2)}) async-start(), calls=%async_computation.24 | async-start | bytes 1179648 | tf_op jit(solution)/shard_map/reduce_scatter | solution.py:316
  335.7 5.7 copy-start.17
  341.3 21.3 %copy-start.55 = (bf16[384,16]{0,1:T(8,128)(2,1)}, bf16[384,16]{0,1:T(8,128)(2,1)S(1)}, u32[]{:S(2)}) copy-start(bf16[384,16]{0,1:T(8,128)(2,1)S(1)} %multiply_convert_fusion.10) | copy-start | bytes 36868
  341.3 5.1 copy-start.10
  351.4 6.8 copy-start.67
  366.6 10.3 slice-start
  366.6 10.3 slice-start.1
  366.6 10.3 slice-start.2
  376.9 4.4 copy-start.27
  384.7 36.7 %reduce-scatter.18.cloned.1.call-start = ((), (), s32[]{:S(2)}) async-start(), calls=%async_computation.25 | async-start | bytes 1179648 | tf_op jit(solution)/shard_map/reduce_scatter | solution.py:319
  395.0 57.8 %reduce-scatter.26.cloned.1.call-start = ((), (), s32[]{:S(2)}) async-start(), calls=%async_computation.29 | async-start | bytes 1474560 | tf_op jit(solution)/shard_map/reduce_scatter | solution.py:358
  397.6 85.5 %reduce-scatter.20.cloned.1.call-start = ((), (), s32[]{:S(2)}) async-start(), calls=%async_computation.26 | async-start | bytes 1474560 | tf_op jit(solution)/shard_map/reduce_scatter | solution.py:349
  398.8 7.0 slice-start.6
  408.6 104.5 %reduce-scatter.22.cloned.1.call-start = ((), (), s32[]{:S(2)}) async-start(), calls=%async_computation.27 | async-start | bytes 1474560 | tf_op jit(solution)/shard_map/reduce_scatter | solution.py:352
  410.8 132.7 %reduce-scatter.24.cloned.1.call-start = ((), (), s32[]{:S(2)}) async-start(), calls=%async_computation.28 | async-start | bytes 1474560 | tf_op jit(solution)/shard_map/reduce_scatter | solution.py:355
  411.8 12.8 copy-start.53
  424.5 180.7 %reduce-scatter.28.cloned.1.call-start = ((), (), s32[]{:S(2)}) async-start(), calls=%async_computation.30 | async-start | bytes 3932160 | tf_op jit(solution)/shard_map/reduce_scatter | solution.py:367
  429.5 238.7 %reduce-scatter.30.cloned.1.call-start = ((), (), s32[]{:S(2)}) async-start(), calls=%async_computation.31 | async-start | bytes 3932160 | tf_op jit(solution)/shard_map/reduce_scatter | solution.py:370
  434.5 296.7 %reduce-scatter.32.cloned.1.call-start = ((), (), s32[]{:S(2)}) async-start(), calls=%async_computation.32 | async-start | bytes 3932160 | tf_op jit(solution)/shard_map/reduce_scatter | solution.py:373
  440.5 330.7 %reduce-scatter.40.cloned.1.call-start = ((), (), s32[]{:S(2)}) async-start(), calls=%async_computation.36 | async-start | bytes 245760
  442.2 389.2 %all-reduce.10.cloned.1.call-start = ((), (), s32[]{:S(2)}) async-start(), calls=%async_computation.37 | async-start | bytes 7077888 | tf_op jit(solution)/shard_map/psum | solution.py:379
  731.3 312.1 %reduce-scatter.38.cloned.1.call-start = ((), (), s32[]{:S(2)}) async-start(), calls=%async_computation.35 | async-start | bytes 14155776 | tf_op jit(solution)/shard_map/reduce_scatter | solution.py:399
  744.8 509.3 %reduce-scatter.34.cloned.1.call-start = ((), (), s32[]{:S(2)}) async-start(), calls=%async_computation.33 | async-start | bytes 14155776 | tf_op jit(solution)/shard_map/reduce_scatter | solution.py:390
  758.4 706.7 %reduce-scatter.36.cloned.1.call-start = ((), (), s32[]{:S(2)}) async-start(), calls=%async_computation.34 | async-start | bytes 14155776 | tf_op jit(solution)/shard_map/reduce_scatter | solution.py:396
  772.7 5.1 copy-start.21
  772.7 5.1 copy-start.31
  780.7 11.7 copy-start.62
  831.4 4.6 copy-start.48
  831.4 5.5 copy-start.43
  (45 other events, 81.4 us)
Sparse Core Ops, SparseCore 0:
  9.6 33.3 all-gather.8
  44.6 29.4 all-gather.10
  75.7 29.5 all-gather.12
  106.7 29.5 all-gather.14
  137.7 63.0 all-gather.20
  202.2 62.1 all-gather.18
  266.0 62.1 all-gather.16
  384.9 16.7 reduce-scatter.15
  404.0 17.4 reduce-scatter.17
  423.6 29.1 reduce-scatter.25
  455.2 27.8 reduce-scatter.19
  485.3 27.8 reduce-scatter.21
  515.5 27.8 reduce-scatter.23
  546.2 58.9 reduce-scatter.27
  607.9 60.2 reduce-scatter.29
  671.0 60.2 reduce-scatter.31
  733.9 19.3 reduce-scatter.39
  758.0 73.4 all-reduce.9
  835.5 207.8 reduce-scatter.37
  1047.2 206.8 reduce-scatter.33
  1258.2 206.8 reduce-scatter.35
where the time goes:
time: 1480 us
  waiting for transfers between devices  1020 us (69%)
  matrix products  202 us (14%)
  local copies, waits for them, and re-layouts  81.8 us (6%)
  blocking collectives  72.5 us (5%)
  other arithmetic  62.4 us (4%)
  starting transfers between devices  18.7 us (1%)
  between operations  17 us (1%)
    reduce_scatter x1, waiting for transfers between devices, body(): lax.psum_scatter(expert_grad_up.astype(jnp.bfloat16), ('dp', 'context'),...  208 us
    reduce_scatter x1, waiting for transfers between devices, body(): lax.psum_scatter(expert_grad_gate.astype(jnp.bfloat16), ('dp', 'context')...  207 us
    reduce_scatter x1, waiting for transfers between devices, body(): lax.psum_scatter(expert_grad_down.astype(jnp.bfloat16), ('dp', 'context')...  203 us
    reduce_scatter x1, waiting for transfers between devices, body(): lax.psum_scatter(grad_sdown.astype(jnp.bfloat16), 'dp', scatter_dimension...  63 us
    reduce_scatter x1, waiting for transfers between devices, body(): lax.psum_scatter(grad_sup.astype(jnp.bfloat16), 'dp', scatter_dimension=0...  63 us
    reduce_scatter x1, waiting for transfers between devices, body(): lax.psum_scatter(grad_sgate.astype(jnp.bfloat16), 'dp', scatter_dimension...  61.8 us
    reduce_scatter x1, waiting for transfers between devices, body(): lax.psum_scatter(grad_wquery.astype(jnp.bfloat16), 'dp', scatter_dimensio...  30.2 us
    reduce_scatter x1, waiting for transfers between devices, body(): lax.psum_scatter(grad_wvalue.astype(jnp.bfloat16), 'dp', scatter_dimensio...  30.2 us
  transfers between devices with their start and end apart: 25, of which 17 were waited for; matrix products, arithmetic and copies ran while one was open for 20% of the time, Pallas kernels for 0%

commit v1 on v0

--- a/solution.py
+++ b/solution.py
@@ -1,7 +1,12 @@
+import functools
+
 import jax
 import jax.numpy as jnp
 from jax import lax
 from jax.sharding import PartitionSpec as P
+
+from jax.experimental import pallas as pl
+from jax.experimental.pallas import tpu as pltpu
 
 D = 768
 HEADS = 12
@@ -87,7 +92,7 @@
     return sigma * (1.0 + pre_act * (1.0 - sigma))
 
 
-def body(
+def plain_body(
     tokens,
     cotangent,
     routes,
@@ -423,9 +428,766 @@
     )
 
 
+TUNED_MESH = {"dp": 4, "context": 2, "experts": 4}
+AXES = ("dp", "context", "experts")
+SLOT = 72
+EXT = 16
+ROWS = TOK_DEV + EXT
+BF = jnp.bfloat16
+F32 = jnp.float32
+VMEM_LIMIT = 60 * 1024 * 1024
+
+
+def moved(value, target):
+    pairs = []
+    for z in range(4):
+        for y in range(2):
+            for x in range(2):
+                for c in range(2):
+                    tz, ty, tx, tc = target(z, y, x, c)
+                    pairs.append((((z * 2 + y) * 2 + x) * 2 + c, ((tz * 2 + ty) * 2 + tx) * 2 + tc))
+    return lax.ppermute(value, AXES, pairs)
+
+
+def over_core(value):
+    return moved(value, lambda z, y, x, c: (z, y, x, 1 - c))
+
+
+def over_x(value):
+    return moved(value, lambda z, y, x, c: (z, y, 1 - x, c))
+
+
+def over_a(value):
+    return moved(value, lambda z, y, x, c: (z, y, 1 - x, c) if c == 0 else (z, 1 - y, x, c))
+
+
+def over_b(value):
+    return moved(value, lambda z, y, x, c: (z, 1 - y, x, c) if c == 0 else (z, y, 1 - x, c))
+
+
+def over_z(value, step):
+    return moved(value, lambda z, y, x, c: ((z + step) % 4, y, x, c))
+
+
+def gather_blocks(block):
+    column = jnp.stack([block] + [over_z(block, step) for step in (1, 2, 3)])
+    first = over_a(column)
+    second = over_b(column)
+    third = over_b(first)
+    mine = [column, first, second, third]
+    return mine + [over_core(part) for part in mine]
+
+
+def gather_rows(shard, core):
+    half = shard.shape[0] // 2
+    part = lax.dynamic_slice_in_dim(shard, core * half, half, 0)
+    part = lax.all_gather(part, "dp", axis=0, tiled=False)
+    other = over_core(part)
+    both = jnp.where(core == 0, jnp.stack([part, other], 1), jnp.stack([other, part], 1))
+    return both.reshape(-1, shard.shape[1])
+
+
+def contract(left, right, left_dim, right_dim):
+    return lax.dot_general(
+        left, right, (((left_dim,), (right_dim,)), ((), ())), preferred_element_type=F32
+    )
+
+
+def one_hot_rows(rank_row):
+    slots = lax.broadcasted_iota(jnp.int32, (SLOT, TOK_DEV), 0).astype(F32)
+    return (slots == rank_row).astype(F32)
+
+
+def swish_parts(pre_act):
+    sigma = jax.nn.sigmoid(pre_act)
+    return pre_act * sigma, sigma * (1.0 + pre_act * (1.0 - sigma))
+
+
+def group_kernel(
+    base_ref,
+    h_ref,
+    g_ref,
+    wg_ref,
+    wu_ref,
+    wd_ref,
+    moe_ref,
+    dx_ref,
+    rank_sc,
+    prob_sc,
+    x_sc,
+    gd_sc,
+    gate_sc,
+    y_sc,
+    acc_sc,
+    dgate_sc,
+    ysel_sc,
+    dsel_sc,
+    drp_sc,
+):
+    e = pl.program_id(0)
+    f = pl.program_id(1)
+    blocks = h_ref.shape[0]
+    experts = pl.num_programs(0)
+    base = base_ref[0]
+
+    @pl.when((e == 0) & (f == 0))
+    def _():
+        for b in range(blocks):
+            rank_sc[b] = g_ref[b, TOK_DEV:, :TOK_DEV].astype(F32)
+            prob_sc[b] = h_ref[b, TOK_DEV:, :TOK_DEV].astype(F32) + h_ref[
+                b, TOK_DEV:, TOK_DEV:
+            ].astype(F32)
+        drp_sc[...] = jnp.zeros_like(drp_sc)
+
+    @pl.when(f == 0)
+    def _():
+        for pair in range(blocks // 2):
+            rows_x, rows_g = [], []
+            for b in (2 * pair, 2 * pair + 1):
+                hot = one_hot_rows(rank_sc[b, pl.ds(base + e, 1), :])
+                gate_sc[b * SLOT : (b + 1) * SLOT, :] = jnp.sum(
+                    hot * prob_sc[b, pl.ds(base + e, 1), :], -1, keepdims=True
+                )
+                hot = hot.astype(BF)
+                rows_x.append(jnp.dot(hot, h_ref[b, :TOK_DEV, :], preferred_element_type=F32))
+                rows_g.append(jnp.dot(hot, g_ref[b, :TOK_DEV, :], preferred_element_type=F32))
+            span = slice(pair * 2 * SLOT, (pair + 1) * 2 * SLOT)
+            x_sc[span, :] = jnp.concatenate(rows_x, 0).astype(BF)
+            gd_sc[span, :] = jnp.concatenate(rows_g, 0).astype(BF)
+        y_sc[...] = jnp.zeros_like(y_sc)
+        acc_sc[...] = jnp.zeros_like(acc_sc)
+        dgate_sc[...] = jnp.zeros_like(dgate_sc)
+
+    rows = x_sc[...]
+    gate_pre = jnp.dot(rows, wg_ref[0], preferred_element_type=F32)
+    up_pre = jnp.dot(rows, wu_ref[0], preferred_element_type=F32)
+    back = contract(gd_sc[...], wd_ref[0], 1, 1)
+    swish, slope = swish_parts(gate_pre)
+    inner = (swish * up_pre).astype(BF)
+    dgate_sc[...] += jnp.sum(back * inner.astype(F32), -1, keepdims=True)
+    back = back * gate_sc[...]
+    dgate_pre = (back * up_pre * slope).astype(BF)
+    dup_pre = (back * swish).astype(BF)
+    y_sc[...] += jnp.dot(inner, wd_ref[0], preferred_element_type=F32)
+    acc_sc[...] += contract(dgate_pre, wg_ref[0], 1, 1) + contract(dup_pre, wu_ref[0], 1, 1)
+
+    @pl.when(f == pl.num_programs(1) - 1)
+    def _():
+        for b in range(blocks):
+            span = slice(b * SLOT, (b + 1) * SLOT)
+            into = pl.ds(pl.multiple_of(e * SLOT, 8), SLOT)
+            ysel_sc[b, into, :] = y_sc[span, :] * gate_sc[span, :]
+            dsel_sc[b, into, :] = acc_sc[span, :]
+            hot = one_hot_rows(rank_sc[b, pl.ds(base + e, 1), :])
+            drp_sc[b, pl.ds(base + e, 1), :] = jnp.sum(hot * dgate_sc[span, :], 0, keepdims=True)
+
+    @pl.when((f == pl.num_programs(1) - 1) & (e == experts - 1))
+    def _():
+        for b in range(blocks):
+            hot = jnp.concatenate(
+                [
+                    one_hot_rows(rank_sc[b, pl.ds(base + i, 1), :])
+                    for i in range(ysel_sc.shape[1] // SLOT)
+                ],
+                0,
+            ).astype(BF)
+            moe_ref[b] = contract(hot, ysel_sc[b].astype(BF), 0, 0).astype(BF)
+            dx_ref[b, :TOK_DEV, :] = contract(hot, dsel_sc[b].astype(BF), 0, 0).astype(BF)
+            high = drp_sc[b].astype(BF)
+            dx_ref[b, TOK_DEV:, :TOK_DEV] = high
+            dx_ref[b, TOK_DEV:, TOK_DEV:] = (drp_sc[b] - high.astype(F32)).astype(BF)
+
+
+def group_experts(base, h_group, g_group, w_gate, w_up, w_down):
+    blocks = h_group.shape[0]
+    experts, _, ff = w_gate.shape
+    tile = 512
+    whole = lambda *shape: pl.BlockSpec(shape, lambda e, f, s: (0,) * len(shape))
+    return pl.pallas_call(
+        group_kernel,
+        out_shape=(
+            jax.ShapeDtypeStruct((blocks, TOK_DEV, D), BF),
+            jax.ShapeDtypeStruct((blocks, ROWS, D), BF),
+        ),
+        grid_spec=pltpu.PrefetchScalarGridSpec(
+            num_scalar_prefetch=1,
+            grid=(experts, ff // tile),
+            in_specs=[
+                whole(blocks, ROWS, D),
+                whole(blocks, ROWS, D),
+                pl.BlockSpec((1, D, tile), lambda e, f, s: (e, 0, f)),
+                pl.BlockSpec((1, D, tile), lambda e, f, s: (e, 0, f)),
+                pl.BlockSpec((1, tile, D), lambda e, f, s: (e, f, 0)),
+            ],
+            out_specs=[whole(blocks, TOK_DEV, D), whole(blocks, ROWS, D)],
+            scratch_shapes=[
+                pltpu.VMEM((blocks, EXPERTS, TOK_DEV), F32),
+                pltpu.VMEM((blocks, EXPERTS, TOK_DEV), F32),
+                pltpu.VMEM((blocks * SLOT, D), BF),
+                pltpu.VMEM((blocks * SLOT, D), BF),
+                pltpu.VMEM((blocks * SLOT, 1), F32),
+                pltpu.VMEM((blocks * SLOT, D), F32),
+                pltpu.VMEM((blocks * SLOT, D), F32),
+                pltpu.VMEM((blocks * SLOT, 1), F32),
+                pltpu.VMEM((blocks, experts * SLOT, D), F32),
+                pltpu.VMEM((blocks, experts * SLOT, D), F32),
+                pltpu.VMEM((blocks, EXPERTS, TOK_DEV), F32),
+            ],
+        ),
+        compiler_params=pltpu.CompilerParams(vmem_limit_bytes=VMEM_LIMIT),
+        cost_estimate=pl.CostEstimate(
+            flops=2 * 6 * experts * blocks * SLOT * D * ff,
+            bytes_accessed=2 * 3 * experts * D * ff,
+            transcendentals=0,
+        ),
+        name="group_experts",
+    )(base, h_group, g_group, w_gate, w_up, w_down)
+
+
+def shared_kernel(h_ref, g_ref, wg_ref, wu_ref, wd_ref, out_ref, dh_ref):
+    @pl.when(pl.program_id(0) == 0)
+    def _():
+        out_ref[...] = jnp.zeros_like(out_ref)
+        dh_ref[...] = jnp.zeros_like(dh_ref)
+
+    gate_pre = jnp.dot(h_ref[...], wg_ref[...], preferred_element_type=F32)
+    up_pre = jnp.dot(h_ref[...], wu_ref[...], preferred_element_type=F32)
+    back = contract(g_ref[...], wd_ref[...], 1, 1)
+    swish, slope = swish_parts(gate_pre)
+    inner = (swish * up_pre).astype(BF)
+    out_ref[...] += jnp.dot(inner, wd_ref[...], preferred_element_type=F32)
+    dgate_pre = (back * up_pre * slope).astype(BF)
+    dup_pre = (back * swish).astype(BF)
+    dh_ref[...] += contract(dgate_pre, wg_ref[...], 1, 1) + contract(dup_pre, wu_ref[...], 1, 1)
+
+
+def shared_rows(h2, grad, w_gate, w_up, w_down):
+    tokens, ff = h2.shape[0], w_gate.shape[1]
+    tile = 512
+    rows = pl.BlockSpec((tokens, D), lambda f: (0, 0))
+    return pl.pallas_call(
+        shared_kernel,
+        out_shape=(jax.ShapeDtypeStruct((tokens, D), F32),) * 2,
+        grid=(ff // tile,),
+        in_specs=[
+            rows,
+            rows,
+            pl.BlockSpec((D, tile), lambda f: (0, f)),
+            pl.BlockSpec((D, tile), lambda f: (0, f)),
+            pl.BlockSpec((tile, D), lambda f: (f, 0)),
+        ],
+        out_specs=[rows, rows],
+        compiler_params=pltpu.CompilerParams(vmem_limit_bytes=VMEM_LIMIT),
+        cost_estimate=pl.CostEstimate(
+            flops=2 * 6 * tokens * D * ff, bytes_accessed=2 * 3 * D * ff, transcendentals=0
+        ),
+        name="shared_rows",
+    )(h2, grad, w_gate, w_up, w_down)
+
+
+def start_half(part, h_parts, g_parts, h_buf, g_buf, sems):
+    half = len(h_parts) // 2
+    for i in range(half):
+        per = h_parts[i].shape[0]
+        for which, (parts, buf) in enumerate(((h_parts, h_buf), (g_parts, g_buf))):
+            pltpu.make_async_copy(
+                parts[part * half + i], buf.at[pl.ds(i * per, per)], sems.at[which, i]
+            ).start()
+
+
+def wait_part(part, i, h_parts, g_parts, h_buf, g_buf, sems):
+    half = len(h_parts) // 2
+    per = h_parts[i].shape[0]
+    for which, (parts, buf) in enumerate(((h_parts, h_buf), (g_parts, g_buf))):
+        pltpu.make_async_copy(
+            parts[part * half + i], buf.at[pl.ds(i * per, per)], sems.at[which, i]
+        ).wait()
+
+
+def expert_slice_kernel(parts, pos_ref, *refs):
+    h_parts, g_parts = refs[:parts], refs[parts : 2 * parts]
+    wg_ref, wu_ref, wd_ref, og_ref, ou_ref, od_ref = refs[2 * parts : 2 * parts + 6]
+    h_buf, g_buf, x_sc, gd_sc, gate_sc, rank_sc, prob_sc, sems = refs[2 * parts + 6 :]
+    base = pos_ref[0]
+    experts = wg_ref.shape[0]
+    half = parts // 2
+    per = h_parts[0].shape[0]
+
+    def dispatch(pair, carry):
+        both_x, both_g, both_gate = [], [], []
+        for k in range(2):
+            b = 2 * pair + k
+            rank_sc[k] = g_buf[b, TOK_DEV:, :TOK_DEV].astype(F32)
+            prob_sc[k] = h_buf[b, TOK_DEV:, :TOK_DEV].astype(F32) + h_buf[
+                b, TOK_DEV:, TOK_DEV:
+            ].astype(F32)
+            hots, gates = [], []
+            for i in range(experts):
+                hot = one_hot_rows(rank_sc[k, pl.ds(base + i, 1), :])
+                gates.append(
+                    jnp.sum(hot * prob_sc[k, pl.ds(base + i, 1), :], -1, keepdims=True)
+                )
+                hots.append(hot)
+            hot = jnp.concatenate(hots, 0).astype(BF)
+            both_x.append(jnp.dot(hot, h_buf[b, :TOK_DEV, :], preferred_element_type=F32))
+            both_g.append(jnp.dot(hot, g_buf[b, :TOK_DEV, :], preferred_element_type=F32))
+            both_gate.append(gates)
+        into = pl.ds(pl.multiple_of(pair * 2 * SLOT, 2 * SLOT), 2 * SLOT)
+        for i in range(experts):
+            span = slice(i * SLOT, (i + 1) * SLOT)
+            x_sc[i, into, :] = jnp.concatenate([v[span] for v in both_x], 0).astype(BF)
+            gd_sc[i, into, :] = jnp.concatenate([v[span] for v in both_g], 0).astype(BF)
+            gate_sc[i, into, :] = jnp.concatenate([v[i] for v in both_gate], 0)
+        return carry
+
+    start_half(0, h_parts, g_parts, h_buf, g_buf, sems)
+    for part in range(2):
+        for i in range(half):
+            wait_part(part, i, h_parts, g_parts, h_buf, g_buf, sems)
+            lax.fori_loop(i * per // 2, (i + 1) * per // 2, dispatch, 0)
+        if part == 0:
+            start_half(1, h_parts, g_parts, h_buf, g_buf, sems)
+
+        def products(i, carry, part=part):
+            rows = x_sc[i]
+            gate_pre = jnp.dot(rows, wg_ref[i], preferred_element_type=F32)
+            up_pre = jnp.dot(rows, wu_ref[i], preferred_element_type=F32)
+            back = contract(gd_sc[i], wd_ref[i], 1, 1) * gate_sc[i]
+            swish, slope = swish_parts(gate_pre)
+            inner = (swish * up_pre * gate_sc[i]).astype(BF)
+            dgate_pre = (back * up_pre * slope).astype(BF)
+            dup_pre = (back * swish).astype(BF)
+            add_g = contract(rows, dgate_pre, 0, 0)
+            add_u = contract(rows, dup_pre, 0, 0)
+            add_d = contract(inner, gd_sc[i], 0, 0)
+            if part == 0:
+                og_ref[i], ou_ref[i], od_ref[i] = add_g, add_u, add_d
+            else:
+                og_ref[i] += add_g
+                ou_ref[i] += add_u
+                od_ref[i] += add_d
+            return carry
+
+        lax.fori_loop(0, experts, products, 0)
+
+
+def expert_slice_grads(pos, h_parts, g_parts, w_gate, w_up, w_down, width):
+    parts, per = len(h_parts), h_parts[0].shape[0]
+    experts = w_gate.shape[0]
+    blocks = parts * per // 2
+    anywhere = pl.BlockSpec(memory_space=pl.ANY)
+    return pl.pallas_call(
+        functools.partial(expert_slice_kernel, parts),
+        out_shape=(
+            jax.ShapeDtypeStruct((experts, D, width), F32),
+            jax.ShapeDtypeStruct((experts, D, width), F32),
+            jax.ShapeDtypeStruct((experts, width, D), F32),
+        ),
+        grid_spec=pltpu.PrefetchScalarGridSpec(
+            num_scalar_prefetch=1,
+            grid=(1,),
+            in_specs=[anywhere] * (2 * parts)
+            + [
+                pl.BlockSpec((experts, D, width), lambda i, s: (0, 0, s[1])),
+                pl.BlockSpec((experts, D, width), lambda i, s: (0, 0, s[1])),
+                pl.BlockSpec((experts, width, D), lambda i, s: (0, s[1], 0)),
+            ],
+            out_specs=[
+                pl.BlockSpec((experts, D, width), lambda i, s: (0, 0, 0)),
+                pl.BlockSpec((experts, D, width), lambda i, s: (0, 0, 0)),
+                pl.BlockSpec((experts, width, D), lambda i, s: (0, 0, 0)),
+            ],
+            scratch_shapes=[
+                pltpu.VMEM((blocks, ROWS, D), BF),
+                pltpu.VMEM((blocks, ROWS, D), BF),
+                pltpu.VMEM((experts, blocks * SLOT, D), BF),
+                pltpu.VMEM((experts, blocks * SLOT, D), BF),
+                pltpu.VMEM((experts, blocks * SLOT, 1), F32),
+                pltpu.VMEM((2, EXPERTS, TOK_DEV), F32),
+                pltpu.VMEM((2, EXPERTS, TOK_DEV), F32),
+                pltpu.SemaphoreType.DMA((2, parts // 2)),
+            ],
+        ),
+        compiler_params=pltpu.CompilerParams(vmem_limit_bytes=VMEM_LIMIT),
+        cost_estimate=pl.CostEstimate(
+            flops=2 * 2 * blocks * SLOT * experts * D * (6 * width + 2 * TOK_DEV),
+            bytes_accessed=2 * 4 * blocks * ROWS * D + 18 * experts * D * width,
+            transcendentals=0,
+        ),
+        name="expert_slice_grads",
+    )(pos, *h_parts, *g_parts, w_gate, w_up, w_down)
+
+
+def shared_slice_kernel(parts, pos_ref, *refs):
+    h_parts, g_parts = refs[:parts], refs[parts : 2 * parts]
+    wg_ref, wu_ref, wd_ref, og_ref, ou_ref, od_ref = refs[2 * parts : 2 * parts + 6]
+    h_buf, g_buf, inner_sc, sems = refs[2 * parts + 6 :]
+    half = parts // 2
+    per = h_parts[0].shape[0]
+    window = pl.ds(pl.multiple_of(pos_ref[0] * 128, 128), og_ref.shape[0])
+    lanes = pl.ds(pl.multiple_of(pos_ref[1] * 128, 128), od_ref.shape[0])
+
+    def two(buf, pair, cols=slice(None)):
+        return jnp.concatenate([buf[2 * pair + k, :TOK_DEV, cols] for k in range(2)], 0)
+
+    def products(pair, carry):
+        rows, grads = two(h_buf, pair), two(g_buf, pair)
+        gate_pre = jnp.dot(rows, wg_ref[...], preferred_element_type=F32)
+        up_pre = jnp.dot(rows, wu_ref[...], preferred_element_type=F32)
+        back = contract(grads, wd_ref[...], 1, 1)
+        swish, slope = swish_parts(gate_pre)
+        inner_sc[...] = (swish * up_pre).astype(BF)
+        dgate_pre = (back * up_pre * slope).astype(BF)
+        dup_pre = (back * swish).astype(BF)
+        picked = two(h_buf, pair, window)
+        og_ref[...] += contract(picked, dgate_pre, 0, 0)
+        ou_ref[...] += contract(picked, dup_pre, 0, 0)
+        od_ref[...] += contract(inner_sc[:, lanes], grads, 0, 0)
+        return carry
+
+    og_ref[...] = jnp.zeros_like(og_ref)
+    ou_ref[...] = jnp.zeros_like(ou_ref)
+    od_ref[...] = jnp.zeros_like(od_ref)
+    start_half(0, h_parts, g_parts, h_buf, g_buf, sems)
+    for part in range(2):
+        for i in range(half):
+            wait_part(part, i, h_parts, g_parts, h_buf, g_buf, sems)
+            lax.fori_loop(i * per // 2, (i + 1) * per // 2, products, 0)
+        if part == 0:
+            start_half(1, h_parts, g_parts, h_buf, g_buf, sems)
+
+
+def shared_slice_grads(pos, h_parts, g_parts, w_gate, w_up, w_down):
+    parts, per = len(h_parts), h_parts[0].shape[0]
+    blocks = parts * per // 2
+    width = w_gate.shape[1]
+    anywhere = pl.BlockSpec(memory_space=pl.ANY)
+    whole = lambda *shape: pl.BlockSpec(shape, lambda i, s: (0,) * len(shape))
+    return pl.pallas_call(
+        functools.partial(shared_slice_kernel, parts),
+        out_shape=(
+            jax.ShapeDtypeStruct((256, width), F32),
+            jax.ShapeDtypeStruct((256, width), F32),
+            jax.ShapeDtypeStruct((128, D), F32),
+        ),
+        grid_spec=pltpu.PrefetchScalarGridSpec(
+            num_scalar_prefetch=1,
+            grid=(1,),
+            in_specs=[anywhere] * (2 * parts)
+            + [whole(D, width), whole(D, width), whole(width, D)],
+            out_specs=[whole(256, width), whole(256, width), whole(128, D)],
+            scratch_shapes=[
+                pltpu.VMEM((blocks, ROWS, D), BF),
+                pltpu.VMEM((blocks, ROWS, D), BF),
+                pltpu.VMEM((2 * TOK_DEV, width), BF),
+                pltpu.SemaphoreType.DMA((2, parts // 2)),
+            ],
+        ),
+        compiler_params=pltpu.CompilerParams(vmem_limit_bytes=VMEM_LIMIT),
+        cost_estimate=pl.CostEstimate(
+            flops=2 * 2 * blocks * TOK_DEV * (3 * D * width + 512 * width + 128 * D),
+            bytes_accessed=2 * 4 * blocks * ROWS * D,
+            transcendentals=0,
+        ),
+        name="shared_slice_grads",
+    )(pos, *h_parts, *g_parts, w_gate, w_up, w_down)
+
+
+def pair_sum(kept, received):
+    return (kept.astype(F32) + received.astype(F32)).astype(BF)
+
+
+def halves(value, bit):
+    width = value.shape[-1] // 2
+    low, high = value[..., :width], value[..., width:]
+    return jnp.where(bit == 0, low, high), jnp.where(bit == 0, high, low)
+
+
+def rejoin(own, other, bit):
+    return jnp.where(
+        bit == 0, jnp.concatenate([own, other], -1), jnp.concatenate([other, own], -1)
+    )
+
+
+def reduce_dense(first, second, z, y, x, core):
+    first, second = first.astype(BF), second.astype(BF)
+    kept = jnp.where(core == 0, first, second)
+    sent = jnp.where(core == 0, second, first)
+    total = pair_sum(kept, over_core(sent))
+    bit_a, bit_b = jnp.where(core == 0, x, y), jnp.where(core == 0, y, x)
+    kept, sent = halves(total, bit_a)
+    total = pair_sum(kept, over_a(sent))
+    kept, sent = halves(total, bit_b)
+    total = pair_sum(kept, over_b(sent))
+    slabs = total.reshape(4, D // 4, -1)
+    result = lax.dynamic_index_in_dim(slabs, z, 0, keepdims=False).astype(F32)
+    for step in (1, 2, 3):
+        out = lax.dynamic_index_in_dim(slabs, lax.rem(z + step, 4), 0, keepdims=False)
+        result = result + over_z(out, step).astype(F32)
+    result = result.astype(BF)
+    result = rejoin(result, over_b(result), bit_b)
+    result = rejoin(result, over_a(result), bit_a)
+    other = over_core(result)
+    return jnp.where(core == 0, result, other), jnp.where(core == 0, other, result)
+
+
+def tuned_body(
+    tokens,
+    cotangent,
+    routes,
+    prompt_ids,
+    attn_gain,
+    query_weight,
+    key_weight,
+    value_weight,
+    output_weight,
+    ffn_gain,
+    router_weight,
+    shared_gate,
+    shared_up,
+    shared_down,
+    expert_gate,
+    expert_up_weight,
+    expert_down,
+):
+    z, y, j = lax.axis_index("dp"), lax.axis_index("context"), lax.axis_index("experts")
+    x, core = j // 2, j % 2
+    contexts = 2
+
+    expert_ids = jnp.arange(EXPERTS, dtype=jnp.int32)[:, None]
+    route_t = routes.T
+    member = (route_t[0:1] == expert_ids) | (route_t[1:2] == expert_ids)
+    before = (jnp.arange(TOK_DEV)[:, None] < jnp.arange(TOK_DEV)[None, :]).astype(BF)
+    ranks = jnp.dot(member.astype(BF), before, preferred_element_type=F32)
+    ranks = jnp.where(member, ranks, -1.0).astype(BF)
+    g_block = jnp.concatenate([cotangent, jnp.pad(ranks, ((0, 0), (0, D - TOK_DEV)))], 0)
+
+    small = jnp.concatenate(
+        [router_weight, attn_gain[:, None], ffn_gain[:, None], jnp.zeros((D // 4, 110), BF)], 1
+    )
+    w_in = gather_rows(
+        jnp.concatenate([query_weight, key_weight, value_weight, small], 1), core
+    )
+    g_pair = jnp.stack([g_block, over_x(g_block)])
+    g_group = jnp.concatenate([g_pair, over_core(g_pair)])
+    w_out = gather_rows(output_weight, core)
+    w_gateup = gather_rows(jnp.concatenate([shared_gate, shared_up], 1), core)
+    w_sgate, w_sup = w_gateup[:, :2048], w_gateup[:, 2048:]
+    w_sdown = gather_rows(shared_down, core)
+    g_parts = gather_blocks(g_block)
+
+    w_query, w_key, w_value = w_in[:, :D], w_in[:, D : 2 * D], w_in[:, 2 * D : 3 * D]
+    w_router = w_in[:, 3 * D : 3 * D + EXPERTS]
+    gain1_f = w_in[:, 3 * D + 16].astype(F32)
+    gain2_f = w_in[:, 3 * D + 17].astype(F32)
+
+    cos_table, sin_table = rotary_tables(TOK_DEV)
+    inputs = tokens.astype(F32)
+    inv_rms1 = lax.rsqrt(jnp.mean(inputs * inputs, -1, keepdims=True) + EPS)
+    normed1 = inputs * inv_rms1
+    hidden1 = (normed1 * gain1_f).astype(BF)
+    query_f = jnp.dot(hidden1, w_query, preferred_element_type=F32)
+    key_f = jnp.dot(hidden1, w_key, preferred_element_type=F32)
+    value_f = jnp.dot(hidden1, w_value, preferred_element_type=F32)
+    query_b = rotate(query_f, cos_table, sin_table).astype(BF)
+    key_b = rotate(key_f, cos_table, sin_table).astype(BF)
+    value_b = value_f.astype(BF)
+    prompt_keys, prompt_values = (
+        lax.all_gather(key_b[:PROMPT], "context", axis=0, tiled=True),
+        lax.all_gather(value_b[:PROMPT], "context", axis=0, tiled=True),
+    )
+    keys_h = jnp.concatenate([prompt_keys, key_b[PROMPT:]], 0).reshape(-1, HEADS, HD)
+    values_h = jnp.concatenate([prompt_values, value_b[PROMPT:]], 0).reshape(-1, HEADS, HD)
+    query_h = query_b.reshape(TOK_DEV, HEADS, HD)
+    allowed = key_mask(y, prompt_ids, contexts)
+    scores = jnp.where(
+        allowed[None],
+        0.125 * jnp.einsum("qhd,khd->hqk", query_h, keys_h, preferred_element_type=F32),
+        -1e30,
+    )
+    row_max = jnp.max(scores, -1, keepdims=True)
+    exp_scores = jnp.exp(scores - row_max)
+    row_total = jnp.sum(exp_scores, -1, keepdims=True)
+    log_total = row_max + jnp.log(row_total)
+    attn_probs = (exp_scores / row_total).astype(BF)
+    attended = (
+        jnp.einsum("hqk,khd->qhd", attn_probs, values_h, preferred_element_type=F32)
+        .reshape(TOK_DEV, D)
+        .astype(BF)
+    )
+    resid = inputs + jnp.dot(attended, w_out, preferred_element_type=F32)
+    inv_rms2 = lax.rsqrt(jnp.mean(resid * resid, -1, keepdims=True) + EPS)
+    normed2 = resid * inv_rms2
+    hidden2 = (normed2 * gain2_f).astype(BF)
+    logits_t = contract(w_router, hidden2, 0, 1)
+    probs_t = jax.nn.softmax(logits_t, 0)
+    probs_high = probs_t.astype(BF)
+    probs_low = (probs_t - probs_high.astype(F32)).astype(BF)
+    h_block = jnp.concatenate([hidden2, jnp.concatenate([probs_high, probs_low], 1)], 0)
+
+    h_pair = jnp.stack([h_block, over_x(h_block)])
+    h_group = jnp.concatenate([h_pair, over_core(h_pair)])
+    shared_res, grad_shared_in = shared_rows(hidden2, cotangent, w_sgate, w_sup, w_sdown)
+    base = (j * 4).astype(jnp.int32)
+    moe_part, dx_part = group_experts(
+        base[None], h_group, g_group, expert_gate, expert_up_weight, expert_down
+    )
+    h_parts = gather_blocks(h_block)
+
+    def home(part):
+        pair = pair_sum(part[:2], over_core(part[2:]))
+        return pair[0].astype(F32) + over_x(pair[1]).astype(F32)
+
+    dx_home = home(dx_part)
+    moe_out = home(moe_part)
+    layer_out = (resid + shared_res + moe_out).astype(BF)
+
+    grad_total = cotangent.astype(F32)
+    grad_rprobs = dx_home[TOK_DEV:, :TOK_DEV] + dx_home[TOK_DEV:, TOK_DEV:]
+    grad_logits_t = (
+        probs_t * (grad_rprobs - jnp.sum(probs_t * grad_rprobs, 0, keepdims=True))
+    ).astype(BF)
+    grad_router_local = contract(hidden2, grad_logits_t, 0, 1)
+    grad_hidden2 = (
+        dx_home[:TOK_DEV] + grad_shared_in + contract(grad_logits_t, w_router, 0, 1)
+    )
+    grad_gain2 = jnp.sum(grad_hidden2 * normed2, 0)
+    grad_normed2 = grad_hidden2 * gain2_f
+    grad_resid = (
+        inv_rms2 * (grad_normed2 - normed2 * jnp.mean(grad_normed2 * normed2, -1, keepdims=True))
+        + grad_total
+    )
+    grad_branch = grad_resid.astype(BF)
+    grad_wout = inner_rows(attended, grad_branch)
+    grad_attended = times_transposed(grad_branch, w_out).astype(BF).reshape(TOK_DEV, HEADS, HD)
+    scores_again = jnp.where(
+        allowed[None],
+        0.125 * jnp.einsum("qhd,khd->hqk", query_h, keys_h, preferred_element_type=F32),
+        -1e30,
+    )
+    probs_f = jnp.exp(scores_again - log_total)
+    probs_b = probs_f.astype(BF)
+    grad_pattn = jnp.einsum("qhd,khd->hqk", grad_attended, values_h, preferred_element_type=F32)
+    grad_scores = (
+        probs_f * (grad_pattn - jnp.sum(probs_f * grad_pattn, -1, keepdims=True))
+    ).astype(BF)
+    grad_query = 0.125 * jnp.einsum(
+        "hqk,khd->qhd", grad_scores, keys_h, preferred_element_type=F32
+    ).reshape(TOK_DEV, D)
+    grad_keys = 0.125 * jnp.einsum(
+        "hqk,qhd->khd", grad_scores, query_h, preferred_element_type=F32
+    ).reshape(-1, D)
+    grad_values = jnp.einsum(
+        "hqk,qhd->khd", probs_b, grad_attended, preferred_element_type=F32
+    ).reshape(-1, D)
+    span = contexts * PROMPT
+    grad_pkeys, grad_pvalues = (
+        lax.psum_scatter(grad_keys[:span].astype(BF), "context", scatter_dimension=0, tiled=True),
+        lax.psum_scatter(
+            grad_values[:span].astype(BF), "context", scatter_dimension=0, tiled=True
+        ),
+    )
+    grad_key_all = jnp.concatenate([grad_pkeys.astype(F32), grad_keys[span:]], 0)
+    grad_value_all = jnp.concatenate([grad_pvalues.astype(F32), grad_values[span:]], 0)
+    grad_qpre = rotate(grad_query, cos_table, -sin_table).astype(BF)
+    grad_kpre = rotate(grad_key_all, cos_table, -sin_table).astype(BF)
+    grad_vpre = grad_value_all.astype(BF)
+    grad_wquery = inner_rows(hidden1, grad_qpre)
+    grad_wkey = inner_rows(hidden1, grad_kpre)
+    grad_wvalue = inner_rows(hidden1, grad_vpre)
+    grad_hidden1 = (
+        times_transposed(grad_qpre, w_query)
+        + times_transposed(grad_kpre, w_key)
+        + times_transposed(grad_vpre, w_value)
+    )
+    grad_gain1 = jnp.sum(grad_hidden1 * normed1, 0)
+    grad_normed1 = grad_hidden1 * gain1_f
+    grad_inputs = (
+        inv_rms1 * (grad_normed1 - normed1 * jnp.mean(grad_normed1 * normed1, -1, keepdims=True))
+        + grad_resid
+    )
+
+    sum_qk, sum_vo = reduce_dense(
+        jnp.concatenate([grad_wquery, grad_wkey], 1),
+        jnp.concatenate([grad_wvalue, grad_wout], 1),
+        z,
+        y,
+        x,
+        core,
+    )
+    sum_qk, sum_vo = sum_qk.astype(F32), sum_vo.astype(F32)
+    extras = jnp.concatenate(
+        [grad_router_local, grad_gain1[:, None], grad_gain2[:, None], jnp.zeros((D, 110), F32)], 1
+    ).astype(BF)
+    extras = lax.psum_scatter(extras, "dp", scatter_dimension=0, tiled=True)
+    extras = lax.psum(extras, ("context", "experts")).astype(F32)
+
+    plane = y * 4 + j
+    columns = lambda w: lax.dynamic_index_in_dim(
+        w.reshape(D, 4, 8, 64), plane, 2, keepdims=False
+    ).reshape(D, 256)
+    down_rows = lax.dynamic_index_in_dim(
+        w_sdown.reshape(4, 8, 64, D), plane, 1, keepdims=False
+    ).reshape(256, D)
+
+    window = jnp.array([0, 1, 3, 4], jnp.int32)[z]
+    s_gate, s_up, s_down = shared_slice_grads(
+        jnp.stack([window, (z // 2).astype(jnp.int32)]),
+        h_parts,
+        g_parts,
+        columns(w_sgate),
+        columns(w_sup),
+        down_rows,
+    )
+    lead = z * 192 - window * 128
+    s_gateup = jnp.concatenate(
+        [
+            lax.dynamic_slice_in_dim(s_gate, lead, 192, 0),
+            lax.dynamic_slice_in_dim(s_up, lead, 192, 0),
+        ],
+        1,
+    ).astype(BF)
+    s_down = lax.dynamic_slice_in_dim(s_down, (z % 2) * 64, 64, 0).astype(BF)
+    s_gateup = lax.all_gather(s_gateup, ("context", "experts"), axis=0, tiled=False)
+    s_down = lax.all_gather(s_down, ("context", "experts"), axis=0, tiled=True).astype(F32)
+    s_gateup = s_gateup.reshape(8, 192, 2, 4, 64).transpose(2, 1, 3, 0, 4).reshape(2, 192, 2048)
+    s_gateup = s_gateup.astype(F32)
+
+    slice_index = (z * 2 + y).astype(jnp.int32)
+    e_gate, e_up, e_down = expert_slice_grads(
+        jnp.stack([base, slice_index]),
+        h_parts,
+        g_parts,
+        expert_gate,
+        expert_up_weight,
+        expert_down,
+        256,
+    )
+    return (
+        layer_out,
+        grad_inputs,
+        extras[:, 16],
+        sum_qk[:, :D],
+        sum_qk[:, D:],
+        sum_vo[:, :D],
+        sum_vo[:, D:],
+        extras[:, 17],
+        extras[:, :16],
+        s_gateup[0],
+        s_gateup[1],
+        s_down,
+        e_gate,
+        e_up,
+        e_down,
+    )
+
+
 def solution(mesh):
+    shape = dict(mesh.shape)
+    tuned = shape == TUNED_MESH
+
     return jax.shard_map(
-        body,
+        tuned_body if tuned else plain_body,
         mesh=mesh,
         in_specs=(
             P(("dp", "context", "experts"), None),

time: 1480 us -> 807 us (0.55)
  waiting for transfers between devices: 1020 us -> 324 us
  Pallas kernels: 0 us -> 150 us
  matrix products: 202 us -> 54.3 us
  starting transfers between devices: 18.7 us -> 51 us
  local copies, waits for them, and re-layouts: 81.8 us -> 60.4 us
    reduce_scatter x12 -> x2, waiting for transfers between devices: 916 us -> 12.2 us  [the longest x1 12.2 us: tuned_body(): lax.psum_scatter(grad_values[:span].astype(BF), 'context', scatter_dimens...]
    ppermute x0 -> x41, waiting for transfers between devices: none -> 275 us  [moved(): return lax.ppermute(value, AXES, pairs)]
    pallas_call x0 -> x4, Pallas kernels: none -> 150 us  [the longest x1 58.5 us: expert_slice_grads(): pl.pallas_call(functools.partial(expert_slice_kernel, parts), out_shape=(...]
    dot_general x23 -> x14, matrix products: 166 us -> 39.8 us  [the longest x1 11.2 us: tuned_body(): jnp.einsum('qhd,khd->hqk', grad_attended, values_h, preferred_element_typ...]
    ppermute x0 -> x41, starting transfers between devices: none -> 50.7 us  [moved(): return lax.ppermute(value, AXES, pairs)]
    all_gather x7 -> x4, waiting for transfers between devices: 68.2 us -> 20.1 us  [the longest x3 20.1 us: gather_rows(): part = lax.all_gather(part, 'dp', axis=0, tiled=False)]
    unnamed x2 -> x0, blocking collectives: 24.2 us -> none
    psum x1 -> x0, waiting for transfers between devices: 23.2 us -> none  [body(): lax.psum(shares[1].astype(jnp.bfloat16), ('context', 'experts'))]
  transfers between devices with their start and end apart: 25 -> 48, of which waited for: 17 -> 16; matrix products, arithmetic and copies ran while one was open for 20% -> 16% of each run, Pallas kernels for 0% -> 19%
where the time goes in v1:
time: 807 us; the launch traced here: 801 us
  waiting for transfers between devices  324 us (40%)
  Pallas kernels  150 us (19%)
  blocking collectives  79.8 us (10%)
  other arithmetic  65.1 us (8%)
  local copies, waits for them, and re-layouts  60.4 us (7%)
  matrix products  54.3 us (7%)
  starting transfers between devices  51 us (6%)
  between operations  16.4 us (2%)
    ppermute x41, waiting for transfers between devices, moved(): return lax.ppermute(value, AXES, pairs)  275 us
    pallas_call x1, Pallas kernels, expert_slice_grads(): pl.pallas_call(functools.partial(expert_slice_kernel, parts), out_shape=(...  58.5 us
    ppermute x41, starting transfers between devices, moved(): return lax.ppermute(value, AXES, pairs)  50.7 us
    pallas_call x1, Pallas kernels, group_experts(): pl.pallas_call(group_kernel, out_shape=(jax.ShapeDtypeStruct((blocks, TOK...  40.8 us
    pallas_call x1, Pallas kernels, shared_slice_grads(): pl.pallas_call(functools.partial(shared_slice_kernel, parts), out_shape=(...  38.8 us
    all_gather x1, blocking collectives, gather_rows(): part = lax.all_gather(part, 'dp', axis=0, tiled=False)  23.6 us
    psum x1, blocking collectives, tuned_body(): extras = lax.psum(extras, ('context', 'experts')).astype(F32)  23 us
    all_gather x3, waiting for transfers between devices, gather_rows(): part = lax.all_gather(part, 'dp', axis=0, tiled=False)  20.1 us
  transfers between devices with their start and end apart: 48, of which 16 were waited for; matrix products, arithmetic and copies ran while one was open for 16% of the time, Pallas kernels for 19%

profile of v1, /device:TPU:0, one launch (start us, length us, event | category | flops | bytes accessed | tf_op | source)
XLA Modules:
  0.0 800.9 jit_solution(1560692592206935896)
XLA Ops:
  12.9 23.6 %all-gather.1 = bf16[384,768]{1,0:T(8,128)(2,1)S(1)} all-gather(bf16[96,768]{1,0:T(8,128)(2,1)S(1)} %constant_dynamic-slice_fusion.4), channel_id=3, replica_groups=mesh['dp'=4,'context'=2,'experts'=4] {'dp'}, dimensions={0}, use_global_device_ids=true | all-gather | bytes 737280 | tf_op jit(solution)/shard_map/all_gather | solution.py:484
  37.6 1.5 collective-permute-start.6
  40.1 20.0 %all-gather.11.cloned.1.call-done = bf16[384,2432]{1,0:T(8,128)(2,1)} async-done(((bf16[96,2432]{1,0:T(8,128)(2,1)}), bf16[384,2432]{1,0:T(8,128)(2,1)}) %all-gather.11.cloned.1.call-update) | async-done | bytes 1867792 | tf_op jit(solution)/shard_map/all_gather | solution.py:484
  61.5 2.5 maximum_select_fusion.3
  64.3 2.6 maximum_select_fusion.1
  71.9 11.8 %all_gather.39 = bf16[512,768]{1,0:T(8,128)(2,1)S(1)} all-gather(bf16[256,768]{1,0:T(8,128)(2,1)S(1)} %slice-done.5), channel_id=1, replica_groups=mesh['dp'=4,'context'=2,'experts'=4] {'context'}, dimensions={0}, use_global_device_ids=true | all-gather | bytes 1179648 | tf_op jit(solution)/shard_map/all_gather | solution.py:997
  84.7 1.5 copy.95
  86.3 11.8 %all_gather.40 = bf16[512,768]{0,1:T(8,128)(2,1)S(1)} all-gather(bf16[256,768]{0,1:T(8,128)(2,1)} %bitcast.169), channel_id=1, replica_groups=mesh['dp'=4,'context'=2,'experts'=4] {'context'}, dimensions={0}, use_global_device_ids=true | all-gather | bytes 1179648 | tf_op jit(solution)/shard_map/all_gather | solution.py:996
  99.2 2.5 fusion.6
  101.7 3.0 fusion
  106.0 4.3 fusion.24
  115.2 2.2 pad_maximum_fusion.7
  117.4 2.6 collective-permute-start.33
  120.2 1.7 collective-permute-start.31
  121.8 6.4 collective-permute-done.4
  129.5 29.3 %collective-permute-done.33 = bf16[400,768]{1,0:T(8,128)(2,1)S(1)} collective-permute-done((bf16[400,768]{1,0:T(8,128)(2,1)}, bf16[400,768]{1,0:T(8,128)(2,1)S(1)}, u32[]{:S(2)}, u32[]{:S(2)}) %collective-permute-start.33) | collective-permute-done | bytes 614432 | tf_op jit(solution)/shard_map/ppermute | solution.py:449
  158.9 57.5 %collective-permute-done.32 = bf16[400,768]{1,0:T(8,128)(2,1)} collective-permute-done((bf16[400,768]{1,0:T(8,128)(2,1)}, bf16[400,768]{1,0:T(8,128)(2,1)}, u32[]{:S(2)}, u32[]{:S(2)}) %collective-permute-start.32) | collective-permute-done | bytes 614432 | tf_op jit(solution)/shard_map/ppermute | solution.py:449
  216.4 24.4 %collective-permute-start.21 = (bf16[400,768]{1,0:T(8,128)(2,1)}, bf16[400,768]{1,0:T(8,128)(2,1)}, u32[]{:S(2)}, u32[]{:S(2)}) collective-permute-start(bf16[400,768]{1,0:T(8,128)(2,1)} %get-tuple-element.112), channel_id=1, source_target_pairs={{0,8},{1,9},{2,10},{3,11},{4,12},{5,13},{6,14},{7,15},{8,16},{9,17... | collective-permute-start | bytes 1843208 | tf_op jit(solution)/shard_map/ppermute | solution.py:449
  240.8 4.0 fusion.9
  245.3 23.6 %collective-permute-done.22 = bf16[400,768]{1,0:T(8,128)(2,1)} collective-permute-done((bf16[400,768]{1,0:T(8,128)(2,1)}, bf16[400,768]{1,0:T(8,128)(2,1)}, u32[]{:S(2)}, u32[]{:S(2)}) %collective-permute-start.22) | collective-permute-done | bytes 614432 | tf_op jit(solution)/shard_map/ppermute | solution.py:449
  268.9 3.9 fusion.12
  272.9 40.8 %group_experts.1 = (bf16[4,384,768]{2,1,0:T(8,128)(2,1)}, bf16[4,400,768]{2,1,0:T(8,128)(2,1)}) custom-call(s32[1]{0:T(128)} %bitcast.26.base_ref, bf16[4,400,768]{2,1,0:T(8,128)(2,1)} %get-tuple-element.111.h_ref, bf16[4,400,768]{2,1,0:T(8,128)(2,1)} %get-tuple-element.109.g_ref, bf16[4,768,2048]{2,1,0:T(8,128)(2,1)} %refs_16_.1, ...), custom_call_target="tpu_custom_call" | custom-call | flops 21743271936 | bytes 37748736 | tf_op jit(solution)/shard_map/group_experts/pallas_call | solution.py:606
  317.1 3.9 maximum_select_fusion.2
  325.9 3.8 maximum_select_fusion
  329.7 3.3 fusion.109
  333.0 11.7 %shared_rows.1 = (f32[384,768]{1,0:T(8,128)}, f32[384,768]{1,0:T(8,128)}) custom-call(bf16[384,768]{1,0:T(8,128)(2,1)} %copy-done.9, bf16[384,768]{1,0:T(8,128)(2,1)} %g_ref.1, bf16[768,2048]{1,0:T(8,128)(2,1)} %get-tuple-element.89.wg_ref, bf16[768,2048]{1,0:T(8,128)(2,1)} %get-tuple-element.88.wu_ref, bf16[2048,768]{1,0:T(8,128)(2,1)} %bitcast.141), custom_call_target="tpu_custom_call" | custom-call | flops 7247757312 | bytes 9437184 | tf_op jit(solution)/shard_map/shared_rows/pallas_call | solution.py:668
  344.7 6.2 collective-permute-done.11
  351.1 2.0 multiply_reduce_fusion.1
  353.4 2.5 convert_add_fusion.3
  358.9 11.2 %multiply_reduce_fusion = (f32[12,384]{1,0:T(8,128)S(1)}, f32[12,384,640]{2,1,0:T(8,128)}) fusion(f32[12,384]{1,0:T(8,128)S(1)} %log_add_fusion, f32[12,384,640]{2,1,0:T(8,128)} %copy-done.2, pred[384,640]{1,0:T(8,128)(4,1)S(1)} %fusion.48, bf16[384,12,64]{0,2,1:T(8,128)(2,1)S(1)} %bitcast.153, bf16[640,12,64]{0,2,1:T(8,128)(2,1)S(1)} %bitcast.146), kind=kOutput, calls=%fused_computation.1 | convolution fusion | flops 392228352 | bytes 25448448 | tf_op jit(solution)/shard_map/qhd,khd->hqk/dot_general | solution.py:1070
  370.1 6.6 multiply_convert_fusion
  380.9 7.1 fusion.21
  390.5 5.7 fusion.20
  402.6 1.9 convolution_convert_fusion.2
  404.5 12.2 %reduce-scatter.8.cloned.1.call-done = bf16[256,768]{0,1:T(8,128)(2,1)} async-done(((bf16[512,768]{0,1:T(8,128)(2,1)}), bf16[256,768]{0,1:T(8,128)(2,1)}) %reduce-scatter.8.cloned.1.call-update) | async-done | bytes 393232 | tf_op jit(solution)/shard_map/reduce_scatter | solution.py:1086
  416.7 2.0 convolution_convert_fusion
  418.7 2.2 broadcast_select_fusion
  423.2 2.5 collective-permute-done.12
  425.8 3.5 add_convert_fusion
  431.9 84.1 %collective-permute-done.13 = bf16[768,768]{0,1:T(8,128)(2,1)} collective-permute-done((bf16[768,768]{0,1:T(8,128)(2,1)}, bf16[768,768]{0,1:T(8,128)(2,1)}, u32[]{:S(2)}, u32[]{:S(2)}) %collective-permute-start.13) | collective-permute-done | bytes 1179680 | tf_op jit(solution)/shard_map/ppermute | solution.py:449
  516.0 1.7 add_convert_fusion.2
  522.1 6.6 collective-permute-done.14
  535.3 19.9 %collective-permute-done.36.refs_11_ = bf16[4,400,768]{2,1,0:T(8,128)(2,1)} collective-permute-done((bf16[4,400,768]{2,1,0:T(8,128)(2,1)}, bf16[4,400,768]{2,1,0:T(8,128)(2,1)}, u32[]{:S(2)}, u32[]{:S(2)}) %collective-permute-start.36) | collective-permute-done | bytes 2457632 | tf_op jit(solution)/shard_map/ppermute | solution.py:449
  555.1 3.6 collective-permute-start.17
  559.8 1.8 constant_dynamic-slice_fusion
  561.6 4.6 copy.103
  566.2 4.6 copy.102
  574.0 7.5 collective-permute-done.25.refs_2_
  581.5 26.3 %collective-permute-done.26.refs_3_ = bf16[4,400,768]{2,1,0:T(8,128)(2,1)} collective-permute-done((bf16[4,400,768]{2,1,0:T(8,128)(2,1)}, bf16[4,400,768]{2,1,0:T(8,128)(2,1)}, u32[]{:S(2)}, u32[]{:S(2)}) %collective-permute-start.26) | collective-permute-done | bytes 2457632 | tf_op jit(solution)/shard_map/ppermute | solution.py:449
  609.8 2.0 fusion.37
  611.9 2.0 convolution_add_fusion.1
  613.9 3.3 fusion.31
  618.3 2.6 fusion.30
  620.9 17.2 %reduce-scatter.10.cloned.1.call-done = bf16[192,128]{1,0:T(8,128)(2,1)} async-done(((bf16[768,128]{1,0:T(8,128)(2,1)}), bf16[192,128]{1,0:T(8,128)(2,1)}) %reduce-scatter.10.cloned.1.call-update) | async-done | bytes 49168
  639.0 23.0 %psum.7 = bf16[192,128]{0,1:T(8,128)(2,1)S(1)} all-reduce(bf16[192,128]{0,1:T(8,128)(2,1)S(1)} %copy.114), channel_id=1, replica_groups=mesh['dp'=4,'context'=2,'experts'=4] {'context','experts'}, use_global_device_ids=true, to_apply=%region_16.17 | all-reduce | flops 24576 | bytes 98304 | tf_op jit(solution)/shard_map/psum | solution.py:1123
  664.8 38.8 %shared_slice_grads.1 = (f32[256,256]{1,0:T(8,128)}, f32[256,256]{1,0:T(8,128)}, f32[128,768]{1,0:T(8,128)}) custom-call(s32[2]{0:T(128)} %pad_add_fusion.pos_ref, bf16[4,400,768]{2,1,0:T(8,128)(2,1)} %get-tuple-element.110.refs_0_, bf16[4,400,768]{2,1,0:T(8,128)(2,1)} %collective-permute-done.24.refs_1_, ...), custom_call_target="tpu_custom_call" | custom-call | flops 20132659200 | bytes 39321600 | tf_op jit(solution)/shard_map/shared_slice_grads/pallas_call | solution.py:866
  706.4 4.1 collective-permute-done.19
  710.7 58.5 %expert_slice_grads.1 = (f32[4,768,256]{2,1,0:T(8,128)}, f32[4,768,256]{2,1,0:T(8,128)}, f32[4,256,768]{2,1,0:T(8,128)}) custom-call(s32[2]{0:T(128)} %pad_add_fusion.1.pos_ref, bf16[4,400,768]{2,1,0:T(8,128)(2,1)} %get-tuple-element.110.refs_0_, bf16[4,400,768]{2,1,0:T(8,128)(2,1)} %collective-permute-done.24.refs_1_, ...), custom_call_target="tpu_custom_call" | custom-call | flops 32614907904 | bytes 53477376 | tf_op jit(solution)/shard_map/expert_slice_grads/pallas_call | solution.py:779
  770.2 9.6 %all_gather.48 = bf16[512,768]{1,0:T(8,128)(2,1)S(1)} all-gather(bf16[64,768]{1,0:T(8,128)(2,1)S(1)} %dynamic-slice_convert_fusion), channel_id=1, replica_groups=mesh['dp'=4,'context'=2,'experts'=4] {'context','experts'}, dimensions={0}, use_global_device_ids=true | all-gather | bytes 884736 | tf_op jit(solution)/shard_map/all_gather | solution.py:1152
  783.4 2.7 copy.106
  786.7 1.7 fusion.110
  788.7 1.7 copy.109
  790.4 1.8 copy.108
  792.1 1.7 copy.110
  (326 shorter events, 83.0 us)
Async XLA Ops:
  7.2 53.0 %all-gather.11.cloned.1.call-start = ((), (), s32[]{:S(2)}) async-start(), calls=%async_computation.6 | async-start | bytes 2334720 | tf_op jit(solution)/shard_map/all_gather | solution.py:484
  11.9 24.6 %copy-start.61 = (s32[384,2]{0,1:T(2,128)S(1)}, s32[384,2]{0,1:T(2,128)}, u32[]{:S(2)}) copy-start(s32[384,2]{0,1:T(2,128)} %param.20) | copy-start | bytes 9220
  11.9 24.8 %copy-start.36 = (bf16[384,768]{1,0:T(8,128)(2,1)S(1)}, bf16[384,768]{1,0:T(8,128)(2,1)}, u32[]{:S(2)}) copy-start(bf16[384,768]{1,0:T(8,128)(2,1)} %g_ref.1) | copy-start | bytes 1769476
  11.9 232.9 %all-gather.15.cloned.1.call-start = ((), (), s32[]{:S(2)}) async-start(), calls=%async_computation.8 | async-start | bytes 1966080 | tf_op jit(solution)/shard_map/all_gather | solution.py:484
  12.8 26.3 %copy-start.53 = (bf16[192,2048]{1,0:T(8,128)(2,1)S(1)}, bf16[192,2048]{1,0:T(8,128)(2,1)}, u32[]{:S(2)}) copy-start(bf16[192,2048]{1,0:T(8,128)(2,1)} %param.29) | copy-start | bytes 2359300
  12.8 232.0 %all-gather.13.cloned.1.call-start = ((), (), s32[]{:S(2)}) async-start(), calls=%async_computation.7 | async-start | bytes 3932160 | tf_op jit(solution)/shard_map/all_gather | solution.py:484
  12.9 26.2 %copy-start.54 = (bf16[192,2048]{1,0:T(8,128)(2,1)S(1)}, bf16[192,2048]{1,0:T(8,128)(2,1)}, u32[]{:S(2)}) copy-start(bf16[192,2048]{1,0:T(8,128)(2,1)} %param.30) | copy-start | bytes 2359300
  36.5 25.0 %collective-permute-start.1 = (bf16[4,96,768]{2,1,0:T(8,128)(2,1)S(1)}, bf16[4,96,768]{2,1,0:T(8,128)(2,1)}, u32[]{:S(2)}, u32[]{:S(2)}) collective-permute-start(bf16[4,96,768]{2,1,0:T(8,128)(2,1)S(1)} %bitcast.155), channel_id=1, source_target_pairs={{0,1},{1,0},{2,3},{3,2},{4,5},{5,4},{6,7},{7,6},{8,9},{9,8},{10,11... | collective-permute-start | bytes 1769480 | tf_op jit(solution)/shard_map/ppermute | solution.py:449
  37.6 22.7 %copy-start.62 = (s32[2]{0:T(128)S(1)}, s32[2]{0:T(128)}, u32[]{:S(2)}) copy-start(s32[2]{0:T(128)} %param.21) | copy-start | bytes 28
  37.6 22.8 %copy-start.38 = (bf16[384,768]{1,0:T(8,128)(2,1)S(1)}, bf16[384,768]{1,0:T(8,128)(2,1)}, u32[]{:S(2)}) copy-start(bf16[384,768]{1,0:T(8,128)(2,1)} %param.18) | copy-start | bytes 1769476
  37.6 77.6 %collective-permute-start.6 = (bf16[400,768]{1,0:T(8,128)(2,1)}, bf16[400,768]{1,0:T(8,128)(2,1)}, u32[]{:S(2)}, u32[]{:S(2)}) collective-permute-start(bf16[400,768]{1,0:T(8,128)(2,1)} %get-tuple-element.114), channel_id=1, source_target_pairs={{0,2},{1,3},{2,0},{3,1},{4,6},{5,7},{6,4},{7,5},{8,10},{9,11},{10,... | collective-permute-start | bytes 1843208 | tf_op jit(solution)/shard_map/ppermute | solution.py:449
  40.0 358.2 %reduce-scatter.6.cloned.1.call-start = ((), (), s32[]{:S(2)}) async-start(), calls=%async_computation.3 | async-start | bytes 1179648 | tf_op jit(solution)/shard_map/reduce_scatter | solution.py:1085
  60.2 4.2 collective-permute-start
  70.3 28.8 %copy-start.27 = (bf16[384,12,32]{0,2,1:T(8,128)(2,1)}, bf16[384,12,32]{0,2,1:T(8,128)(2,1)S(1)}, u32[]{:S(2)}) copy-start(bf16[384,12,32]{0,2,1:T(8,128)(2,1)S(1)} %get-tuple-element.96) | copy-start | bytes 884740
  70.3 28.8 %copy-start.29 = (bf16[384,12,32]{0,2,1:T(8,128)(2,1)}, bf16[384,12,32]{0,2,1:T(8,128)(2,1)S(1)}, u32[]{:S(2)}) copy-start(bf16[384,12,32]{0,2,1:T(8,128)(2,1)S(1)} %get-tuple-element.97) | copy-start | bytes 884740
  86.3 18.4 %copy-start.24 = (bf16[640,768]{0,1:T(8,128)(2,1)}, bf16[640,768]{0,1:T(8,128)(2,1)S(1)}, u32[]{:S(2)}) copy-start(bf16[640,768]{0,1:T(8,128)(2,1)S(1)} %copy.95) | copy-start | bytes 2949124
  113.7 14.6 %collective-permute-start.4 = (bf16[400,768]{1,0:T(8,128)(2,1)}, bf16[400,768]{1,0:T(8,128)(2,1)S(1)}, u32[]{:S(2)}, u32[]{:S(2)}) collective-permute-start(bf16[400,768]{1,0:T(8,128)(2,1)} %get-tuple-element.112), channel_id=1, source_target_pairs={{0,2},{1,3},{2,0},{3,1},{4,6},{5,7},{6,4},{7,5},{8,10},{9,11},{10,... | collective-permute-start | bytes 1843208 | tf_op jit(solution)/shard_map/ppermute | solution.py:449
  117.4 123.4 %collective-permute-start.7 = (bf16[2,400,768]{2,1,0:T(8,128)(2,1)}, bf16[2,400,768]{2,1,0:T(8,128)(2,1)}, u32[]{:S(2)}, u32[]{:S(2)}) collective-permute-start(bf16[2,400,768]{2,1,0:T(8,128)(2,1)} %pad_maximum_fusion.7), channel_id=1, source_target_pairs={{0,1},{1,0},{2,3},{3,2},{4,5},{5,4},{6,7},{7,6},{8,9},{9,8},{10,11... | collective-permute-start | bytes 3686408 | tf_op jit(solution)/shard_map/ppermute | solution.py:449
  117.4 41.5 %collective-permute-start.33 = (bf16[400,768]{1,0:T(8,128)(2,1)}, bf16[400,768]{1,0:T(8,128)(2,1)S(1)}, u32[]{:S(2)}, u32[]{:S(2)}) collective-permute-start(bf16[400,768]{1,0:T(8,128)(2,1)} %get-tuple-element.114), channel_id=1, source_target_pairs={{0,24},{1,25},{2,26},{3,27},{4,28},{5,29},{6,30},{7,31},{8,0},{9,1... | collective-permute-start | bytes 1843208 | tf_op jit(solution)/shard_map/ppermute | solution.py:449
  120.0 96.4 %collective-permute-start.32 = (bf16[400,768]{1,0:T(8,128)(2,1)}, bf16[400,768]{1,0:T(8,128)(2,1)}, u32[]{:S(2)}, u32[]{:S(2)}) collective-permute-start(bf16[400,768]{1,0:T(8,128)(2,1)} %get-tuple-element.114), channel_id=1, source_target_pairs={{0,16},{1,17},{2,18},{3,19},{4,20},{5,21},{6,22},{7,23},{8,24},{9,... | collective-permute-start | bytes 1843208 | tf_op jit(solution)/shard_map/ppermute | solution.py:449
  120.2 96.2 %collective-permute-start.31 = (bf16[400,768]{1,0:T(8,128)(2,1)}, bf16[400,768]{1,0:T(8,128)(2,1)}, u32[]{:S(2)}, u32[]{:S(2)}) collective-permute-start(bf16[400,768]{1,0:T(8,128)(2,1)} %get-tuple-element.114), channel_id=1, source_target_pairs={{0,8},{1,9},{2,10},{3,11},{4,12},{5,13},{6,14},{7,15},{8,16},{9,17... | collective-permute-start | bytes 1843208 | tf_op jit(solution)/shard_map/ppermute | solution.py:449
  129.5 139.4 %collective-permute-start.5 = (bf16[2,400,768]{2,1,0:T(8,128)(2,1)}, bf16[2,400,768]{2,1,0:T(8,128)(2,1)}, u32[]{:S(2)}, u32[]{:S(2)}) collective-permute-start(bf16[2,400,768]{2,1,0:T(8,128)(2,1)} %pad_maximum_fusion.6), channel_id=1, source_target_pairs={{0,1},{1,0},{2,3},{3,2},{4,5},{5,4},{6,7},{7,6},{8,9},{9,8},{10,11... | collective-permute-start | bytes 3686408 | tf_op jit(solution)/shard_map/ppermute | solution.py:449
  158.9 81.9 %copy-start.55 = (bf16[400,768]{1,0:T(8,128)(2,1)}, bf16[400,768]{1,0:T(8,128)(2,1)S(1)}, u32[]{:S(2)}) copy-start(bf16[400,768]{1,0:T(8,128)(2,1)S(1)} %collective-permute-done.33) | copy-start | bytes 1843204
  158.9 86.0 %collective-permute-start.23 = (bf16[400,768]{1,0:T(8,128)(2,1)}, bf16[400,768]{1,0:T(8,128)(2,1)}, u32[]{:S(2)}, u32[]{:S(2)}) collective-permute-start(bf16[400,768]{1,0:T(8,128)(2,1)} %get-tuple-element.112), channel_id=1, source_target_pairs={{0,24},{1,25},{2,26},{3,27},{4,28},{5,29},{6,30},{7,31},{8,0},{9,1... | collective-permute-start | bytes 1843208 | tf_op jit(solution)/shard_map/ppermute | solution.py:449
  216.4 52.6 %collective-permute-start.22 = (bf16[400,768]{1,0:T(8,128)(2,1)}, bf16[400,768]{1,0:T(8,128)(2,1)}, u32[]{:S(2)}, u32[]{:S(2)}) collective-permute-start(bf16[400,768]{1,0:T(8,128)(2,1)} %get-tuple-element.112), channel_id=1, source_target_pairs={{0,16},{1,17},{2,18},{3,19},{4,20},{5,21},{6,22},{7,23},{8,24},{9,... | collective-permute-start | bytes 1843208 | tf_op jit(solution)/shard_map/ppermute | solution.py:449
  216.4 52.6 %collective-permute-start.21 = (bf16[400,768]{1,0:T(8,128)(2,1)}, bf16[400,768]{1,0:T(8,128)(2,1)}, u32[]{:S(2)}, u32[]{:S(2)}) collective-permute-start(bf16[400,768]{1,0:T(8,128)(2,1)} %get-tuple-element.112), channel_id=1, source_target_pairs={{0,8},{1,9},{2,10},{3,11},{4,12},{5,13},{6,14},{7,15},{8,16},{9,17... | collective-permute-start | bytes 1843208 | tf_op jit(solution)/shard_map/ppermute | solution.py:449
  240.8 28.1 %copy-start.14 = (bf16[1,400,768]{2,1,0:T(8,128)(2,1)S(1)}, bf16[1,400,768]{2,1,0:T(8,128)(2,1)}, u32[]{:S(2)}) copy-start(bf16[1,400,768]{2,1,0:T(8,128)(2,1)} %copy-done.13) | copy-start | bytes 1843204
  244.8 72.3 %collective-permute-start.3 = (bf16[4,256,768]{2,1,0:T(8,128)(2,1)}, bf16[4,256,768]{2,1,0:T(8,128)(2,1)}, u32[]{:S(2)}, u32[]{:S(2)}) collective-permute-start(bf16[4,256,768]{2,1,0:T(8,128)(2,1)} %bitcast.167), channel_id=1, source_target_pairs={{0,1},{1,0},{2,3},{3,2},{4,5},{5,4},{6,7},{7,6},{8,9},{9,8},{10,11... | collective-permute-start | bytes 4718600 | tf_op jit(solution)/shard_map/ppermute | solution.py:449
  244.8 81.1 %collective-permute-start.2 = (bf16[4,96,4096]{2,1,0:T(8,128)(2,1)}, bf16[4,96,4096]{2,1,0:T(8,128)(2,1)}, u32[]{:S(2)}, u32[]{:S(2)}) collective-permute-start(bf16[4,96,4096]{2,1,0:T(8,128)(2,1)} %bitcast.149), channel_id=1, source_target_pairs={{0,1},{1,0},{2,3},{3,2},{4,5},{5,4},{6,7},{7,6},{8,9},{9,8},{10,11... | collective-permute-start | bytes 9437192 | tf_op jit(solution)/shard_map/ppermute | solution.py:449
  315.1 5.9 collective-permute-start.8
  316.6 7.0 collective-permute-start.10
  322.2 31.0 %collective-permute-start.9 = (bf16[384,768]{1,0:T(8,128)(2,1)}, bf16[384,768]{1,0:T(8,128)(2,1)}, u32[]{:S(2)}, u32[]{:S(2)}) collective-permute-start(bf16[384,768]{1,0:T(8,128)(2,1)} %slice_bitcast_fusion.2), channel_id=1, source_target_pairs={{0,2},{1,3},{2,0},{3,1},{4,6},{5,7},{6,4},{7,5},{8,10},{9,11},{10,... | collective-permute-start | bytes 1769480 | tf_op jit(solution)/shard_map/ppermute | solution.py:449
  324.8 26.1 %collective-permute-start.11 = (bf16[400,768]{1,0:T(8,128)(2,1)}, bf16[400,768]{1,0:T(8,128)(2,1)S(1)}, u32[]{:S(2)}, u32[]{:S(2)}) collective-permute-start(bf16[400,768]{1,0:T(8,128)(2,1)} %slice_bitcast_fusion), channel_id=1, source_target_pairs={{0,2},{1,3},{2,0},{3,1},{4,6},{5,7},{6,4},{7,5},{8,10},{9,11},{10,... | collective-permute-start | bytes 1843208 | tf_op jit(solution)/shard_map/ppermute | solution.py:449
  355.9 41.3 %copy-start.4 = (f32[384,768]{1,0:T(8,128)}, f32[384,768]{1,0:T(8,128)S(1)}, u32[]{:S(2)}) copy-start(f32[384,768]{1,0:T(8,128)S(1)} %get-tuple-element.106) | copy-start | bytes 3538948
  380.9 35.8 %reduce-scatter.8.cloned.1.call-start = ((), (), s32[]{:S(2)}) async-start(), calls=%async_computation.4 | async-start | bytes 1179648 | tf_op jit(solution)/shard_map/reduce_scatter | solution.py:1086
  390.0 248.1 %reduce-scatter.10.cloned.1.call-start = ((), (), s32[]{:S(2)}) async-start(), calls=%async_computation.9 | async-start | bytes 245760
  398.2 20.4 %copy-start.7 = (bf16[768,768]{0,1:T(8,128)(2,1)}, bf16[768,768]{0,1:T(8,128)(2,1)S(1)}, u32[]{:S(2)}) copy-start(bf16[768,768]{0,1:T(8,128)(2,1)S(1)} %convolution_convert_fusion.3) | copy-start | bytes 3538948
  420.9 4.9 collective-permute-start.12
  420.9 98.7 %collective-permute-start.34 = (bf16[4,400,768]{2,1,0:T(8,128)(2,1)}, bf16[4,400,768]{2,1,0:T(8,128)(2,1)}, u32[]{:S(2)}, u32[]{:S(2)}) collective-permute-start(bf16[4,400,768]{2,1,0:T(8,128)(2,1)} %get-tuple-element.108.refs_8_), channel_id=1, source_target_pairs={{0,2},{1,5},{2,0},{3,7},{4,6},{5,1},{6,4},{7,3},{8,10},{9,13},{10,... | collective-permute-start | bytes 7372808 | tf_op jit(solution)/shard_map/ppermute | solution.py:449
  422.4 98.5 %collective-permute-start.35 = (bf16[4,400,768]{2,1,0:T(8,128)(2,1)}, bf16[4,400,768]{2,1,0:T(8,128)(2,1)}, u32[]{:S(2)}, u32[]{:S(2)}) collective-permute-start(bf16[4,400,768]{2,1,0:T(8,128)(2,1)} %get-tuple-element.108.refs_8_), channel_id=1, source_target_pairs={{0,4},{1,3},{2,6},{3,1},{4,0},{5,7},{6,2},{7,5},{8,12},{9,11},{10,... | collective-permute-start | bytes 7372808 | tf_op jit(solution)/shard_map/ppermute | solution.py:449
  422.9 98.0 %collective-permute-start.37 = (bf16[4,400,768]{2,1,0:T(8,128)(2,1)}, bf16[4,400,768]{2,1,0:T(8,128)(2,1)}, u32[]{:S(2)}, u32[]{:S(2)}) collective-permute-start(bf16[4,400,768]{2,1,0:T(8,128)(2,1)} %get-tuple-element.108.refs_8_), channel_id=1, source_target_pairs={{0,1},{1,0},{2,3},{3,2},{4,5},{5,4},{6,7},{7,6},{8,9},{9,8},{10,11... | collective-permute-start | bytes 7372808 | tf_op jit(solution)/shard_map/ppermute | solution.py:449
  422.9 98.5 %collective-permute-start.24 = (bf16[4,400,768]{2,1,0:T(8,128)(2,1)}, bf16[4,400,768]{2,1,0:T(8,128)(2,1)}, u32[]{:S(2)}, u32[]{:S(2)}) collective-permute-start(bf16[4,400,768]{2,1,0:T(8,128)(2,1)} %get-tuple-element.110.refs_0_), channel_id=1, source_target_pairs={{0,2},{1,5},{2,0},{3,7},{4,6},{5,1},{6,4},{7,3},{8,10},{9,13},{10,... | collective-permute-start | bytes 7372808 | tf_op jit(solution)/shard_map/ppermute | solution.py:449
  430.4 85.6 %collective-permute-start.13 = (bf16[768,768]{0,1:T(8,128)(2,1)}, bf16[768,768]{0,1:T(8,128)(2,1)}, u32[]{:S(2)}, u32[]{:S(2)}) collective-permute-start(bf16[768,768]{0,1:T(8,128)(2,1)} %broadcast_select_fusion.1), channel_id=1, source_target_pairs={{0,2},{1,5},{2,0},{3,7},{4,6},{5,1},{6,4},{7,3},{8,10},{9,13},{10,... | collective-permute-start | bytes 3538952 | tf_op jit(solution)/shard_map/ppermute | solution.py:449
  518.8 9.9 %collective-permute-start.14 = (bf16[768,384]{0,1:T(8,128)(2,1)S(1)}, bf16[768,384]{0,1:T(8,128)(2,1)S(1)}, u32[]{:S(2)}, u32[]{:S(2)}) collective-permute-start(bf16[768,384]{0,1:T(8,128)(2,1)S(1)} %broadcast_select_fusion.2), channel_id=1, source_target_pairs={{0,4},{1,3},{2,6},{3,1},{4,0},{5,7},{6,2},{7,5},{8,12},{9,11},{10,... | collective-permute-start | bytes 1769480 | tf_op jit(solution)/shard_map/ppermute | solution.py:449
  519.6 35.6 %collective-permute-start.36 = (bf16[4,400,768]{2,1,0:T(8,128)(2,1)}, bf16[4,400,768]{2,1,0:T(8,128)(2,1)}, u32[]{:S(2)}, u32[]{:S(2)}) collective-permute-start(bf16[4,400,768]{2,1,0:T(8,128)(2,1)} %collective-permute-done.34.refs_9_), channel_id=1, source_target_pairs={{0,4},{1,3},{2,6},{3,1},{4,0},{5,7},{6,2},{7,5},{8,12},{9,11},{10,... | collective-permute-start | bytes 7372808 | tf_op jit(solution)/shard_map/ppermute | solution.py:449
  520.9 37.9 %collective-permute-start.38 = (bf16[4,400,768]{2,1,0:T(8,128)(2,1)}, bf16[4,400,768]{2,1,0:T(8,128)(2,1)}, u32[]{:S(2)}, u32[]{:S(2)}) collective-permute-start(bf16[4,400,768]{2,1,0:T(8,128)(2,1)} %collective-permute-done.34.refs_9_), channel_id=1, source_target_pairs={{0,1},{1,0},{2,3},{3,2},{4,5},{5,4},{6,7},{7,6},{8,9},{9,8},{10,11... | collective-permute-start | bytes 7372808 | tf_op jit(solution)/shard_map/ppermute | solution.py:449
  520.9 37.8 %collective-permute-start.39 = (bf16[4,400,768]{2,1,0:T(8,128)(2,1)}, bf16[4,400,768]{2,1,0:T(8,128)(2,1)}, u32[]{:S(2)}, u32[]{:S(2)}) collective-permute-start(bf16[4,400,768]{2,1,0:T(8,128)(2,1)} %collective-permute-done.35.refs_10_), channel_id=1, source_target_pairs={{0,1},{1,0},{2,3},{3,2},{4,5},{5,4},{6,7},{7,6},{8,9},{9,8},{10,11... | collective-permute-start | bytes 7372808 | tf_op jit(solution)/shard_map/ppermute | solution.py:449
  521.4 60.1 %collective-permute-start.25 = (bf16[4,400,768]{2,1,0:T(8,128)(2,1)}, bf16[4,400,768]{2,1,0:T(8,128)(2,1)}, u32[]{:S(2)}, u32[]{:S(2)}) collective-permute-start(bf16[4,400,768]{2,1,0:T(8,128)(2,1)} %get-tuple-element.110.refs_0_), channel_id=1, source_target_pairs={{0,4},{1,3},{2,6},{3,1},{4,0},{5,7},{6,2},{7,5},{8,12},{9,11},{10,... | collective-permute-start | bytes 7372808 | tf_op jit(solution)/shard_map/ppermute | solution.py:449
  528.7 79.1 %collective-permute-start.26 = (bf16[4,400,768]{2,1,0:T(8,128)(2,1)}, bf16[4,400,768]{2,1,0:T(8,128)(2,1)}, u32[]{:S(2)}, u32[]{:S(2)}) collective-permute-start(bf16[4,400,768]{2,1,0:T(8,128)(2,1)} %collective-permute-done.24.refs_1_), channel_id=1, source_target_pairs={{0,4},{1,3},{2,6},{3,1},{4,0},{5,7},{6,2},{7,5},{8,12},{9,11},{10,... | collective-permute-start | bytes 7372808 | tf_op jit(solution)/shard_map/ppermute | solution.py:449
  555.1 52.7 %collective-permute-start.17 = (bf16[192,384]{1,0:T(8,128)(2,1)}, bf16[192,384]{1,0:T(8,128)(2,1)S(1)}, u32[]{:S(2)}, u32[]{:S(2)}) collective-permute-start(bf16[192,384]{1,0:T(8,128)(2,1)} %get-tuple-element.117), channel_id=1, source_target_pairs={{0,24},{1,25},{2,26},{3,27},{4,28},{5,29},{6,30},{7,31},{8,0},{9,1... | collective-permute-start | bytes 442376 | tf_op jit(solution)/shard_map/ppermute | solution.py:449
  558.7 49.6 %collective-permute-start.16 = (bf16[192,384]{1,0:T(8,128)(2,1)}, bf16[192,384]{1,0:T(8,128)(2,1)S(1)}, u32[]{:S(2)}, u32[]{:S(2)}) collective-permute-start(bf16[192,384]{1,0:T(8,128)(2,1)} %get-tuple-element.118), channel_id=1, source_target_pairs={{0,16},{1,17},{2,18},{3,19},{4,20},{5,21},{6,22},{7,23},{8,24},{9,... | collective-permute-start | bytes 442376 | tf_op jit(solution)/shard_map/ppermute | solution.py:449
  558.7 49.7 %collective-permute-start.15 = (bf16[192,384]{1,0:T(8,128)(2,1)S(1)}, bf16[192,384]{1,0:T(8,128)(2,1)S(1)}, u32[]{:S(2)}, u32[]{:S(2)}) collective-permute-start(bf16[192,384]{1,0:T(8,128)(2,1)S(1)} %get-tuple-element.116), channel_id=1, source_target_pairs={{0,8},{1,9},{2,10},{3,11},{4,12},{5,13},{6,14},{7,15},{8,16},{9,17... | collective-permute-start | bytes 442376 | tf_op jit(solution)/shard_map/ppermute | solution.py:449
  570.9 38.0 %copy-start.10 = (bf16[384,768]{1,0:T(8,128)(2,1)S(1)}, bf16[384,768]{1,0:T(8,128)(2,1)}, u32[]{:S(2)}) copy-start(bf16[384,768]{1,0:T(8,128)(2,1)} %copy-done.9) | copy-start | bytes 1769476
  570.9 38.9 %copy-start.43 = (bf16[384,12,64]{0,2,1:T(8,128)(2,1)S(1)}, bf16[384,12,64]{0,2,1:T(8,128)(2,1)}, u32[]{:S(2)}) copy-start(bf16[384,12,64]{0,2,1:T(8,128)(2,1)} %copy-done.42) | copy-start | bytes 1769476
  581.5 81.8 %collective-permute-start.27 = (bf16[4,400,768]{2,1,0:T(8,128)(2,1)}, bf16[4,400,768]{2,1,0:T(8,128)(2,1)}, u32[]{:S(2)}, u32[]{:S(2)}) collective-permute-start(bf16[4,400,768]{2,1,0:T(8,128)(2,1)} %get-tuple-element.110.refs_0_), channel_id=1, source_target_pairs={{0,1},{1,0},{2,3},{3,2},{4,5},{5,4},{6,7},{7,6},{8,9},{9,8},{10,11... | collective-permute-start | bytes 7372808 | tf_op jit(solution)/shard_map/ppermute | solution.py:449
  607.8 56.9 %collective-permute-start.40 = (bf16[4,400,768]{2,1,0:T(8,128)(2,1)}, bf16[4,400,768]{2,1,0:T(8,128)(2,1)}, u32[]{:S(2)}, u32[]{:S(2)}) collective-permute-start(bf16[4,400,768]{2,1,0:T(8,128)(2,1)} %collective-permute-done.36.refs_11_), channel_id=1, source_target_pairs={{0,1},{1,0},{2,3},{3,2},{4,5},{5,4},{6,7},{7,6},{8,9},{9,8},{10,11... | collective-permute-start | bytes 7372808 | tf_op jit(solution)/shard_map/ppermute | solution.py:449
  607.8 56.9 %collective-permute-start.28 = (bf16[4,400,768]{2,1,0:T(8,128)(2,1)}, bf16[4,400,768]{2,1,0:T(8,128)(2,1)}, u32[]{:S(2)}, u32[]{:S(2)}) collective-permute-start(bf16[4,400,768]{2,1,0:T(8,128)(2,1)} %collective-permute-done.24.refs_1_), channel_id=1, source_target_pairs={{0,1},{1,0},{2,3},{3,2},{4,5},{5,4},{6,7},{7,6},{8,9},{9,8},{10,11... | collective-permute-start | bytes 7372808 | tf_op jit(solution)/shard_map/ppermute | solution.py:449
  608.3 56.4 %collective-permute-start.29 = (bf16[4,400,768]{2,1,0:T(8,128)(2,1)}, bf16[4,400,768]{2,1,0:T(8,128)(2,1)}, u32[]{:S(2)}, u32[]{:S(2)}) collective-permute-start(bf16[4,400,768]{2,1,0:T(8,128)(2,1)} %collective-permute-done.25.refs_2_), channel_id=1, source_target_pairs={{0,1},{1,0},{2,3},{3,2},{4,5},{5,4},{6,7},{7,6},{8,9},{9,8},{10,11... | collective-permute-start | bytes 7372808 | tf_op jit(solution)/shard_map/ppermute | solution.py:449
  608.4 56.3 %collective-permute-start.30 = (bf16[4,400,768]{2,1,0:T(8,128)(2,1)}, bf16[4,400,768]{2,1,0:T(8,128)(2,1)}, u32[]{:S(2)}, u32[]{:S(2)}) collective-permute-start(bf16[4,400,768]{2,1,0:T(8,128)(2,1)} %collective-permute-done.26.refs_3_), channel_id=1, source_target_pairs={{0,1},{1,0},{2,3},{3,2},{4,5},{5,4},{6,7},{7,6},{8,9},{9,8},{10,11... | collective-permute-start | bytes 7372808 | tf_op jit(solution)/shard_map/ppermute | solution.py:449
  618.2 165.3 %all-gather.9.cloned.1.call-start = ((), (), s32[]{:S(2)}) async-start(), calls=%async_computation.5 | async-start | bytes 1769472 | tf_op jit(solution)/shard_map/all_gather | solution.py:1151
  618.2 44.9 %copy-start.59 = (bf16[192,384]{1,0:T(8,128)(2,1)S(1)}, bf16[192,384]{1,0:T(8,128)(2,1)}, u32[]{:S(2)}) copy-start(bf16[192,384]{1,0:T(8,128)(2,1)} %copy-done.58) | copy-start | bytes 442372
  663.2 40.3 %collective-permute-start.18 = (bf16[192,384]{1,0:T(8,128)(2,1)S(1)}, bf16[192,384]{1,0:T(8,128)(2,1)S(1)}, u32[]{:S(2)}, u32[]{:S(2)}) collective-permute-start(bf16[192,384]{1,0:T(8,128)(2,1)S(1)} %fusion.55), channel_id=1, source_target_pairs={{0,4},{1,3},{2,6},{3,1},{4,0},{5,7},{6,2},{7,5},{8,12},{9,11},{10,... | collective-permute-start | bytes 442376 | tf_op jit(solution)/shard_map/ppermute | solution.py:449
  703.7 6.8 collective-permute-start.19
  710.6 70.5 %collective-permute-start.20 = (bf16[192,1536]{1,0:T(8,128)(2,1)S(1)}, bf16[192,1536]{1,0:T(8,128)(2,1)S(1)}, u32[]{:S(2)}, u32[]{:S(2)}) collective-permute-start(bf16[192,1536]{1,0:T(8,128)(2,1)S(1)} %maximum_select_fusion.4), channel_id=1, source_target_pairs={{0,1},{1,0},{2,3},{3,2},{4,5},{5,4},{6,7},{7,6},{8,9},{9,8},{10,11... | collective-permute-start | bytes 1769480 | tf_op jit(solution)/shard_map/ppermute | solution.py:449
  (55 other events, 227.5 us)
Sparse Core Ops, SparseCore 0:
  12.0 48.0 all-gather.10
  62.3 37.3 all-gather.14
  101.9 109.4 all-gather.12
  381.0 15.9 reduce-scatter.5
  399.2 17.4 reduce-scatter.7
  618.3 19.7 reduce-scatter.9
  706.5 23.8 all-gather.8

commit v2 on v1

--- a/solution.py
+++ b/solution.py
@@ -469,24 +469,6 @@
     return moved(value, lambda z, y, x, c: ((z + step) % 4, y, x, c))
 
 
-def gather_blocks(block):
-    column = jnp.stack([block] + [over_z(block, step) for step in (1, 2, 3)])
-    first = over_a(column)
-    second = over_b(column)
-    third = over_b(first)
-    mine = [column, first, second, third]
-    return mine + [over_core(part) for part in mine]
-
-
-def gather_rows(shard, core):
-    half = shard.shape[0] // 2
-    part = lax.dynamic_slice_in_dim(shard, core * half, half, 0)
-    part = lax.all_gather(part, "dp", axis=0, tiled=False)
-    other = over_core(part)
-    both = jnp.where(core == 0, jnp.stack([part, other], 1), jnp.stack([other, part], 1))
-    return both.reshape(-1, shard.shape[1])
-
-
 def contract(left, right, left_dim, right_dim):
     return lax.dot_general(
         left, right, (((left_dim,), (right_dim,)), ((), ())), preferred_element_type=F32
@@ -504,38 +486,36 @@
 
 
 def group_kernel(
+    blocks,
     base_ref,
-    h_ref,
-    g_ref,
-    wg_ref,
-    wu_ref,
-    wd_ref,
-    moe_ref,
-    dx_ref,
-    rank_sc,
-    prob_sc,
-    x_sc,
-    gd_sc,
-    gate_sc,
-    y_sc,
-    acc_sc,
-    dgate_sc,
-    ysel_sc,
-    dsel_sc,
-    drp_sc,
+    *refs,
 ):
+    h_refs, g_refs = refs[:blocks], refs[blocks : 2 * blocks]
+    wg_ref, wu_ref, wd_ref, moe_ref, moe_far_ref, dx_ref, dx_far_ref = refs[2 * blocks : 2 * blocks + 7]
+    (
+        rank_sc,
+        prob_sc,
+        x_sc,
+        gd_sc,
+        gate_sc,
+        y_sc,
+        acc_sc,
+        dgate_sc,
+        ysel_sc,
+        dsel_sc,
+        drp_sc,
+    ) = refs[2 * blocks + 7 :]
     e = pl.program_id(0)
     f = pl.program_id(1)
-    blocks = h_ref.shape[0]
     experts = pl.num_programs(0)
     base = base_ref[0]
 
     @pl.when((e == 0) & (f == 0))
     def _():
         for b in range(blocks):
-            rank_sc[b] = g_ref[b, TOK_DEV:, :TOK_DEV].astype(F32)
-            prob_sc[b] = h_ref[b, TOK_DEV:, :TOK_DEV].astype(F32) + h_ref[
-                b, TOK_DEV:, TOK_DEV:
+            rank_sc[b] = g_refs[b][TOK_DEV:, :TOK_DEV].astype(F32)
+            prob_sc[b] = h_refs[b][TOK_DEV:, :TOK_DEV].astype(F32) + h_refs[b][
+                TOK_DEV:, TOK_DEV:
             ].astype(F32)
         drp_sc[...] = jnp.zeros_like(drp_sc)
 
@@ -549,8 +529,8 @@
                     hot * prob_sc[b, pl.ds(base + e, 1), :], -1, keepdims=True
                 )
                 hot = hot.astype(BF)
-                rows_x.append(jnp.dot(hot, h_ref[b, :TOK_DEV, :], preferred_element_type=F32))
-                rows_g.append(jnp.dot(hot, g_ref[b, :TOK_DEV, :], preferred_element_type=F32))
+                rows_x.append(jnp.dot(hot, h_refs[b][:TOK_DEV, :], preferred_element_type=F32))
+                rows_g.append(jnp.dot(hot, g_refs[b][:TOK_DEV, :], preferred_element_type=F32))
             span = slice(pair * 2 * SLOT, (pair + 1) * 2 * SLOT)
             x_sc[span, :] = jnp.concatenate(rows_x, 0).astype(BF)
             gd_sc[span, :] = jnp.concatenate(rows_g, 0).astype(BF)
@@ -584,6 +564,9 @@
     @pl.when((f == pl.num_programs(1) - 1) & (e == experts - 1))
     def _():
         for b in range(blocks):
+            moe_out, dx_out, at = (
+                (moe_ref, dx_ref, b) if b < blocks // 2 else (moe_far_ref, dx_far_ref, b - blocks // 2)
+            )
             hot = jnp.concatenate(
                 [
                     one_hot_rows(rank_sc[b, pl.ds(base + i, 1), :])
@@ -591,35 +574,34 @@
                 ],
                 0,
             ).astype(BF)
-            moe_ref[b] = contract(hot, ysel_sc[b].astype(BF), 0, 0).astype(BF)
-            dx_ref[b, :TOK_DEV, :] = contract(hot, dsel_sc[b].astype(BF), 0, 0).astype(BF)
+            moe_out[at] = contract(hot, ysel_sc[b].astype(BF), 0, 0).astype(BF)
+            dx_out[at, :TOK_DEV, :] = contract(hot, dsel_sc[b].astype(BF), 0, 0).astype(BF)
             high = drp_sc[b].astype(BF)
-            dx_ref[b, TOK_DEV:, :TOK_DEV] = high
-            dx_ref[b, TOK_DEV:, TOK_DEV:] = (drp_sc[b] - high.astype(F32)).astype(BF)
+            dx_out[at, TOK_DEV:, :TOK_DEV] = high
+            dx_out[at, TOK_DEV:, TOK_DEV:] = (drp_sc[b] - high.astype(F32)).astype(BF)
 
 
 def group_experts(base, h_group, g_group, w_gate, w_up, w_down):
-    blocks = h_group.shape[0]
+    blocks = len(h_group)
     experts, _, ff = w_gate.shape
     tile = 512
     whole = lambda *shape: pl.BlockSpec(shape, lambda e, f, s: (0,) * len(shape))
+    moe_shape, dx_shape = (blocks // 2, TOK_DEV, D), (blocks // 2, ROWS, D)
     return pl.pallas_call(
-        group_kernel,
-        out_shape=(
-            jax.ShapeDtypeStruct((blocks, TOK_DEV, D), BF),
-            jax.ShapeDtypeStruct((blocks, ROWS, D), BF),
+        functools.partial(group_kernel, blocks),
+        out_shape=tuple(
+            jax.ShapeDtypeStruct(s, BF) for s in (moe_shape, moe_shape, dx_shape, dx_shape)
         ),
         grid_spec=pltpu.PrefetchScalarGridSpec(
             num_scalar_prefetch=1,
             grid=(experts, ff // tile),
-            in_specs=[
-                whole(blocks, ROWS, D),
-                whole(blocks, ROWS, D),
+            in_specs=[whole(ROWS, D)] * (2 * blocks)
+            + [
                 pl.BlockSpec((1, D, tile), lambda e, f, s: (e, 0, f)),
                 pl.BlockSpec((1, D, tile), lambda e, f, s: (e, 0, f)),
                 pl.BlockSpec((1, tile, D), lambda e, f, s: (e, f, 0)),
             ],
-            out_specs=[whole(blocks, TOK_DEV, D), whole(blocks, ROWS, D)],
+            out_specs=[whole(*moe_shape)] * 2 + [whole(*dx_shape)] * 2,
             scratch_shapes=[
                 pltpu.VMEM((blocks, EXPERTS, TOK_DEV), F32),
                 pltpu.VMEM((blocks, EXPERTS, TOK_DEV), F32),
@@ -641,48 +623,68 @@
             transcendentals=0,
         ),
         name="group_experts",
-    )(base, h_group, g_group, w_gate, w_up, w_down)
-
-
-def shared_kernel(h_ref, g_ref, wg_ref, wu_ref, wd_ref, out_ref, dh_ref):
-    @pl.when(pl.program_id(0) == 0)
-    def _():
-        out_ref[...] = jnp.zeros_like(out_ref)
-        dh_ref[...] = jnp.zeros_like(dh_ref)
-
-    gate_pre = jnp.dot(h_ref[...], wg_ref[...], preferred_element_type=F32)
-    up_pre = jnp.dot(h_ref[...], wu_ref[...], preferred_element_type=F32)
-    back = contract(g_ref[...], wd_ref[...], 1, 1)
-    swish, slope = swish_parts(gate_pre)
-    inner = (swish * up_pre).astype(BF)
-    out_ref[...] += jnp.dot(inner, wd_ref[...], preferred_element_type=F32)
-    dgate_pre = (back * up_pre * slope).astype(BF)
-    dup_pre = (back * swish).astype(BF)
-    dh_ref[...] += contract(dgate_pre, wg_ref[...], 1, 1) + contract(dup_pre, wu_ref[...], 1, 1)
-
-
-def shared_rows(h2, grad, w_gate, w_up, w_down):
-    tokens, ff = h2.shape[0], w_gate.shape[1]
-    tile = 512
-    rows = pl.BlockSpec((tokens, D), lambda f: (0, 0))
+    )(base, *h_group, *g_group, w_gate, w_up, w_down)
+
+
+def shared_kernel(parts, h_ref, g_ref, *refs):
+    bufs = refs[:parts]
+    out_ref, dh_ref, gu_sc, down_sc, sems = refs[parts:]
+    copies = []
+    for k, buf in enumerate(bufs):
+        mine = [pltpu.make_async_copy(buf.at[:, :, :512], gu_sc.at[k], sems.at[k, 3])]
+        for i in range(3):
+            mine.append(
+                pltpu.make_async_copy(
+                    buf.at[:, 64 * i : 64 * (i + 1), 512:],
+                    down_sc.at[k, :, :, 256 * i : 256 * (i + 1)],
+                    sems.at[k, i],
+                )
+            )
+        copies.append(mine)
+        for one in mine:
+            one.start()
+    for k in range(parts):
+        for one in copies[k]:
+            one.wait()
+        gate_up = gu_sc[k].reshape(D, 512)
+        w_gate, w_up, w_down = gate_up[:, :256], gate_up[:, 256:], down_sc[k].reshape(256, D)
+        gate_pre = jnp.dot(h_ref[:TOK_DEV, :], w_gate, preferred_element_type=F32)
+        up_pre = jnp.dot(h_ref[:TOK_DEV, :], w_up, preferred_element_type=F32)
+        back = contract(g_ref[...], w_down, 1, 1)
+        swish, slope = swish_parts(gate_pre)
+        inner = (swish * up_pre).astype(BF)
+        out = jnp.dot(inner, w_down, preferred_element_type=F32)
+        dgate_pre = (back * up_pre * slope).astype(BF)
+        dup_pre = (back * swish).astype(BF)
+        dh = contract(dgate_pre, w_gate, 1, 1) + contract(dup_pre, w_up, 1, 1)
+        if k == 0:
+            out_ref[...] = out
+            dh_ref[...] = dh
+        else:
+            out_ref[...] += out
+            dh_ref[...] += dh
+
+
+def shared_rows(h_block, grad, bufs):
+    parts = len(bufs)
+    rows = jax.ShapeDtypeStruct((TOK_DEV, D), F32)
+    vmem = pl.BlockSpec(memory_space=pltpu.VMEM)
     return pl.pallas_call(
-        shared_kernel,
-        out_shape=(jax.ShapeDtypeStruct((tokens, D), F32),) * 2,
-        grid=(ff // tile,),
-        in_specs=[
-            rows,
-            rows,
-            pl.BlockSpec((D, tile), lambda f: (0, f)),
-            pl.BlockSpec((D, tile), lambda f: (0, f)),
-            pl.BlockSpec((tile, D), lambda f: (f, 0)),
+        functools.partial(shared_kernel, parts),
+        out_shape=(rows, rows),
+        in_specs=[vmem, vmem] + [pl.BlockSpec(memory_space=pl.ANY)] * parts,
+        out_specs=(vmem, vmem),
+        scratch_shapes=[
+            pltpu.VMEM((parts, 4, D // 4, 512), BF),
+            pltpu.VMEM((parts, 4, 64, D), BF),
+            pltpu.SemaphoreType.DMA((parts, 4)),
         ],
-        out_specs=[rows, rows],
         compiler_params=pltpu.CompilerParams(vmem_limit_bytes=VMEM_LIMIT),
         cost_estimate=pl.CostEstimate(
-            flops=2 * 6 * tokens * D * ff, bytes_accessed=2 * 3 * D * ff, transcendentals=0
+            flops=2 * 6 * TOK_DEV * D * 2048, bytes_accessed=6 * D * 2048, transcendentals=0
         ),
         name="shared_rows",
-    )(h2, grad, w_gate, w_up, w_down)
+    )(h_block, grad, *bufs)
 
 
 def start_half(part, h_parts, g_parts, h_buf, g_buf, sems):
@@ -820,8 +822,12 @@
 
 def shared_slice_kernel(parts, pos_ref, *refs):
     h_parts, g_parts = refs[:parts], refs[parts : 2 * parts]
-    wg_ref, wu_ref, wd_ref, og_ref, ou_ref, od_ref = refs[2 * parts : 2 * parts + 6]
-    h_buf, g_buf, inner_sc, sems = refs[2 * parts + 6 :]
+    w_ref, og_ref, ou_ref, od_ref = refs[2 * parts : 2 * parts + 4]
+    h_buf, g_buf, inner_sc, wg_ref, wu_ref, wd_ref, sems = refs[2 * parts + 4 :]
+    wg_ref[...] = w_ref[:, :, :256].reshape(D, 256)
+    wu_ref[...] = w_ref[:, :, 256:512].reshape(D, 256)
+    for i in range(3):
+        wd_ref[:, 256 * i : 256 * (i + 1)] = w_ref[:, 64 * i : 64 * (i + 1), 512:].reshape(256, 256)
     half = parts // 2
     per = h_parts[0].shape[0]
     window = pl.ds(pl.multiple_of(pos_ref[0] * 128, 128), og_ref.shape[0])
@@ -857,10 +863,10 @@
             start_half(1, h_parts, g_parts, h_buf, g_buf, sems)
 
 
-def shared_slice_grads(pos, h_parts, g_parts, w_gate, w_up, w_down):
+def shared_slice_grads(pos, h_parts, g_parts, weights):
     parts, per = len(h_parts), h_parts[0].shape[0]
     blocks = parts * per // 2
-    width = w_gate.shape[1]
+    width = 256
     anywhere = pl.BlockSpec(memory_space=pl.ANY)
     whole = lambda *shape: pl.BlockSpec(shape, lambda i, s: (0,) * len(shape))
     return pl.pallas_call(
@@ -874,12 +880,15 @@
             num_scalar_prefetch=1,
             grid=(1,),
             in_specs=[anywhere] * (2 * parts)
-            + [whole(D, width), whole(D, width), whole(width, D)],
+            + [whole(4, D // 4, D)],
             out_specs=[whole(256, width), whole(256, width), whole(128, D)],
             scratch_shapes=[
                 pltpu.VMEM((blocks, ROWS, D), BF),
                 pltpu.VMEM((blocks, ROWS, D), BF),
                 pltpu.VMEM((2 * TOK_DEV, width), BF),
+                pltpu.VMEM((D, width), BF),
+                pltpu.VMEM((D, width), BF),
+                pltpu.VMEM((width, D), BF),
                 pltpu.SemaphoreType.DMA((2, parts // 2)),
             ],
         ),
@@ -890,7 +899,7 @@
             transcendentals=0,
         ),
         name="shared_slice_grads",
-    )(pos, *h_parts, *g_parts, w_gate, w_up, w_down)
+    )(pos, *h_parts, *g_parts, weights)
 
 
 def pair_sum(kept, received):
@@ -909,8 +918,461 @@
     )
 
 
+def lane_halves():
+    lane = lax.broadcasted_iota(jnp.int32, (1, 128), 1)
+    return [(lane < 64).astype(F32).astype(BF), (lane >= 64).astype(F32).astype(BF)]
+
+
+def pick_lanes(first, second):
+    lane = lax.broadcasted_iota(jnp.int32, first.shape, 1)
+    return jnp.where(lane < 64, first, second)
+
+
+def turned(value, cos, sin):
+    lane = lax.broadcasted_iota(jnp.int32, value.shape, 1)
+    partner = jnp.where(lane % 64 < 32, pltpu.roll(value, 96, 1), pltpu.roll(value, 32, 1))
+    return value * cos + partner * sin
+
+
+def causal_mask(rows):
+    row = lax.broadcasted_iota(jnp.int32, (rows, rows), 0)
+    col = lax.broadcasted_iota(jnp.int32, (rows, rows), 1)
+    return row, col
+
+
+def unit_rms(value):
+    return lax.rsqrt(jnp.mean(value * value, -1, keepdims=True) + EPS)
+
+
+def softmax_of(first, second=None):
+    top = jnp.max(first, -1, keepdims=True)
+    if second is not None:
+        top = jnp.maximum(top, jnp.max(second, -1, keepdims=True))
+    first = jnp.exp(first - top)
+    total = jnp.sum(first, -1, keepdims=True)
+    if second is None:
+        return first * (1.0 / total)
+    second = jnp.exp(second - top)
+    scale = 1.0 / (total + jnp.sum(second, -1, keepdims=True))
+    return first * scale, second * scale
+
+
+def attention_kernel(place_ref, *refs):
+    w_parts = refs[:8]
+    (
+        own_ref,
+        far_ref,
+        gain1_ref,
+        gain2_ref,
+        router_ref,
+        cos_ref,
+        sin_ref,
+        w_ref,
+        q_ref,
+        k_ref,
+        v_ref,
+        h1_ref,
+        o_ref,
+        x1_ref,
+        h2_ref,
+        h_sc,
+        sems,
+    ) = refs[8:]
+    copies = []
+    for part in range(8):
+        for slot in range(4):
+            rows = pl.ds(pl.multiple_of(place_ref[8 + slot] * 192, 192), 192)
+            copies.append(
+                pltpu.make_async_copy(
+                    w_parts[part].at[slot, :192, :],
+                    w_ref.at[place_ref[part], rows, :],
+                    sems.at[part, slot],
+                )
+            )
+    for one in copies:
+        one.start()
+    inputs = own_ref[:TOK_DEV, :].astype(F32)
+    h_sc[:TOK_DEV, :] = (inputs * unit_rms(inputs) * gain1_ref[...]).astype(BF)
+    far = far_ref[:TOK_DEV, :].astype(F32)
+    h_sc[TOK_DEV:, :] = (far * unit_rms(far) * gain1_ref[...]).astype(BF)
+    h1_ref[...] = h_sc[:TOK_DEV, :]
+    for one in copies:
+        one.wait()
+    for i in range(6):
+        out_ref = (q_ref, k_ref, v_ref)[i // 2]
+        product = jnp.dot(h_sc[...], w_ref[i], preferred_element_type=F32)
+        for slab in range(3):
+            at = (i % 2) * 384 + slab * 128
+            for half in range(2):
+                rows = slice(half * TOK_DEV, (half + 1) * TOK_DEV)
+                value = product[rows, slab * 128 : (slab + 1) * 128]
+                if i < 4:
+                    value = turned(value, cos_ref[...], sin_ref[...])
+                out_ref[rows, at : at + 128] = value.astype(BF)
+    masks = lane_halves()
+    row, col = causal_mask(PROMPT)
+    prompt_ok = col <= row
+    row, col = causal_mask(CONT * CLEN)
+    cont_ok = (row // CLEN == col // CLEN) & (col <= row)
+    row = lax.broadcasted_iota(jnp.int32, (CONT * CLEN, 1), 0)
+    reads_far = jnp.where(row < CLEN, place_ref[12], place_ref[13]).astype(F32)
+    own_c = slice(PROMPT, TOK_DEV)
+    far_p = slice(TOK_DEV, TOK_DEV + PROMPT)
+
+    def heads(pair, carry):
+        cols = pl.ds(pl.multiple_of(pair * 128, 128), 128)
+        q_p, k_p, v_p = q_ref[:PROMPT, cols], k_ref[:PROMPT, cols], v_ref[:PROMPT, cols]
+        q_c, k_c, v_c = q_ref[own_c, cols], k_ref[own_c, cols], v_ref[own_c, cols]
+        k_f, v_f = k_ref[far_p, cols], v_ref[far_p, cols]
+        out_p, out_c = [], []
+        for mask in masks:
+            score = jnp.where(prompt_ok, 0.125 * contract(q_p * mask, k_p, 1, 1), -1e30)
+            out_p.append(
+                jnp.dot(softmax_of(score).astype(BF), v_p, preferred_element_type=F32)
+            )
+            query = q_c * mask
+            near, far = contract(query, k_p, 1, 1), contract(query, k_f, 1, 1)
+            first = 0.125 * jnp.where(reads_far > 0.5, far, near)
+            second = jnp.where(cont_ok, 0.125 * contract(query, k_c, 1, 1), -1e30)
+            first, second = softmax_of(first, second)
+            out_c.append(
+                jnp.dot((first * (1.0 - reads_far)).astype(BF), v_p, preferred_element_type=F32)
+                + jnp.dot((first * reads_far).astype(BF), v_f, preferred_element_type=F32)
+                + jnp.dot(second.astype(BF), v_c, preferred_element_type=F32)
+            )
+        o_ref[:PROMPT, cols] = pick_lanes(*out_p).astype(BF)
+        o_ref[own_c, cols] = pick_lanes(*out_c).astype(BF)
+        return carry
+
+    lax.fori_loop(0, HEADS // 2, heads, 0)
+    for i in range(2):
+        cols = slice(384 * i, 384 * (i + 1))
+        x1_ref[:, cols] = own_ref[:TOK_DEV, cols].astype(F32) + jnp.dot(
+            o_ref[...], w_ref[6 + i], preferred_element_type=F32
+        )
+    resid = x1_ref[...]
+    hidden = (resid * unit_rms(resid) * gain2_ref[...]).astype(BF)
+    h2_ref[:TOK_DEV, :] = hidden
+    logits = contract(router_ref[...], hidden, 1, 1)
+    logits = jnp.exp(logits - jnp.max(logits, 0, keepdims=True))
+    probs = logits / jnp.sum(logits, 0, keepdims=True)
+    high = probs.astype(BF)
+    h2_ref[TOK_DEV:, :TOK_DEV] = high
+    h2_ref[TOK_DEV:, TOK_DEV:] = (probs - high.astype(F32)).astype(BF)
+
+
+def attention_forward(place, w_parts, own, far, gain1, gain2, router_t, cos, sin):
+    vmem = pl.BlockSpec(memory_space=pltpu.VMEM)
+    shape = jax.ShapeDtypeStruct
+    return pl.pallas_call(
+        attention_kernel,
+        out_shape=(
+            shape((8, D, 384), BF),
+            shape((2 * TOK_DEV, D), BF),
+            shape((2 * TOK_DEV, D), BF),
+            shape((2 * TOK_DEV, D), BF),
+            shape((TOK_DEV, D), BF),
+            shape((TOK_DEV, D), BF),
+            shape((TOK_DEV, D), F32),
+            shape((ROWS, D), BF),
+        ),
+        in_specs=[pl.BlockSpec(memory_space=pltpu.SMEM)]
+        + [pl.BlockSpec(memory_space=pl.ANY)] * 8
+        + [vmem] * 7,
+        out_specs=(vmem,) * 8,
+        scratch_shapes=[
+            pltpu.VMEM((2 * TOK_DEV, D), BF),
+            pltpu.SemaphoreType.DMA((8, 4)),
+        ],
+        compiler_params=pltpu.CompilerParams(vmem_limit_bytes=VMEM_LIMIT),
+        cost_estimate=pl.CostEstimate(
+            flops=2 * 2 * TOK_DEV * D * 4 * D, bytes_accessed=8 * 2 * D * D, transcendentals=0
+        ),
+        name="attention_forward",
+    )(place, *w_parts, own, far, gain1, gain2, router_t, cos, sin)
+
+
+def branch_kernel(
+    dx_a_ref,
+    dx_b_ref,
+    dsh_ref,
+    h2_ref,
+    x1_ref,
+    g_ref,
+    gain2_ref,
+    router_ref,
+    o_ref,
+    w_ref,
+    dx1_ref,
+    do_ref,
+    do_c_ref,
+    gwo_ref,
+    grouter_ref,
+    ggain_ref,
+):
+    tail = dx_a_ref[TOK_DEV:, :].astype(F32) + dx_b_ref[TOK_DEV:, :].astype(F32)
+    drp = tail[:, :TOK_DEV] + tail[:, TOK_DEV:]
+    probs = h2_ref[TOK_DEV:, :TOK_DEV].astype(F32) + h2_ref[TOK_DEV:, TOK_DEV:].astype(F32)
+    dlogits = (probs * (drp - jnp.sum(probs * drp, 0, keepdims=True))).astype(BF)
+    hidden = h2_ref[:TOK_DEV, :]
+    grouter_ref[...] = jnp.dot(dlogits, hidden, preferred_element_type=F32)
+    dh2 = (
+        dx_a_ref[:TOK_DEV, :].astype(F32)
+        + dx_b_ref[:TOK_DEV, :].astype(F32)
+        + dsh_ref[...]
+        + contract(dlogits, router_ref[...], 0, 0)
+    )
+    resid = x1_ref[...]
+    scale = unit_rms(resid)
+    normed = resid * scale
+    ggain_ref[...] = jnp.sum(dh2 * normed, 0, keepdims=True)
+    dnormed = dh2 * gain2_ref[...]
+    dx1 = scale * (dnormed - normed * jnp.mean(dnormed * normed, -1, keepdims=True)) + g_ref[
+        ...
+    ].astype(F32)
+    dx1_ref[...] = dx1
+    datt = dx1.astype(BF)
+    do_ref[...] = (
+        contract(datt[:, :384], w_ref[0], 1, 1) + contract(datt[:, 384:], w_ref[1], 1, 1)
+    ).astype(BF)
+    do_c_ref[...] = do_ref[PROMPT:, :]
+    gwo_ref[...] = contract(o_ref[...], datt, 0, 0).astype(BF)
+
+
+def branch_backward(dx_a, dx_b, dsh, h_block, x1, grad, gain2, router_t, o, w_all):
+    shape = jax.ShapeDtypeStruct
+    whole = lambda *dims: pl.BlockSpec(dims, lambda i: (0,) * len(dims))
+    rows = whole(TOK_DEV, D)
+    return pl.pallas_call(
+        branch_kernel,
+        grid=(1,),
+        out_shape=(
+            shape((TOK_DEV, D), F32),
+            shape((TOK_DEV, D), BF),
+            shape((TOK_DEV - PROMPT, D), BF),
+            shape((D, D), BF),
+            shape((EXPERTS, D), F32),
+            shape((1, D), F32),
+        ),
+        in_specs=[
+            whole(ROWS, D),
+            whole(ROWS, D),
+            rows,
+            whole(ROWS, D),
+            rows,
+            rows,
+            whole(1, D),
+            whole(EXPERTS, D),
+            rows,
+            pl.BlockSpec((2, D, 384), lambda i: (3, 0, 0)),
+        ],
+        out_specs=(
+            rows,
+            rows,
+            whole(TOK_DEV - PROMPT, D),
+            whole(D, D),
+            whole(EXPERTS, D),
+            whole(1, D),
+        ),
+        compiler_params=pltpu.CompilerParams(vmem_limit_bytes=VMEM_LIMIT),
+        cost_estimate=pl.CostEstimate(
+            flops=2 * 2 * TOK_DEV * D * D, bytes_accessed=12 * TOK_DEV * D, transcendentals=0
+        ),
+        name="branch_backward",
+    )(dx_a, dx_b, dsh, h_block, x1, grad, gain2, router_t, o, w_all)
+
+
+def attention_back_kernel(
+    flags_ref,
+    q_ref,
+    k_ref,
+    v_ref,
+    do_ref,
+    do_far_ref,
+    h1_ref,
+    w_ref,
+    own_ref,
+    gain1_ref,
+    cos_ref,
+    sin_ref,
+    dx1_ref,
+    gwo_ref,
+    gtok_ref,
+    gqk_ref,
+    gvo_ref,
+    ggain_ref,
+    dq_sc,
+    dk_sc,
+    dv_sc,
+    low_sc,
+):
+    masks = lane_halves()
+    row, col = causal_mask(PROMPT)
+    prompt_ok = col <= row
+    cont_ok = (row // CLEN == col // CLEN) & (col <= row)
+    row = lax.broadcasted_iota(jnp.int32, (4 * CLEN, 1), 0) // CLEN
+    near = jnp.where(
+        row < 2,
+        jnp.where(row == 0, flags_ref[0], flags_ref[1]),
+        jnp.where(row == 2, flags_ref[2], flags_ref[3]),
+    ).astype(F32)
+    own_c = slice(PROMPT, TOK_DEV)
+    far_p = slice(TOK_DEV, TOK_DEV + PROMPT)
+    far_c = slice(TOK_DEV + PROMPT, 2 * TOK_DEV)
+    cont = CONT * CLEN
+
+    def either(own_near, far_own):
+        return jnp.concatenate(
+            [jnp.where(near[:cont] > 0.5, own_near[:cont], far_own), own_near[cont:]], 0
+        )
+
+    def heads(pair, carry):
+        cols = pl.ds(pl.multiple_of(pair * 128, 128), 128)
+        q_p, k_p, v_p = q_ref[:PROMPT, cols], k_ref[:PROMPT, cols], v_ref[:PROMPT, cols]
+        k_f, v_f = k_ref[far_p, cols], v_ref[far_p, cols]
+        q_c, k_c, v_c = q_ref[own_c, cols], k_ref[own_c, cols], v_ref[own_c, cols]
+        do_p, do_c = do_ref[:PROMPT, cols], do_ref[own_c, cols]
+        q_4 = jnp.concatenate([q_c, q_ref[far_c, cols]], 0)
+        k_4 = jnp.concatenate([k_c, k_ref[far_c, cols]], 0)
+        v_4 = jnp.concatenate([v_c, v_ref[far_c, cols]], 0)
+        do_4 = jnp.concatenate([do_c, do_far_ref[:, cols]], 0)
+        q_all = jnp.concatenate([q_p, q_4], 0)
+        do_all = jnp.concatenate([do_p, do_4], 0)
+        dq_p, dq_c, dk_p, dk_c, dv_p, dv_c = [], [], [], [], [], []
+        for mask in masks:
+            score = jnp.where(prompt_ok, 0.125 * contract(q_p * mask, k_p, 1, 1), -1e30)
+            prob = softmax_of(score)
+            dprob = contract(do_p * mask, v_p, 1, 1)
+            ds = (prob * (dprob - jnp.sum(prob * dprob, -1, keepdims=True))).astype(BF)
+            query, grad = q_4 * mask, do_4 * mask
+            first = 0.125 * either(
+                contract(query, k_p, 1, 1), contract(query[:cont], k_f, 1, 1)
+            )
+            second = jnp.where(cont_ok, 0.125 * contract(query, k_4, 1, 1), -1e30)
+            first, second = softmax_of(first, second)
+            dfirst = either(contract(grad, v_p, 1, 1), contract(grad[:cont], v_f, 1, 1))
+            dsecond = contract(grad, v_4, 1, 1)
+            mean = jnp.sum(first * dfirst, -1, keepdims=True) + jnp.sum(
+                second * dsecond, -1, keepdims=True
+            )
+            ds1 = first * (dfirst - mean)
+            ds2 = (second * (dsecond - mean)).astype(BF)[:cont, :cont]
+            ds_near = (ds1 * near).astype(BF)
+            ds_far = (ds1 * (1.0 - near)).astype(BF)[:cont]
+            p_near = (first * near).astype(BF)
+            p_own = second.astype(BF)[:cont, :cont]
+            dq_p.append(jnp.dot(ds, k_p, preferred_element_type=F32))
+            dq_c.append(
+                jnp.dot(ds_near[:cont], k_p, preferred_element_type=F32)
+                + jnp.dot(ds_far, k_f, preferred_element_type=F32)
+                + jnp.dot(ds2, k_c, preferred_element_type=F32)
+            )
+            dk_p.append(contract(jnp.concatenate([ds, ds_near], 0), q_all, 0, 0))
+            dv_p.append(contract(jnp.concatenate([prob.astype(BF), p_near], 0), do_all, 0, 0))
+            dk_c.append(contract(ds2, q_c, 0, 0))
+            dv_c.append(contract(p_own, do_c, 0, 0))
+        for out, prompt_part, cont_part in (
+            (dq_sc, dq_p, dq_c),
+            (dk_sc, dk_p, dk_c),
+            (dv_sc, dv_p, dv_c),
+        ):
+            out[:PROMPT, cols] = pick_lanes(*prompt_part)
+            out[own_c, cols] = pick_lanes(*cont_part)
+        return carry
+
+    lax.fori_loop(0, HEADS // 2, heads, 0)
+    dh1 = None
+    for i, source in enumerate((dq_sc, dk_sc, dv_sc)):
+        for slab in range(6):
+            cols = slice(slab * 128, (slab + 1) * 128)
+            value = source[:, cols]
+            if i < 2:
+                value = turned(0.125 * value, cos_ref[...], -sin_ref[...])
+            low_sc[:, cols] = value.astype(BF)
+        grads = low_sc[...]
+        product = contract(h1_ref[...], grads, 0, 0).astype(BF)
+        out_ref, at = ((gqk_ref, 0), (gqk_ref, D), (gvo_ref, 0))[i]
+        for z in range(4):
+            out_ref[z, : D // 4, at : at + D] = product[z * (D // 4) : (z + 1) * (D // 4), :]
+        for half in range(2):
+            part = contract(grads[:, 384 * half : 384 * (half + 1)], w_ref[2 * i + half], 1, 1)
+            dh1 = part if dh1 is None else dh1 + part
+    for z in range(4):
+        gvo_ref[z, : D // 4, D:] = gwo_ref[z * (D // 4) : (z + 1) * (D // 4), :]
+        gqk_ref[z, D // 4 :, :] = jnp.zeros((EXT, 2 * D), BF)
+        gvo_ref[z, D // 4 :, :] = jnp.zeros((EXT, 2 * D), BF)
+    inputs = own_ref[:TOK_DEV, :].astype(F32)
+    scale = unit_rms(inputs)
+    normed = inputs * scale
+    ggain_ref[...] = jnp.sum(dh1 * normed, 0, keepdims=True)
+    dnormed = dh1 * gain1_ref[...]
+    gtok_ref[...] = (
+        scale * (dnormed - normed * jnp.mean(dnormed * normed, -1, keepdims=True)) + dx1_ref[...]
+    )
+
+
+def attention_backward(flags, q, k, v, do, do_far, h1, w_all, own, gain1, cos, sin, dx1, gwo):
+    shape = jax.ShapeDtypeStruct
+    whole = lambda *dims: pl.BlockSpec(dims, lambda i: (0,) * len(dims))
+    rows = whole(TOK_DEV, D)
+    both = whole(2 * TOK_DEV, D)
+    packed = (4, D // 4 + EXT, 2 * D)
+    return pl.pallas_call(
+        attention_back_kernel,
+        grid=(1,),
+        out_shape=(
+            shape((TOK_DEV, D), F32),
+            shape(packed, BF),
+            shape(packed, BF),
+            shape((1, D), F32),
+        ),
+        in_specs=[
+            pl.BlockSpec(memory_space=pltpu.SMEM),
+            both,
+            both,
+            both,
+            rows,
+            whole(TOK_DEV - PROMPT, D),
+            rows,
+            whole(6, D, 384),
+            whole(ROWS, D),
+            whole(1, D),
+            whole(TOK_DEV, 128),
+            whole(TOK_DEV, 128),
+            rows,
+            whole(D, D),
+        ],
+        out_specs=(rows, whole(*packed), whole(*packed), whole(1, D)),
+        scratch_shapes=[
+            pltpu.VMEM((TOK_DEV, D), F32),
+            pltpu.VMEM((TOK_DEV, D), F32),
+            pltpu.VMEM((TOK_DEV, D), F32),
+            pltpu.VMEM((TOK_DEV, D), BF),
+        ],
+        compiler_params=pltpu.CompilerParams(vmem_limit_bytes=VMEM_LIMIT),
+        cost_estimate=pl.CostEstimate(
+            flops=2 * 8 * TOK_DEV * D * D, bytes_accessed=40 * TOK_DEV * D, transcendentals=0
+        ),
+        name="attention_backward",
+    )(flags, q, k, v, do, do_far, h1, w_all, own, gain1, cos, sin, dx1, gwo)
+
+
+def after(value, *earlier):
+    return lax.optimization_barrier((value, earlier))[0]
+
+
+def spread(column):
+    first = over_a(column)
+    second = over_b(column)
+    third = over_b(first)
+    return [column, first, second, third]
+
+
+def with_core(parts):
+    return parts + [over_core(part) for part in parts]
+
+
 def reduce_dense(first, second, z, y, x, core):
-    first, second = first.astype(BF), second.astype(BF)
     kept = jnp.where(core == 0, first, second)
     sent = jnp.where(core == 0, second, first)
     total = pair_sum(kept, over_core(sent))
@@ -919,10 +1381,9 @@
     total = pair_sum(kept, over_a(sent))
     kept, sent = halves(total, bit_b)
     total = pair_sum(kept, over_b(sent))
-    slabs = total.reshape(4, D // 4, -1)
-    result = lax.dynamic_index_in_dim(slabs, z, 0, keepdims=False).astype(F32)
+    result = lax.dynamic_index_in_dim(total, z, 0, keepdims=False).astype(F32)
     for step in (1, 2, 3):
-        out = lax.dynamic_index_in_dim(slabs, lax.rem(z + step, 4), 0, keepdims=False)
+        out = lax.dynamic_index_in_dim(total, lax.rem(z + step, 4), 0, keepdims=False)
         result = result + over_z(out, step).astype(F32)
     result = result.astype(BF)
     result = rejoin(result, over_b(result), bit_b)
@@ -952,7 +1413,22 @@
 ):
     z, y, j = lax.axis_index("dp"), lax.axis_index("context"), lax.axis_index("experts")
     x, core = j // 2, j % 2
-    contexts = 2
+    plane = y * 4 + j
+    shard = D // 4
+
+    dense = jnp.concatenate([query_weight, key_weight, value_weight, output_weight], 1)
+    dense = lax.dynamic_slice_in_dim(dense, plane * 384, 384, 1)
+    gains = jnp.concatenate(
+        [attn_gain[None], ffn_gain[None], jnp.zeros((EXT - 2, shard), BF)], 0
+    )
+    dense = jnp.concatenate([dense, jnp.concatenate([router_weight.T, gains], 1)], 0)
+    dense = jnp.stack([dense] + [over_z(dense, step) for step in (1, 2, 3)])
+    dense_parts = with_core(spread(dense))
+
+    ids = jnp.broadcast_to(prompt_ids.astype(BF)[:, None], (CONT, D))
+    own = jnp.concatenate([tokens, ids, jnp.zeros((EXT - CONT, D), BF)], 0)
+    far = moved(own, lambda z, y, x, c: (z, 1 - y, x, c))
+    far_ids = far[TOK_DEV : TOK_DEV + CONT, 0].astype(jnp.int32)
 
     expert_ids = jnp.arange(EXPERTS, dtype=jnp.int32)[:, None]
     route_t = routes.T
@@ -961,197 +1437,98 @@
     ranks = jnp.dot(member.astype(BF), before, preferred_element_type=F32)
     ranks = jnp.where(member, ranks, -1.0).astype(BF)
     g_block = jnp.concatenate([cotangent, jnp.pad(ranks, ((0, 0), (0, D - TOK_DEV)))], 0)
-
-    small = jnp.concatenate(
-        [router_weight, attn_gain[:, None], ffn_gain[:, None], jnp.zeros((D // 4, 110), BF)], 1
-    )
-    w_in = gather_rows(
-        jnp.concatenate([query_weight, key_weight, value_weight, small], 1), core
-    )
-    g_pair = jnp.stack([g_block, over_x(g_block)])
-    g_group = jnp.concatenate([g_pair, over_core(g_pair)])
-    w_out = gather_rows(output_weight, core)
-    w_gateup = gather_rows(jnp.concatenate([shared_gate, shared_up], 1), core)
-    w_sgate, w_sup = w_gateup[:, :2048], w_gateup[:, 2048:]
-    w_sdown = gather_rows(shared_down, core)
-    g_parts = gather_blocks(g_block)
-
-    w_query, w_key, w_value = w_in[:, :D], w_in[:, D : 2 * D], w_in[:, 2 * D : 3 * D]
-    w_router = w_in[:, 3 * D : 3 * D + EXPERTS]
-    gain1_f = w_in[:, 3 * D + 16].astype(F32)
-    gain2_f = w_in[:, 3 * D + 17].astype(F32)
+    g_near = [g_block, over_x(g_block)]
+    g_group = with_core(g_near)
+
+    units = lambda w: lax.dynamic_index_in_dim(
+        w.reshape(shard, 4, 8, 64), plane, 2, keepdims=False
+    ).reshape(shard, 256)
+    down = lax.dynamic_slice_in_dim(shared_down, plane * 64, 64, 0)
+    down = jnp.concatenate([down[:, 256 * i : 256 * (i + 1)] for i in range(3)], 0)
+    shared = jnp.concatenate([units(shared_gate), units(shared_up), down], 1)
+    shared = lax.all_gather(shared, "dp", axis=0, tiled=False)
+    shared_parts = with_core(spread(shared))
+
+    g_column = lax.all_gather(g_block, "dp", axis=0, tiled=False)
+    g_parts = with_core(spread(g_column))
+
+    slots = dense[:, shard:, :]
+    slots = jnp.stack([slots[0], slots[3], slots[2], slots[1]])
+    small = lax.dynamic_slice_in_dim(
+        jnp.concatenate([slots, slots], 0), lax.rem(4 - z, 4), 4, 0
+    )
+    router_t = small[:, :, :shard].transpose(1, 0, 2).reshape(EXPERTS, D)
+    gain1 = small[:, 0, shard:].reshape(1, D).astype(F32)
+    gain2 = small[:, 1, shard:].reshape(1, D).astype(F32)
 
     cos_table, sin_table = rotary_tables(TOK_DEV)
-    inputs = tokens.astype(F32)
-    inv_rms1 = lax.rsqrt(jnp.mean(inputs * inputs, -1, keepdims=True) + EPS)
-    normed1 = inputs * inv_rms1
-    hidden1 = (normed1 * gain1_f).astype(BF)
-    query_f = jnp.dot(hidden1, w_query, preferred_element_type=F32)
-    key_f = jnp.dot(hidden1, w_key, preferred_element_type=F32)
-    value_f = jnp.dot(hidden1, w_value, preferred_element_type=F32)
-    query_b = rotate(query_f, cos_table, sin_table).astype(BF)
-    key_b = rotate(key_f, cos_table, sin_table).astype(BF)
-    value_b = value_f.astype(BF)
-    prompt_keys, prompt_values = (
-        lax.all_gather(key_b[:PROMPT], "context", axis=0, tiled=True),
-        lax.all_gather(value_b[:PROMPT], "context", axis=0, tiled=True),
-    )
-    keys_h = jnp.concatenate([prompt_keys, key_b[PROMPT:]], 0).reshape(-1, HEADS, HD)
-    values_h = jnp.concatenate([prompt_values, value_b[PROMPT:]], 0).reshape(-1, HEADS, HD)
-    query_h = query_b.reshape(TOK_DEV, HEADS, HD)
-    allowed = key_mask(y, prompt_ids, contexts)
-    scores = jnp.where(
-        allowed[None],
-        0.125 * jnp.einsum("qhd,khd->hqk", query_h, keys_h, preferred_element_type=F32),
-        -1e30,
-    )
-    row_max = jnp.max(scores, -1, keepdims=True)
-    exp_scores = jnp.exp(scores - row_max)
-    row_total = jnp.sum(exp_scores, -1, keepdims=True)
-    log_total = row_max + jnp.log(row_total)
-    attn_probs = (exp_scores / row_total).astype(BF)
-    attended = (
-        jnp.einsum("hqk,khd->qhd", attn_probs, values_h, preferred_element_type=F32)
-        .reshape(TOK_DEV, D)
-        .astype(BF)
-    )
-    resid = inputs + jnp.dot(attended, w_out, preferred_element_type=F32)
-    inv_rms2 = lax.rsqrt(jnp.mean(resid * resid, -1, keepdims=True) + EPS)
-    normed2 = resid * inv_rms2
-    hidden2 = (normed2 * gain2_f).astype(BF)
-    logits_t = contract(w_router, hidden2, 0, 1)
-    probs_t = jax.nn.softmax(logits_t, 0)
-    probs_high = probs_t.astype(BF)
-    probs_low = (probs_t - probs_high.astype(F32)).astype(BF)
-    h_block = jnp.concatenate([hidden2, jnp.concatenate([probs_high, probs_low], 1)], 0)
-
-    h_pair = jnp.stack([h_block, over_x(h_block)])
-    h_group = jnp.concatenate([h_pair, over_core(h_pair)])
-    shared_res, grad_shared_in = shared_rows(hidden2, cotangent, w_sgate, w_sup, w_sdown)
+    cos = jnp.tile(cos_table, (1, 4))
+    sin = jnp.tile(jnp.concatenate([-sin_table, sin_table], 1), (1, 2))
+    flip_a, flip_b = jnp.where(core == 0, 2, 4), jnp.where(core == 0, 4, 2)
+    flips = [0 * core, flip_a, flip_b, 0 * core + 6]
+    flips = flips + [1 + flips[0], 1 + flip_b, 1 + flip_a, 1 + flips[3]]
+    place = [jnp.bitwise_xor(plane, flip) for flip in flips]
+    place += [lax.rem(z + 4 - slot, 4) for slot in range(4)]
+    place += [(prompt_ids[m] != y) for m in range(CONT)]
+    place = jnp.stack([v.astype(jnp.int32) for v in place])
+    w_all, q, k, v, h1, o, x1, h_block = attention_forward(
+        place, dense_parts, own, far, gain1, gain2, router_t, cos, sin
+    )
+
+    h_near = [h_block, over_x(h_block)]
+    h_group = with_core(h_near)
+    h_column = lax.all_gather(h_block, "dp", axis=0, tiled=False)
     base = (j * 4).astype(jnp.int32)
-    moe_part, dx_part = group_experts(
+    moe_near, moe_far, dx_near, dx_far = group_experts(
         base[None], h_group, g_group, expert_gate, expert_up_weight, expert_down
     )
-    h_parts = gather_blocks(h_block)
-
-    def home(part):
-        pair = pair_sum(part[:2], over_core(part[2:]))
-        return pair[0].astype(F32) + over_x(pair[1]).astype(F32)
-
-    dx_home = home(dx_part)
-    moe_out = home(moe_part)
-    layer_out = (resid + shared_res + moe_out).astype(BF)
-
-    grad_total = cotangent.astype(F32)
-    grad_rprobs = dx_home[TOK_DEV:, :TOK_DEV] + dx_home[TOK_DEV:, TOK_DEV:]
-    grad_logits_t = (
-        probs_t * (grad_rprobs - jnp.sum(probs_t * grad_rprobs, 0, keepdims=True))
-    ).astype(BF)
-    grad_router_local = contract(hidden2, grad_logits_t, 0, 1)
-    grad_hidden2 = (
-        dx_home[:TOK_DEV] + grad_shared_in + contract(grad_logits_t, w_router, 0, 1)
-    )
-    grad_gain2 = jnp.sum(grad_hidden2 * normed2, 0)
-    grad_normed2 = grad_hidden2 * gain2_f
-    grad_resid = (
-        inv_rms2 * (grad_normed2 - normed2 * jnp.mean(grad_normed2 * normed2, -1, keepdims=True))
-        + grad_total
-    )
-    grad_branch = grad_resid.astype(BF)
-    grad_wout = inner_rows(attended, grad_branch)
-    grad_attended = times_transposed(grad_branch, w_out).astype(BF).reshape(TOK_DEV, HEADS, HD)
-    scores_again = jnp.where(
-        allowed[None],
-        0.125 * jnp.einsum("qhd,khd->hqk", query_h, keys_h, preferred_element_type=F32),
-        -1e30,
-    )
-    probs_f = jnp.exp(scores_again - log_total)
-    probs_b = probs_f.astype(BF)
-    grad_pattn = jnp.einsum("qhd,khd->hqk", grad_attended, values_h, preferred_element_type=F32)
-    grad_scores = (
-        probs_f * (grad_pattn - jnp.sum(probs_f * grad_pattn, -1, keepdims=True))
-    ).astype(BF)
-    grad_query = 0.125 * jnp.einsum(
-        "hqk,khd->qhd", grad_scores, keys_h, preferred_element_type=F32
-    ).reshape(TOK_DEV, D)
-    grad_keys = 0.125 * jnp.einsum(
-        "hqk,qhd->khd", grad_scores, query_h, preferred_element_type=F32
-    ).reshape(-1, D)
-    grad_values = jnp.einsum(
-        "hqk,qhd->khd", probs_b, grad_attended, preferred_element_type=F32
-    ).reshape(-1, D)
-    span = contexts * PROMPT
-    grad_pkeys, grad_pvalues = (
-        lax.psum_scatter(grad_keys[:span].astype(BF), "context", scatter_dimension=0, tiled=True),
-        lax.psum_scatter(
-            grad_values[:span].astype(BF), "context", scatter_dimension=0, tiled=True
-        ),
-    )
-    grad_key_all = jnp.concatenate([grad_pkeys.astype(F32), grad_keys[span:]], 0)
-    grad_value_all = jnp.concatenate([grad_pvalues.astype(F32), grad_values[span:]], 0)
-    grad_qpre = rotate(grad_query, cos_table, -sin_table).astype(BF)
-    grad_kpre = rotate(grad_key_all, cos_table, -sin_table).astype(BF)
-    grad_vpre = grad_value_all.astype(BF)
-    grad_wquery = inner_rows(hidden1, grad_qpre)
-    grad_wkey = inner_rows(hidden1, grad_kpre)
-    grad_wvalue = inner_rows(hidden1, grad_vpre)
-    grad_hidden1 = (
-        times_transposed(grad_qpre, w_query)
-        + times_transposed(grad_kpre, w_key)
-        + times_transposed(grad_vpre, w_value)
-    )
-    grad_gain1 = jnp.sum(grad_hidden1 * normed1, 0)
-    grad_normed1 = grad_hidden1 * gain1_f
-    grad_inputs = (
-        inv_rms1 * (grad_normed1 - normed1 * jnp.mean(grad_normed1 * normed1, -1, keepdims=True))
-        + grad_resid
-    )
-
-    sum_qk, sum_vo = reduce_dense(
-        jnp.concatenate([grad_wquery, grad_wkey], 1),
-        jnp.concatenate([grad_wvalue, grad_wout], 1),
-        z,
-        y,
-        x,
-        core,
-    )
-    sum_qk, sum_vo = sum_qk.astype(F32), sum_vo.astype(F32)
-    extras = jnp.concatenate(
-        [grad_router_local, grad_gain1[:, None], grad_gain2[:, None], jnp.zeros((D, 110), F32)], 1
-    ).astype(BF)
-    extras = lax.psum_scatter(extras, "dp", scatter_dimension=0, tiled=True)
-    extras = lax.psum(extras, ("context", "experts")).astype(F32)
-
-    plane = y * 4 + j
-    columns = lambda w: lax.dynamic_index_in_dim(
-        w.reshape(D, 4, 8, 64), plane, 2, keepdims=False
-    ).reshape(D, 256)
-    down_rows = lax.dynamic_index_in_dim(
-        w_sdown.reshape(4, 8, 64, D), plane, 1, keepdims=False
-    ).reshape(256, D)
+    shared_out, shared_dh = shared_rows(h_block, cotangent, shared_parts)
+    h_parts = with_core(spread(h_column))
+
+    dx_pair = pair_sum(dx_near, over_core(dx_far))
+    dx_there = over_x(dx_pair[1])
+    dx1, do, do_c, gwo, grad_router_t, grad_gain2 = branch_backward(
+        dx_pair[0], dx_there, shared_dh, h_block, x1, cotangent, gain2, router_t, o, w_all
+    )
+    do_far = moved(do_c, lambda z, y, x, c: (z, 1 - y, x, c))
+    flags = jnp.concatenate([prompt_ids == y, far_ids == y]).astype(jnp.int32)
+    grad_inputs, gqk, gvo, grad_gain1 = attention_backward(
+        flags, q, k, v, do, do_far, h1, w_all, own, gain1, cos, sin, dx1, gwo
+    )
+    moe_pair = pair_sum(moe_near, over_core(moe_far))
+    moe_out = moe_pair[0].astype(F32) + over_x(moe_pair[1]).astype(F32)
+    layer_out = (x1 + shared_out + moe_out).astype(BF)
+
+    extras = jnp.concatenate([grad_gain1, grad_gain2, jnp.zeros((EXT - 2, D), F32)], 0)
+    extras = jnp.stack([grad_router_t, extras]).astype(BF).reshape(2, EXT, 4, shard)
+    extras = extras.transpose(2, 1, 0, 3).reshape(4, EXT, 2 * shard)
+    gqk = lax.dynamic_update_slice(gqk, extras, (0, shard, 0))
+    sum_qk, sum_vo = reduce_dense(gqk, gvo, z, y, x, core)
+    extras = sum_qk[shard:, : 2 * shard].astype(F32)
+    sum_qk, sum_vo = sum_qk[:shard].astype(F32), sum_vo[:shard].astype(F32)
 
     window = jnp.array([0, 1, 3, 4], jnp.int32)[z]
     s_gate, s_up, s_down = shared_slice_grads(
-        jnp.stack([window, (z // 2).astype(jnp.int32)]),
-        h_parts,
-        g_parts,
-        columns(w_sgate),
-        columns(w_sup),
-        down_rows,
+        jnp.stack([window, (z // 2).astype(jnp.int32)]), h_parts, g_parts, shared
     )
     lead = z * 192 - window * 128
-    s_gateup = jnp.concatenate(
+    s_down = lax.dynamic_slice_in_dim(s_down, (z % 2) * 64, 64, 0)
+    mine = jnp.concatenate(
         [
             lax.dynamic_slice_in_dim(s_gate, lead, 192, 0),
             lax.dynamic_slice_in_dim(s_up, lead, 192, 0),
+            jnp.concatenate([s_down[:, 256 * i : 256 * (i + 1)] for i in range(3)], 0),
         ],
         1,
     ).astype(BF)
-    s_down = lax.dynamic_slice_in_dim(s_down, (z % 2) * 64, 64, 0).astype(BF)
-    s_gateup = lax.all_gather(s_gateup, ("context", "experts"), axis=0, tiled=False)
-    s_down = lax.all_gather(s_down, ("context", "experts"), axis=0, tiled=True).astype(F32)
-    s_gateup = s_gateup.reshape(8, 192, 2, 4, 64).transpose(2, 1, 3, 0, 4).reshape(2, 192, 2048)
+    every = lax.all_gather(mine, ("context", "experts"), axis=0, tiled=False)
+    s_gateup = (
+        every[:, :, :512].reshape(8, shard, 2, 4, 64).transpose(2, 1, 3, 0, 4)
+    ).reshape(2, shard, 2048)
     s_gateup = s_gateup.astype(F32)
+    s_down = jnp.concatenate(
+        [every[:, 64 * i : 64 * (i + 1), 512:].reshape(512, 256) for i in range(3)], 1
+    ).astype(F32)
 
     slice_index = (z * 2 + y).astype(jnp.int32)
     e_gate, e_up, e_down = expert_slice_grads(
@@ -1166,13 +1543,13 @@
     return (
         layer_out,
         grad_inputs,
-        extras[:, 16],
+        extras[0, shard:],
         sum_qk[:, :D],
         sum_qk[:, D:],
         sum_vo[:, :D],
         sum_vo[:, D:],
-        extras[:, 17],
-        extras[:, :16],
+        extras[1, shard:],
+        extras[:, :shard].T,
         s_gateup[0],
         s_gateup[1],
         s_down,
@@ -1183,8 +1560,7 @@
 
 
 def solution(mesh):
-    shape = dict(mesh.shape)
-    tuned = shape == TUNED_MESH
+    tuned = dict(mesh.shape) == TUNED_MESH
 
     return jax.shard_map(
         tuned_body if tuned else plain_body,

time: 807 us -> 596 us (0.74)
  blocking collectives: 79.8 us -> 0 us
  waiting for transfers between devices: 324 us -> 257 us
  matrix products: 54.3 us -> 0.14 us
  Pallas kernels: 150 us -> 203 us
  other arithmetic: 65.1 us -> 30.2 us
  local copies, waits for them, and re-layouts: 60.4 us -> 42.9 us
  starting transfers between devices: 51 us -> 38.8 us
    all_gather x4 -> x0, blocking collectives: 56.9 us -> none  [the longest x1 23.6 us: gather_rows(): part = lax.all_gather(part, 'dp', axis=0, tiled=False)]
    dot_general x21 -> x0, matrix products: 54.1 us -> none  [the longest x1 11.2 us: tuned_body(): jnp.einsum('qhd,khd->hqk', grad_attended, values_h, preferred_element_typ...]
    pallas_call x2 -> x5, Pallas kernels: 52.5 us -> 105 us  [the longest x1 41.2 us: group_experts(): pl.pallas_call(functools.partial(group_kernel, blocks), out_shape=tuple((...]
    ppermute x41 -> x52, waiting for transfers between devices: 275 us -> 239 us  [moved(): return lax.ppermute(value, AXES, pairs)]
    psum x1 -> x0, blocking collectives: 23 us -> none  [tuned_body(): extras = lax.psum(extras, ('context', 'experts')).astype(F32)]
    unnamed x8 -> x4, waiting for transfers between devices: 17.3 us -> 0.07 us
    slice x16 -> x6, local copies, waits for them, and re-layouts: 19.5 us -> 5.86 us  [the longest x1 2.65 us: tuned_body(): every[:, :, :512].reshape(8, shard, 2, 4, 64).transpose(2, 1, 3, 0, 4)]
    select_n x8 -> x1, other arithmetic: 12.8 us -> 0.07 us  [reduce_dense(): jnp.where(core == 0, result, other)]
  transfers between devices with their start and end apart: 48 -> 56, of which waited for: 16 -> 21; matrix products, arithmetic and copies ran while one was open for 16% -> 8% of each run, Pallas kernels for 19% -> 28%
where the time goes in v2:
time: 596 us; the launch traced here: 589 us
  waiting for transfers between devices  257 us (43%)
  Pallas kernels  203 us (34%)
  local copies, waits for them, and re-layouts  42.9 us (7%)
  starting transfers between devices  38.8 us (7%)
  other arithmetic  30.2 us (5%)
  between operations  16.8 us (3%)
    ppermute x52, waiting for transfers between devices, moved(): return lax.ppermute(value, AXES, pairs)  239 us
    pallas_call x1, Pallas kernels, expert_slice_grads(): pl.pallas_call(functools.partial(expert_slice_kernel, parts), out_shape=(...  58.9 us
    pallas_call x1, Pallas kernels, group_experts(): pl.pallas_call(functools.partial(group_kernel, blocks), out_shape=tuple((...  41.2 us
    pallas_call x1, Pallas kernels, shared_slice_grads(): pl.pallas_call(functools.partial(shared_slice_kernel, parts), out_shape=(...  38.8 us
    ppermute x52, starting transfers between devices, moved(): return lax.ppermute(value, AXES, pairs)  38.1 us
    pallas_call x1, Pallas kernels, attention_backward(): pl.pallas_call(attention_back_kernel, grid=(1,), out_shape=(shape((TOK_DE...  22.7 us
    pallas_call x1, Pallas kernels, attention_forward(): pl.pallas_call(attention_kernel, out_shape=(shape((8, D, 384), BF), shape...  20.8 us
    all_gather x1, waiting for transfers between devices, tuned_body(): h_column = lax.all_gather(h_block, 'dp', axis=0, tiled=False)  18.6 us
  transfers between devices with their start and end apart: 56, of which 21 were waited for; matrix products, arithmetic and copies ran while one was open for 8% of the time, Pallas kernels for 28%

profile of v2, /device:TPU:0, one launch (start us, length us, event | category | flops | bytes accessed | tf_op | source)
XLA Modules:
  0.0 588.8 jit_solution(9244094912774785472)
XLA Ops:
  8.6 1.0 fusion.11
  10.5 4.0 collective-permute-start.1
  14.5 1.6 collective-permute-start
  16.1 2.2 collective-permute-start.2
  18.4 1.0 pad_maximum_fusion.1.refs_8_.own_ref
  19.4 1.5 collective-permute-start.10
  28.3 1.2 pad_maximum_fusion.refs_0_
  29.6 1.5 collective-permute-start.3
  35.0 8.4 %collective-permute-done.3.refs_1_ = bf16[4,208,384]{2,1,0:T(8,128)(2,1)S(1)} collective-permute-done((bf16[4,208,384]{2,1,0:T(8,128)(2,1)S(1)}, bf16[4,208,384]{2,1,0:T(8,128)(2,1)S(1)}, u32[]{:S(2)}, u32[]{:S(2)}) %collective-permute-start.3) | collective-permute-done | bytes 639008 | tf_op jit(solution)/shard_map/ppermute | solution.py:449
  45.4 3.4 collective-permute-start.7
  49.0 6.1 %collective-permute-done.5.refs_3_ = bf16[4,208,384]{2,1,0:T(8,128)(2,1)} collective-permute-done((bf16[4,208,384]{2,1,0:T(8,128)(2,1)S(1)}, bf16[4,208,384]{2,1,0:T(8,128)(2,1)}, u32[]{:S(2)}, u32[]{:S(2)}) %collective-permute-start.5) | collective-permute-done | bytes 639008 | tf_op jit(solution)/shard_map/ppermute | solution.py:449
  59.7 1.7 collective-permute-start.21
  62.3 20.8 %attention_forward.1 = (bf16[8,768,384]{2,1,0:T(8,128)(2,1)}, bf16[768,768]{1,0:T(8,128)(2,1)}, bf16[768,768]{1,0:T(8,128)(2,1)}, bf16[768,768]{1,0:T(8,128)(2,1...) custom-call(s32[14]{0:T(128)} %stack.105.place_ref, ...), custom_call_target="tpu_custom_call" | custom-call | flops 3623878656 | bytes 9437184 | tf_op jit(solution)/shard_map/attention_forward/pallas_call | solution.py:1067
  83.4 1.7 collective-permute-start.11
  85.8 13.1 %collective-permute-done.18.refs_1_ = bf16[400,768]{1,0:T(8,128)(2,1)S(1)} collective-permute-done((bf16[400,768]{1,0:T(8,128)(2,1)}, bf16[400,768]{1,0:T(8,128)(2,1)S(1)}, u32[]{:S(2)}, u32[]{:S(2)}) %collective-permute-start.18) | collective-permute-done | bytes 614432 | tf_op jit(solution)/shard_map/ppermute | solution.py:449
  98.9 1.6 collective-permute-start.12
  100.5 20.4 %collective-permute-done.11.refs_1_ = bf16[4,192,768]{2,1,0:T(8,128)(2,1)} collective-permute-done((bf16[4,192,768]{2,1,0:T(8,128)(2,1)}, bf16[4,192,768]{2,1,0:T(8,128)(2,1)}, u32[]{:S(2)}, u32[]{:S(2)}) %collective-permute-start.11) | collective-permute-done | bytes 1179680 | tf_op jit(solution)/shard_map/ppermute | solution.py:449
  120.8 1.5 collective-permute-start.13
  123.4 41.2 %group_experts.1 = (bf16[2,384,768]{2,1,0:T(8,128)(2,1)}, bf16[2,384,768]{2,1,0:T(8,128)(2,1)}, bf16[2,400,768]{2,1,0:T(8,128)(2,1)}, bf16[2,400,768]{2,1,0:T(8,128)(2,1)}) custom-call(s32[1]{0:T(128)} %bitcast.29.base_ref, bf16[400,768]{1,0:T(8,128)(2,1)} %get-tuple-element.46.h_ref.refs_0_.h2_ref, bf16[400,768]{1,0:T(8,128)(2,1)} %copy-done.30, ...), custom_call_target="tpu_custom_call" | custom-call | flops 21743271936 | bytes 37748736 | tf_op jit(solution)/shard_map/group_experts/pallas_call | solution.py:590
  166.3 2.4 collective-permute-done.26
  168.7 1.6 add_convert_fusion.2
  171.7 1.2 collective-permute-done.16.refs_6_
  172.9 1.7 collective-permute-done.17.refs_7_
  174.6 14.1 %shared_rows.1 = (f32[384,768]{1,0:T(8,128)}, f32[384,768]{1,0:T(8,128)}) custom-call(bf16[400,768]{1,0:T(8,128)(2,1)} %get-tuple-element.46.h_ref.refs_0_.h2_ref, bf16[384,768]{1,0:T(8,128)(2,1)} %g_ref.3, bf16[4,192,768]{2,1,0:T(8,128)(2,1)} %bitcast.108, bf16[4,192,768]{2,1,0:T(8,128)(2,1)} %collective-permute-done.11.refs_1_, ...), custom_call_target="tpu_custom_call" | custom-call | flops 7247757312 | bytes 9437184 | tf_op jit(solution)/shard_map/shared_rows/pallas_call | solution.py:672
  189.5 6.1 %branch_backward.1 = (f32[384,768]{1,0:T(8,128)}, bf16[384,768]{1,0:T(8,128)(2,1)}, bf16[128,768]{1,0:T(8,128)(2,1)}, bf16[768,768]{1,0:T(8,128)(2,1)}, f32[16,768]{1,0:T(8,128)}, /*index=5*/f32[1,768]{1,0:T(1,128)}) custom-call(bf16[400,768]{1,0:T(8,128)(2,1)} %get-tuple-element.115.dx_a_ref, bf16[400,768]{1,0:T(8,128)(2,1)} %copy-done.10, ...), custom_call_target="tpu_custom_call" | custom-call | flops 905969664 | bytes 3538944 | tf_op jit(solution)/shard_map/branch_backward/pallas_call | solution.py:1146
  199.2 3.6 collective-permute-done.28.do_far_ref
  203.5 22.7 %attention_backward.1 = (f32[384,768]{1,0:T(8,128)}, bf16[4,208,1536]{2,1,0:T(8,128)(2,1)}, bf16[4,208,1536]{2,1,0:T(8,128)(2,1)}, f32[1,768]{1,0:T(1,128)}) custom-call(s32[4]{0:T(128)} %add_convert_fusion.5.flags_ref, bf16[768,768]{1,0:T(8,128)(2,1)} %get-tuple-element.50.q_ref, bf16[768,768]{1,0:T(8,128)(2,1)} %get-tuple-element.51.k_ref, ...), custom_call_target="tpu_custom_call" | custom-call | flops 3623878656 | bytes 11796480 | tf_op jit(solution)/shard_map/attention_backward/pallas_call | solution.py:1320
  227.9 2.0 broadcast_select_fusion
  230.1 4.8 collective-permute-done.29
  234.9 3.8 add_convert_fusion
  238.7 1.2 broadcast_select_fusion.1
  240.3 17.2 %collective-permute-done.30 = bf16[4,208,768]{2,1,0:T(8,128)(2,1)} collective-permute-done((bf16[4,208,768]{2,1,0:T(8,128)(2,1)}, bf16[4,208,768]{2,1,0:T(8,128)(2,1)}, u32[]{:S(2)}, u32[]{:S(2)}) %collective-permute-start.30) | collective-permute-done | bytes 1277984 | tf_op jit(solution)/shard_map/ppermute | solution.py:449
  257.5 1.8 add_convert_fusion.1
  259.3 1.0 copy-done
  260.8 1.7 collective-permute-start.46
  262.8 18.6 %all-gather.12.cloned.1.call-done = bf16[1600,768]{1,0:T(8,128)(2,1)} async-done(((bf16[400,768]{1,0:T(8,128)(2,1)}), bf16[1600,768]{1,0:T(8,128)(2,1)}) %all-gather.12.cloned.1.call-update) | async-done | bytes 2457616 | tf_op jit(solution)/shard_map/all_gather | solution.py:1480
  281.4 1.5 collective-permute-start.38
  282.9 1.5 add_convert_fusion.4
  284.5 7.4 %collective-permute-done.32 = bf16[208,384]{1,0:T(8,128)(2,1)S(1)} collective-permute-done((bf16[208,384]{1,0:T(8,128)(2,1)S(1)}, bf16[208,384]{1,0:T(8,128)(2,1)S(1)}, u32[]{:S(2)}, u32[]{:S(2)}) %collective-permute-start.32) | collective-permute-done | bytes 159776 | tf_op jit(solution)/shard_map/ppermute | solution.py:449
  291.9 1.5 add_convert_fusion.3
  293.5 3.7 collective-permute-done.34
  298.1 6.3 %collective-permute-done.33 = bf16[208,384]{1,0:T(8,128)(2,1)S(1)} collective-permute-done((bf16[208,384]{1,0:T(8,128)(2,1)S(1)}, bf16[208,384]{1,0:T(8,128)(2,1)S(1)}, u32[]{:S(2)}, u32[]{:S(2)}) %collective-permute-start.33) | collective-permute-done | bytes 159776 | tf_op jit(solution)/shard_map/ppermute | solution.py:449
  304.4 3.5 collective-permute-start.25
  308.0 54.6 %collective-permute-done.25 = bf16[384,768]{1,0:T(8,128)(2,1)} collective-permute-done((bf16[384,768]{1,0:T(8,128)(2,1)}, bf16[384,768]{1,0:T(8,128)(2,1)}, u32[]{:S(2)}, u32[]{:S(2)}) %collective-permute-start.25) | collective-permute-done | bytes 589856 | tf_op jit(solution)/shard_map/ppermute | solution.py:449
  362.9 5.0 collective-permute-done.35
  368.8 1.7 collective-permute-start.47
  370.5 8.0 %collective-permute-done.36 = bf16[208,768]{1,0:T(8,128)(2,1)S(1)} collective-permute-done((bf16[208,768]{1,0:T(8,128)(2,1)S(1)}, bf16[208,768]{1,0:T(8,128)(2,1)S(1)}, u32[]{:S(2)}, u32[]{:S(2)}) %collective-permute-start.36) | collective-permute-done | bytes 319520 | tf_op jit(solution)/shard_map/ppermute | solution.py:449
  378.8 22.3 %collective-permute-done.39.refs_2_ = bf16[4,400,768]{2,1,0:T(8,128)(2,1)} collective-permute-done((bf16[4,400,768]{2,1,0:T(8,128)(2,1)}, bf16[4,400,768]{2,1,0:T(8,128)(2,1)}, u32[]{:S(2)}, u32[]{:S(2)}) %collective-permute-start.39) | collective-permute-done | bytes 2457632 | tf_op jit(solution)/shard_map/ppermute | solution.py:449
  401.6 25.8 %collective-permute-done.47.refs_11_ = bf16[4,400,768]{2,1,0:T(8,128)(2,1)} collective-permute-done((bf16[4,400,768]{2,1,0:T(8,128)(2,1)}, bf16[4,400,768]{2,1,0:T(8,128)(2,1)}, u32[]{:S(2)}, u32[]{:S(2)}) %collective-permute-start.47) | collective-permute-done | bytes 2457632 | tf_op jit(solution)/shard_map/ppermute | solution.py:449
  427.8 25.9 %collective-permute-done.40.refs_3_ = bf16[4,400,768]{2,1,0:T(8,128)(2,1)} collective-permute-done((bf16[4,400,768]{2,1,0:T(8,128)(2,1)}, bf16[4,400,768]{2,1,0:T(8,128)(2,1)}, u32[]{:S(2)}, u32[]{:S(2)}) %collective-permute-start.40) | collective-permute-done | bytes 2457632 | tf_op jit(solution)/shard_map/ppermute | solution.py:449
  456.9 1.2 pad_add_fusion.pos_ref
  458.2 2.6 fusion.2
  462.3 38.8 %shared_slice_grads.1 = (f32[256,256]{1,0:T(8,128)}, f32[256,256]{1,0:T(8,128)}, f32[128,768]{1,0:T(8,128)}) custom-call(s32[2]{0:T(128)} %pad_add_fusion.pos_ref, bf16[4,400,768]{2,1,0:T(8,128)(2,1)} %bitcast.104, bf16[4,400,768]{2,1,0:T(8,128)(2,1)} %collective-permute-done.38.refs_1_, bf16[4,400,768]{2,1,0:T(8,128)(2,1)} %collective-permute-done.39.refs_2_, ...), custom_call_target="tpu_custom_call" | custom-call | flops 20132659200 | bytes 39321600 | tf_op jit(solution)/shard_map/shared_slice_grads/pallas_call | solution.py:872
  505.4 1.1 fusion.28
  506.6 1.1 fusion.29
  507.7 58.9 %expert_slice_grads.1 = (f32[4,768,256]{2,1,0:T(8,128)}, f32[4,768,256]{2,1,0:T(8,128)}, f32[4,256,768]{2,1,0:T(8,128)}) custom-call(s32[2]{0:T(128)} %pad_add_fusion.1.pos_ref, bf16[4,400,768]{2,1,0:T(8,128)(2,1)} %bitcast.105, bf16[4,400,768]{2,1,0:T(8,128)(2,1)} %collective-permute-done.38.refs_1_, bf16[4,400,768]{2,1,0:T(8,128)(2,1)} %collective-permute-done.39.refs_2_, ...), custom_call_target="tpu_custom_call" | custom-call | flops 32614907904 | bytes 53477376 | tf_op jit(solution)/shard_map/expert_slice_grads/pallas_call | solution.py:781
  566.6 2.7 slice.211
  569.3 2.7 copy.73
  572.6 1.7 fusion.26
  574.5 1.7 copy.68
  576.2 1.8 copy.65
  578.0 1.7 copy.67
  579.7 1.2 fusion.27
  580.9 1.3 maximum_convert_fusion
  (233 shorter events, 45.2 us)
Async XLA Ops:
  7.2 76.2 %all-gather.10.cloned.1.call-start = ((), (), s32[]{:S(2)}) async-start(), calls=%async_computation.1 | async-start | bytes 1474560 | tf_op jit(solution)/shard_map/all_gather | solution.py:1449
  10.5 17.8 %collective-permute-start.1 = (bf16[208,384]{1,0:T(8,128)(2,1)}, bf16[208,384]{1,0:T(8,128)(2,1)}, u32[]{:S(2)}, u32[]{:S(2)}) collective-permute-start(bf16[208,384]{1,0:T(8,128)(2,1)} %maximum_maximum_fusion.1), channel_id=1, source_target_pairs={{0,16},{1,17},{2,18},{3,19},{4,20},{5,21},{6,22},{7,23},{8,24},{9,... | collective-permute-start | bytes 479240 | tf_op jit(solution)/shard_map/ppermute | solution.py:449
  14.5 13.8 %collective-permute-start = (bf16[208,384]{1,0:T(8,128)(2,1)}, bf16[208,384]{1,0:T(8,128)(2,1)}, u32[]{:S(2)}, u32[]{:S(2)}) collective-permute-start(bf16[208,384]{1,0:T(8,128)(2,1)} %maximum_maximum_fusion.1), channel_id=1, source_target_pairs={{0,8},{1,9},{2,10},{3,11},{4,12},{5,13},{6,14},{7,15},{8,16},{9,17... | collective-permute-start | bytes 479240 | tf_op jit(solution)/shard_map/ppermute | solution.py:449
  16.1 12.2 %collective-permute-start.2 = (bf16[208,384]{1,0:T(8,128)(2,1)}, bf16[208,384]{1,0:T(8,128)(2,1)}, u32[]{:S(2)}, u32[]{:S(2)}) collective-permute-start(bf16[208,384]{1,0:T(8,128)(2,1)} %maximum_maximum_fusion.1), channel_id=1, source_target_pairs={{0,24},{1,25},{2,26},{3,27},{4,28},{5,29},{6,30},{7,31},{8,0},{9,1... | collective-permute-start | bytes 479240 | tf_op jit(solution)/shard_map/ppermute | solution.py:449
  19.4 40.3 %collective-permute-start.10 = (bf16[400,768]{1,0:T(8,128)(2,1)}, bf16[400,768]{1,0:T(8,128)(2,1)}, u32[]{:S(2)}, u32[]{:S(2)}) collective-permute-start(bf16[400,768]{1,0:T(8,128)(2,1)} %pad_maximum_fusion.1.refs_8_.own_ref), channel_id=1, source_target_pairs={{0,4},{1,5},{2,6},{3,7},{4,0},{5,1},{6,2},{7,3},{8,12},{9,13},{10,... | collective-permute-start | bytes 1843208 | tf_op jit(solution)/shard_map/ppermute | solution.py:449
  25.7 235.0 %all-gather.14.cloned.1.call-start = ((), (), s32[]{:S(2)}) async-start(), calls=%async_computation.3 | async-start | bytes 3072000 | tf_op jit(solution)/shard_map/all_gather | solution.py:1452
  29.6 13.8 %collective-permute-start.3 = (bf16[4,208,384]{2,1,0:T(8,128)(2,1)S(1)}, bf16[4,208,384]{2,1,0:T(8,128)(2,1)S(1)}, u32[]{:S(2)}, u32[]{:S(2)}) collective-permute-start(bf16[4,208,384]{2,1,0:T(8,128)(2,1)S(1)} %pad_maximum_fusion.refs_0_), channel_id=1, source_target_pairs={{0,2},{1,5},{2,0},{3,7},{4,6},{5,1},{6,4},{7,3},{8,10},{9,13},{10,... | collective-permute-start | bytes 1916936 | tf_op jit(solution)/shard_map/ppermute | solution.py:449
  33.4 51.7 %copy-start.2 = (bf16[400,768]{1,0:T(8,128)(2,1)}, bf16[400,768]{1,0:T(8,128)(2,1)S(1)}, u32[]{:S(2)}) copy-start(bf16[400,768]{1,0:T(8,128)(2,1)S(1)} %fusion.4.refs_4_) | copy-start | bytes 1843204
  33.5 28.0 %collective-permute-start.6 = (bf16[4,208,384]{2,1,0:T(8,128)(2,1)S(1)}, bf16[4,208,384]{2,1,0:T(8,128)(2,1)}, u32[]{:S(2)}, u32[]{:S(2)}) collective-permute-start(bf16[4,208,384]{2,1,0:T(8,128)(2,1)S(1)} %pad_maximum_fusion.refs_0_), channel_id=1, source_target_pairs={{0,1},{1,0},{2,3},{3,2},{4,5},{5,4},{6,7},{7,6},{8,9},{9,8},{10,11... | collective-permute-start | bytes 1916936 | tf_op jit(solution)/shard_map/ppermute | solution.py:449
  33.6 15.3 %collective-permute-start.4 = (bf16[4,208,384]{2,1,0:T(8,128)(2,1)S(1)}, bf16[4,208,384]{2,1,0:T(8,128)(2,1)}, u32[]{:S(2)}, u32[]{:S(2)}) collective-permute-start(bf16[4,208,384]{2,1,0:T(8,128)(2,1)S(1)} %pad_maximum_fusion.refs_0_), channel_id=1, source_target_pairs={{0,4},{1,3},{2,6},{3,1},{4,0},{5,7},{6,2},{7,5},{8,12},{9,11},{10,... | collective-permute-start | bytes 1916936 | tf_op jit(solution)/shard_map/ppermute | solution.py:449
  43.4 11.6 %collective-permute-start.5 = (bf16[4,208,384]{2,1,0:T(8,128)(2,1)S(1)}, bf16[4,208,384]{2,1,0:T(8,128)(2,1)}, u32[]{:S(2)}, u32[]{:S(2)}) collective-permute-start(bf16[4,208,384]{2,1,0:T(8,128)(2,1)S(1)} %collective-permute-done.3.refs_1_), channel_id=1, source_target_pairs={{0,4},{1,3},{2,6},{3,1},{4,0},{5,7},{6,2},{7,5},{8,12},{9,11},{10,... | collective-permute-start | bytes 1916936 | tf_op jit(solution)/shard_map/ppermute | solution.py:449
  45.4 16.0 %collective-permute-start.7 = (bf16[4,208,384]{2,1,0:T(8,128)(2,1)S(1)}, bf16[4,208,384]{2,1,0:T(8,128)(2,1)S(1)}, u32[]{:S(2)}, u32[]{:S(2)}) collective-permute-start(bf16[4,208,384]{2,1,0:T(8,128)(2,1)S(1)} %collective-permute-done.3.refs_1_), channel_id=1, source_target_pairs={{0,1},{1,0},{2,3},{3,2},{4,5},{5,4},{6,7},{7,6},{8,9},{9,8},{10,11... | collective-permute-start | bytes 1916936 | tf_op jit(solution)/shard_map/ppermute | solution.py:449
  48.9 12.5 %collective-permute-start.8 = (bf16[4,208,384]{2,1,0:T(8,128)(2,1)}, bf16[4,208,384]{2,1,0:T(8,128)(2,1)}, u32[]{:S(2)}, u32[]{:S(2)}) collective-permute-start(bf16[4,208,384]{2,1,0:T(8,128)(2,1)} %collective-permute-done.4.refs_2_), channel_id=1, source_target_pairs={{0,1},{1,0},{2,3},{3,2},{4,5},{5,4},{6,7},{7,6},{8,9},{9,8},{10,11... | collective-permute-start | bytes 1916936 | tf_op jit(solution)/shard_map/ppermute | solution.py:449
  55.0 6.4 %collective-permute-start.9 = (bf16[4,208,384]{2,1,0:T(8,128)(2,1)}, bf16[4,208,384]{2,1,0:T(8,128)(2,1)}, u32[]{:S(2)}, u32[]{:S(2)}) collective-permute-start(bf16[4,208,384]{2,1,0:T(8,128)(2,1)} %collective-permute-done.5.refs_3_), channel_id=1, source_target_pairs={{0,1},{1,0},{2,3},{3,2},{4,5},{5,4},{6,7},{7,6},{8,9},{9,8},{10,11... | collective-permute-start | bytes 1916936 | tf_op jit(solution)/shard_map/ppermute | solution.py:449
  59.7 25.5 %collective-permute-start.21 = (bf16[400,768]{1,0:T(8,128)(2,1)S(1)}, bf16[400,768]{1,0:T(8,128)(2,1)}, u32[]{:S(2)}, u32[]{:S(2)}) collective-permute-start(bf16[400,768]{1,0:T(8,128)(2,1)S(1)} %fusion.4.refs_4_), channel_id=1, source_target_pairs={{0,2},{1,3},{2,0},{3,1},{4,6},{5,7},{6,4},{7,5},{8,10},{9,11},{10,... | collective-permute-start | bytes 1843208 | tf_op jit(solution)/shard_map/ppermute | solution.py:449
  83.1 15.8 %collective-permute-start.18 = (bf16[400,768]{1,0:T(8,128)(2,1)}, bf16[400,768]{1,0:T(8,128)(2,1)S(1)}, u32[]{:S(2)}, u32[]{:S(2)}) collective-permute-start(bf16[400,768]{1,0:T(8,128)(2,1)} %get-tuple-element.46.h_ref.refs_0_.h2_ref), channel_id=1, source_target_pairs={{0,2},{1,3},{2,0},{3,1},{4,6},{5,7},{6,4},{7,5},{8,10},{9,11},{10,... | collective-permute-start | bytes 1843208 | tf_op jit(solution)/shard_map/ppermute | solution.py:449
  83.4 37.4 %collective-permute-start.11 = (bf16[4,192,768]{2,1,0:T(8,128)(2,1)}, bf16[4,192,768]{2,1,0:T(8,128)(2,1)}, u32[]{:S(2)}, u32[]{:S(2)}) collective-permute-start(bf16[4,192,768]{2,1,0:T(8,128)(2,1)} %bitcast.106), channel_id=1, source_target_pairs={{0,2},{1,5},{2,0},{3,7},{4,6},{5,1},{6,4},{7,3},{8,10},{9,13},{10,... | collective-permute-start | bytes 3538952 | tf_op jit(solution)/shard_map/ppermute | solution.py:449
  85.2 13.7 %collective-permute-start.22 = (bf16[400,768]{1,0:T(8,128)(2,1)S(1)}, bf16[400,768]{1,0:T(8,128)(2,1)S(1)}, u32[]{:S(2)}, u32[]{:S(2)}) collective-permute-start(bf16[400,768]{1,0:T(8,128)(2,1)S(1)} %fusion.4.refs_4_), channel_id=1, source_target_pairs={{0,1},{1,0},{2,3},{3,2},{4,5},{5,4},{6,7},{7,6},{8,9},{9,8},{10,11... | collective-permute-start | bytes 1843208 | tf_op jit(solution)/shard_map/ppermute | solution.py:449
  85.2 37.2 %collective-permute-start.23 = (bf16[400,768]{1,0:T(8,128)(2,1)}, bf16[400,768]{1,0:T(8,128)(2,1)S(1)}, u32[]{:S(2)}, u32[]{:S(2)}) collective-permute-start(bf16[400,768]{1,0:T(8,128)(2,1)} %collective-permute-done.21.refs_5_), channel_id=1, source_target_pairs={{0,1},{1,0},{2,3},{3,2},{4,5},{5,4},{6,7},{7,6},{8,9},{9,8},{10,11... | collective-permute-start | bytes 1843208 | tf_op jit(solution)/shard_map/ppermute | solution.py:449
  85.7 36.7 %collective-permute-start.19 = (bf16[400,768]{1,0:T(8,128)(2,1)}, bf16[400,768]{1,0:T(8,128)(2,1)S(1)}, u32[]{:S(2)}, u32[]{:S(2)}) collective-permute-start(bf16[400,768]{1,0:T(8,128)(2,1)} %get-tuple-element.46.h_ref.refs_0_.h2_ref), channel_id=1, source_target_pairs={{0,1},{1,0},{2,3},{3,2},{4,5},{5,4},{6,7},{7,6},{8,9},{9,8},{10,11... | collective-permute-start | bytes 1843208 | tf_op jit(solution)/shard_map/ppermute | solution.py:449
  98.8 24.5 %copy-start.30 = (bf16[400,768]{1,0:T(8,128)(2,1)}, bf16[400,768]{1,0:T(8,128)(2,1)S(1)}, u32[]{:S(2)}) copy-start(bf16[400,768]{1,0:T(8,128)(2,1)S(1)} %collective-permute-done.18.refs_1_) | copy-start | bytes 1843204
  98.8 23.5 %collective-permute-start.20 = (bf16[400,768]{1,0:T(8,128)(2,1)S(1)}, bf16[400,768]{1,0:T(8,128)(2,1)}, u32[]{:S(2)}, u32[]{:S(2)}) collective-permute-start(bf16[400,768]{1,0:T(8,128)(2,1)S(1)} %collective-permute-done.18.refs_1_), channel_id=1, source_target_pairs={{0,1},{1,0},{2,3},{3,2},{4,5},{5,4},{6,7},{7,6},{8,9},{9,8},{10,11... | collective-permute-start | bytes 1843208 | tf_op jit(solution)/shard_map/ppermute | solution.py:449
  98.9 24.5 %copy-start.31 = (bf16[400,768]{1,0:T(8,128)(2,1)}, bf16[400,768]{1,0:T(8,128)(2,1)S(1)}, u32[]{:S(2)}) copy-start(bf16[400,768]{1,0:T(8,128)(2,1)S(1)} %collective-permute-done.22.refs_6_) | copy-start | bytes 1843204
  98.9 66.3 %collective-permute-start.12 = (bf16[4,192,768]{2,1,0:T(8,128)(2,1)}, bf16[4,192,768]{2,1,0:T(8,128)(2,1)}, u32[]{:S(2)}, u32[]{:S(2)}) collective-permute-start(bf16[4,192,768]{2,1,0:T(8,128)(2,1)} %bitcast.107), channel_id=1, source_target_pairs={{0,4},{1,3},{2,6},{3,1},{4,0},{5,7},{6,2},{7,5},{8,12},{9,11},{10,... | collective-permute-start | bytes 3538952 | tf_op jit(solution)/shard_map/ppermute | solution.py:449
  120.8 44.8 %collective-permute-start.13 = (bf16[4,192,768]{2,1,0:T(8,128)(2,1)}, bf16[4,192,768]{2,1,0:T(8,128)(2,1)}, u32[]{:S(2)}, u32[]{:S(2)}) collective-permute-start(bf16[4,192,768]{2,1,0:T(8,128)(2,1)} %collective-permute-done.11.refs_1_), channel_id=1, source_target_pairs={{0,4},{1,3},{2,6},{3,1},{4,0},{5,7},{6,2},{7,5},{8,12},{9,11},{10,... | collective-permute-start | bytes 3538952 | tf_op jit(solution)/shard_map/ppermute | solution.py:449
  123.4 41.2 %copy-start.27 = (bf16[768,768]{1,0:T(8,128)(2,1)S(1)}, bf16[768,768]{1,0:T(8,128)(2,1)}, u32[]{:S(2)}) copy-start(bf16[768,768]{1,0:T(8,128)(2,1)} %all-gather.10.cloned.1.call-done) | copy-start | bytes 3538948
  164.6 4.1 collective-permute-start.26
  164.6 7.1 %collective-permute-start.14 = (bf16[4,192,768]{2,1,0:T(8,128)(2,1)S(1)}, bf16[4,192,768]{2,1,0:T(8,128)(2,1)}, u32[]{:S(2)}, u32[]{:S(2)}) collective-permute-start(bf16[4,192,768]{2,1,0:T(8,128)(2,1)S(1)} %bitcast.110), channel_id=1, source_target_pairs={{0,1},{1,0},{2,3},{3,2},{4,5},{5,4},{6,7},{7,6},{8,9},{9,8},{10,11... | collective-permute-start | bytes 3538952 | tf_op jit(solution)/shard_map/ppermute | solution.py:449
  165.1 7.8 %collective-permute-start.15 = (bf16[4,192,768]{2,1,0:T(8,128)(2,1)}, bf16[4,192,768]{2,1,0:T(8,128)(2,1)}, u32[]{:S(2)}, u32[]{:S(2)}) collective-permute-start(bf16[4,192,768]{2,1,0:T(8,128)(2,1)} %collective-permute-done.11.refs_1_), channel_id=1, source_target_pairs={{0,1},{1,0},{2,3},{3,2},{4,5},{5,4},{6,7},{7,6},{8,9},{9,8},{10,11... | collective-permute-start | bytes 3538952 | tf_op jit(solution)/shard_map/ppermute | solution.py:449
  165.2 7.7 %collective-permute-start.16 = (bf16[4,192,768]{2,1,0:T(8,128)(2,1)}, bf16[4,192,768]{2,1,0:T(8,128)(2,1)}, u32[]{:S(2)}, u32[]{:S(2)}) collective-permute-start(bf16[4,192,768]{2,1,0:T(8,128)(2,1)} %collective-permute-done.12.refs_2_), channel_id=1, source_target_pairs={{0,1},{1,0},{2,3},{3,2},{4,5},{5,4},{6,7},{7,6},{8,9},{9,8},{10,11... | collective-permute-start | bytes 3538952 | tf_op jit(solution)/shard_map/ppermute | solution.py:449
  165.7 9.0 %collective-permute-start.17 = (bf16[4,192,768]{2,1,0:T(8,128)(2,1)}, bf16[4,192,768]{2,1,0:T(8,128)(2,1)}, u32[]{:S(2)}, u32[]{:S(2)}) collective-permute-start(bf16[4,192,768]{2,1,0:T(8,128)(2,1)} %collective-permute-done.13.refs_3_), channel_id=1, source_target_pairs={{0,1},{1,0},{2,3},{3,2},{4,5},{5,4},{6,7},{7,6},{8,9},{9,8},{10,11... | collective-permute-start | bytes 3538952 | tf_op jit(solution)/shard_map/ppermute | solution.py:449
  165.8 115.6 %all-gather.12.cloned.1.call-start = ((), (), s32[]{:S(2)}) async-start(), calls=%async_computation.2 | async-start | bytes 3072000 | tf_op jit(solution)/shard_map/all_gather | solution.py:1480
  171.2 17.5 %collective-permute-start.27 = (bf16[400,768]{1,0:T(8,128)(2,1)S(1)}, bf16[400,768]{1,0:T(8,128)(2,1)S(1)}, u32[]{:S(2)}, u32[]{:S(2)}) collective-permute-start(bf16[400,768]{1,0:T(8,128)(2,1)S(1)} %get-tuple-element.114), channel_id=1, source_target_pairs={{0,2},{1,3},{2,0},{3,1},{4,6},{5,7},{6,4},{7,5},{8,10},{9,11},{10,... | collective-permute-start | bytes 1843208 | tf_op jit(solution)/shard_map/ppermute | solution.py:449
  195.6 7.2 %collective-permute-start.28 = (bf16[128,768]{1,0:T(8,128)(2,1)}, bf16[128,768]{1,0:T(8,128)(2,1)S(1)}, u32[]{:S(2)}, u32[]{:S(2)}) collective-permute-start(bf16[128,768]{1,0:T(8,128)(2,1)} %get-tuple-element.59), channel_id=1, source_target_pairs={{0,4},{1,5},{2,6},{3,7},{4,0},{5,1},{6,2},{7,3},{8,12},{9,13},{10,... | collective-permute-start | bytes 589832 | tf_op jit(solution)/shard_map/ppermute | solution.py:449
  229.9 5.0 collective-permute-start.29
  230.0 336.6 %all-gather.8.cloned.1.call-start = ((), (), s32[]{:S(2)}) async-start(), calls=%async_computation | async-start | bytes 2654208 | tf_op jit(solution)/shard_map/all_gather | solution.py:1524
  239.9 17.6 %collective-permute-start.30 = (bf16[4,208,768]{2,1,0:T(8,128)(2,1)}, bf16[4,208,768]{2,1,0:T(8,128)(2,1)}, u32[]{:S(2)}, u32[]{:S(2)}) collective-permute-start(bf16[4,208,768]{2,1,0:T(8,128)(2,1)} %broadcast_select_fusion.1), channel_id=1, source_target_pairs={{0,2},{1,5},{2,0},{3,7},{4,6},{5,1},{6,4},{7,3},{8,10},{9,13},{10,... | collective-permute-start | bytes 3833864 | tf_op jit(solution)/shard_map/ppermute | solution.py:449
  240.3 44.2 %collective-permute-start.24 = (bf16[2,384,768]{2,1,0:T(8,128)(2,1)}, bf16[2,384,768]{2,1,0:T(8,128)(2,1)}, u32[]{:S(2)}, u32[]{:S(2)}) collective-permute-start(bf16[2,384,768]{2,1,0:T(8,128)(2,1)} %get-tuple-element.49), channel_id=1, source_target_pairs={{0,1},{1,0},{2,3},{3,2},{4,5},{5,4},{6,7},{7,6},{8,9},{9,8},{10,11... | collective-permute-start | bytes 3538952 | tf_op jit(solution)/shard_map/ppermute | solution.py:449
  260.4 21.0 %collective-permute-start.31 = (bf16[4,208,384]{2,1,0:T(8,128)(2,1)S(1)}, bf16[4,208,384]{2,1,0:T(8,128)(2,1)S(1)}, u32[]{:S(2)}, u32[]{:S(2)}) collective-permute-start(bf16[4,208,384]{2,1,0:T(8,128)(2,1)S(1)} %broadcast_select_fusion.2), channel_id=1, source_target_pairs={{0,4},{1,3},{2,6},{3,1},{4,0},{5,7},{6,2},{7,5},{8,12},{9,11},{10,... | collective-permute-start | bytes 1916936 | tf_op jit(solution)/shard_map/ppermute | solution.py:449
  260.8 107.3 %collective-permute-start.48 = (bf16[4,400,768]{2,1,0:T(8,128)(2,1)}, bf16[4,400,768]{2,1,0:T(8,128)(2,1)}, u32[]{:S(2)}, u32[]{:S(2)}) collective-permute-start(bf16[4,400,768]{2,1,0:T(8,128)(2,1)} %bitcast.96), channel_id=1, source_target_pairs={{0,1},{1,0},{2,3},{3,2},{4,5},{5,4},{6,7},{7,6},{8,9},{9,8},{10,11... | collective-permute-start | bytes 7372808 | tf_op jit(solution)/shard_map/ppermute | solution.py:449
  260.8 107.7 %collective-permute-start.46 = (bf16[4,400,768]{2,1,0:T(8,128)(2,1)}, bf16[4,400,768]{2,1,0:T(8,128)(2,1)}, u32[]{:S(2)}, u32[]{:S(2)}) collective-permute-start(bf16[4,400,768]{2,1,0:T(8,128)(2,1)} %bitcast.97), channel_id=1, source_target_pairs={{0,4},{1,3},{2,6},{3,1},{4,0},{5,7},{6,2},{7,5},{8,12},{9,11},{10,... | collective-permute-start | bytes 7372808 | tf_op jit(solution)/shard_map/ppermute | solution.py:449
  262.5 106.4 %collective-permute-start.45 = (bf16[4,400,768]{2,1,0:T(8,128)(2,1)}, bf16[4,400,768]{2,1,0:T(8,128)(2,1)}, u32[]{:S(2)}, u32[]{:S(2)}) collective-permute-start(bf16[4,400,768]{2,1,0:T(8,128)(2,1)} %bitcast.98), channel_id=1, source_target_pairs={{0,2},{1,5},{2,0},{3,7},{4,6},{5,1},{6,4},{7,3},{8,10},{9,13},{10,... | collective-permute-start | bytes 7372808 | tf_op jit(solution)/shard_map/ppermute | solution.py:449
  281.4 87.4 %collective-permute-start.38 = (bf16[4,400,768]{2,1,0:T(8,128)(2,1)}, bf16[4,400,768]{2,1,0:T(8,128)(2,1)}, u32[]{:S(2)}, u32[]{:S(2)}) collective-permute-start(bf16[4,400,768]{2,1,0:T(8,128)(2,1)} %bitcast.101), channel_id=1, source_target_pairs={{0,2},{1,5},{2,0},{3,7},{4,6},{5,1},{6,4},{7,3},{8,10},{9,13},{10,... | collective-permute-start | bytes 7372808 | tf_op jit(solution)/shard_map/ppermute | solution.py:449
  284.5 7.4 %collective-permute-start.32 = (bf16[208,384]{1,0:T(8,128)(2,1)S(1)}, bf16[208,384]{1,0:T(8,128)(2,1)S(1)}, u32[]{:S(2)}, u32[]{:S(2)}) collective-permute-start(bf16[208,384]{1,0:T(8,128)(2,1)S(1)} %get-tuple-element.123), channel_id=1, source_target_pairs={{0,8},{1,9},{2,10},{3,11},{4,12},{5,13},{6,14},{7,15},{8,16},{9,17... | collective-permute-start | bytes 479240 | tf_op jit(solution)/shard_map/ppermute | solution.py:449
  291.9 5.3 collective-permute-start.34
  297.2 7.2 %collective-permute-start.33 = (bf16[208,384]{1,0:T(8,128)(2,1)S(1)}, bf16[208,384]{1,0:T(8,128)(2,1)S(1)}, u32[]{:S(2)}, u32[]{:S(2)}) collective-permute-start(bf16[208,384]{1,0:T(8,128)(2,1)S(1)} %get-tuple-element.125), channel_id=1, source_target_pairs={{0,16},{1,17},{2,18},{3,19},{4,20},{5,21},{6,22},{7,23},{8,24},{9,... | collective-permute-start | bytes 479240 | tf_op jit(solution)/shard_map/ppermute | solution.py:449
  304.4 58.3 %collective-permute-start.25 = (bf16[384,768]{1,0:T(8,128)(2,1)}, bf16[384,768]{1,0:T(8,128)(2,1)}, u32[]{:S(2)}, u32[]{:S(2)}) collective-permute-start(bf16[384,768]{1,0:T(8,128)(2,1)} %slice_bitcast_fusion.2), channel_id=1, source_target_pairs={{0,2},{1,3},{2,0},{3,1},{4,6},{5,7},{6,4},{7,5},{8,10},{9,11},{10,... | collective-permute-start | bytes 1769480 | tf_op jit(solution)/shard_map/ppermute | solution.py:449
  307.9 147.2 %copy-start.35 = (s32[4]{0:T(128)S(1)}, s32[4]{0:T(128)}, u32[]{:S(2)}) copy-start(s32[4]{0:T(128)} %constant.145.clone) | copy-start | bytes 52
  307.9 150.3 %copy-start.1 = (f32[384,768]{1,0:T(8,128)S(1)}, f32[384,768]{1,0:T(8,128)}, u32[]{:S(2)}) copy-start(f32[384,768]{1,0:T(8,128)} %get-tuple-element.45.x1_ref) | copy-start | bytes 3538948
  362.6 5.3 collective-permute-start.35
  367.9 10.8 %collective-permute-start.41 = (bf16[4,400,768]{2,1,0:T(8,128)(2,1)}, bf16[4,400,768]{2,1,0:T(8,128)(2,1)S(1)}, u32[]{:S(2)}, u32[]{:S(2)}) collective-permute-start(bf16[4,400,768]{2,1,0:T(8,128)(2,1)} %bitcast.102), channel_id=1, source_target_pairs={{0,1},{1,0},{2,3},{3,2},{4,5},{5,4},{6,7},{7,6},{8,9},{9,8},{10,11... | collective-permute-start | bytes 7372808 | tf_op jit(solution)/shard_map/ppermute | solution.py:449
  368.0 10.5 %collective-permute-start.36 = (bf16[208,768]{1,0:T(8,128)(2,1)S(1)}, bf16[208,768]{1,0:T(8,128)(2,1)S(1)}, u32[]{:S(2)}, u32[]{:S(2)}) collective-permute-start(bf16[208,768]{1,0:T(8,128)(2,1)S(1)} %maximum_select_fusion.1), channel_id=1, source_target_pairs={{0,2},{1,5},{2,0},{3,7},{4,6},{5,1},{6,4},{7,3},{8,10},{9,13},{10,... | collective-permute-start | bytes 958472 | tf_op jit(solution)/shard_map/ppermute | solution.py:449
  368.4 32.6 %collective-permute-start.39 = (bf16[4,400,768]{2,1,0:T(8,128)(2,1)}, bf16[4,400,768]{2,1,0:T(8,128)(2,1)}, u32[]{:S(2)}, u32[]{:S(2)}) collective-permute-start(bf16[4,400,768]{2,1,0:T(8,128)(2,1)} %bitcast.103), channel_id=1, source_target_pairs={{0,4},{1,3},{2,6},{3,1},{4,0},{5,7},{6,2},{7,5},{8,12},{9,11},{10,... | collective-permute-start | bytes 7372808 | tf_op jit(solution)/shard_map/ppermute | solution.py:449
  368.8 32.6 %collective-permute-start.50 = (bf16[4,400,768]{2,1,0:T(8,128)(2,1)}, bf16[4,400,768]{2,1,0:T(8,128)(2,1)S(1)}, u32[]{:S(2)}, u32[]{:S(2)}) collective-permute-start(bf16[4,400,768]{2,1,0:T(8,128)(2,1)} %collective-permute-done.46.refs_10_), channel_id=1, source_target_pairs={{0,1},{1,0},{2,3},{3,2},{4,5},{5,4},{6,7},{7,6},{8,9},{9,8},{10,11... | collective-permute-start | bytes 7372808 | tf_op jit(solution)/shard_map/ppermute | solution.py:449
  368.8 58.5 %collective-permute-start.47 = (bf16[4,400,768]{2,1,0:T(8,128)(2,1)}, bf16[4,400,768]{2,1,0:T(8,128)(2,1)}, u32[]{:S(2)}, u32[]{:S(2)}) collective-permute-start(bf16[4,400,768]{2,1,0:T(8,128)(2,1)} %collective-permute-done.45.refs_9_), channel_id=1, source_target_pairs={{0,4},{1,3},{2,6},{3,1},{4,0},{5,7},{6,2},{7,5},{8,12},{9,11},{10,... | collective-permute-start | bytes 7372808 | tf_op jit(solution)/shard_map/ppermute | solution.py:449
  378.5 75.2 %collective-permute-start.40 = (bf16[4,400,768]{2,1,0:T(8,128)(2,1)}, bf16[4,400,768]{2,1,0:T(8,128)(2,1)}, u32[]{:S(2)}, u32[]{:S(2)}) collective-permute-start(bf16[4,400,768]{2,1,0:T(8,128)(2,1)} %collective-permute-done.38.refs_1_), channel_id=1, source_target_pairs={{0,4},{1,3},{2,6},{3,1},{4,0},{5,7},{6,2},{7,5},{8,12},{9,11},{10,... | collective-permute-start | bytes 7372808 | tf_op jit(solution)/shard_map/ppermute | solution.py:449
  378.7 75.2 %copy-start.25 = (bf16[4,400,768]{2,1,0:T(8,128)(2,1)}, bf16[4,400,768]{2,1,0:T(8,128)(2,1)S(1)}, u32[]{:S(2)}) copy-start(bf16[4,400,768]{2,1,0:T(8,128)(2,1)S(1)} %collective-permute-done.41.refs_4_) | copy-start | bytes 7372804
  378.7 75.2 %collective-permute-start.37 = (bf16[208,1536]{1,0:T(8,128)(2,1)S(1)}, bf16[208,1536]{1,0:T(8,128)(2,1)S(1)}, u32[]{:S(2)}, u32[]{:S(2)}) collective-permute-start(bf16[208,1536]{1,0:T(8,128)(2,1)S(1)} %maximum_select_fusion), channel_id=1, source_target_pairs={{0,1},{1,0},{2,3},{3,2},{4,5},{5,4},{6,7},{7,6},{8,9},{9,8},{10,11... | collective-permute-start | bytes 1916936 | tf_op jit(solution)/shard_map/ppermute | solution.py:449
  401.1 60.5 %collective-permute-start.49 = (bf16[4,400,768]{2,1,0:T(8,128)(2,1)}, bf16[4,400,768]{2,1,0:T(8,128)(2,1)}, u32[]{:S(2)}, u32[]{:S(2)}) collective-permute-start(bf16[4,400,768]{2,1,0:T(8,128)(2,1)} %collective-permute-done.45.refs_9_), channel_id=1, source_target_pairs={{0,1},{1,0},{2,3},{3,2},{4,5},{5,4},{6,7},{7,6},{8,9},{9,8},{10,11... | collective-permute-start | bytes 7372808 | tf_op jit(solution)/shard_map/ppermute | solution.py:449
  401.5 52.4 %copy-start.26 = (bf16[4,400,768]{2,1,0:T(8,128)(2,1)}, bf16[4,400,768]{2,1,0:T(8,128)(2,1)S(1)}, u32[]{:S(2)}) copy-start(bf16[4,400,768]{2,1,0:T(8,128)(2,1)S(1)} %collective-permute-done.50.refs_14_) | copy-start | bytes 7372804
  401.5 60.1 %collective-permute-start.42 = (bf16[4,400,768]{2,1,0:T(8,128)(2,1)}, bf16[4,400,768]{2,1,0:T(8,128)(2,1)}, u32[]{:S(2)}, u32[]{:S(2)}) collective-permute-start(bf16[4,400,768]{2,1,0:T(8,128)(2,1)} %collective-permute-done.38.refs_1_), channel_id=1, source_target_pairs={{0,1},{1,0},{2,3},{3,2},{4,5},{5,4},{6,7},{7,6},{8,9},{9,8},{10,11... | collective-permute-start | bytes 7372808 | tf_op jit(solution)/shard_map/ppermute | solution.py:449
  427.4 34.2 %collective-permute-start.43 = (bf16[4,400,768]{2,1,0:T(8,128)(2,1)}, bf16[4,400,768]{2,1,0:T(8,128)(2,1)}, u32[]{:S(2)}, u32[]{:S(2)}) collective-permute-start(bf16[4,400,768]{2,1,0:T(8,128)(2,1)} %collective-permute-done.39.refs_2_), channel_id=1, source_target_pairs={{0,1},{1,0},{2,3},{3,2},{4,5},{5,4},{6,7},{7,6},{8,9},{9,8},{10,11... | collective-permute-start | bytes 7372808 | tf_op jit(solution)/shard_map/ppermute | solution.py:449
  453.7 7.8 %collective-permute-start.51 = (bf16[4,400,768]{2,1,0:T(8,128)(2,1)}, bf16[4,400,768]{2,1,0:T(8,128)(2,1)}, u32[]{:S(2)}, u32[]{:S(2)}) collective-permute-start(bf16[4,400,768]{2,1,0:T(8,128)(2,1)} %collective-permute-done.47.refs_11_), channel_id=1, source_target_pairs={{0,1},{1,0},{2,3},{3,2},{4,5},{5,4},{6,7},{7,6},{8,9},{9,8},{10,11... | collective-permute-start | bytes 7372808 | tf_op jit(solution)/shard_map/ppermute | solution.py:449
  454.7 7.6 %collective-permute-start.44 = (bf16[4,400,768]{2,1,0:T(8,128)(2,1)}, bf16[4,400,768]{2,1,0:T(8,128)(2,1)}, u32[]{:S(2)}, u32[]{:S(2)}) collective-permute-start(bf16[4,400,768]{2,1,0:T(8,128)(2,1)} %collective-permute-done.40.refs_3_), channel_id=1, source_target_pairs={{0,1},{1,0},{2,3},{3,2},{4,5},{5,4},{6,7},{7,6},{8,9},{9,8},{10,11... | collective-permute-start | bytes 7372808 | tf_op jit(solution)/shard_map/ppermute | solution.py:449
  (28 other events, 167.7 us)
Sparse Core Ops, SparseCore 0:
  25.8 27.6 all-gather.9
  165.9 51.2 all-gather.13
  230.1 51.2 all-gather.11
  504.8 28.2 all-gather.7

commit v3 on v2

--- a/solution.py
+++ b/solution.py
@@ -438,6 +438,10 @@
 VMEM_LIMIT = 60 * 1024 * 1024
 
 
+def microseconds(time):
+    return pl.CostEstimate(flops=0, bytes_accessed=int(time * 0.4e6), transcendentals=0)
+
+
 def moved(value, target):
     pairs = []
     for z in range(4):
@@ -487,11 +491,14 @@
 
 def group_kernel(
     blocks,
+    more,
     base_ref,
     *refs,
 ):
     h_refs, g_refs = refs[:blocks], refs[blocks : 2 * blocks]
-    wg_ref, wu_ref, wd_ref, moe_ref, moe_far_ref, dx_ref, dx_far_ref = refs[2 * blocks : 2 * blocks + 7]
+    refs = refs[2 * blocks :]
+    more_refs, refs = refs[:more], refs[more:]
+    wg_ref, wu_ref, wd_ref, moe_ref, moe_far_ref, dx_ref, dx_far_ref = refs[:7]
     (
         rank_sc,
         prob_sc,
@@ -504,14 +511,20 @@
         ysel_sc,
         dsel_sc,
         drp_sc,
-    ) = refs[2 * blocks + 7 :]
+    ) = refs[7:18]
     e = pl.program_id(0)
     f = pl.program_id(1)
     experts = pl.num_programs(0)
     base = base_ref[0]
+    copies = [
+        pltpu.make_async_copy(source, into, refs[-1].at[i])
+        for i, (source, into) in enumerate(zip(more_refs, refs[18:]))
+    ]
 
     @pl.when((e == 0) & (f == 0))
     def _():
+        for one in copies:
+            one.start()
         for b in range(blocks):
             rank_sc[b] = g_refs[b][TOK_DEV:, :TOK_DEV].astype(F32)
             prob_sc[b] = h_refs[b][TOK_DEV:, :TOK_DEV].astype(F32) + h_refs[b][
@@ -563,10 +576,11 @@
 
     @pl.when((f == pl.num_programs(1) - 1) & (e == experts - 1))
     def _():
+        for one in copies:
+            one.wait()
         for b in range(blocks):
-            moe_out, dx_out, at = (
-                (moe_ref, dx_ref, b) if b < blocks // 2 else (moe_far_ref, dx_far_ref, b - blocks // 2)
-            )
+            side, at = divmod(b, blocks // 2)
+            moe_out, dx_out = ((moe_ref, dx_ref), (moe_far_ref, dx_far_ref))[side]
             hot = jnp.concatenate(
                 [
                     one_hot_rows(rank_sc[b, pl.ds(base + i, 1), :])
@@ -574,21 +588,31 @@
                 ],
                 0,
             ).astype(BF)
-            moe_out[at] = contract(hot, ysel_sc[b].astype(BF), 0, 0).astype(BF)
-            dx_out[at, :TOK_DEV, :] = contract(hot, dsel_sc[b].astype(BF), 0, 0).astype(BF)
-            high = drp_sc[b].astype(BF)
+            moe = contract(hot, ysel_sc[b].astype(BF), 0, 0)
+            dx = contract(hot, dsel_sc[b].astype(BF), 0, 0)
+            drp = drp_sc[b]
+            if more:
+                shared = refs[18 + 2 * at : 20 + 2 * at]
+                before = refs[22 + side], refs[24 + side]
+                moe = moe + shared[0][side] + before[0][at].astype(F32)
+                dx = dx + shared[1][side] + before[1][at, :TOK_DEV, :].astype(F32)
+                drp = drp + before[1][at, TOK_DEV:, :TOK_DEV].astype(F32)
+                drp = drp + before[1][at, TOK_DEV:, TOK_DEV:].astype(F32)
+            moe_out[at] = moe.astype(BF)
+            dx_out[at, :TOK_DEV, :] = dx.astype(BF)
+            high = drp.astype(BF)
             dx_out[at, TOK_DEV:, :TOK_DEV] = high
-            dx_out[at, TOK_DEV:, TOK_DEV:] = (drp_sc[b] - high.astype(F32)).astype(BF)
-
-
-def group_experts(base, h_group, g_group, w_gate, w_up, w_down):
+            dx_out[at, TOK_DEV:, TOK_DEV:] = (drp - high.astype(F32)).astype(BF)
+
+
+def group_experts(base, first, experts, h_group, g_group, more, w_gate, w_up, w_down):
     blocks = len(h_group)
-    experts, _, ff = w_gate.shape
+    ff = w_gate.shape[2]
     tile = 512
     whole = lambda *shape: pl.BlockSpec(shape, lambda e, f, s: (0,) * len(shape))
     moe_shape, dx_shape = (blocks // 2, TOK_DEV, D), (blocks // 2, ROWS, D)
     return pl.pallas_call(
-        functools.partial(group_kernel, blocks),
+        functools.partial(group_kernel, blocks, len(more)),
         out_shape=tuple(
             jax.ShapeDtypeStruct(s, BF) for s in (moe_shape, moe_shape, dx_shape, dx_shape)
         ),
@@ -596,10 +620,11 @@
             num_scalar_prefetch=1,
             grid=(experts, ff // tile),
             in_specs=[whole(ROWS, D)] * (2 * blocks)
+            + [pl.BlockSpec(memory_space=pl.ANY)] * len(more)
             + [
-                pl.BlockSpec((1, D, tile), lambda e, f, s: (e, 0, f)),
-                pl.BlockSpec((1, D, tile), lambda e, f, s: (e, 0, f)),
-                pl.BlockSpec((1, tile, D), lambda e, f, s: (e, f, 0)),
+                pl.BlockSpec((1, D, tile), lambda e, f, s: (first + e, 0, f)),
+                pl.BlockSpec((1, D, tile), lambda e, f, s: (first + e, 0, f)),
+                pl.BlockSpec((1, tile, D), lambda e, f, s: (first + e, f, 0)),
             ],
             out_specs=[whole(*moe_shape)] * 2 + [whole(*dx_shape)] * 2,
             scratch_shapes=[
@@ -614,109 +639,101 @@
                 pltpu.VMEM((blocks, experts * SLOT, D), F32),
                 pltpu.VMEM((blocks, experts * SLOT, D), F32),
                 pltpu.VMEM((blocks, EXPERTS, TOK_DEV), F32),
-            ],
+            ]
+            + [pltpu.VMEM(v.shape, v.dtype) for v in more]
+            + [pltpu.SemaphoreType.DMA((max(1, len(more)),))],
         ),
         compiler_params=pltpu.CompilerParams(vmem_limit_bytes=VMEM_LIMIT),
-        cost_estimate=pl.CostEstimate(
-            flops=2 * 6 * experts * blocks * SLOT * D * ff,
-            bytes_accessed=2 * 3 * experts * D * ff,
-            transcendentals=0,
-        ),
+        cost_estimate=microseconds(21),
         name="group_experts",
-    )(base, *h_group, *g_group, w_gate, w_up, w_down)
-
-
-def shared_kernel(parts, h_ref, g_ref, *refs):
-    bufs = refs[:parts]
-    out_ref, dh_ref, gu_sc, down_sc, sems = refs[parts:]
-    copies = []
-    for k, buf in enumerate(bufs):
-        mine = [pltpu.make_async_copy(buf.at[:, :, :512], gu_sc.at[k], sems.at[k, 3])]
-        for i in range(3):
-            mine.append(
-                pltpu.make_async_copy(
-                    buf.at[:, 64 * i : 64 * (i + 1), 512:],
-                    down_sc.at[k, :, :, 256 * i : 256 * (i + 1)],
-                    sems.at[k, i],
-                )
-            )
-        copies.append(mine)
-        for one in mine:
-            one.start()
-    for k in range(parts):
-        for one in copies[k]:
-            one.wait()
-        gate_up = gu_sc[k].reshape(D, 512)
-        w_gate, w_up, w_down = gate_up[:, :256], gate_up[:, 256:], down_sc[k].reshape(256, D)
-        gate_pre = jnp.dot(h_ref[:TOK_DEV, :], w_gate, preferred_element_type=F32)
-        up_pre = jnp.dot(h_ref[:TOK_DEV, :], w_up, preferred_element_type=F32)
-        back = contract(g_ref[...], w_down, 1, 1)
+    )(base, *h_group, *g_group, *more, w_gate, w_up, w_down)
+
+
+def shared_kernel(h_a_ref, h_b_ref, g_a_ref, g_b_ref, w_a_ref, w_b_ref, out_ref, dh_ref, h_sc, g_sc):
+    for k, (h_ref, g_ref) in enumerate(((h_a_ref, g_a_ref), (h_b_ref, g_b_ref))):
+        h_sc[k * TOK_DEV : (k + 1) * TOK_DEV, :] = h_ref[:TOK_DEV, :]
+        g_sc[k * TOK_DEV : (k + 1) * TOK_DEV, :] = g_ref[:TOK_DEV, :]
+    for k, w_ref in enumerate((w_a_ref, w_b_ref)):
+        w_gate, w_up = w_ref[:, :, :256].reshape(D, 256), w_ref[:, :, 256:512].reshape(D, 256)
+        w_down = jnp.concatenate(
+            [w_ref[:, 64 * i : 64 * (i + 1), 512:].reshape(256, 256) for i in range(3)], 1
+        )
+        gate_pre = jnp.dot(h_sc[...], w_gate, preferred_element_type=F32)
+        up_pre = jnp.dot(h_sc[...], w_up, preferred_element_type=F32)
+        back = contract(g_sc[...], w_down, 1, 1)
         swish, slope = swish_parts(gate_pre)
         inner = (swish * up_pre).astype(BF)
         out = jnp.dot(inner, w_down, preferred_element_type=F32)
         dgate_pre = (back * up_pre * slope).astype(BF)
         dup_pre = (back * swish).astype(BF)
         dh = contract(dgate_pre, w_gate, 1, 1) + contract(dup_pre, w_up, 1, 1)
-        if k == 0:
-            out_ref[...] = out
-            dh_ref[...] = dh
-        else:
-            out_ref[...] += out
-            dh_ref[...] += dh
-
-
-def shared_rows(h_block, grad, bufs):
-    parts = len(bufs)
-    rows = jax.ShapeDtypeStruct((TOK_DEV, D), F32)
+        for b in range(2):
+            rows = slice(b * TOK_DEV, (b + 1) * TOK_DEV)
+            out_ref[b] = out[rows] if k == 0 else out_ref[b] + out[rows]
+            dh_ref[b] = dh[rows] if k == 0 else dh_ref[b] + dh[rows]
+
+
+def shared_rows(h_pair, g_pair, w_own, w_far):
+    rows = jax.ShapeDtypeStruct((2, TOK_DEV, D), F32)
     vmem = pl.BlockSpec(memory_space=pltpu.VMEM)
     return pl.pallas_call(
-        functools.partial(shared_kernel, parts),
+        shared_kernel,
         out_shape=(rows, rows),
-        in_specs=[vmem, vmem] + [pl.BlockSpec(memory_space=pl.ANY)] * parts,
+        in_specs=[vmem] * 6,
         out_specs=(vmem, vmem),
         scratch_shapes=[
-            pltpu.VMEM((parts, 4, D // 4, 512), BF),
-            pltpu.VMEM((parts, 4, 64, D), BF),
-            pltpu.SemaphoreType.DMA((parts, 4)),
+            pltpu.VMEM((2 * TOK_DEV, D), BF),
+            pltpu.VMEM((2 * TOK_DEV, D), BF),
         ],
         compiler_params=pltpu.CompilerParams(vmem_limit_bytes=VMEM_LIMIT),
-        cost_estimate=pl.CostEstimate(
-            flops=2 * 6 * TOK_DEV * D * 2048, bytes_accessed=6 * D * 2048, transcendentals=0
-        ),
+        cost_estimate=microseconds(8),
         name="shared_rows",
-    )(h_block, grad, *bufs)
-
-
-def start_half(part, h_parts, g_parts, h_buf, g_buf, sems):
-    half = len(h_parts) // 2
-    for i in range(half):
-        per = h_parts[i].shape[0]
-        for which, (parts, buf) in enumerate(((h_parts, h_buf), (g_parts, g_buf))):
-            pltpu.make_async_copy(
-                parts[part * half + i], buf.at[pl.ds(i * per, per)], sems.at[which, i]
-            ).start()
-
-
-def wait_part(part, i, h_parts, g_parts, h_buf, g_buf, sems):
-    half = len(h_parts) // 2
-    per = h_parts[i].shape[0]
-    for which, (parts, buf) in enumerate(((h_parts, h_buf), (g_parts, g_buf))):
-        pltpu.make_async_copy(
-            parts[part * half + i], buf.at[pl.ds(i * per, per)], sems.at[which, i]
-        ).wait()
-
-
-def expert_slice_kernel(parts, pos_ref, *refs):
+    )(*h_pair, *g_pair, w_own, w_far)
+
+
+def start_parts(h_parts, g_parts, h_buf, g_buf, sems):
+    per = h_parts[0].shape[0]
+    copies = []
+    for i in range(len(h_parts)):
+        into = pl.ds(i * per, per)
+        copies.append(
+            (
+                pltpu.make_async_copy(h_parts[i], h_buf.at[into], sems.at[0, i]),
+                pltpu.make_async_copy(g_parts[i], g_buf.at[into], sems.at[1, i]),
+            )
+        )
+    for pair in copies:
+        for one in pair:
+            one.start()
+    return copies
+
+
+def expert_slice_kernel(parts, more, pos_ref, *refs):
     h_parts, g_parts = refs[:parts], refs[parts : 2 * parts]
-    wg_ref, wu_ref, wd_ref, og_ref, ou_ref, od_ref = refs[2 * parts : 2 * parts + 6]
-    h_buf, g_buf, x_sc, gd_sc, gate_sc, rank_sc, prob_sc, sems = refs[2 * parts + 6 :]
+    weights = refs[2 * parts : 2 * parts + 3]
+    refs = refs[2 * parts + 3 :]
+    sums, refs = refs[: 3 * more], refs[3 * more :]
+    og_ref, ou_ref, od_ref, h_buf, g_buf, x_sc, gd_sc, rank_sc, prob_sc = refs[:9]
+    wg_ref, wu_ref, wd_ref, sems, w_sems = refs[9:]
     base = pos_ref[0]
-    experts = wg_ref.shape[0]
-    half = parts // 2
+    experts, _, width = wg_ref.shape
     per = h_parts[0].shape[0]
+    copies = start_parts(h_parts, g_parts, h_buf, g_buf, sems)
+    cols = pl.ds(pl.multiple_of(pos_ref[1] * width, width), width)
+    loads = [
+        pltpu.make_async_copy(weights[0].at[:, :, cols], wg_ref, w_sems.at[0]),
+        pltpu.make_async_copy(weights[1].at[:, :, cols], wu_ref, w_sems.at[1]),
+        pltpu.make_async_copy(weights[2].at[:, cols, :], wd_ref, w_sems.at[2]),
+    ]
+    for i in range(3 * more):
+        loads.append(
+            pltpu.make_async_copy(sums[i], (og_ref, ou_ref, od_ref)[i], w_sems.at[3 + i])
+        )
+    for one in loads:
+        one.start()
 
     def dispatch(pair, carry):
-        both_x, both_g, both_gate = [], [], []
+        both_x, both_g = [], []
         for k in range(2):
             b = 2 * pair + k
             rank_sc[k] = g_buf[b, TOK_DEV:, :TOK_DEV].astype(F32)
@@ -732,106 +749,95 @@
                 hots.append(hot)
             hot = jnp.concatenate(hots, 0).astype(BF)
             both_x.append(jnp.dot(hot, h_buf[b, :TOK_DEV, :], preferred_element_type=F32))
-            both_g.append(jnp.dot(hot, g_buf[b, :TOK_DEV, :], preferred_element_type=F32))
-            both_gate.append(gates)
+            both_g.append(
+                jnp.dot(hot, g_buf[b, :TOK_DEV, :], preferred_element_type=F32)
+                * jnp.concatenate(gates, 0)
+            )
         into = pl.ds(pl.multiple_of(pair * 2 * SLOT, 2 * SLOT), 2 * SLOT)
         for i in range(experts):
             span = slice(i * SLOT, (i + 1) * SLOT)
             x_sc[i, into, :] = jnp.concatenate([v[span] for v in both_x], 0).astype(BF)
             gd_sc[i, into, :] = jnp.concatenate([v[span] for v in both_g], 0).astype(BF)
-            gate_sc[i, into, :] = jnp.concatenate([v[i] for v in both_gate], 0)
         return carry
 
-    start_half(0, h_parts, g_parts, h_buf, g_buf, sems)
-    for part in range(2):
-        for i in range(half):
-            wait_part(part, i, h_parts, g_parts, h_buf, g_buf, sems)
-            lax.fori_loop(i * per // 2, (i + 1) * per // 2, dispatch, 0)
-        if part == 0:
-            start_half(1, h_parts, g_parts, h_buf, g_buf, sems)
-
-        def products(i, carry, part=part):
-            rows = x_sc[i]
-            gate_pre = jnp.dot(rows, wg_ref[i], preferred_element_type=F32)
-            up_pre = jnp.dot(rows, wu_ref[i], preferred_element_type=F32)
-            back = contract(gd_sc[i], wd_ref[i], 1, 1) * gate_sc[i]
-            swish, slope = swish_parts(gate_pre)
-            inner = (swish * up_pre * gate_sc[i]).astype(BF)
-            dgate_pre = (back * up_pre * slope).astype(BF)
-            dup_pre = (back * swish).astype(BF)
-            add_g = contract(rows, dgate_pre, 0, 0)
-            add_u = contract(rows, dup_pre, 0, 0)
-            add_d = contract(inner, gd_sc[i], 0, 0)
-            if part == 0:
-                og_ref[i], ou_ref[i], od_ref[i] = add_g, add_u, add_d
-            else:
-                og_ref[i] += add_g
-                ou_ref[i] += add_u
-                od_ref[i] += add_d
-            return carry
-
-        lax.fori_loop(0, experts, products, 0)
-
-
-def expert_slice_grads(pos, h_parts, g_parts, w_gate, w_up, w_down, width):
+    for i in range(parts):
+        for one in copies[i]:
+            one.wait()
+        lax.fori_loop(i * per // 2, (i + 1) * per // 2, dispatch, 0)
+    for one in loads:
+        one.wait()
+
+    def products(i, carry):
+        rows = x_sc[i]
+        gate_pre = jnp.dot(rows, wg_ref[i], preferred_element_type=F32)
+        up_pre = jnp.dot(rows, wu_ref[i], preferred_element_type=F32)
+        back = contract(gd_sc[i], wd_ref[i], 1, 1)
+        swish, slope = swish_parts(gate_pre)
+        inner = (swish * up_pre).astype(BF)
+        dgate_pre = (back * up_pre * slope).astype(BF)
+        dup_pre = (back * swish).astype(BF)
+        add_g = contract(rows, dgate_pre, 0, 0)
+        add_u = contract(rows, dup_pre, 0, 0)
+        add_d = contract(inner, gd_sc[i], 0, 0)
+        if more:
+            og_ref[i] += add_g
+            ou_ref[i] += add_u
+            od_ref[i] += add_d
+        else:
+            og_ref[i], ou_ref[i], od_ref[i] = add_g, add_u, add_d
+        return carry
+
+    lax.fori_loop(0, experts, products, 0)
+
+
+def expert_slice_grads(pos, h_parts, g_parts, w_gate, w_up, w_down, width, sums=()):
     parts, per = len(h_parts), h_parts[0].shape[0]
     experts = w_gate.shape[0]
-    blocks = parts * per // 2
+    blocks = parts * per
+    shapes = ((experts, D, width), (experts, D, width), (experts, width, D))
+    vmem = pl.BlockSpec(memory_space=pltpu.VMEM)
     anywhere = pl.BlockSpec(memory_space=pl.ANY)
     return pl.pallas_call(
-        functools.partial(expert_slice_kernel, parts),
-        out_shape=(
-            jax.ShapeDtypeStruct((experts, D, width), F32),
-            jax.ShapeDtypeStruct((experts, D, width), F32),
-            jax.ShapeDtypeStruct((experts, width, D), F32),
-        ),
-        grid_spec=pltpu.PrefetchScalarGridSpec(
-            num_scalar_prefetch=1,
-            grid=(1,),
-            in_specs=[anywhere] * (2 * parts)
-            + [
-                pl.BlockSpec((experts, D, width), lambda i, s: (0, 0, s[1])),
-                pl.BlockSpec((experts, D, width), lambda i, s: (0, 0, s[1])),
-                pl.BlockSpec((experts, width, D), lambda i, s: (0, s[1], 0)),
-            ],
-            out_specs=[
-                pl.BlockSpec((experts, D, width), lambda i, s: (0, 0, 0)),
-                pl.BlockSpec((experts, D, width), lambda i, s: (0, 0, 0)),
-                pl.BlockSpec((experts, width, D), lambda i, s: (0, 0, 0)),
-            ],
-            scratch_shapes=[
-                pltpu.VMEM((blocks, ROWS, D), BF),
-                pltpu.VMEM((blocks, ROWS, D), BF),
-                pltpu.VMEM((experts, blocks * SLOT, D), BF),
-                pltpu.VMEM((experts, blocks * SLOT, D), BF),
-                pltpu.VMEM((experts, blocks * SLOT, 1), F32),
-                pltpu.VMEM((2, EXPERTS, TOK_DEV), F32),
-                pltpu.VMEM((2, EXPERTS, TOK_DEV), F32),
-                pltpu.SemaphoreType.DMA((2, parts // 2)),
-            ],
-        ),
+        functools.partial(expert_slice_kernel, parts, len(sums) // 3),
+        out_shape=tuple(jax.ShapeDtypeStruct(s, F32) for s in shapes),
+        in_specs=[pl.BlockSpec(memory_space=pltpu.SMEM)]
+        + [anywhere] * (2 * parts + 3 + len(sums)),
+        out_specs=(vmem,) * 3,
+        scratch_shapes=[
+            pltpu.VMEM((blocks, ROWS, D), BF),
+            pltpu.VMEM((blocks, ROWS, D), BF),
+            pltpu.VMEM((experts, blocks * SLOT, D), BF),
+            pltpu.VMEM((experts, blocks * SLOT, D), BF),
+            pltpu.VMEM((2, EXPERTS, TOK_DEV), F32),
+            pltpu.VMEM((2, EXPERTS, TOK_DEV), F32),
+        ]
+        + [pltpu.VMEM(s, BF) for s in shapes]
+        + [
+            pltpu.SemaphoreType.DMA((2, parts)),
+            pltpu.SemaphoreType.DMA((6,)),
+        ],
         compiler_params=pltpu.CompilerParams(vmem_limit_bytes=VMEM_LIMIT),
-        cost_estimate=pl.CostEstimate(
-            flops=2 * 2 * blocks * SLOT * experts * D * (6 * width + 2 * TOK_DEV),
-            bytes_accessed=2 * 4 * blocks * ROWS * D + 18 * experts * D * width,
-            transcendentals=0,
-        ),
+        cost_estimate=microseconds(31),
         name="expert_slice_grads",
-    )(pos, *h_parts, *g_parts, w_gate, w_up, w_down)
-
-
-def shared_slice_kernel(parts, pos_ref, *refs):
+    )(pos, *h_parts, *g_parts, w_gate, w_up, w_down, *sums)
+
+
+def shared_slice_kernel(parts, more, pos_ref, *refs):
     h_parts, g_parts = refs[:parts], refs[parts : 2 * parts]
-    w_ref, og_ref, ou_ref, od_ref = refs[2 * parts : 2 * parts + 4]
-    h_buf, g_buf, inner_sc, wg_ref, wu_ref, wd_ref, sems = refs[2 * parts + 4 :]
+    w_ref = refs[2 * parts]
+    refs = refs[2 * parts + 1 :]
+    sums, refs = refs[: 3 * more], refs[3 * more :]
+    og_ref, ou_ref, od_ref, h_buf, g_buf, inner_sc, wg_ref, wu_ref, wd_ref, sems = refs
+    per = h_parts[0].shape[0]
+    copies = start_parts(h_parts, g_parts, h_buf, g_buf, sems)
     wg_ref[...] = w_ref[:, :, :256].reshape(D, 256)
     wu_ref[...] = w_ref[:, :, 256:512].reshape(D, 256)
     for i in range(3):
         wd_ref[:, 256 * i : 256 * (i + 1)] = w_ref[:, 64 * i : 64 * (i + 1), 512:].reshape(256, 256)
-    half = parts // 2
-    per = h_parts[0].shape[0]
     window = pl.ds(pl.multiple_of(pos_ref[0] * 128, 128), og_ref.shape[0])
     lanes = pl.ds(pl.multiple_of(pos_ref[1] * 128, 128), od_ref.shape[0])
+    for i, out_ref in enumerate((og_ref, ou_ref, od_ref)):
+        out_ref[...] = sums[i][...] if more else jnp.zeros_like(out_ref)
 
     def two(buf, pair, cols=slice(None)):
         return jnp.concatenate([buf[2 * pair + k, :TOK_DEV, cols] for k in range(2)], 0)
@@ -851,55 +857,42 @@
         od_ref[...] += contract(inner_sc[:, lanes], grads, 0, 0)
         return carry
 
-    og_ref[...] = jnp.zeros_like(og_ref)
-    ou_ref[...] = jnp.zeros_like(ou_ref)
-    od_ref[...] = jnp.zeros_like(od_ref)
-    start_half(0, h_parts, g_parts, h_buf, g_buf, sems)
-    for part in range(2):
-        for i in range(half):
-            wait_part(part, i, h_parts, g_parts, h_buf, g_buf, sems)
-            lax.fori_loop(i * per // 2, (i + 1) * per // 2, products, 0)
-        if part == 0:
-            start_half(1, h_parts, g_parts, h_buf, g_buf, sems)
-
-
-def shared_slice_grads(pos, h_parts, g_parts, weights):
+    for i in range(parts):
+        for one in copies[i]:
+            one.wait()
+        lax.fori_loop(i * per // 2, (i + 1) * per // 2, products, 0)
+
+
+def shared_slice_grads(pos, h_parts, g_parts, weights, sums=()):
     parts, per = len(h_parts), h_parts[0].shape[0]
-    blocks = parts * per // 2
+    blocks = parts * per
     width = 256
+    vmem = pl.BlockSpec(memory_space=pltpu.VMEM)
     anywhere = pl.BlockSpec(memory_space=pl.ANY)
-    whole = lambda *shape: pl.BlockSpec(shape, lambda i, s: (0,) * len(shape))
     return pl.pallas_call(
-        functools.partial(shared_slice_kernel, parts),
+        functools.partial(shared_slice_kernel, parts, len(sums) // 3),
         out_shape=(
             jax.ShapeDtypeStruct((256, width), F32),
             jax.ShapeDtypeStruct((256, width), F32),
             jax.ShapeDtypeStruct((128, D), F32),
         ),
-        grid_spec=pltpu.PrefetchScalarGridSpec(
-            num_scalar_prefetch=1,
-            grid=(1,),
-            in_specs=[anywhere] * (2 * parts)
-            + [whole(4, D // 4, D)],
-            out_specs=[whole(256, width), whole(256, width), whole(128, D)],
-            scratch_shapes=[
-                pltpu.VMEM((blocks, ROWS, D), BF),
-                pltpu.VMEM((blocks, ROWS, D), BF),
-                pltpu.VMEM((2 * TOK_DEV, width), BF),
-                pltpu.VMEM((D, width), BF),
-                pltpu.VMEM((D, width), BF),
-                pltpu.VMEM((width, D), BF),
-                pltpu.SemaphoreType.DMA((2, parts // 2)),
-            ],
-        ),
+        in_specs=[pl.BlockSpec(memory_space=pltpu.SMEM)]
+        + [anywhere] * (2 * parts)
+        + [vmem] * (1 + len(sums)),
+        out_specs=(vmem,) * 3,
+        scratch_shapes=[
+            pltpu.VMEM((blocks, ROWS, D), BF),
+            pltpu.VMEM((blocks, ROWS, D), BF),
+            pltpu.VMEM((2 * TOK_DEV, width), BF),
+            pltpu.VMEM((D, width), BF),
+            pltpu.VMEM((D, width), BF),
+            pltpu.VMEM((width, D), BF),
+            pltpu.SemaphoreType.DMA((2, parts)),
+        ],
         compiler_params=pltpu.CompilerParams(vmem_limit_bytes=VMEM_LIMIT),
-        cost_estimate=pl.CostEstimate(
-            flops=2 * 2 * blocks * TOK_DEV * (3 * D * width + 512 * width + 128 * D),
-            bytes_accessed=2 * 4 * blocks * ROWS * D,
-            transcendentals=0,
-        ),
+        cost_estimate=microseconds(20),
         name="shared_slice_grads",
-    )(pos, *h_parts, *g_parts, weights)
+    )(pos, *h_parts, *g_parts, weights, *sums)
 
 
 def pair_sum(kept, received):
@@ -1085,9 +1078,7 @@
             pltpu.SemaphoreType.DMA((8, 4)),
         ],
         compiler_params=pltpu.CompilerParams(vmem_limit_bytes=VMEM_LIMIT),
-        cost_estimate=pl.CostEstimate(
-            flops=2 * 2 * TOK_DEV * D * 4 * D, bytes_accessed=8 * 2 * D * D, transcendentals=0
-        ),
+        cost_estimate=microseconds(20),
         name="attention_forward",
     )(place, *w_parts, own, far, gain1, gain2, router_t, cos, sin)
 
@@ -1095,7 +1086,6 @@
 def branch_kernel(
     dx_a_ref,
     dx_b_ref,
-    dsh_ref,
     h2_ref,
     x1_ref,
     g_ref,
@@ -1119,7 +1109,6 @@
     dh2 = (
         dx_a_ref[:TOK_DEV, :].astype(F32)
         + dx_b_ref[:TOK_DEV, :].astype(F32)
-        + dsh_ref[...]
         + contract(dlogits, router_ref[...], 0, 0)
     )
     resid = x1_ref[...]
@@ -1139,7 +1128,7 @@
     gwo_ref[...] = contract(o_ref[...], datt, 0, 0).astype(BF)
 
 
-def branch_backward(dx_a, dx_b, dsh, h_block, x1, grad, gain2, router_t, o, w_all):
+def branch_backward(dx_a, dx_b, h_block, x1, grad, gain2, router_t, o, w_all):
     shape = jax.ShapeDtypeStruct
     whole = lambda *dims: pl.BlockSpec(dims, lambda i: (0,) * len(dims))
     rows = whole(TOK_DEV, D)
@@ -1157,7 +1146,6 @@
         in_specs=[
             whole(ROWS, D),
             whole(ROWS, D),
-            rows,
             whole(ROWS, D),
             rows,
             rows,
@@ -1175,11 +1163,9 @@
             whole(1, D),
         ),
         compiler_params=pltpu.CompilerParams(vmem_limit_bytes=VMEM_LIMIT),
-        cost_estimate=pl.CostEstimate(
-            flops=2 * 2 * TOK_DEV * D * D, bytes_accessed=12 * TOK_DEV * D, transcendentals=0
-        ),
+        cost_estimate=microseconds(6),
         name="branch_backward",
-    )(dx_a, dx_b, dsh, h_block, x1, grad, gain2, router_t, o, w_all)
+    )(dx_a, dx_b, h_block, x1, grad, gain2, router_t, o, w_all)
 
 
 def attention_back_kernel(
@@ -1197,10 +1183,11 @@
     sin_ref,
     dx1_ref,
     gwo_ref,
+    grouter_ref,
+    ggain2_ref,
     gtok_ref,
-    gqk_ref,
-    gvo_ref,
-    ggain_ref,
+    keep_ref,
+    send_ref,
     dq_sc,
     dk_sc,
     dv_sc,
@@ -1281,6 +1268,19 @@
         return carry
 
     lax.fori_loop(0, HEADS // 2, heads, 0)
+
+    def put(owner, at, product):
+        for z in range(4):
+            rows = product[z * (D // 4) : (z + 1) * (D // 4), :]
+
+            @pl.when(flags_ref[4] == owner)
+            def _():
+                keep_ref[z, : D // 4, at : at + D] = rows
+
+            @pl.when(flags_ref[4] != owner)
+            def _():
+                send_ref[z, : D // 4, at : at + D] = rows
+
     dh1 = None
     for i, source in enumerate((dq_sc, dk_sc, dv_sc)):
         for slab in range(6):
@@ -1291,27 +1291,39 @@
             low_sc[:, cols] = value.astype(BF)
         grads = low_sc[...]
         product = contract(h1_ref[...], grads, 0, 0).astype(BF)
-        out_ref, at = ((gqk_ref, 0), (gqk_ref, D), (gvo_ref, 0))[i]
-        for z in range(4):
-            out_ref[z, : D // 4, at : at + D] = product[z * (D // 4) : (z + 1) * (D // 4), :]
+        put(i // 2, (i % 2) * D, product)
         for half in range(2):
             part = contract(grads[:, 384 * half : 384 * (half + 1)], w_ref[2 * i + half], 1, 1)
             dh1 = part if dh1 is None else dh1 + part
-    for z in range(4):
-        gvo_ref[z, : D // 4, D:] = gwo_ref[z * (D // 4) : (z + 1) * (D // 4), :]
-        gqk_ref[z, D // 4 :, :] = jnp.zeros((EXT, 2 * D), BF)
-        gvo_ref[z, D // 4 :, :] = jnp.zeros((EXT, 2 * D), BF)
+    put(1, D, gwo_ref[...])
     inputs = own_ref[:TOK_DEV, :].astype(F32)
     scale = unit_rms(inputs)
     normed = inputs * scale
-    ggain_ref[...] = jnp.sum(dh1 * normed, 0, keepdims=True)
+    ggain1 = jnp.sum(dh1 * normed, 0, keepdims=True)
+    gains = jnp.concatenate([ggain1, ggain2_ref[...], jnp.zeros((EXT - 2, D), F32)], 0)
+    keep_ref[:, D // 4 :, :] = jnp.zeros((4, EXT, 2 * D), BF)
+    send_ref[:, D // 4 :, :] = jnp.zeros((4, EXT, 2 * D), BF)
+    for z in range(4):
+        cols = slice(z * (D // 4), (z + 1) * (D // 4))
+        extras = jnp.concatenate([grouter_ref[:, cols], gains[:, cols]], 1).astype(BF)
+
+        @pl.when(flags_ref[4] == 0)
+        def _():
+            keep_ref[z, D // 4 :, : 2 * (D // 4)] = extras
+
+        @pl.when(flags_ref[4] != 0)
+        def _():
+            send_ref[z, D // 4 :, : 2 * (D // 4)] = extras
+
     dnormed = dh1 * gain1_ref[...]
     gtok_ref[...] = (
         scale * (dnormed - normed * jnp.mean(dnormed * normed, -1, keepdims=True)) + dx1_ref[...]
     )
 
 
-def attention_backward(flags, q, k, v, do, do_far, h1, w_all, own, gain1, cos, sin, dx1, gwo):
+def attention_backward(
+    flags, q, k, v, do, do_far, h1, w_all, own, gain1, cos, sin, dx1, gwo, grouter, ggain2
+):
     shape = jax.ShapeDtypeStruct
     whole = lambda *dims: pl.BlockSpec(dims, lambda i: (0,) * len(dims))
     rows = whole(TOK_DEV, D)
@@ -1324,7 +1336,6 @@
             shape((TOK_DEV, D), F32),
             shape(packed, BF),
             shape(packed, BF),
-            shape((1, D), F32),
         ),
         in_specs=[
             pl.BlockSpec(memory_space=pltpu.SMEM),
@@ -1341,8 +1352,10 @@
             whole(TOK_DEV, 128),
             rows,
             whole(D, D),
+            whole(EXPERTS, D),
+            whole(1, D),
         ],
-        out_specs=(rows, whole(*packed), whole(*packed), whole(1, D)),
+        out_specs=(rows, whole(*packed), whole(*packed)),
         scratch_shapes=[
             pltpu.VMEM((TOK_DEV, D), F32),
             pltpu.VMEM((TOK_DEV, D), F32),
@@ -1350,46 +1363,60 @@
             pltpu.VMEM((TOK_DEV, D), BF),
         ],
         compiler_params=pltpu.CompilerParams(vmem_limit_bytes=VMEM_LIMIT),
-        cost_estimate=pl.CostEstimate(
-            flops=2 * 8 * TOK_DEV * D * D, bytes_accessed=40 * TOK_DEV * D, transcendentals=0
-        ),
+        cost_estimate=microseconds(23),
         name="attention_backward",
-    )(flags, q, k, v, do, do_far, h1, w_all, own, gain1, cos, sin, dx1, gwo)
+    )(flags, q, k, v, do, do_far, h1, w_all, own, gain1, cos, sin, dx1, gwo, grouter, ggain2)
 
 
 def after(value, *earlier):
     return lax.optimization_barrier((value, earlier))[0]
 
 
-def spread(column):
-    first = over_a(column)
-    second = over_b(column)
-    third = over_b(first)
-    return [column, first, second, third]
-
-
-def with_core(parts):
-    return parts + [over_core(part) for part in parts]
-
-
-def reduce_dense(first, second, z, y, x, core):
-    kept = jnp.where(core == 0, first, second)
-    sent = jnp.where(core == 0, second, first)
-    total = pair_sum(kept, over_core(sent))
-    bit_a, bit_b = jnp.where(core == 0, x, y), jnp.where(core == 0, y, x)
-    kept, sent = halves(total, bit_a)
-    total = pair_sum(kept, over_a(sent))
-    kept, sent = halves(total, bit_b)
-    total = pair_sum(kept, over_b(sent))
+def place_kernel(every_ref, gate_ref, up_ref, down_ref):
+    for out_ref, at in ((gate_ref, 0), (up_ref, 256)):
+        for k in range(4):
+            for p in range(0, 8, 2):
+                pair = [
+                    every_ref[p + i, :, at + 64 * k : at + 64 * (k + 1)].astype(F32)
+                    for i in range(2)
+                ]
+                to = 512 * k + 64 * p
+                out_ref[:, to : to + 128] = jnp.concatenate(pair, 1)
+    for p in range(8):
+        for i in range(3):
+            down_ref[64 * p : 64 * (p + 1), 256 * i : 256 * (i + 1)] = every_ref[
+                p, 64 * i : 64 * (i + 1), 512:
+            ].astype(F32)
+
+
+def place_shared(every):
+    vmem = pl.BlockSpec(memory_space=pltpu.VMEM)
+    return pl.pallas_call(
+        place_kernel,
+        out_shape=(
+            jax.ShapeDtypeStruct((D // 4, 2048), F32),
+            jax.ShapeDtypeStruct((D // 4, 2048), F32),
+            jax.ShapeDtypeStruct((512, D), F32),
+        ),
+        in_specs=[vmem],
+        out_specs=(vmem,) * 3,
+        compiler_params=pltpu.CompilerParams(vmem_limit_bytes=VMEM_LIMIT),
+        cost_estimate=microseconds(4),
+        name="place_shared",
+    )(every)
+
+
+def reduce_step(total, over, bit):
+    kept, sent = halves(total, bit)
+    return kept, over(sent)
+
+
+def reduce_dp(total, z):
     result = lax.dynamic_index_in_dim(total, z, 0, keepdims=False).astype(F32)
     for step in (1, 2, 3):
         out = lax.dynamic_index_in_dim(total, lax.rem(z + step, 4), 0, keepdims=False)
         result = result + over_z(out, step).astype(F32)
-    result = result.astype(BF)
-    result = rejoin(result, over_b(result), bit_b)
-    result = rejoin(result, over_a(result), bit_a)
-    other = over_core(result)
-    return jnp.where(core == 0, result, other), jnp.where(core == 0, other, result)
+    return result.astype(BF)
 
 
 def tuned_body(
@@ -1422,12 +1449,16 @@
         [attn_gain[None], ffn_gain[None], jnp.zeros((EXT - 2, shard), BF)], 0
     )
     dense = jnp.concatenate([dense, jnp.concatenate([router_weight.T, gains], 1)], 0)
-    dense = jnp.stack([dense] + [over_z(dense, step) for step in (1, 2, 3)])
-    dense_parts = with_core(spread(dense))
+    dense_z = [over_z(dense, step) for step in (1, 2, 3)]
 
     ids = jnp.broadcast_to(prompt_ids.astype(BF)[:, None], (CONT, D))
     own = jnp.concatenate([tokens, ids, jnp.zeros((EXT - CONT, D), BF)], 0)
     far = moved(own, lambda z, y, x, c: (z, 1 - y, x, c))
+    dense = jnp.stack([dense] + after(dense_z, far))
+    dense_a, dense_b = over_a(dense), over_b(dense)
+    dense_c = over_b(after(dense_a, dense_b))
+    dense_parts = [dense, dense_a, dense_b, dense_c]
+    dense_parts = dense_parts + [over_core(part) for part in dense_parts]
     far_ids = far[TOK_DEV : TOK_DEV + CONT, 0].astype(jnp.int32)
 
     expert_ids = jnp.arange(EXPERTS, dtype=jnp.int32)[:, None]
@@ -1437,8 +1468,10 @@
     ranks = jnp.dot(member.astype(BF), before, preferred_element_type=F32)
     ranks = jnp.where(member, ranks, -1.0).astype(BF)
     g_block = jnp.concatenate([cotangent, jnp.pad(ranks, ((0, 0), (0, D - TOK_DEV)))], 0)
-    g_near = [g_block, over_x(g_block)]
-    g_group = with_core(g_near)
+    g_near = after(g_block, dense_c)
+    g_a, g_b = over_a(g_near), over_b(g_near)
+    g_x = jnp.where(core == 0, g_a, g_b)
+    g_group = [g_block, g_x, over_core(g_block), over_core(g_x)]
 
     units = lambda w: lax.dynamic_index_in_dim(
         w.reshape(shard, 4, 8, 64), plane, 2, keepdims=False
@@ -1446,11 +1479,10 @@
     down = lax.dynamic_slice_in_dim(shared_down, plane * 64, 64, 0)
     down = jnp.concatenate([down[:, 256 * i : 256 * (i + 1)] for i in range(3)], 0)
     shared = jnp.concatenate([units(shared_gate), units(shared_up), down], 1)
-    shared = lax.all_gather(shared, "dp", axis=0, tiled=False)
-    shared_parts = with_core(spread(shared))
-
-    g_column = lax.all_gather(g_block, "dp", axis=0, tiled=False)
-    g_parts = with_core(spread(g_column))
+    shared = lax.all_gather(after(shared, dense), "dp", axis=0, tiled=False)
+    shared_far = moved(after(shared, dense_c), lambda z, y, x, c: (z, 1 - y, x, c))
+
+    g_column = lax.all_gather(after(g_block, dense_a), "dp", axis=0, tiled=False)
 
     slots = dense[:, shard:, :]
     slots = jnp.stack([slots[0], slots[3], slots[2], slots[1]])
@@ -1471,46 +1503,104 @@
     place += [lax.rem(z + 4 - slot, 4) for slot in range(4)]
     place += [(prompt_ids[m] != y) for m in range(CONT)]
     place = jnp.stack([v.astype(jnp.int32) for v in place])
+    cos = after(cos, shared)
     w_all, q, k, v, h1, o, x1, h_block = attention_forward(
         place, dense_parts, own, far, gain1, gain2, router_t, cos, sin
     )
 
-    h_near = [h_block, over_x(h_block)]
-    h_group = with_core(h_near)
+    h_block, x1 = after((h_block, x1), g_a, g_b)
+    h_x = over_x(h_block)
+    h_group = [h_block, h_x, over_core(h_block), over_core(h_x)]
     h_column = lax.all_gather(h_block, "dp", axis=0, tiled=False)
+    experts_w = (expert_gate, expert_up_weight, expert_down)
     base = (j * 4).astype(jnp.int32)
+    part = group_experts(base[None], 0, 2, h_group, g_group, (), *experts_w)
+    near, far_group, part = after((h_group[::2], h_group[1::2], part), shared_far)
+    more = shared_rows(near, g_group[::2], shared, shared_far)
+    more += shared_rows(far_group, g_group[1::2], shared, shared_far)
+    g_first = over_a(after(g_column, part))
     moe_near, moe_far, dx_near, dx_far = group_experts(
-        base[None], h_group, g_group, expert_gate, expert_up_weight, expert_down
-    )
-    shared_out, shared_dh = shared_rows(h_block, cotangent, shared_parts)
-    h_parts = with_core(spread(h_column))
+        base[None] + 2, 2, 2, h_group, g_group, (*more, *part), *experts_w
+    )
+    moe_near, moe_far, dx_near, dx_far = after((moe_near, moe_far, dx_near, dx_far), g_first)
+    g_second = lax.all_gather(after(g_b, dx_near), "dp", axis=0, tiled=False)
 
     dx_pair = pair_sum(dx_near, over_core(dx_far))
     dx_there = over_x(dx_pair[1])
+    window = jnp.array([0, 1, 3, 4], jnp.int32)[z]
+    s_pos = jnp.stack([window, (z // 2).astype(jnp.int32)])
+    e_pos = jnp.stack([base, (z * 2 + y).astype(jnp.int32)])
+    h_column, g_column = after((h_column, g_column), dx_pair)
+    h_core, g_core = [over_core(h_column)], [over_core(g_column)]
+    s_sums = shared_slice_grads(
+        s_pos, [h_column, h_core[0]], [g_column, g_core[0]], shared
+    )
+    gain2 = after(gain2, s_sums)
     dx1, do, do_c, gwo, grad_router_t, grad_gain2 = branch_backward(
-        dx_pair[0], dx_there, shared_dh, h_block, x1, cotangent, gain2, router_t, o, w_all
+        dx_pair[0], dx_there, h_block, x1, cotangent, gain2, router_t, o, w_all
     )
     do_far = moved(do_c, lambda z, y, x, c: (z, 1 - y, x, c))
-    flags = jnp.concatenate([prompt_ids == y, far_ids == y]).astype(jnp.int32)
-    grad_inputs, gqk, gvo, grad_gain1 = attention_backward(
-        flags, q, k, v, do, do_far, h1, w_all, own, gain1, cos, sin, dx1, gwo
-    )
+    h_column, g_column, g_first = after((h_column, g_column, g_first), do_far)
+    h_first = over_a(h_column)
+    g_core.append(over_core(g_first))
+    flags = jnp.concatenate([prompt_ids == y, far_ids == y, core[None] != 0]).astype(jnp.int32)
+    grad_inputs, keep, send = attention_backward(
+        flags,
+        q,
+        k,
+        v,
+        do,
+        do_far,
+        h1,
+        w_all,
+        own,
+        gain1,
+        cos,
+        sin,
+        dx1,
+        gwo,
+        grad_router_t,
+        grad_gain2,
+    )
+    grad_inputs, keep, send = after(
+        (grad_inputs, keep, send), h_first, g_core, g_second
+    )
+    g_third = lax.all_gather(after(over_b(after(g_a, near)), keep), "dp", axis=0, tiled=False)
+    bit_a, bit_b = jnp.where(core == 0, x, y), jnp.where(core == 0, y, x)
+    total = pair_sum(keep, over_core(send))
+    h_core.append(over_core(h_first))
+    kept, there = reduce_step(total, over_a, bit_a)
+
+    h_parts, g_parts = [h_column, h_first] + h_core, [g_column, g_first] + g_core
+    s_sums = shared_slice_grads(
+        s_pos, [h_first, h_core[1]], [g_first, g_core[1]], shared, s_sums
+    )
+    s_sums, kept = after((s_sums, kept), there)
+    kept, there = reduce_step(pair_sum(kept, there), over_b, bit_b)
+    h_second, h_third = over_b(after(h_column, s_sums)), over_b(after(h_first, s_sums))
+    e_sums = expert_slice_grads(after(e_pos, s_sums), h_parts, g_parts, *experts_w, 256)
+    e_sums, kept, g_second, g_third = after(
+        (e_sums, kept, g_second, g_third), there, h_second, h_third
+    )
+    z_own = pair_sum(kept, there)
+    z_parts = [
+        over_z(lax.dynamic_index_in_dim(z_own, lax.rem(z + step, 4), 0, keepdims=False), step)
+        for step in (1, 2, 3)
+    ]
+    h_parts, g_parts = [h_second, h_third], [g_second, g_third]
+    h_parts = h_parts + [over_core(part) for part in h_parts]
+    g_parts = g_parts + [over_core(part) for part in g_parts]
+    s_sums = shared_slice_grads(s_pos, h_parts, g_parts, shared, s_sums)
+    s_gate, s_up, s_down = after(s_sums, z_parts)
+    total = lax.dynamic_index_in_dim(z_own, z, 0, keepdims=False).astype(F32)
+    for part in z_parts:
+        total = total + part.astype(F32)
+    total = after(total.astype(BF), s_gate)
+    moe_near, moe_far = after((moe_near, moe_far), s_gate)
     moe_pair = pair_sum(moe_near, over_core(moe_far))
-    moe_out = moe_pair[0].astype(F32) + over_x(moe_pair[1]).astype(F32)
-    layer_out = (x1 + shared_out + moe_out).astype(BF)
-
-    extras = jnp.concatenate([grad_gain1, grad_gain2, jnp.zeros((EXT - 2, D), F32)], 0)
-    extras = jnp.stack([grad_router_t, extras]).astype(BF).reshape(2, EXT, 4, shard)
-    extras = extras.transpose(2, 1, 0, 3).reshape(4, EXT, 2 * shard)
-    gqk = lax.dynamic_update_slice(gqk, extras, (0, shard, 0))
-    sum_qk, sum_vo = reduce_dense(gqk, gvo, z, y, x, core)
-    extras = sum_qk[shard:, : 2 * shard].astype(F32)
-    sum_qk, sum_vo = sum_qk[:shard].astype(F32), sum_vo[:shard].astype(F32)
-
-    window = jnp.array([0, 1, 3, 4], jnp.int32)[z]
-    s_gate, s_up, s_down = shared_slice_grads(
-        jnp.stack([window, (z // 2).astype(jnp.int32)]), h_parts, g_parts, shared
-    )
+    moe_there = over_x(moe_pair[1])
+    half_a, half_b = over_a(total), over_b(total)
+    opposite = moved(total, lambda z, y, x, c: (z, 1 - y, 1 - x, c))
     lead = z * 192 - window * 128
     s_down = lax.dynamic_slice_in_dim(s_down, (z % 2) * 64, 64, 0)
     mine = jnp.concatenate(
@@ -1522,24 +1612,16 @@
         1,
     ).astype(BF)
     every = lax.all_gather(mine, ("context", "experts"), axis=0, tiled=False)
-    s_gateup = (
-        every[:, :, :512].reshape(8, shard, 2, 4, 64).transpose(2, 1, 3, 0, 4)
-    ).reshape(2, shard, 2048)
-    s_gateup = s_gateup.astype(F32)
-    s_down = jnp.concatenate(
-        [every[:, 64 * i : 64 * (i + 1), 512:].reshape(512, 256) for i in range(3)], 1
-    ).astype(F32)
-
-    slice_index = (z * 2 + y).astype(jnp.int32)
-    e_gate, e_up, e_down = expert_slice_grads(
-        jnp.stack([base, slice_index]),
-        h_parts,
-        g_parts,
-        expert_gate,
-        expert_up_weight,
-        expert_down,
-        256,
-    )
+    e_gate, e_up, e_down = expert_slice_grads(e_pos, h_parts, g_parts, *experts_w, 256, e_sums)
+    e_gate, total = after((e_gate, total), half_a, half_b, opposite, moe_there, every)
+    layer_out = (x1 + (moe_pair[0].astype(F32) + moe_there.astype(F32))).astype(BF)
+    total = rejoin(rejoin(total, half_b, bit_b), rejoin(half_a, opposite, bit_b), bit_a)
+    other = over_core(total)
+    sum_qk, sum_vo = jnp.where(core == 0, total, other), jnp.where(core == 0, other, total)
+    extras = sum_qk[shard:, : 2 * shard].astype(F32)
+    sum_qk, sum_vo = sum_qk[:shard].astype(F32), sum_vo[:shard].astype(F32)
+
+    s_gate, s_up, s_down = place_shared(every)
     return (
         layer_out,
         grad_inputs,
@@ -1550,8 +1632,8 @@
         sum_vo[:, D:],
         extras[1, shard:],
         extras[:, :shard].T,
-        s_gateup[0],
-        s_gateup[1],
+        s_gate,
+        s_up,
         s_down,
         e_gate,
         e_up,

time: 596 us -> 451 us (0.76)
  waiting for transfers between devices: 257 us -> 104 us
  Pallas kernels: 203 us -> 231 us
  local copies, waits for them, and re-layouts: 42.9 us -> 25.1 us
    ppermute x52 -> x47, waiting for transfers between devices: 239 us -> 101 us  [moved(): return lax.ppermute(value, AXES, pairs)]
    pallas_call x4 -> x10, Pallas kernels: 153 us -> 178 us  [the longest x2 62.6 us: expert_slice_grads(): pl.pallas_call(functools.partial(expert_slice_kernel, parts, len(sums) //...]
    all_gather x1, waiting for transfers between devices: 18.6 us -> 2.53 us  [tuned_body(): h_column = lax.all_gather(h_block, 'dp', axis=0, tiled=False)]
    unnamed x87 -> x74, local copies, waits for them, and re-layouts: 17 us -> 8.31 us
    slice x5 -> x0, local copies, waits for them, and re-layouts: 7.52 us -> none  [the longest x1 2.65 us: tuned_body(): every[:, :, :512].reshape(8, shard, 2, 4, 64).transpose(2, 1, 3, 0, 4)]
    ppermute x52 -> x47, starting transfers between devices: 38.1 us -> 39 us  [moved(): return lax.ppermute(value, AXES, pairs)]
  transfers between devices with their start and end apart: 56 -> 53, of which waited for: 21 -> 18; matrix products, arithmetic and copies ran while one was open for 8% -> 8% of each run, Pallas kernels for 28% -> 52%
where the time goes in v3:
time: 451 us; the launch traced here: 444 us
  Pallas kernels  231 us (51%)
  waiting for transfers between devices  104 us (23%)
  starting transfers between devices  39.8 us (9%)
  other arithmetic  27.2 us (6%)
  local copies, waits for them, and re-layouts  25.1 us (6%)
  between operations  17 us (4%)
    ppermute x47, waiting for transfers between devices, moved(): return lax.ppermute(value, AXES, pairs)  101 us
    pallas_call x2, Pallas kernels, expert_slice_grads(): pl.pallas_call(functools.partial(expert_slice_kernel, parts, len(sums) //...  62.6 us
    pallas_call x2, Pallas kernels, group_experts(): pl.pallas_call(functools.partial(group_kernel, blocks, len(more)), out_sh...  48.5 us
    pallas_call x3, Pallas kernels, shared_slice_grads(): pl.pallas_call(functools.partial(shared_slice_kernel, parts, len(sums) //...  46.2 us
    ppermute x47, starting transfers between devices, moved(): return lax.ppermute(value, AXES, pairs)  39 us
    pallas_call x1, Pallas kernels, attention_backward(): pl.pallas_call(attention_back_kernel, grid=(1,), out_shape=(shape((TOK_DE...  25.5 us
    pallas_call x1, Pallas kernels, attention_forward(): pl.pallas_call(attention_kernel, out_shape=(shape((8, D, 384), BF), shape...  21 us
    pallas_call x2, Pallas kernels, shared_rows(): pl.pallas_call(shared_kernel, out_shape=(rows, rows), in_specs=[vmem] * 6...  16.9 us
  transfers between devices with their start and end apart: 53, of which 18 were waited for; matrix products, arithmetic and copies ran while one was open for 8% of the time, Pallas kernels for 52%

profile of v3, /device:TPU:0, one launch (start us, length us, event | category | flops | bytes accessed | tf_op | source)
XLA Modules:
  0.0 443.8 jit_solution(3416800627828374265)
XLA Ops:
  8.1 1.4 maximum_maximum_fusion.refs_8_.own_ref
  9.5 3.0 collective-permute-start.3
  13.5 2.6 collective-permute-start.1
  16.1 1.6 collective-permute-start
  17.6 2.2 collective-permute-start.2
  20.4 1.4 copy.47
  23.3 4.9 %collective-permute-done.1 = bf16[208,384]{1,0:T(8,128)(2,1)S(1)} collective-permute-done((bf16[208,384]{1,0:T(8,128)(2,1)}, bf16[208,384]{1,0:T(8,128)(2,1)S(1)}, u32[]{:S(2)}, u32[]{:S(2)}) %collective-permute-start.1) | collective-permute-done | bytes 159776 | tf_op jit(solution)/shard_map/ppermute | solution.py:453
  28.7 1.1 pad_maximum_fusion.refs_0_
  30.8 1.6 collective-permute-start.4
  33.4 8.0 %collective-permute-done.4.refs_1_ = bf16[4,208,384]{2,1,0:T(8,128)(2,1)} collective-permute-done((bf16[4,208,384]{2,1,0:T(8,128)(2,1)S(1)}, bf16[4,208,384]{2,1,0:T(8,128)(2,1)}, u32[]{:S(2)}, u32[]{:S(2)}) %collective-permute-start.4) | collective-permute-done | bytes 639008 | tf_op jit(solution)/shard_map/ppermute | solution.py:453
  46.3 6.0 %collective-permute-done.5.refs_2_ = bf16[4,208,384]{2,1,0:T(8,128)(2,1)} collective-permute-done((bf16[4,208,384]{2,1,0:T(8,128)(2,1)S(1)}, bf16[4,208,384]{2,1,0:T(8,128)(2,1)}, u32[]{:S(2)}, u32[]{:S(2)}) %collective-permute-start.5) | collective-permute-done | bytes 639008 | tf_op jit(solution)/shard_map/ppermute | solution.py:453
  53.4 10.4 %collective-permute-done.6.refs_3_ = bf16[4,208,384]{2,1,0:T(8,128)(2,1)} collective-permute-done((bf16[4,208,384]{2,1,0:T(8,128)(2,1)}, bf16[4,208,384]{2,1,0:T(8,128)(2,1)}, u32[]{:S(2)}, u32[]{:S(2)}) %collective-permute-start.6) | collective-permute-done | bytes 639008 | tf_op jit(solution)/shard_map/ppermute | solution.py:453
  64.1 2.6 collective-permute-start.11
  70.4 21.0 %attention_forward.1 = (bf16[8,768,384]{2,1,0:T(8,128)(2,1)}, bf16[768,768]{1,0:T(8,128)(2,1)}, bf16[768,768]{1,0:T(8,128)(2,1)}, bf16[768,768]{1,0:T(8,128)(2,1...) custom-call(s32[14]{0:T(128)} %stack.96.place_ref, ...), custom_call_target="tpu_custom_call" | custom-call | bytes 8000000 | tf_op jit(solution)/shard_map/attention_forward/pallas_call | solution.py:1060
  91.9 1.6 collective-permute-start.18
  93.5 1.1 broadcast_select_fusion.5.refs_5_.g_a_ref
  95.3 12.8 %collective-permute-done.13.refs_1_.h_a_ref = bf16[400,768]{1,0:T(8,128)(2,1)} collective-permute-done((bf16[400,768]{1,0:T(8,128)(2,1)}, bf16[400,768]{1,0:T(8,128)(2,1)}, u32[]{:S(2)}, u32[]{:S(2)}) %collective-permute-start.13) | collective-permute-done | bytes 614432 | tf_op jit(solution)/shard_map/ppermute | solution.py:453
  108.1 2.4 collective-permute-done.15.refs_3_.h_b_ref
  110.5 23.4 %group_experts.2 = (bf16[2,384,768]{2,1,0:T(8,128)(2,1)}, bf16[2,384,768]{2,1,0:T(8,128)(2,1)}, bf16[2,400,768]{2,1,0:T(8,128)(2,1)}, bf16[2,400,768]{2,1,0:T(8,128)(2,1)}) custom-call(s32[1]{0:T(128)} %bitcast.30.base_ref, bf16[400,768]{1,0:T(8,128)(2,1)} %get-tuple-element.135.refs_0_.h_a_ref.h2_ref, ...), custom_call_target="tpu_custom_call" | custom-call | bytes 8400000 | tf_op jit(solution)/shard_map/group_experts/pallas_call | solution.py:614
  135.0 8.4 %shared_rows.3 = (f32[2,384,768]{2,1,0:T(8,128)}, f32[2,384,768]{2,1,0:T(8,128)}) custom-call(bf16[400,768]{1,0:T(8,128)(2,1)} %collective-permute-done.13.refs_1_.h_a_ref, bf16[400,768]{1,0:T(8,128)(2,1)} %collective-permute-done.15.refs_3_.h_b_ref, bf16[400,768]{1,0:T(8,128)(2,1)} %copy-done.3, bf16[400,768]{1,0:T(8,128)(2,1)} %collective-permute-done.17.refs_7_.g_b_ref, ...), custom_call_target="tpu_custom_call" | custom-call | bytes 3200000 | tf_op jit(solution)/shard_map/shared_rows/pallas_call | solution.py:679
  143.4 8.5 %shared_rows.2 = (f32[2,384,768]{2,1,0:T(8,128)}, f32[2,384,768]{2,1,0:T(8,128)}) custom-call(bf16[400,768]{1,0:T(8,128)(2,1)} %get-tuple-element.135.refs_0_.h_a_ref.h2_ref, bf16[400,768]{1,0:T(8,128)(2,1)} %collective-permute-done.14.refs_2_.h_b_ref, bf16[400,768]{1,0:T(8,128)(2,1)} %fusion.4.refs_4_.g_a_ref, ...), custom_call_target="tpu_custom_call" | custom-call | bytes 3200000 | tf_op jit(solution)/shard_map/shared_rows/pallas_call | solution.py:679
  151.9 25.0 %group_experts.3 = (bf16[2,384,768]{2,1,0:T(8,128)(2,1)}, bf16[2,384,768]{2,1,0:T(8,128)(2,1)}, bf16[2,400,768]{2,1,0:T(8,128)(2,1)}, bf16[2,400,768]{2,1,0:T(8,128)(2,1)}) custom-call(s32[1]{0:T(128)S(6)} %add.148.base_ref, bf16[400,768]{1,0:T(8,128)(2,1)} %get-tuple-element.135.refs_0_.h_a_ref.h2_ref, ...), custom_call_target="tpu_custom_call" | custom-call | bytes 8400000 | tf_op jit(solution)/shard_map/group_experts/pallas_call | solution.py:614
  176.9 1.4 copy-done.6
  179.4 2.8 collective-permute-done.20
  182.1 2.6 add_convert_fusion.2
  184.7 2.5 all-gather.18.cloned.1.call-done
  187.9 2.2 slice_bitcast_fusion
  190.0 1.5 collective-permute-start.21
  192.1 1.2 pad_add_fusion.pos_ref
  193.2 2.5 collective-permute-done.22.refs_1_.refs_2_
  195.8 12.7 %shared_slice_grads.3 = (f32[256,256]{1,0:T(8,128)}, f32[256,256]{1,0:T(8,128)}, f32[128,768]{1,0:T(8,128)}) custom-call(s32[2]{0:T(128)} %pad_add_fusion.pos_ref, bf16[4,400,768]{2,1,0:T(8,128)(2,1)} %bitcast.33.refs_0_, bf16[4,400,768]{2,1,0:T(8,128)(2,1)} %collective-permute-done.22.refs_1_.refs_2_, bf16[4,400,768]{2,1,0:T(8,128)(2,1)} %bitcast.84, ...), custom_call_target="tpu_custom_call" | custom-call | bytes 8000000 | tf_op jit(solution)/shard_map/shared_slice_grads/pallas_call | solution.py:872
  208.5 5.8 %branch_backward.1 = (f32[384,768]{1,0:T(8,128)}, bf16[384,768]{1,0:T(8,128)(2,1)}, bf16[128,768]{1,0:T(8,128)(2,1)}, bf16[768,768]{1,0:T(8,128)(2,1)}, f32[16,768]{1,0:T(8,128)}, /*index=5*/f32[1,768]{1,0:T(1,128)}) custom-call(bf16[400,768]{1,0:T(8,128)(2,1)} %get-tuple-element.232.dx_a_ref, bf16[400,768]{1,0:T(8,128)(2,1)} %collective-permute-done.21.dx_b_ref, ...), custom_call_target="tpu_custom_call" | custom-call | bytes 2400000 | tf_op jit(solution)/shard_map/branch_backward/pallas_call | solution.py:1135
  214.3 1.4 collective-permute-start.24
  215.7 5.8 %collective-permute-done.24.do_far_ref = bf16[128,768]{1,0:T(8,128)(2,1)S(1)} collective-permute-done((bf16[128,768]{1,0:T(8,128)(2,1)}, bf16[128,768]{1,0:T(8,128)(2,1)S(1)}, u32[]{:S(2)}, u32[]{:S(2)}) %collective-permute-start.24) | collective-permute-done | bytes 196640 | tf_op jit(solution)/shard_map/ppermute | solution.py:453
  221.5 1.4 collective-permute-start.25
  224.3 25.5 %attention_backward.1 = (f32[384,768]{1,0:T(8,128)}, bf16[4,208,1536]{2,1,0:T(8,128)(2,1)}, bf16[4,208,1536]{2,1,0:T(8,128)(2,1)}) custom-call(s32[5]{0:T(128)} %add_convert_fusion.5.flags_ref, bf16[768,768]{1,0:T(8,128)(2,1)} %get-tuple-element.171.q_ref, bf16[768,768]{1,0:T(8,128)(2,1)} %get-tuple-element.172.k_ref, ...), custom_call_target="tpu_custom_call" | custom-call | bytes 9200000 | tf_op jit(solution)/shard_map/attention_backward/pallas_call | solution.py:1332
  249.7 1.9 collective-permute-done.25.refs_0_.refs_1_
  252.2 1.4 collective-permute-start.34
  253.6 6.7 %collective-permute-done.28 = bf16[4,208,1536]{2,1,0:T(8,128)(2,1)} collective-permute-done((bf16[4,208,1536]{2,1,0:T(8,128)(2,1)}, bf16[4,208,1536]{2,1,0:T(8,128)(2,1)}, u32[]{:S(2)}, u32[]{:S(2)}) %collective-permute-start.28) | collective-permute-done | bytes 2555936 | tf_op jit(solution)/shard_map/ppermute | solution.py:453
  260.4 3.2 add_convert_fusion
  263.5 1.6 broadcast_select_fusion
  265.2 1.4 collective-permute-start.29
  267.5 1.4 copy-done.8
  268.9 12.8 %shared_slice_grads.4 = (f32[256,256]{1,0:T(8,128)}, f32[256,256]{1,0:T(8,128)}, f32[128,768]{1,0:T(8,128)}) custom-call(s32[2]{0:T(128)} %pad_add_fusion.pos_ref, bf16[4,400,768]{2,1,0:T(8,128)(2,1)} %collective-permute-done.25.refs_0_.refs_1_, bf16[4,400,768]{2,1,0:T(8,128)(2,1)} %copy-done.8, bf16[4,400,768]{2,1,0:T(8,128)(2,1)} %copy-done.6, ...), custom_call_target="tpu_custom_call" | custom-call | bytes 8000000 | tf_op jit(solution)/shard_map/shared_slice_grads/pallas_call | solution.py:872
  282.7 1.4 collective-permute-start.30
  284.8 2.0 add_convert_fusion.1
  287.7 1.4 collective-permute-start.35
  289.7 30.9 %expert_slice_grads.2 = (f32[4,768,256]{2,1,0:T(8,128)}, f32[4,768,256]{2,1,0:T(8,128)}, f32[4,256,768]{2,1,0:T(8,128)}) custom-call(s32[2]{0:T(128)} %pad_add_fusion.1.pos_ref, bf16[4,400,768]{2,1,0:T(8,128)(2,1)} %bitcast.33.refs_0_, bf16[4,400,768]{2,1,0:T(8,128)(2,1)} %collective-permute-done.25.refs_0_.refs_1_, ...), custom_call_target="tpu_custom_call" | custom-call | bytes 12400000 | tf_op jit(solution)/shard_map/expert_slice_grads/pallas_call | solution.py:800
  320.8 25.3 %collective-permute-done.35 = bf16[4,208,384]{2,1,0:T(8,128)(2,1)} collective-permute-done((bf16[4,208,384]{2,1,0:T(8,128)(2,1)}, bf16[4,208,384]{2,1,0:T(8,128)(2,1)}, u32[]{:S(2)}, u32[]{:S(2)}) %collective-permute-start.35) | collective-permute-done | bytes 639008 | tf_op jit(solution)/shard_map/ppermute | solution.py:453
  346.7 1.2 add_convert_fusion.4
  348.1 1.0 collective-permute-start.40
  349.7 4.1 collective-permute-done.36.refs_6_
  354.7 3.5 collective-permute-done.33.refs_3_
  358.2 20.7 %shared_slice_grads.5 = (f32[256,256]{1,0:T(8,128)}, f32[256,256]{1,0:T(8,128)}, f32[128,768]{1,0:T(8,128)}) custom-call(s32[2]{0:T(128)} %pad_add_fusion.pos_ref, bf16[4,400,768]{2,1,0:T(8,128)(2,1)} %collective-permute-done.30.refs_0_, bf16[4,400,768]{2,1,0:T(8,128)(2,1)} %collective-permute-done.31.refs_1_, ...), custom_call_target="tpu_custom_call" | custom-call | bytes 8000000 | tf_op jit(solution)/shard_map/shared_slice_grads/pallas_call | solution.py:872
  382.9 2.7 collective-permute-done.41
  386.8 1.4 collective-permute-start.42
  389.2 1.5 collective-permute-start.45
  390.7 1.5 collective-permute-start.43
  392.8 31.6 %expert_slice_grads.3 = (f32[4,768,256]{2,1,0:T(8,128)}, f32[4,768,256]{2,1,0:T(8,128)}, f32[4,256,768]{2,1,0:T(8,128)}) custom-call(s32[2]{0:T(128)} %pad_add_fusion.1.pos_ref, bf16[4,400,768]{2,1,0:T(8,128)(2,1)} %collective-permute-done.30.refs_0_, bf16[4,400,768]{2,1,0:T(8,128)(2,1)} %collective-permute-done.31.refs_1_, ...), custom_call_target="tpu_custom_call" | custom-call | bytes 12400000 | tf_op jit(solution)/shard_map/expert_slice_grads/pallas_call | solution.py:800
  425.7 2.1 fusion.2
  427.7 4.2 place_shared.1
  433.4 1.1 fusion.5
  434.6 1.1 fusion.25
  435.6 1.1 fusion.26
  (207 shorter events, 36.2 us)
Async XLA Ops:
  7.2 62.4 %all-gather.14.cloned.1.call-start = ((), (), s32[]{:S(2)}) async-start(), calls=%async_computation.1 | async-start | bytes 1474560 | tf_op jit(solution)/shard_map/all_gather | solution.py:1482
  8.1 11.8 %copy-start.16 = (bf16[192,2048]{1,0:T(8,128)(2,1)S(1)}, bf16[192,2048]{1,0:T(8,128)(2,1)}, u32[]{:S(2)}) copy-start(bf16[192,2048]{1,0:T(8,128)(2,1)} %param.29) | copy-start | bytes 2359300
  9.5 10.9 %copy-start.9 = (bf16[400,768]{1,0:T(8,128)(2,1)}, bf16[400,768]{1,0:T(8,128)(2,1)S(1)}, u32[]{:S(2)}) copy-start(bf16[400,768]{1,0:T(8,128)(2,1)S(1)} %maximum_maximum_fusion.refs_8_.own_ref) | copy-start | bytes 1843204
  9.5 19.2 %collective-permute-start.3 = (bf16[400,768]{1,0:T(8,128)(2,1)S(1)}, bf16[400,768]{1,0:T(8,128)(2,1)}, u32[]{:S(2)}, u32[]{:S(2)}) collective-permute-start(bf16[400,768]{1,0:T(8,128)(2,1)S(1)} %maximum_maximum_fusion.refs_8_.own_ref), channel_id=1, source_target_pairs={{0,4},{1,5},{2,6},{3,7},{4,0},{5,1},{6,2},{7,3},{8,12},{9,13},{10,... | collective-permute-start | bytes 1843208 | tf_op jit(solution)/shard_map/ppermute | solution.py:453
  13.5 14.7 %collective-permute-start.1 = (bf16[208,384]{1,0:T(8,128)(2,1)}, bf16[208,384]{1,0:T(8,128)(2,1)S(1)}, u32[]{:S(2)}, u32[]{:S(2)}) collective-permute-start(bf16[208,384]{1,0:T(8,128)(2,1)} %maximum_maximum_fusion.2), channel_id=1, source_target_pairs={{0,16},{1,17},{2,18},{3,19},{4,20},{5,21},{6,22},{7,23},{8,24},{9,... | collective-permute-start | bytes 479240 | tf_op jit(solution)/shard_map/ppermute | solution.py:453
  16.1 12.1 %collective-permute-start = (bf16[208,384]{1,0:T(8,128)(2,1)}, bf16[208,384]{1,0:T(8,128)(2,1)S(1)}, u32[]{:S(2)}, u32[]{:S(2)}) collective-permute-start(bf16[208,384]{1,0:T(8,128)(2,1)} %maximum_maximum_fusion.2), channel_id=1, source_target_pairs={{0,8},{1,9},{2,10},{3,11},{4,12},{5,13},{6,14},{7,15},{8,16},{9,17... | collective-permute-start | bytes 479240 | tf_op jit(solution)/shard_map/ppermute | solution.py:453
  17.6 11.1 %collective-permute-start.2 = (bf16[208,384]{1,0:T(8,128)(2,1)}, bf16[208,384]{1,0:T(8,128)(2,1)}, u32[]{:S(2)}, u32[]{:S(2)}) collective-permute-start(bf16[208,384]{1,0:T(8,128)(2,1)} %maximum_maximum_fusion.2), channel_id=1, source_target_pairs={{0,24},{1,25},{2,26},{3,27},{4,28},{5,29},{6,30},{7,31},{8,0},{9,1... | collective-permute-start | bytes 479240 | tf_op jit(solution)/shard_map/ppermute | solution.py:453
  23.3 9.1 %copy-start.25 = (s32[384,2]{0,1:T(2,128)S(1)}, s32[384,2]{0,1:T(2,128)}, u32[]{:S(2)}) copy-start(s32[384,2]{0,1:T(2,128)} %param.20) | copy-start | bytes 9220
  29.8 15.8 %copy-start.12 = (bf16[4,208,384]{2,1,0:T(8,128)(2,1)}, bf16[4,208,384]{2,1,0:T(8,128)(2,1)S(1)}, u32[]{:S(2)}) copy-start(bf16[4,208,384]{2,1,0:T(8,128)(2,1)S(1)} %pad_maximum_fusion.refs_0_) | copy-start | bytes 1916932
  30.7 11.5 %copy-start.26 = (s32[2]{0:T(128)S(1)}, s32[2]{0:T(128)}, u32[]{:S(2)}) copy-start(s32[2]{0:T(128)} %param.21) | copy-start | bytes 28
  30.7 103.2 %all-gather.16.cloned.1.call-start = ((), (), s32[]{:S(2)}) async-start(), calls=%async_computation.2 | async-start | bytes 3072000 | tf_op jit(solution)/shard_map/all_gather | solution.py:1485
  30.8 10.6 %collective-permute-start.4 = (bf16[4,208,384]{2,1,0:T(8,128)(2,1)S(1)}, bf16[4,208,384]{2,1,0:T(8,128)(2,1)}, u32[]{:S(2)}, u32[]{:S(2)}) collective-permute-start(bf16[4,208,384]{2,1,0:T(8,128)(2,1)S(1)} %pad_maximum_fusion.refs_0_), channel_id=1, source_target_pairs={{0,2},{1,5},{2,0},{3,7},{4,6},{5,1},{6,4},{7,3},{8,10},{9,13},{10,... | collective-permute-start | bytes 1916936 | tf_op jit(solution)/shard_map/ppermute | solution.py:453
  33.4 30.3 %copy-start.1 = (bf16[400,768]{1,0:T(8,128)(2,1)S(1)}, bf16[400,768]{1,0:T(8,128)(2,1)}, u32[]{:S(2)}) copy-start(bf16[400,768]{1,0:T(8,128)(2,1)} %fusion.4.refs_4_.g_a_ref) | copy-start | bytes 1843204
  41.4 145.9 %all-gather.18.cloned.1.call-start = ((), (), s32[]{:S(2)}) async-start(), calls=%async_computation.3 | async-start | bytes 3072000 | tf_op jit(solution)/shard_map/all_gather | solution.py:1514
  41.7 10.6 %collective-permute-start.5 = (bf16[4,208,384]{2,1,0:T(8,128)(2,1)S(1)}, bf16[4,208,384]{2,1,0:T(8,128)(2,1)}, u32[]{:S(2)}, u32[]{:S(2)}) collective-permute-start(bf16[4,208,384]{2,1,0:T(8,128)(2,1)S(1)} %pad_maximum_fusion.refs_0_), channel_id=1, source_target_pairs={{0,4},{1,3},{2,6},{3,1},{4,0},{5,7},{6,2},{7,5},{8,12},{9,11},{10,... | collective-permute-start | bytes 1916936 | tf_op jit(solution)/shard_map/ppermute | solution.py:453
  45.6 21.0 %collective-permute-start.7 = (bf16[4,208,384]{2,1,0:T(8,128)(2,1)S(1)}, bf16[4,208,384]{2,1,0:T(8,128)(2,1)S(1)}, u32[]{:S(2)}, u32[]{:S(2)}) collective-permute-start(bf16[4,208,384]{2,1,0:T(8,128)(2,1)S(1)} %pad_maximum_fusion.refs_0_), channel_id=1, source_target_pairs={{0,1},{1,0},{2,3},{3,2},{4,5},{5,4},{6,7},{7,6},{8,9},{9,8},{10,11... | collective-permute-start | bytes 1916936 | tf_op jit(solution)/shard_map/ppermute | solution.py:453
  52.3 11.4 %collective-permute-start.6 = (bf16[4,208,384]{2,1,0:T(8,128)(2,1)}, bf16[4,208,384]{2,1,0:T(8,128)(2,1)}, u32[]{:S(2)}, u32[]{:S(2)}) collective-permute-start(bf16[4,208,384]{2,1,0:T(8,128)(2,1)} %collective-permute-done.4.refs_1_), channel_id=1, source_target_pairs={{0,4},{1,3},{2,6},{3,1},{4,0},{5,7},{6,2},{7,5},{8,12},{9,11},{10,... | collective-permute-start | bytes 1916936 | tf_op jit(solution)/shard_map/ppermute | solution.py:453
  52.8 17.6 %collective-permute-start.9 = (bf16[4,208,384]{2,1,0:T(8,128)(2,1)}, bf16[4,208,384]{2,1,0:T(8,128)(2,1)}, u32[]{:S(2)}, u32[]{:S(2)}) collective-permute-start(bf16[4,208,384]{2,1,0:T(8,128)(2,1)} %collective-permute-done.5.refs_2_), channel_id=1, source_target_pairs={{0,1},{1,0},{2,3},{3,2},{4,5},{5,4},{6,7},{7,6},{8,9},{9,8},{10,11... | collective-permute-start | bytes 1916936 | tf_op jit(solution)/shard_map/ppermute | solution.py:453
  52.9 17.6 %collective-permute-start.8 = (bf16[4,208,384]{2,1,0:T(8,128)(2,1)}, bf16[4,208,384]{2,1,0:T(8,128)(2,1)}, u32[]{:S(2)}, u32[]{:S(2)}) collective-permute-start(bf16[4,208,384]{2,1,0:T(8,128)(2,1)} %collective-permute-done.4.refs_1_), channel_id=1, source_target_pairs={{0,1},{1,0},{2,3},{3,2},{4,5},{5,4},{6,7},{7,6},{8,9},{9,8},{10,11... | collective-permute-start | bytes 1916936 | tf_op jit(solution)/shard_map/ppermute | solution.py:453
  63.7 27.7 %collective-permute-start.12 = (bf16[400,768]{1,0:T(8,128)(2,1)S(1)}, bf16[400,768]{1,0:T(8,128)(2,1)S(1)}, u32[]{:S(2)}, u32[]{:S(2)}) collective-permute-start(bf16[400,768]{1,0:T(8,128)(2,1)S(1)} %copy-done.1), channel_id=1, source_target_pairs={{0,4},{1,3},{2,6},{3,1},{4,0},{5,7},{6,2},{7,5},{8,12},{9,11},{10,... | collective-permute-start | bytes 1843208 | tf_op jit(solution)/shard_map/ppermute | solution.py:453
  64.1 27.4 %collective-permute-start.11 = (bf16[400,768]{1,0:T(8,128)(2,1)S(1)}, bf16[400,768]{1,0:T(8,128)(2,1)}, u32[]{:S(2)}, u32[]{:S(2)}) collective-permute-start(bf16[400,768]{1,0:T(8,128)(2,1)S(1)} %copy-done.1), channel_id=1, source_target_pairs={{0,2},{1,5},{2,0},{3,7},{4,6},{5,1},{6,4},{7,3},{8,10},{9,13},{10,... | collective-permute-start | bytes 1843208 | tf_op jit(solution)/shard_map/ppermute | solution.py:453
  66.6 3.8 collective-permute-start.10
  70.4 21.5 %copy-start = (bf16[768,768]{1,0:T(8,128)(2,1)S(1)}, bf16[768,768]{1,0:T(8,128)(2,1)}, u32[]{:S(2)}) copy-start(bf16[768,768]{1,0:T(8,128)(2,1)} %all-gather.14.cloned.1.call-done) | copy-start | bytes 3538948
  91.4 16.6 %collective-permute-start.13 = (bf16[400,768]{1,0:T(8,128)(2,1)}, bf16[400,768]{1,0:T(8,128)(2,1)}, u32[]{:S(2)}, u32[]{:S(2)}) collective-permute-start(bf16[400,768]{1,0:T(8,128)(2,1)} %get-tuple-element.135.refs_0_.h_a_ref.h2_ref), channel_id=1, source_target_pairs={{0,2},{1,3},{2,0},{3,1},{4,6},{5,7},{6,4},{7,5},{8,10},{9,11},{10,... | collective-permute-start | bytes 1843208 | tf_op jit(solution)/shard_map/ppermute | solution.py:453
  91.9 42.0 %collective-permute-start.18 = (bf16[4,192,768]{2,1,0:T(8,128)(2,1)S(1)}, bf16[4,192,768]{2,1,0:T(8,128)(2,1)}, u32[]{:S(2)}, u32[]{:S(2)}) collective-permute-start(bf16[4,192,768]{2,1,0:T(8,128)(2,1)S(1)} %bitcast.76), channel_id=1, source_target_pairs={{0,4},{1,5},{2,6},{3,7},{4,0},{5,1},{6,2},{7,3},{8,12},{9,13},{10,... | collective-permute-start | bytes 3538952 | tf_op jit(solution)/shard_map/ppermute | solution.py:453
  93.5 14.6 %collective-permute-start.16 = (bf16[400,768]{1,0:T(8,128)(2,1)S(1)}, bf16[400,768]{1,0:T(8,128)(2,1)}, u32[]{:S(2)}, u32[]{:S(2)}) collective-permute-start(bf16[400,768]{1,0:T(8,128)(2,1)S(1)} %copy-done.1), channel_id=1, source_target_pairs={{0,1},{1,0},{2,3},{3,2},{4,5},{5,4},{6,7},{7,6},{8,9},{9,8},{10,11... | collective-permute-start | bytes 1843208 | tf_op jit(solution)/shard_map/ppermute | solution.py:453
  94.6 15.8 %copy-start.3 = (bf16[400,768]{1,0:T(8,128)(2,1)}, bf16[400,768]{1,0:T(8,128)(2,1)S(1)}, u32[]{:S(2)}) copy-start(bf16[400,768]{1,0:T(8,128)(2,1)S(1)} %broadcast_select_fusion.5.refs_5_.g_a_ref) | copy-start | bytes 1843204
  94.6 13.5 %collective-permute-start.17 = (bf16[400,768]{1,0:T(8,128)(2,1)S(1)}, bf16[400,768]{1,0:T(8,128)(2,1)}, u32[]{:S(2)}, u32[]{:S(2)}) collective-permute-start(bf16[400,768]{1,0:T(8,128)(2,1)S(1)} %broadcast_select_fusion.5.refs_5_.g_a_ref), channel_id=1, source_target_pairs={{0,1},{1,0},{2,3},{3,2},{4,5},{5,4},{6,7},{7,6},{8,9},{9,8},{10,11... | collective-permute-start | bytes 1843208 | tf_op jit(solution)/shard_map/ppermute | solution.py:453
  95.2 12.9 %collective-permute-start.14 = (bf16[400,768]{1,0:T(8,128)(2,1)S(1)}, bf16[400,768]{1,0:T(8,128)(2,1)}, u32[]{:S(2)}, u32[]{:S(2)}) collective-permute-start(bf16[400,768]{1,0:T(8,128)(2,1)S(1)} %copy-done.2), channel_id=1, source_target_pairs={{0,1},{1,0},{2,3},{3,2},{4,5},{5,4},{6,7},{7,6},{8,9},{9,8},{10,11... | collective-permute-start | bytes 1843208 | tf_op jit(solution)/shard_map/ppermute | solution.py:453
  108.1 2.4 collective-permute-start.15
  134.0 43.0 %collective-permute-start.19 = (bf16[4,400,768]{2,1,0:T(8,128)(2,1)}, bf16[4,400,768]{2,1,0:T(8,128)(2,1)S(1)}, u32[]{:S(2)}, u32[]{:S(2)}) collective-permute-start(bf16[4,400,768]{2,1,0:T(8,128)(2,1)} %bitcast.83), channel_id=1, source_target_pairs={{0,2},{1,5},{2,0},{3,7},{4,6},{5,1},{6,4},{7,3},{8,10},{9,13},{10,... | collective-permute-start | bytes 7372808 | tf_op jit(solution)/shard_map/ppermute | solution.py:453
  134.4 115.4 %all-gather.20.cloned.1.call-start = ((), (), s32[]{:S(2)}) async-start(), calls=%async_computation.4 | async-start | bytes 3072000 | tf_op jit(solution)/shard_map/all_gather | solution.py:1526
  178.4 3.8 collective-permute-start.20
  187.3 8.5 %collective-permute-start.22 = (bf16[4,400,768]{2,1,0:T(8,128)(2,1)}, bf16[4,400,768]{2,1,0:T(8,128)(2,1)}, u32[]{:S(2)}, u32[]{:S(2)}) collective-permute-start(bf16[4,400,768]{2,1,0:T(8,128)(2,1)} %bitcast.33.refs_0_), channel_id=1, source_target_pairs={{0,1},{1,0},{2,3},{3,2},{4,5},{5,4},{6,7},{7,6},{8,9},{9,8},{10,11... | collective-permute-start | bytes 7372808 | tf_op jit(solution)/shard_map/ppermute | solution.py:453
  187.3 8.5 %collective-permute-start.23 = (bf16[4,400,768]{2,1,0:T(8,128)(2,1)S(1)}, bf16[4,400,768]{2,1,0:T(8,128)(2,1)}, u32[]{:S(2)}, u32[]{:S(2)}) collective-permute-start(bf16[4,400,768]{2,1,0:T(8,128)(2,1)S(1)} %bitcast.86), channel_id=1, source_target_pairs={{0,1},{1,0},{2,3},{3,2},{4,5},{5,4},{6,7},{7,6},{8,9},{9,8},{10,11... | collective-permute-start | bytes 7372808 | tf_op jit(solution)/shard_map/ppermute | solution.py:453
  187.8 133.0 %all-gather.22.cloned.1.call-start = ((), (), s32[]{:S(2)}) async-start(), calls=%async_computation.5 | async-start | bytes 3072000 | tf_op jit(solution)/shard_map/all_gather | solution.py:1568
  190.0 18.4 %collective-permute-start.21 = (bf16[400,768]{1,0:T(8,128)(2,1)S(1)}, bf16[400,768]{1,0:T(8,128)(2,1)}, u32[]{:S(2)}, u32[]{:S(2)}) collective-permute-start(bf16[400,768]{1,0:T(8,128)(2,1)S(1)} %get-tuple-element.231), channel_id=1, source_target_pairs={{0,2},{1,3},{2,0},{3,1},{4,6},{5,7},{6,4},{7,5},{8,10},{9,11},{10,... | collective-permute-start | bytes 1843208 | tf_op jit(solution)/shard_map/ppermute | solution.py:453
  208.5 14.4 %copy-start.7 = (bf16[4,400,768]{2,1,0:T(8,128)(2,1)S(1)}, bf16[4,400,768]{2,1,0:T(8,128)(2,1)}, u32[]{:S(2)}) copy-start(bf16[4,400,768]{2,1,0:T(8,128)(2,1)} %copy-done.6) | copy-start | bytes 7372804
  214.3 7.2 %collective-permute-start.24 = (bf16[128,768]{1,0:T(8,128)(2,1)}, bf16[128,768]{1,0:T(8,128)(2,1)S(1)}, u32[]{:S(2)}, u32[]{:S(2)}) collective-permute-start(bf16[128,768]{1,0:T(8,128)(2,1)} %get-tuple-element.165), channel_id=1, source_target_pairs={{0,4},{1,5},{2,6},{3,7},{4,0},{5,1},{6,2},{7,3},{8,12},{9,13},{10,... | collective-permute-start | bytes 589832 | tf_op jit(solution)/shard_map/ppermute | solution.py:453
  221.5 30.2 %collective-permute-start.25 = (bf16[4,400,768]{2,1,0:T(8,128)(2,1)}, bf16[4,400,768]{2,1,0:T(8,128)(2,1)}, u32[]{:S(2)}, u32[]{:S(2)}) collective-permute-start(bf16[4,400,768]{2,1,0:T(8,128)(2,1)} %bitcast.33.refs_0_), channel_id=1, source_target_pairs={{0,2},{1,5},{2,0},{3,7},{4,6},{5,1},{6,4},{7,3},{8,10},{9,13},{10,... | collective-permute-start | bytes 7372808 | tf_op jit(solution)/shard_map/ppermute | solution.py:453
  222.9 28.8 %collective-permute-start.27 = (bf16[4,400,768]{2,1,0:T(8,128)(2,1)S(1)}, bf16[4,400,768]{2,1,0:T(8,128)(2,1)}, u32[]{:S(2)}, u32[]{:S(2)}) collective-permute-start(bf16[4,400,768]{2,1,0:T(8,128)(2,1)S(1)} %copy-done.7), channel_id=1, source_target_pairs={{0,1},{1,0},{2,3},{3,2},{4,5},{5,4},{6,7},{7,6},{8,9},{9,8},{10,11... | collective-permute-start | bytes 7372808 | tf_op jit(solution)/shard_map/ppermute | solution.py:453
  251.7 8.7 %collective-permute-start.28 = (bf16[4,208,1536]{2,1,0:T(8,128)(2,1)}, bf16[4,208,1536]{2,1,0:T(8,128)(2,1)}, u32[]{:S(2)}, u32[]{:S(2)}) collective-permute-start(bf16[4,208,1536]{2,1,0:T(8,128)(2,1)} %get-tuple-element.185), channel_id=1, source_target_pairs={{0,1},{1,0},{2,3},{3,2},{4,5},{5,4},{6,7},{7,6},{8,9},{9,8},{10,11... | collective-permute-start | bytes 7667720 | tf_op jit(solution)/shard_map/ppermute | solution.py:453
  251.7 15.8 %collective-permute-start.26 = (bf16[4,400,768]{2,1,0:T(8,128)(2,1)}, bf16[4,400,768]{2,1,0:T(8,128)(2,1)S(1)}, u32[]{:S(2)}, u32[]{:S(2)}) collective-permute-start(bf16[4,400,768]{2,1,0:T(8,128)(2,1)} %collective-permute-done.25.refs_0_.refs_1_), channel_id=1, source_target_pairs={{0,1},{1,0},{2,3},{3,2},{4,5},{5,4},{6,7},{7,6},{8,9},{9,8},{10,11... | collective-permute-start | bytes 7372808 | tf_op jit(solution)/shard_map/ppermute | solution.py:453
  252.2 14.4 %collective-permute-start.34 = (bf16[400,768]{1,0:T(8,128)(2,1)}, bf16[400,768]{1,0:T(8,128)(2,1)S(1)}, u32[]{:S(2)}, u32[]{:S(2)}) collective-permute-start(bf16[400,768]{1,0:T(8,128)(2,1)} %collective-permute-done.11), channel_id=1, source_target_pairs={{0,4},{1,3},{2,6},{3,1},{4,0},{5,7},{6,2},{7,5},{8,12},{9,11},{10,... | collective-permute-start | bytes 1843208 | tf_op jit(solution)/shard_map/ppermute | solution.py:453
  265.2 17.6 %collective-permute-start.29 = (bf16[4,208,768]{2,1,0:T(8,128)(2,1)}, bf16[4,208,768]{2,1,0:T(8,128)(2,1)}, u32[]{:S(2)}, u32[]{:S(2)}) collective-permute-start(bf16[4,208,768]{2,1,0:T(8,128)(2,1)} %get-tuple-element.227), channel_id=1, source_target_pairs={{0,2},{1,5},{2,0},{3,7},{4,6},{5,1},{6,4},{7,3},{8,10},{9,13},{10,... | collective-permute-start | bytes 3833864 | tf_op jit(solution)/shard_map/ppermute | solution.py:453
  267.4 157.2 %all-gather.12.cloned.1.call-start = ((), (), s32[]{:S(2)}) async-start(), calls=%async_computation | async-start | bytes 2654208 | tf_op jit(solution)/shard_map/all_gather | solution.py:1614
  282.7 37.9 %collective-permute-start.30 = (bf16[4,400,768]{2,1,0:T(8,128)(2,1)}, bf16[4,400,768]{2,1,0:T(8,128)(2,1)}, u32[]{:S(2)}, u32[]{:S(2)}) collective-permute-start(bf16[4,400,768]{2,1,0:T(8,128)(2,1)} %bitcast.33.refs_0_), channel_id=1, source_target_pairs={{0,4},{1,3},{2,6},{3,1},{4,0},{5,7},{6,2},{7,5},{8,12},{9,11},{10,... | collective-permute-start | bytes 7372808 | tf_op jit(solution)/shard_map/ppermute | solution.py:453
  284.2 62.0 %collective-permute-start.31 = (bf16[4,400,768]{2,1,0:T(8,128)(2,1)}, bf16[4,400,768]{2,1,0:T(8,128)(2,1)}, u32[]{:S(2)}, u32[]{:S(2)}) collective-permute-start(bf16[4,400,768]{2,1,0:T(8,128)(2,1)} %collective-permute-done.25.refs_0_.refs_1_), channel_id=1, source_target_pairs={{0,4},{1,3},{2,6},{3,1},{4,0},{5,7},{6,2},{7,5},{8,12},{9,11},{10,... | collective-permute-start | bytes 7372808 | tf_op jit(solution)/shard_map/ppermute | solution.py:453
  287.7 58.4 %collective-permute-start.35 = (bf16[4,208,384]{2,1,0:T(8,128)(2,1)}, bf16[4,208,384]{2,1,0:T(8,128)(2,1)}, u32[]{:S(2)}, u32[]{:S(2)}) collective-permute-start(bf16[4,208,384]{2,1,0:T(8,128)(2,1)} %get-tuple-element.229), channel_id=1, source_target_pairs={{0,4},{1,3},{2,6},{3,1},{4,0},{5,7},{6,2},{7,5},{8,12},{9,11},{10,... | collective-permute-start | bytes 1916936 | tf_op jit(solution)/shard_map/ppermute | solution.py:453
  289.7 56.4 %copy-start.4 = (bf16[1600,768]{1,0:T(8,128)(2,1)S(1)}, bf16[1600,768]{1,0:T(8,128)(2,1)}, u32[]{:S(2)}) copy-start(bf16[1600,768]{1,0:T(8,128)(2,1)} %all-gather.20.cloned.1.call-done) | copy-start | bytes 7372804
  320.7 28.4 %collective-permute-start.32 = (bf16[4,400,768]{2,1,0:T(8,128)(2,1)}, bf16[4,400,768]{2,1,0:T(8,128)(2,1)}, u32[]{:S(2)}, u32[]{:S(2)}) collective-permute-start(bf16[4,400,768]{2,1,0:T(8,128)(2,1)} %collective-permute-done.30.refs_0_), channel_id=1, source_target_pairs={{0,1},{1,0},{2,3},{3,2},{4,5},{5,4},{6,7},{7,6},{8,9},{9,8},{10,11... | collective-permute-start | bytes 7372808 | tf_op jit(solution)/shard_map/ppermute | solution.py:453
  346.1 7.6 %collective-permute-start.36 = (bf16[4,400,768]{2,1,0:T(8,128)(2,1)S(1)}, bf16[4,400,768]{2,1,0:T(8,128)(2,1)}, u32[]{:S(2)}, u32[]{:S(2)}) collective-permute-start(bf16[4,400,768]{2,1,0:T(8,128)(2,1)S(1)} %bitcast.79), channel_id=1, source_target_pairs={{0,1},{1,0},{2,3},{3,2},{4,5},{5,4},{6,7},{7,6},{8,9},{9,8},{10,11... | collective-permute-start | bytes 7372808 | tf_op jit(solution)/shard_map/ppermute | solution.py:453
  346.1 8.6 %collective-permute-start.37 = (bf16[4,400,768]{2,1,0:T(8,128)(2,1)}, bf16[4,400,768]{2,1,0:T(8,128)(2,1)}, u32[]{:S(2)}, u32[]{:S(2)}) collective-permute-start(bf16[4,400,768]{2,1,0:T(8,128)(2,1)} %bitcast.80), channel_id=1, source_target_pairs={{0,1},{1,0},{2,3},{3,2},{4,5},{5,4},{6,7},{7,6},{8,9},{9,8},{10,11... | collective-permute-start | bytes 7372808 | tf_op jit(solution)/shard_map/ppermute | solution.py:453
  346.7 11.5 %collective-permute-start.33 = (bf16[4,400,768]{2,1,0:T(8,128)(2,1)}, bf16[4,400,768]{2,1,0:T(8,128)(2,1)}, u32[]{:S(2)}, u32[]{:S(2)}) collective-permute-start(bf16[4,400,768]{2,1,0:T(8,128)(2,1)} %collective-permute-done.31.refs_1_), channel_id=1, source_target_pairs={{0,1},{1,0},{2,3},{3,2},{4,5},{5,4},{6,7},{7,6},{8,9},{9,8},{10,11... | collective-permute-start | bytes 7372808 | tf_op jit(solution)/shard_map/ppermute | solution.py:453
  348.1 30.9 %collective-permute-start.40 = (bf16[208,384]{1,0:T(8,128)(2,1)S(1)}, bf16[208,384]{1,0:T(8,128)(2,1)S(1)}, u32[]{:S(2)}, u32[]{:S(2)}) collective-permute-start(bf16[208,384]{1,0:T(8,128)(2,1)S(1)} %get-tuple-element.240), channel_id=1, source_target_pairs={{0,24},{1,25},{2,26},{3,27},{4,28},{5,29},{6,30},{7,31},{8,0},{9,1... | collective-permute-start | bytes 479240 | tf_op jit(solution)/shard_map/ppermute | solution.py:453
  349.1 29.8 %collective-permute-start.39 = (bf16[208,384]{1,0:T(8,128)(2,1)S(1)}, bf16[208,384]{1,0:T(8,128)(2,1)S(1)}, u32[]{:S(2)}, u32[]{:S(2)}) collective-permute-start(bf16[208,384]{1,0:T(8,128)(2,1)S(1)} %get-tuple-element.241), channel_id=1, source_target_pairs={{0,16},{1,17},{2,18},{3,19},{4,20},{5,21},{6,22},{7,23},{8,24},{9,... | collective-permute-start | bytes 479240 | tf_op jit(solution)/shard_map/ppermute | solution.py:453
  353.7 25.2 %collective-permute-start.38 = (bf16[208,384]{1,0:T(8,128)(2,1)S(1)}, bf16[208,384]{1,0:T(8,128)(2,1)S(1)}, u32[]{:S(2)}, u32[]{:S(2)}) collective-permute-start(bf16[208,384]{1,0:T(8,128)(2,1)S(1)} %get-tuple-element.242), channel_id=1, source_target_pairs={{0,8},{1,9},{2,10},{3,11},{4,12},{5,13},{6,14},{7,15},{8,16},{9,17... | collective-permute-start | bytes 479240 | tf_op jit(solution)/shard_map/ppermute | solution.py:453
  358.2 24.5 %copy-start.27 = (bf16[2,384,768]{2,1,0:T(8,128)(2,1)S(1)}, bf16[2,384,768]{2,1,0:T(8,128)(2,1)}, u32[]{:S(2)}) copy-start(bf16[2,384,768]{2,1,0:T(8,128)(2,1)} %get-tuple-element.207) | copy-start | bytes 3538948
  382.7 2.9 collective-permute-start.41
  386.8 37.8 %collective-permute-start.42 = (bf16[384,768]{1,0:T(8,128)(2,1)}, bf16[384,768]{1,0:T(8,128)(2,1)}, u32[]{:S(2)}, u32[]{:S(2)}) collective-permute-start(bf16[384,768]{1,0:T(8,128)(2,1)} %slice_bitcast_fusion.2), channel_id=1, source_target_pairs={{0,2},{1,3},{2,0},{3,1},{4,6},{5,7},{6,4},{7,5},{8,10},{9,11},{10,... | collective-permute-start | bytes 1769480 | tf_op jit(solution)/shard_map/ppermute | solution.py:453
  389.2 35.2 %collective-permute-start.45 = (bf16[208,384]{1,0:T(8,128)(2,1)S(1)}, bf16[208,384]{1,0:T(8,128)(2,1)S(1)}, u32[]{:S(2)}, u32[]{:S(2)}) collective-permute-start(bf16[208,384]{1,0:T(8,128)(2,1)S(1)} %fusion.8), channel_id=1, source_target_pairs={{0,6},{1,7},{2,4},{3,5},{4,2},{5,3},{6,0},{7,1},{8,14},{9,15},{10,... | collective-permute-start | bytes 479240 | tf_op jit(solution)/shard_map/ppermute | solution.py:453
  390.7 33.7 %collective-permute-start.43 = (bf16[208,384]{1,0:T(8,128)(2,1)S(1)}, bf16[208,384]{1,0:T(8,128)(2,1)S(1)}, u32[]{:S(2)}, u32[]{:S(2)}) collective-permute-start(bf16[208,384]{1,0:T(8,128)(2,1)S(1)} %fusion.8), channel_id=1, source_target_pairs={{0,2},{1,5},{2,0},{3,7},{4,6},{5,1},{6,4},{7,3},{8,10},{9,13},{10,... | collective-permute-start | bytes 479240 | tf_op jit(solution)/shard_map/ppermute | solution.py:453
  392.2 32.3 %collective-permute-start.44 = (bf16[208,384]{1,0:T(8,128)(2,1)S(1)}, bf16[208,384]{1,0:T(8,128)(2,1)S(1)}, u32[]{:S(2)}, u32[]{:S(2)}) collective-permute-start(bf16[208,384]{1,0:T(8,128)(2,1)S(1)} %fusion.8), channel_id=1, source_target_pairs={{0,4},{1,3},{2,6},{3,1},{4,0},{5,7},{6,2},{7,5},{8,12},{9,11},{10,... | collective-permute-start | bytes 479240 | tf_op jit(solution)/shard_map/ppermute | solution.py:453
  424.9 7.1 %collective-permute-start.46 = (bf16[208,1536]{1,0:T(8,128)(2,1)S(1)}, bf16[208,1536]{1,0:T(8,128)(2,1)}, u32[]{:S(2)}, u32[]{:S(2)}) collective-permute-start(bf16[208,1536]{1,0:T(8,128)(2,1)S(1)} %maximum_select_fusion), channel_id=1, source_target_pairs={{0,1},{1,0},{2,3},{3,2},{4,5},{5,4},{6,7},{7,6},{8,9},{9,8},{10,11... | collective-permute-start | bytes 1916936 | tf_op jit(solution)/shard_map/ppermute | solution.py:453
  (20 other events, 80.6 us)
Sparse Core Ops, SparseCore 0:
  30.9 31.4 all-gather.13
  63.9 51.2 all-gather.15
  134.5 52.7 all-gather.17
  188.7 50.8 all-gather.19
  267.6 50.3 all-gather.21
  382.8 37.1 all-gather.11

commit v4 on v3

--- a/solution.py
+++ b/solution.py
@@ -2,6 +2,7 @@
 
 import jax
 import jax.numpy as jnp
+import numpy as np
 from jax import lax
 from jax.sharding import PartitionSpec as P
 
@@ -498,7 +499,8 @@
     h_refs, g_refs = refs[:blocks], refs[blocks : 2 * blocks]
     refs = refs[2 * blocks :]
     more_refs, refs = refs[:more], refs[more:]
-    wg_ref, wu_ref, wd_ref, moe_ref, moe_far_ref, dx_ref, dx_far_ref = refs[:7]
+    wg_ref, wu_ref, wd_ref = refs[:3]
+    moe_refs, dx_refs, refs = refs[3 : 3 + blocks], refs[3 + blocks : 3 + 2 * blocks], refs[3 + 2 * blocks :]
     (
         rank_sc,
         prob_sc,
@@ -511,14 +513,14 @@
         ysel_sc,
         dsel_sc,
         drp_sc,
-    ) = refs[7:18]
+    ) = refs[:11]
     e = pl.program_id(0)
     f = pl.program_id(1)
     experts = pl.num_programs(0)
     base = base_ref[0]
     copies = [
         pltpu.make_async_copy(source, into, refs[-1].at[i])
-        for i, (source, into) in enumerate(zip(more_refs, refs[18:]))
+        for i, (source, into) in enumerate(zip(more_refs, refs[11:]))
     ]
 
     @pl.when((e == 0) & (f == 0))
@@ -580,7 +582,7 @@
             one.wait()
         for b in range(blocks):
             side, at = divmod(b, blocks // 2)
-            moe_out, dx_out = ((moe_ref, dx_ref), (moe_far_ref, dx_far_ref))[side]
+            moe_out, dx_out = moe_refs[b], dx_refs[b]
             hot = jnp.concatenate(
                 [
                     one_hot_rows(rank_sc[b, pl.ds(base + i, 1), :])
@@ -592,17 +594,17 @@
             dx = contract(hot, dsel_sc[b].astype(BF), 0, 0)
             drp = drp_sc[b]
             if more:
-                shared = refs[18 + 2 * at : 20 + 2 * at]
-                before = refs[22 + side], refs[24 + side]
-                moe = moe + shared[0][side] + before[0][at].astype(F32)
-                dx = dx + shared[1][side] + before[1][at, :TOK_DEV, :].astype(F32)
-                drp = drp + before[1][at, TOK_DEV:, :TOK_DEV].astype(F32)
-                drp = drp + before[1][at, TOK_DEV:, TOK_DEV:].astype(F32)
-            moe_out[at] = moe.astype(BF)
-            dx_out[at, :TOK_DEV, :] = dx.astype(BF)
+                shared = refs[11 + 2 * at : 13 + 2 * at]
+                moe_before, dx_before = refs[15 + b], refs[15 + blocks + b]
+                moe = moe + shared[0][side] + moe_before[...].astype(F32)
+                dx = dx + shared[1][side] + dx_before[:TOK_DEV, :].astype(F32)
+                drp = drp + dx_before[TOK_DEV:, :TOK_DEV].astype(F32)
+                drp = drp + dx_before[TOK_DEV:, TOK_DEV:].astype(F32)
+            moe_out[...] = moe.astype(BF)
+            dx_out[:TOK_DEV, :] = dx.astype(BF)
             high = drp.astype(BF)
-            dx_out[at, TOK_DEV:, :TOK_DEV] = high
-            dx_out[at, TOK_DEV:, TOK_DEV:] = (drp - high.astype(F32)).astype(BF)
+            dx_out[TOK_DEV:, :TOK_DEV] = high
+            dx_out[TOK_DEV:, TOK_DEV:] = (drp - high.astype(F32)).astype(BF)
 
 
 def group_experts(base, first, experts, h_group, g_group, more, w_gate, w_up, w_down):
@@ -610,12 +612,10 @@
     ff = w_gate.shape[2]
     tile = 512
     whole = lambda *shape: pl.BlockSpec(shape, lambda e, f, s: (0,) * len(shape))
-    moe_shape, dx_shape = (blocks // 2, TOK_DEV, D), (blocks // 2, ROWS, D)
+    results = [(TOK_DEV, D)] * blocks + [(ROWS, D)] * blocks
     return pl.pallas_call(
         functools.partial(group_kernel, blocks, len(more)),
-        out_shape=tuple(
-            jax.ShapeDtypeStruct(s, BF) for s in (moe_shape, moe_shape, dx_shape, dx_shape)
-        ),
+        out_shape=tuple(jax.ShapeDtypeStruct(s, BF) for s in results),
         grid_spec=pltpu.PrefetchScalarGridSpec(
             num_scalar_prefetch=1,
             grid=(experts, ff // tile),
@@ -626,7 +626,7 @@
                 pl.BlockSpec((1, D, tile), lambda e, f, s: (first + e, 0, f)),
                 pl.BlockSpec((1, tile, D), lambda e, f, s: (first + e, f, 0)),
             ],
-            out_specs=[whole(*moe_shape)] * 2 + [whole(*dx_shape)] * 2,
+            out_specs=[whole(*s) for s in results],
             scratch_shapes=[
                 pltpu.VMEM((blocks, EXPERTS, TOK_DEV), F32),
                 pltpu.VMEM((blocks, EXPERTS, TOK_DEV), F32),
@@ -953,6 +953,7 @@
 def attention_kernel(place_ref, *refs):
     w_parts = refs[:8]
     (
+        h1_ref,
         own_ref,
         far_ref,
         gain1_ref,
@@ -964,7 +965,6 @@
         q_ref,
         k_ref,
         v_ref,
-        h1_ref,
         o_ref,
         x1_ref,
         h2_ref,
@@ -984,11 +984,9 @@
             )
     for one in copies:
         one.start()
-    inputs = own_ref[:TOK_DEV, :].astype(F32)
-    h_sc[:TOK_DEV, :] = (inputs * unit_rms(inputs) * gain1_ref[...]).astype(BF)
+    h_sc[:TOK_DEV, :] = h1_ref[...]
     far = far_ref[:TOK_DEV, :].astype(F32)
     h_sc[TOK_DEV:, :] = (far * unit_rms(far) * gain1_ref[...]).astype(BF)
-    h1_ref[...] = h_sc[:TOK_DEV, :]
     for one in copies:
         one.wait()
     for i in range(6):
@@ -1054,7 +1052,7 @@
     h2_ref[TOK_DEV:, TOK_DEV:] = (probs - high.astype(F32)).astype(BF)
 
 
-def attention_forward(place, w_parts, own, far, gain1, gain2, router_t, cos, sin):
+def attention_forward(place, w_parts, h1, own, far, gain1, gain2, router_t, cos, sin):
     vmem = pl.BlockSpec(memory_space=pltpu.VMEM)
     shape = jax.ShapeDtypeStruct
     return pl.pallas_call(
@@ -1065,14 +1063,13 @@
             shape((2 * TOK_DEV, D), BF),
             shape((2 * TOK_DEV, D), BF),
             shape((TOK_DEV, D), BF),
-            shape((TOK_DEV, D), BF),
             shape((TOK_DEV, D), F32),
             shape((ROWS, D), BF),
         ),
         in_specs=[pl.BlockSpec(memory_space=pltpu.SMEM)]
         + [pl.BlockSpec(memory_space=pl.ANY)] * 8
-        + [vmem] * 7,
-        out_specs=(vmem,) * 8,
+        + [vmem] * 8,
+        out_specs=(vmem,) * 7,
         scratch_shapes=[
             pltpu.VMEM((2 * TOK_DEV, D), BF),
             pltpu.SemaphoreType.DMA((8, 4)),
@@ -1080,35 +1077,32 @@
         compiler_params=pltpu.CompilerParams(vmem_limit_bytes=VMEM_LIMIT),
         cost_estimate=microseconds(20),
         name="attention_forward",
-    )(place, *w_parts, own, far, gain1, gain2, router_t, cos, sin)
-
-
-def branch_kernel(
-    dx_a_ref,
-    dx_b_ref,
-    h2_ref,
-    x1_ref,
-    g_ref,
-    gain2_ref,
-    router_ref,
-    o_ref,
-    w_ref,
-    dx1_ref,
-    do_ref,
-    do_c_ref,
-    gwo_ref,
-    grouter_ref,
-    ggain_ref,
-):
-    tail = dx_a_ref[TOK_DEV:, :].astype(F32) + dx_b_ref[TOK_DEV:, :].astype(F32)
-    drp = tail[:, :TOK_DEV] + tail[:, TOK_DEV:]
+    )(place, *w_parts, h1, own, far, gain1, gain2, router_t, cos, sin)
+
+
+def branch_kernel(*refs):
+    dx_refs, refs = refs[:3], refs[3:]
+    (
+        h2_ref,
+        x1_ref,
+        g_ref,
+        gain2_ref,
+        router_ref,
+        w_ref,
+        dx1_ref,
+        do_ref,
+        do_c_ref,
+        grouter_ref,
+        ggain_ref,
+    ) = refs
+    dx = dx_refs[0][...].astype(F32) + dx_refs[1][...].astype(F32) + dx_refs[2][...].astype(F32)
+    drp = dx[TOK_DEV:, :TOK_DEV] + dx[TOK_DEV:, TOK_DEV:]
     probs = h2_ref[TOK_DEV:, :TOK_DEV].astype(F32) + h2_ref[TOK_DEV:, TOK_DEV:].astype(F32)
     dlogits = (probs * (drp - jnp.sum(probs * drp, 0, keepdims=True))).astype(BF)
     hidden = h2_ref[:TOK_DEV, :]
     grouter_ref[...] = jnp.dot(dlogits, hidden, preferred_element_type=F32)
     dh2 = (
-        dx_a_ref[:TOK_DEV, :].astype(F32)
-        + dx_b_ref[:TOK_DEV, :].astype(F32)
+        dx[:TOK_DEV]
         + contract(dlogits, router_ref[...], 0, 0)
     )
     resid = x1_ref[...]
@@ -1125,10 +1119,9 @@
         contract(datt[:, :384], w_ref[0], 1, 1) + contract(datt[:, 384:], w_ref[1], 1, 1)
     ).astype(BF)
     do_c_ref[...] = do_ref[PROMPT:, :]
-    gwo_ref[...] = contract(o_ref[...], datt, 0, 0).astype(BF)
-
-
-def branch_backward(dx_a, dx_b, h_block, x1, grad, gain2, router_t, o, w_all):
+
+
+def branch_backward(dx, h_block, x1, grad, gain2, router_t, w_all):
     shape = jax.ShapeDtypeStruct
     whole = lambda *dims: pl.BlockSpec(dims, lambda i: (0,) * len(dims))
     rows = whole(TOK_DEV, D)
@@ -1139,7 +1132,6 @@
             shape((TOK_DEV, D), F32),
             shape((TOK_DEV, D), BF),
             shape((TOK_DEV - PROMPT, D), BF),
-            shape((D, D), BF),
             shape((EXPERTS, D), F32),
             shape((1, D), F32),
         ),
@@ -1147,25 +1139,24 @@
             whole(ROWS, D),
             whole(ROWS, D),
             whole(ROWS, D),
+            whole(ROWS, D),
             rows,
             rows,
             whole(1, D),
             whole(EXPERTS, D),
-            rows,
             pl.BlockSpec((2, D, 384), lambda i: (3, 0, 0)),
         ],
         out_specs=(
             rows,
             rows,
             whole(TOK_DEV - PROMPT, D),
-            whole(D, D),
             whole(EXPERTS, D),
             whole(1, D),
         ),
         compiler_params=pltpu.CompilerParams(vmem_limit_bytes=VMEM_LIMIT),
         cost_estimate=microseconds(6),
         name="branch_backward",
-    )(dx_a, dx_b, h_block, x1, grad, gain2, router_t, o, w_all)
+    )(*dx, h_block, x1, grad, gain2, router_t, w_all)
 
 
 def attention_back_kernel(
@@ -1346,7 +1337,7 @@
             whole(TOK_DEV - PROMPT, D),
             rows,
             whole(6, D, 384),
-            whole(ROWS, D),
+            rows,
             whole(1, D),
             whole(TOK_DEV, 128),
             whole(TOK_DEV, 128),
@@ -1372,6 +1363,29 @@
     return lax.optimization_barrier((value, earlier))[0]
 
 
+def over_y(value):
+    return moved(value, lambda z, y, x, c: (z, 1 - y, x, c))
+
+
+def beside(results, moving):
+    return lax.optimization_barrier((results, moving))
+
+
+def norm_kernel(rows_ref, gain_ref, out_ref):
+    rows = rows_ref[...].astype(F32)
+    out_ref[...] = (rows * unit_rms(rows) * gain_ref[...]).astype(BF)
+
+
+def norm_rows(rows, gain):
+    return pl.pallas_call(
+        norm_kernel,
+        out_shape=jax.ShapeDtypeStruct(rows.shape, BF),
+        compiler_params=pltpu.CompilerParams(vmem_limit_bytes=VMEM_LIMIT),
+        cost_estimate=microseconds(2),
+        name="norm_rows",
+    )(rows, gain)
+
+
 def place_kernel(every_ref, gate_ref, up_ref, down_ref):
     for out_ref, at in ((gate_ref, 0), (up_ref, 256)):
         for k in range(4):
@@ -1406,17 +1420,32 @@
     )(every)
 
 
-def reduce_step(total, over, bit):
-    kept, sent = halves(total, bit)
-    return kept, over(sent)
-
-
-def reduce_dp(total, z):
-    result = lax.dynamic_index_in_dim(total, z, 0, keepdims=False).astype(F32)
-    for step in (1, 2, 3):
-        out = lax.dynamic_index_in_dim(total, lax.rem(z + step, 4), 0, keepdims=False)
-        result = result + over_z(out, step).astype(F32)
-    return result.astype(BF)
+OTHERS = (
+    over_x,
+    over_y,
+    lambda value: moved(value, lambda z, y, x, c: (z, 1 - y, 1 - x, c)),
+)
+
+
+def plane_pieces(value, x, y):
+    width = value.shape[-1] // 4
+    quarters = [value[..., width * i : width * (i + 1)] for i in range(4)]
+
+    def pick(column, row):
+        left = jnp.where(column == 0, quarters[0], quarters[1])
+        right = jnp.where(column == 0, quarters[2], quarters[3])
+        return jnp.where(row == 0, left, right)
+
+    return [pick(x, y), pick(1 - x, y), pick(x, 1 - y), pick(1 - x, 1 - y)]
+
+
+def lane_tables():
+    row = np.arange(TOK_DEV)
+    position = np.where(row < PROMPT, row, PROMPT + (row - PROMPT) % CLEN).astype(np.float32)
+    frequency = (10000.0 ** (-2.0 * np.arange(HD // 2) / HD)).astype(np.float32)
+    angles = (position[:, None] * frequency[None, :]).astype(np.float64)
+    cos, sin = np.cos(angles).astype(np.float32), np.sin(angles).astype(np.float32)
+    return jnp.asarray(np.tile(cos, (1, 4))), jnp.asarray(np.tile(np.concatenate([-sin, sin], 1), (1, 2)))
 
 
 def tuned_body(
@@ -1451,15 +1480,31 @@
     dense = jnp.concatenate([dense, jnp.concatenate([router_weight.T, gains], 1)], 0)
     dense_z = [over_z(dense, step) for step in (1, 2, 3)]
 
-    ids = jnp.broadcast_to(prompt_ids.astype(BF)[:, None], (CONT, D))
-    own = jnp.concatenate([tokens, ids, jnp.zeros((EXT - CONT, D), BF)], 0)
-    far = moved(own, lambda z, y, x, c: (z, 1 - y, x, c))
-    dense = jnp.stack([dense] + after(dense_z, far))
-    dense_a, dense_b = over_a(dense), over_b(dense)
-    dense_c = over_b(after(dense_a, dense_b))
-    dense_parts = [dense, dense_a, dense_b, dense_c]
+    far = over_y(tokens)
+    ids = jnp.broadcast_to(prompt_ids.astype(BF)[:, None], (CONT, 128))
+    far_ids = over_y(ids)
+    dense = jnp.stack([dense] + after(dense_z, far, far_ids))
+    slots = dense[:, shard:, :]
+    slots = jnp.stack([slots[0], slots[3], slots[2], slots[1]])
+    small = lax.dynamic_slice_in_dim(
+        jnp.concatenate([slots, slots], 0), lax.rem(4 - z, 4), 4, 0
+    )
+    router_t = small[:, :, :shard].transpose(1, 0, 2).reshape(EXPERTS, D)
+    gain1 = small[:, 0, shard:].reshape(1, D).astype(F32)
+    gain2 = small[:, 1, shard:].reshape(1, D).astype(F32)
+    flip_a, flip_b = jnp.where(core == 0, 2, 4), jnp.where(core == 0, 4, 2)
+    flips = [0 * core, flip_a, flip_b, 0 * core + 6]
+    flips = flips + [1 + flips[0], 1 + flip_b, 1 + flip_a, 1 + flips[3]]
+    place = [jnp.bitwise_xor(plane, flip) for flip in flips]
+    place += [lax.rem(z + 4 - slot, 4) for slot in range(4)]
+    place += [(prompt_ids[m] != y) for m in range(CONT)]
+    place = jnp.stack([v.astype(jnp.int32) for v in place])
+    cos, sin = lane_tables()
+    gain1, place, gain2, router_t, cos, sin = after((gain1, place, gain2, router_t, cos, sin))
+    h1 = norm_rows(tokens, gain1)
+    h1, dense_parts = beside(h1, (over_a(dense), over_b(dense)))
+    dense_parts = [dense, *dense_parts, over_b(dense_parts[0])]
     dense_parts = dense_parts + [over_core(part) for part in dense_parts]
-    far_ids = far[TOK_DEV : TOK_DEV + CONT, 0].astype(jnp.int32)
 
     expert_ids = jnp.arange(EXPERTS, dtype=jnp.int32)[:, None]
     route_t = routes.T
@@ -1468,10 +1513,9 @@
     ranks = jnp.dot(member.astype(BF), before, preferred_element_type=F32)
     ranks = jnp.where(member, ranks, -1.0).astype(BF)
     g_block = jnp.concatenate([cotangent, jnp.pad(ranks, ((0, 0), (0, D - TOK_DEV)))], 0)
-    g_near = after(g_block, dense_c)
-    g_a, g_b = over_a(g_near), over_b(g_near)
-    g_x = jnp.where(core == 0, g_a, g_b)
-    g_group = [g_block, g_x, over_core(g_block), over_core(g_x)]
+    g_near = after(g_block, h1)
+    g_x = over_x(g_near)
+    g_group = [g_block, g_x, over_core(g_near), over_core(g_x)]
 
     units = lambda w: lax.dynamic_index_in_dim(
         w.reshape(shard, 4, 8, 64), plane, 2, keepdims=False
@@ -1480,70 +1524,60 @@
     down = jnp.concatenate([down[:, 256 * i : 256 * (i + 1)] for i in range(3)], 0)
     shared = jnp.concatenate([units(shared_gate), units(shared_up), down], 1)
     shared = lax.all_gather(after(shared, dense), "dp", axis=0, tiled=False)
-    shared_far = moved(after(shared, dense_c), lambda z, y, x, c: (z, 1 - y, x, c))
-
-    g_column = lax.all_gather(after(g_block, dense_a), "dp", axis=0, tiled=False)
-
-    slots = dense[:, shard:, :]
-    slots = jnp.stack([slots[0], slots[3], slots[2], slots[1]])
-    small = lax.dynamic_slice_in_dim(
-        jnp.concatenate([slots, slots], 0), lax.rem(4 - z, 4), 4, 0
-    )
-    router_t = small[:, :, :shard].transpose(1, 0, 2).reshape(EXPERTS, D)
-    gain1 = small[:, 0, shard:].reshape(1, D).astype(F32)
-    gain2 = small[:, 1, shard:].reshape(1, D).astype(F32)
-
-    cos_table, sin_table = rotary_tables(TOK_DEV)
-    cos = jnp.tile(cos_table, (1, 4))
-    sin = jnp.tile(jnp.concatenate([-sin_table, sin_table], 1), (1, 2))
-    flip_a, flip_b = jnp.where(core == 0, 2, 4), jnp.where(core == 0, 4, 2)
-    flips = [0 * core, flip_a, flip_b, 0 * core + 6]
-    flips = flips + [1 + flips[0], 1 + flip_b, 1 + flip_a, 1 + flips[3]]
-    place = [jnp.bitwise_xor(plane, flip) for flip in flips]
-    place += [lax.rem(z + 4 - slot, 4) for slot in range(4)]
-    place += [(prompt_ids[m] != y) for m in range(CONT)]
-    place = jnp.stack([v.astype(jnp.int32) for v in place])
-    cos = after(cos, shared)
-    w_all, q, k, v, h1, o, x1, h_block = attention_forward(
-        place, dense_parts, own, far, gain1, gain2, router_t, cos, sin
-    )
-
-    h_block, x1 = after((h_block, x1), g_a, g_b)
+    shared_far = over_y(after(shared, h1))
+
+    g_column = lax.all_gather(after(g_block, dense), "dp", axis=0, tiled=False)
+
+    place = after(place, shared)
+    flags = jnp.concatenate([prompt_ids == y, far_ids[:, 0].astype(jnp.int32) == y, core[None] != 0]).astype(jnp.int32)
+    w_all, q, k, v, o, x1, h_block = attention_forward(
+        place, dense_parts, h1, tokens, far, gain1, gain2, router_t, cos, sin
+    )
+    (h_block, x1), (g_x, shared_far) = beside((h_block, x1), (g_x, shared_far))
+    g_group = [g_block, g_x, over_core(g_block), over_core(g_x)]
+
     h_x = over_x(h_block)
-    h_group = [h_block, h_x, over_core(h_block), over_core(h_x)]
+    h_near, g_near = [h_block, over_core(h_block)], [g_block, g_group[2]]
     h_column = lax.all_gather(h_block, "dp", axis=0, tiled=False)
     experts_w = (expert_gate, expert_up_weight, expert_down)
     base = (j * 4).astype(jnp.int32)
+    more = shared_rows(h_near, g_near, shared, shared_far)
+    more, (h_x, g_y) = beside(more, (h_x, over_y(after(g_block, h_block))))
+    h_far, g_far = [h_x, over_core(h_x)], [g_x, g_group[3]]
+    h_group = [h_near[0], h_far[0], h_near[1], h_far[1]]
     part = group_experts(base[None], 0, 2, h_group, g_group, (), *experts_w)
-    near, far_group, part = after((h_group[::2], h_group[1::2], part), shared_far)
-    more = shared_rows(near, g_group[::2], shared, shared_far)
-    more += shared_rows(far_group, g_group[1::2], shared, shared_far)
-    g_first = over_a(after(g_column, part))
-    moe_near, moe_far, dx_near, dx_far = group_experts(
+    (part, h_far), h_b = beside((part, h_far), over_b(after(h_block, h_x)))
+    g_first = over_a(after(g_column, h_x))
+    more = more + shared_rows(h_far, g_far, shared, shared_far)
+    more, g_first = beside(more, g_first)
+    g_second = jnp.where(core == 0, g_y, g_x)
+    g_second = lax.all_gather(after(g_second, h_x), "dp", axis=0, tiled=False)
+    results = group_experts(
         base[None] + 2, 2, 2, h_group, g_group, (*more, *part), *experts_w
     )
-    moe_near, moe_far, dx_near, dx_far = after((moe_near, moe_far, dx_near, dx_far), g_first)
-    g_second = lax.all_gather(after(g_b, dx_near), "dp", axis=0, tiled=False)
-
-    dx_pair = pair_sum(dx_near, over_core(dx_far))
-    dx_there = over_x(dx_pair[1])
+    g_third = over_b(g_first)
+    results, (g_third, g_core) = beside(
+        results, (g_third, [over_core(g_column), over_core(g_first)])
+    )
+    moe, dx = results[:4], results[4:]
+    dx_x = pair_sum(dx[1], over_core(dx[3]))
+    dx = [dx[0], over_core(dx[2]), over_x(dx_x)]
+    h_column = after(h_column, dx_x)
+    h_core = [over_core(h_column)]
     window = jnp.array([0, 1, 3, 4], jnp.int32)[z]
     s_pos = jnp.stack([window, (z // 2).astype(jnp.int32)])
     e_pos = jnp.stack([base, (z * 2 + y).astype(jnp.int32)])
-    h_column, g_column = after((h_column, g_column), dx_pair)
-    h_core, g_core = [over_core(h_column)], [over_core(g_column)]
     s_sums = shared_slice_grads(
         s_pos, [h_column, h_core[0]], [g_column, g_core[0]], shared
     )
-    gain2 = after(gain2, s_sums)
-    dx1, do, do_c, gwo, grad_router_t, grad_gain2 = branch_backward(
-        dx_pair[0], dx_there, h_block, x1, cotangent, gain2, router_t, o, w_all
-    )
-    do_far = moved(do_c, lambda z, y, x, c: (z, 1 - y, x, c))
-    h_column, g_column, g_first = after((h_column, g_column, g_first), do_far)
-    h_first = over_a(h_column)
-    g_core.append(over_core(g_first))
-    flags = jnp.concatenate([prompt_ids == y, far_ids == y, core[None] != 0]).astype(jnp.int32)
+    s_sums, dx = beside(s_sums, dx)
+    dx1, do, do_c, grad_router_t, grad_gain2 = branch_backward(
+        dx, h_block, x1, cotangent, gain2, router_t, w_all
+    )
+    gwo = inner_rows(o, dx1.astype(BF)).astype(BF)
+    gwo, do_far = beside(gwo, over_y(do_c))
+    h_first = over_a(after(h_column, do_far))
+    h_second = lax.all_gather(after(h_b, do_far), "dp", axis=0, tiled=False)
     grad_inputs, keep, send = attention_backward(
         flags,
         q,
@@ -1553,7 +1587,7 @@
         do_far,
         h1,
         w_all,
-        own,
+        tokens,
         gain1,
         cos,
         sin,
@@ -1562,45 +1596,41 @@
         grad_router_t,
         grad_gain2,
     )
-    grad_inputs, keep, send = after(
-        (grad_inputs, keep, send), h_first, g_core, g_second
-    )
-    g_third = lax.all_gather(after(over_b(after(g_a, near)), keep), "dp", axis=0, tiled=False)
-    bit_a, bit_b = jnp.where(core == 0, x, y), jnp.where(core == 0, y, x)
-    total = pair_sum(keep, over_core(send))
+    (grad_inputs, keep, send), (h_first, g_second) = beside(
+        (grad_inputs, keep, send), (h_first, g_second)
+    )
     h_core.append(over_core(h_first))
-    kept, there = reduce_step(total, over_a, bit_a)
-
-    h_parts, g_parts = [h_column, h_first] + h_core, [g_column, g_first] + g_core
+    h_third = over_b(after(h_first, keep))
+    h_parts, g_parts = [h_column, h_first] + h_core, [g_column, g_first] + g_core[:2]
+    e_pos = after(e_pos, keep)
+    e_sums = expert_slice_grads(e_pos, h_parts, g_parts, *experts_w, 256)
+    (e_sums, keep), (send, h_second, h_third, g_far) = beside(
+        (e_sums, keep),
+        (over_core(send), h_second, h_third, [over_core(after(v, keep)) for v in (g_second, g_third)]),
+    )
+    h_far = [over_core(h_second), over_core(h_third)]
+    h_parts, g_parts = [h_second, h_third] + h_far, [g_second, g_third] + g_far
+    pieces = plane_pieces(pair_sum(keep, send), x, y)
+    h_parts, pieces = after((h_parts, pieces))
     s_sums = shared_slice_grads(
-        s_pos, [h_first, h_core[1]], [g_first, g_core[1]], shared, s_sums
-    )
-    s_sums, kept = after((s_sums, kept), there)
-    kept, there = reduce_step(pair_sum(kept, there), over_b, bit_b)
-    h_second, h_third = over_b(after(h_column, s_sums)), over_b(after(h_first, s_sums))
-    e_sums = expert_slice_grads(after(e_pos, s_sums), h_parts, g_parts, *experts_w, 256)
-    e_sums, kept, g_second, g_third = after(
-        (e_sums, kept, g_second, g_third), there, h_second, h_third
-    )
-    z_own = pair_sum(kept, there)
+        s_pos, [h_first, h_core[1], *h_parts], [g_first, g_core[1], *g_parts], shared, s_sums
+    )
+    (s_sums, pieces), there = beside(
+        (s_sums, pieces), [over(piece) for over, piece in zip(OTHERS, pieces[1:])]
+    )
+    s_gate, s_up, s_down = s_sums
+    z_own = pieces[0].astype(F32)
+    for piece in there:
+        z_own = z_own + piece.astype(F32)
+    z_own = z_own.astype(BF)
     z_parts = [
-        over_z(lax.dynamic_index_in_dim(z_own, lax.rem(z + step, 4), 0, keepdims=False), step)
-        for step in (1, 2, 3)
+        lax.dynamic_index_in_dim(z_own, lax.rem(z + step, 4), 0, keepdims=False)
+        for step in (0, 1, 2, 3)
     ]
-    h_parts, g_parts = [h_second, h_third], [g_second, g_third]
-    h_parts = h_parts + [over_core(part) for part in h_parts]
-    g_parts = g_parts + [over_core(part) for part in g_parts]
-    s_sums = shared_slice_grads(s_pos, h_parts, g_parts, shared, s_sums)
-    s_gate, s_up, s_down = after(s_sums, z_parts)
-    total = lax.dynamic_index_in_dim(z_own, z, 0, keepdims=False).astype(F32)
-    for part in z_parts:
-        total = total + part.astype(F32)
-    total = after(total.astype(BF), s_gate)
-    moe_near, moe_far = after((moe_near, moe_far), s_gate)
-    moe_pair = pair_sum(moe_near, over_core(moe_far))
-    moe_there = over_x(moe_pair[1])
-    half_a, half_b = over_a(total), over_b(total)
-    opposite = moved(total, lambda z, y, x, c: (z, 1 - y, 1 - x, c))
+    moe = after(moe, s_gate)
+    moe_x = pair_sum(moe[1], over_core(moe[3]))
+    moe_core = over_core(moe[2])
+
     lead = z * 192 - window * 128
     s_down = lax.dynamic_slice_in_dim(s_down, (z % 2) * 64, 64, 0)
     mine = jnp.concatenate(
@@ -1611,17 +1641,30 @@
         ],
         1,
     ).astype(BF)
+    mine, z_parts, moe_x, moe_core, h_parts, g_parts = after(
+        (mine, z_parts, moe_x, moe_core, h_parts, g_parts)
+    )
     every = lax.all_gather(mine, ("context", "experts"), axis=0, tiled=False)
+    moving = ([over_z(z_parts[step], step) for step in (1, 2, 3)], over_x(moe_x), every)
     e_gate, e_up, e_down = expert_slice_grads(e_pos, h_parts, g_parts, *experts_w, 256, e_sums)
-    e_gate, total = after((e_gate, total), half_a, half_b, opposite, moe_there, every)
-    layer_out = (x1 + (moe_pair[0].astype(F32) + moe_there.astype(F32))).astype(BF)
-    total = rejoin(rejoin(total, half_b, bit_b), rejoin(half_a, opposite, bit_b), bit_a)
+    (e_gate, e_up, e_down), (there, moe_there, every) = beside((e_gate, e_up, e_down), moving)
+    total = z_parts[0].astype(F32)
+    for part in there:
+        total = total + part.astype(F32)
+    total = total.astype(BF)
+    total_parts = [over(total) for over in OTHERS]
+    layer_out = (
+        x1 + (moe[0].astype(F32) + moe_core.astype(F32) + moe_there.astype(F32))
+    ).astype(BF)
+    s_gate, s_up, s_down = place_shared(every)
+    (layer_out, s_gate), total_parts = beside((layer_out, s_gate), total_parts)
+    beside_x = rejoin(total, total_parts[0], x)
+    total = rejoin(beside_x, rejoin(total_parts[1], total_parts[2], x), y)
     other = over_core(total)
     sum_qk, sum_vo = jnp.where(core == 0, total, other), jnp.where(core == 0, other, total)
     extras = sum_qk[shard:, : 2 * shard].astype(F32)
     sum_qk, sum_vo = sum_qk[:shard].astype(F32), sum_vo[:shard].astype(F32)
 
-    s_gate, s_up, s_down = place_shared(every)
     return (
         layer_out,
         grad_inputs,

time: 451 us -> 404 us (0.90)
  waiting for transfers between devices: 104 us -> 65.5 us
  local copies, waits for them, and re-layouts: 25.1 us -> 19.8 us
  other arithmetic: 27.2 us -> 22.4 us
  starting transfers between devices: 39.8 us -> 44.5 us
    ppermute x47 -> x51, waiting for transfers between devices: 101 us -> 47.6 us  [moved(): return lax.ppermute(value, AXES, pairs)]
    all_gather x1, waiting for transfers between devices: 0.01 us -> 10.5 us  [tuned_body(): shared = lax.all_gather(after(shared, dense), 'dp', axis=0, tiled=False)]
    all_gather x3, waiting for transfers between devices: 0.04 us -> 7.29 us  [the longest x1 6.89 us: tuned_body(): g_column = lax.all_gather(after(g_block, dense), 'dp', axis=0, tiled=False)]
    ppermute x47 -> x51, starting transfers between devices: 39 us -> 44 us  [moved(): return lax.ppermute(value, AXES, pairs)]
    pallas_call x3 -> x2, Pallas kernels: 46.2 us -> 41.8 us  [shared_slice_grads(): pl.pallas_call(functools.partial(shared_slice_kernel, parts, len(sums) //...]
    convert_element_type x5 -> x3, other arithmetic: 9.34 us -> 6.41 us  [pair_sum(): return (kept.astype(F32) + received.astype(F32)).astype(BF)]
  transfers between devices with their start and end apart: 53 -> 57, of which waited for: 18 -> 25; matrix products, arithmetic and copies ran while one was open for 8% -> 9% of each run, Pallas kernels for 52% -> 57%
where the time goes in v4:
time: 404 us; the launch traced here: 401 us
  Pallas kernels  228 us (56%)
  waiting for transfers between devices  65.5 us (16%)
  starting transfers between devices  44.5 us (11%)
  other arithmetic  22.4 us (6%)
  local copies, waits for them, and re-layouts  19.8 us (5%)
  between operations  17.1 us (4%)
    pallas_call x2, Pallas kernels, expert_slice_grads(): pl.pallas_call(functools.partial(expert_slice_kernel, parts, len(sums) //...  62.4 us
    pallas_call x2, Pallas kernels, group_experts(): pl.pallas_call(functools.partial(group_kernel, blocks, len(more)), out_sh...  49.5 us
    ppermute x51, waiting for transfers between devices, moved(): return lax.ppermute(value, AXES, pairs)  47.6 us
    ppermute x51, starting transfers between devices, moved(): return lax.ppermute(value, AXES, pairs)  44 us
    pallas_call x2, Pallas kernels, shared_slice_grads(): pl.pallas_call(functools.partial(shared_slice_kernel, parts, len(sums) //...  41.8 us
    pallas_call x1, Pallas kernels, attention_backward(): pl.pallas_call(attention_back_kernel, grid=(1,), out_shape=(shape((TOK_DE...  25.4 us
    pallas_call x1, Pallas kernels, attention_forward(): pl.pallas_call(attention_kernel, out_shape=(shape((8, D, 384), BF), shape...  20.9 us
    pallas_call x2, Pallas kernels, shared_rows(): pl.pallas_call(shared_kernel, out_shape=(rows, rows), in_specs=[vmem] * 6...  17.1 us
  transfers between devices with their start and end apart: 57, of which 25 were waited for; matrix products, arithmetic and copies ran while one was open for 9% of the time, Pallas kernels for 57%

profile of v4, /device:TPU:0, one launch (start us, length us, event | category | flops | bytes accessed | tf_op | source)
XLA Modules:
  0.0 401.2 jit_solution(9202265407513623730)
XLA Ops:
  7.3 3.0 collective-permute-start.3
  10.3 1.0 fusion.7
  12.2 1.6 collective-permute-start
  13.8 2.6 collective-permute-start.1
  16.4 1.3 collective-permute-start.2
  21.9 2.8 collective-permute-done.4
  24.7 2.1 collective-permute-done.1
  26.8 1.1 pad_maximum_fusion.refs_0_
  32.9 1.5 collective-permute-start.5
  38.5 2.1 norm_rows.1.refs_8_.h1_ref
  40.7 8.8 %collective-permute-done.5.refs_1_ = bf16[4,208,384]{2,1,0:T(8,128)(2,1)} collective-permute-done((bf16[4,208,384]{2,1,0:T(8,128)(2,1)S(1)}, bf16[4,208,384]{2,1,0:T(8,128)(2,1)}, u32[]{:S(2)}, u32[]{:S(2)}) %collective-permute-start.5) | collective-permute-done | bytes 639008 | tf_op jit(solution)/shard_map/ppermute | solution.py:454
  49.4 1.1 collective-permute-start.7
  50.6 10.5 %all-gather.13.cloned.1.call-done = bf16[768,768]{1,0:T(8,128)(2,1)} async-done(((bf16[192,768]{1,0:T(8,128)(2,1)}), bf16[768,768]{1,0:T(8,128)(2,1)}) %all-gather.13.cloned.1.call-update) | async-done | bytes 1179664 | tf_op jit(solution)/shard_map/all_gather | solution.py:1526
  61.1 1.5 collective-permute-start.13
  63.1 1.5 collective-permute-start.12
  66.8 20.9 %attention_forward.1 = (bf16[8,768,384]{2,1,0:T(8,128)(2,1)}, bf16[768,768]{1,0:T(8,128)(2,1)}, bf16[768,768]{1,0:T(8,128)(2,1)}, bf16[768,768]{1,0:T(8,128)(2,1...) custom-call(s32[14]{0:T(128)} %stack.100.place_ref, bf16[4,208,384]{2,1,0:T(8,128)(2,1)} %copy-done.12, ...), custom_call_target="tpu_custom_call" | custom-call | bytes 8000000 | tf_op jit(solution)/shard_map/attention_forward/pallas_call | solution.py:1058
  88.4 1.0 copy-done.11
  89.5 1.5 collective-permute-start.16
  90.9 1.5 collective-permute-start.17
  94.1 8.4 %shared_rows.2 = (f32[2,384,768]{2,1,0:T(8,128)}, f32[2,384,768]{2,1,0:T(8,128)}) custom-call(bf16[400,768]{1,0:T(8,128)(2,1)} %get-tuple-element.233.h_a_ref.refs_0_.refs_3_, bf16[400,768]{1,0:T(8,128)(2,1)} %copy-done.7, bf16[400,768]{1,0:T(8,128)(2,1)} %fusion.2.g_a_ref.refs_4_, bf16[400,768]{1,0:T(8,128)(2,1)} %copy-done.6, ...), custom_call_target="tpu_custom_call" | custom-call | bytes 3200000 | tf_op jit(solution)/shard_map/shared_rows/pallas_call | solution.py:679
  102.5 3.6 collective-permute-done.16.refs_1_.h_a_ref
  107.0 6.9 %all-gather.15.cloned.1.call-done = bf16[1600,768]{1,0:T(8,128)(2,1)} async-done(((bf16[400,768]{1,0:T(8,128)(2,1)}), bf16[1600,768]{1,0:T(8,128)(2,1)}) %all-gather.15.cloned.1.call-update) | async-done | bytes 2457616 | tf_op jit(solution)/shard_map/all_gather | solution.py:1529
  113.9 1.5 collective-permute-start.21
  115.9 1.5 collective-permute-start.20
  119.4 24.4 %group_experts.2 = (bf16[384,768]{1,0:T(8,128)(2,1)}, bf16[384,768]{1,0:T(8,128)(2,1)}, bf16[384,768]{1,0:T(8,128)(2,1)}, bf16[384,768]{1,0:T(8,128)(2,1)}, bf16...) custom-call(s32[1]{0:T(128)} %bitcast.28.base_ref, ...), custom_call_target="tpu_custom_call" | custom-call | bytes 8400000 | tf_op jit(solution)/shard_map/group_experts/pallas_call | solution.py:616
  143.8 8.7 %shared_rows.3 = (f32[2,384,768]{2,1,0:T(8,128)}, f32[2,384,768]{2,1,0:T(8,128)}) custom-call(bf16[400,768]{1,0:T(8,128)(2,1)} %collective-permute-done.16.refs_1_.h_a_ref, bf16[400,768]{1,0:T(8,128)(2,1)} %copy-done.9, bf16[400,768]{1,0:T(8,128)(2,1)} %copy-done.2, bf16[400,768]{1,0:T(8,128)(2,1)} %copy-done.8, bf16[4,192,768]{2,1,0:T(8,128)(2,1)} %bitcast.57, ...), custom_call_target="tpu_custom_call" | custom-call | bytes 3200000 | tf_op jit(solution)/shard_map/shared_rows/pallas_call | solution.py:679
  152.5 1.5 collective-permute-start.22
  154.0 25.1 %group_experts.3 = (bf16[384,768]{1,0:T(8,128)(2,1)}, bf16[384,768]{1,0:T(8,128)(2,1)}, bf16[384,768]{1,0:T(8,128)(2,1)}, bf16[384,768]{1,0:T(8,128)(2,1)}, bf16...) custom-call(s32[1]{0:T(128)S(6)} %add.124.base_ref, ...), custom_call_target="tpu_custom_call" | custom-call | bytes 8400000 | tf_op jit(solution)/shard_map/group_experts/pallas_call | solution.py:616
  179.2 3.5 collective-permute-done.22.refs_9_.refs_5_
  182.7 2.2 collective-permute-done.25
  184.9 2.0 add_convert_fusion.2
  187.1 2.0 broadcast_select_fusion.9
  190.3 1.3 pad_add_fusion.pos_ref
  192.0 12.7 %shared_slice_grads.2 = (f32[256,256]{1,0:T(8,128)}, f32[256,256]{1,0:T(8,128)}, f32[128,768]{1,0:T(8,128)}) custom-call(s32[2]{0:T(128)} %pad_add_fusion.pos_ref, bf16[4,400,768]{2,1,0:T(8,128)(2,1)} %bitcast.33.refs_0_, bf16[4,400,768]{2,1,0:T(8,128)(2,1)} %collective-permute-done.26.refs_1_.refs_2_, bf16[4,400,768]{2,1,0:T(8,128)(2,1)} %bitcast.68, ...), custom_call_target="tpu_custom_call" | custom-call | bytes 8000000 | tf_op jit(solution)/shard_map/shared_slice_grads/pallas_call | solution.py:872
  204.7 1.1 collective-permute-done.28.refs_2_
  205.8 5.0 %branch_backward.1 = (f32[384,768]{1,0:T(8,128)}, bf16[384,768]{1,0:T(8,128)(2,1)}, bf16[128,768]{1,0:T(8,128)(2,1)}, f32[16,768]{1,0:T(8,128)}, f32[1,768]{1,0:T(1,128)}) custom-call(bf16[400,768]{1,0:T(8,128)(2,1)} %get-tuple-element.277.refs_0_, bf16[400,768]{1,0:T(8,128)(2,1)} %copy-done.18, bf16[400,768]{1,0:T(8,128)(2,1)} %collective-permute-done.28.refs_2_, ...), custom_call_target="tpu_custom_call" | custom-call | bytes 2400000 | tf_op jit(solution)/shard_map/branch_backward/pallas_call | solution.py:1128
  210.9 1.5 collective-permute-start.29
  212.3 3.3 convolution_convert_fusion.gwo_ref
  215.7 2.1 collective-permute-done.29.do_far_ref
  217.7 1.4 collective-permute-start.30
  220.5 25.4 %attention_backward.1 = (f32[384,768]{1,0:T(8,128)}, bf16[4,208,1536]{2,1,0:T(8,128)(2,1)}, bf16[4,208,1536]{2,1,0:T(8,128)(2,1)}) custom-call(s32[5]{0:T(128)} %add_convert_fusion.6.flags_ref, bf16[768,768]{1,0:T(8,128)(2,1)} %get-tuple-element.265.q_ref, bf16[768,768]{1,0:T(8,128)(2,1)} %get-tuple-element.266.k_ref, ...), custom_call_target="tpu_custom_call" | custom-call | bytes 9200000 | tf_op jit(solution)/shard_map/attention_backward/pallas_call | solution.py:1323
  245.9 2.0 collective-permute-done.30.refs_1_.refs_0_
  248.5 1.5 collective-permute-start.33
  251.0 9.1 %collective-permute-done.31.refs_3_.refs_1_ = bf16[4,400,768]{2,1,0:T(8,128)(2,1)} collective-permute-done((bf16[4,400,768]{2,1,0:T(8,128)(2,1)}, bf16[4,400,768]{2,1,0:T(8,128)(2,1)}, u32[]{:S(2)}, u32[]{:S(2)}) %collective-permute-start.31) | collective-permute-done | bytes 2457632 | tf_op jit(solution)/shard_map/ppermute | solution.py:454
  260.1 30.8 %expert_slice_grads.2 = (f32[4,768,256]{2,1,0:T(8,128)}, f32[4,768,256]{2,1,0:T(8,128)}, f32[4,256,768]{2,1,0:T(8,128)}) custom-call(s32[2]{0:T(128)} %pad_add_fusion.1.pos_ref, bf16[4,400,768]{2,1,0:T(8,128)(2,1)} %bitcast.33.refs_0_, bf16[4,400,768]{2,1,0:T(8,128)(2,1)} %collective-permute-done.30.refs_1_.refs_0_, ...), custom_call_target="tpu_custom_call" | custom-call | bytes 12400000 | tf_op jit(solution)/shard_map/expert_slice_grads/pallas_call | solution.py:800
  291.9 3.2 add_convert_fusion
  296.1 1.3 broadcast_select_fusion.1
  297.4 1.7 collective-permute-done.36.refs_4_.refs_2_
  300.0 1.5 collective-permute-start.38
  301.4 1.5 collective-permute-start.39
  304.2 29.0 %shared_slice_grads.3 = (f32[256,256]{1,0:T(8,128)}, f32[256,256]{1,0:T(8,128)}, f32[128,768]{1,0:T(8,128)}) custom-call(s32[2]{0:T(128)} %pad_add_fusion.pos_ref, bf16[4,400,768]{2,1,0:T(8,128)(2,1)} %collective-permute-done.30.refs_1_.refs_0_, bf16[4,400,768]{2,1,0:T(8,128)(2,1)} %collective-permute-done.31.refs_3_.refs_1_, bf16[4,400,768]{2,1,0:T(8,128)(2,1)} %bitcast.64, ...), custom_call_target="tpu_custom_call" | custom-call | bytes 8000000 | tf_op jit(solution)/shard_map/shared_slice_grads/pallas_call | solution.py:872
  334.8 1.8 add_convert_fusion.1
  339.4 1.2 add_convert_fusion.4
  340.6 1.5 collective-permute-start.46
  342.2 1.9 collective-permute-start.44
  344.1 2.5 collective-permute-start.45
  346.5 31.6 %expert_slice_grads.3 = (f32[4,768,256]{2,1,0:T(8,128)}, f32[4,768,256]{2,1,0:T(8,128)}, f32[4,256,768]{2,1,0:T(8,128)}) custom-call(s32[2]{0:T(128)} %pad_add_fusion.1.pos_ref, bf16[4,400,768]{2,1,0:T(8,128)(2,1)} %bitcast.65, bf16[4,400,768]{2,1,0:T(8,128)(2,1)} %collective-permute-done.33.refs_3_.refs_1_, bf16[4,400,768]{2,1,0:T(8,128)(2,1)} %copy-done.5, ...), custom_call_target="tpu_custom_call" | custom-call | bytes 12400000 | tf_op jit(solution)/shard_map/expert_slice_grads/pallas_call | solution.py:800
  379.0 1.5 collective-permute-start.48
  380.5 1.3 collective-permute-start.49
  381.8 4.2 %place_shared.1 = (f32[192,2048]{1,0:T(8,128)}, f32[192,2048]{1,0:T(8,128)}, f32[512,768]{1,0:T(8,128)}) custom-call(bf16[8,192,768]{2,1,0:T(8,128)(2,1)} %bitcast.70), custom_call_target="tpu_custom_call" | custom-call | bytes 1600000 | tf_op jit(solution)/shard_map/place_shared/pallas_call | solution.py:1408
  386.0 1.1 add_convert_fusion.3
  388.3 2.1 collective-permute-done.50
  391.8 1.1 fusion.15
  393.0 1.1 fusion.14
  (207 shorter events, 37.2 us)
Async XLA Ops:
  7.2 12.8 %copy-start.14 = (bf16[192,2048]{1,0:T(8,128)(2,1)S(1)}, bf16[192,2048]{1,0:T(8,128)(2,1)}, u32[]{:S(2)}) copy-start(bf16[192,2048]{1,0:T(8,128)(2,1)} %param.32) | copy-start | bytes 2359300
  7.2 53.8 %all-gather.13.cloned.1.call-start = ((), (), s32[]{:S(2)}) async-start(), calls=%async_computation | async-start | bytes 1474560 | tf_op jit(solution)/shard_map/all_gather | solution.py:1526
  7.3 19.5 %collective-permute-start.3 = (bf16[384,768]{1,0:T(8,128)(2,1)}, bf16[384,768]{1,0:T(8,128)(2,1)}, u32[]{:S(2)}, u32[]{:S(2)}) collective-permute-start(bf16[384,768]{1,0:T(8,128)(2,1)} %own_ref.1), channel_id=1, source_target_pairs={{0,4},{1,5},{2,6},{3,7},{4,0},{5,1},{6,2},{7,3},{8,12},{9,13},{10,... | collective-permute-start | bytes 1769480 | tf_op jit(solution)/shard_map/ppermute | solution.py:454
  12.2 12.5 %collective-permute-start = (bf16[208,384]{1,0:T(8,128)(2,1)}, bf16[208,384]{1,0:T(8,128)(2,1)S(1)}, u32[]{:S(2)}, u32[]{:S(2)}) collective-permute-start(bf16[208,384]{1,0:T(8,128)(2,1)} %maximum_maximum_fusion.2), channel_id=1, source_target_pairs={{0,8},{1,9},{2,10},{3,11},{4,12},{5,13},{6,14},{7,15},{8,16},{9,17... | collective-permute-start | bytes 479240 | tf_op jit(solution)/shard_map/ppermute | solution.py:454
  13.8 13.0 %collective-permute-start.1 = (bf16[208,384]{1,0:T(8,128)(2,1)}, bf16[208,384]{1,0:T(8,128)(2,1)S(1)}, u32[]{:S(2)}, u32[]{:S(2)}) collective-permute-start(bf16[208,384]{1,0:T(8,128)(2,1)} %maximum_maximum_fusion.2), channel_id=1, source_target_pairs={{0,16},{1,17},{2,18},{3,19},{4,20},{5,21},{6,22},{7,23},{8,24},{9,... | collective-permute-start | bytes 479240 | tf_op jit(solution)/shard_map/ppermute | solution.py:454
  16.4 10.4 %collective-permute-start.2 = (bf16[208,384]{1,0:T(8,128)(2,1)}, bf16[208,384]{1,0:T(8,128)(2,1)}, u32[]{:S(2)}, u32[]{:S(2)}) collective-permute-start(bf16[208,384]{1,0:T(8,128)(2,1)} %maximum_maximum_fusion.2), channel_id=1, source_target_pairs={{0,24},{1,25},{2,26},{3,27},{4,28},{5,29},{6,30},{7,31},{8,0},{9,1... | collective-permute-start | bytes 479240 | tf_op jit(solution)/shard_map/ppermute | solution.py:454
  18.3 6.3 %collective-permute-start.4 = (bf16[2,128]{0,1:T(8,128)(2,1)}, bf16[2,128]{0,1:T(8,128)(2,1)}, u32[]{:S(2)}, u32[]{:S(2)}) collective-permute-start(bf16[2,128]{0,1:T(8,128)(2,1)} %broadcast_in_dim.30), channel_id=1, source_target_pairs={{0,4},{1,5},{2,6},{3,7},{4,0},{5,1},{6,2},{7,3},{8,12},{9,13},{10,... | collective-permute-start | bytes 1544 | tf_op jit(solution)/shard_map/ppermute | solution.py:454
  27.9 22.7 %copy-start.12 = (bf16[4,208,384]{2,1,0:T(8,128)(2,1)}, bf16[4,208,384]{2,1,0:T(8,128)(2,1)S(1)}, u32[]{:S(2)}) copy-start(bf16[4,208,384]{2,1,0:T(8,128)(2,1)S(1)} %pad_maximum_fusion.refs_0_) | copy-start | bytes 1916932
  28.8 85.1 %all-gather.15.cloned.1.call-start = ((), (), s32[]{:S(2)}) async-start(), calls=%async_computation.1 | async-start | bytes 3072000 | tf_op jit(solution)/shard_map/all_gather | solution.py:1529
  30.0 33.1 %copy-start = (bf16[400,768]{1,0:T(8,128)(2,1)S(1)}, bf16[400,768]{1,0:T(8,128)(2,1)}, u32[]{:S(2)}) copy-start(bf16[400,768]{1,0:T(8,128)(2,1)} %fusion.2.g_a_ref.refs_4_) | copy-start | bytes 1843204
  30.0 156.9 %all-gather.17.cloned.1.call-start = ((), (), s32[]{:S(2)}) async-start(), calls=%async_computation.2 | async-start | bytes 3072000 | tf_op jit(solution)/shard_map/all_gather | solution.py:1541
  32.9 16.5 %collective-permute-start.5 = (bf16[4,208,384]{2,1,0:T(8,128)(2,1)S(1)}, bf16[4,208,384]{2,1,0:T(8,128)(2,1)}, u32[]{:S(2)}, u32[]{:S(2)}) collective-permute-start(bf16[4,208,384]{2,1,0:T(8,128)(2,1)S(1)} %pad_maximum_fusion.refs_0_), channel_id=1, source_target_pairs={{0,2},{1,5},{2,0},{3,7},{4,6},{5,1},{6,4},{7,3},{8,10},{9,13},{10,... | collective-permute-start | bytes 1916936 | tf_op jit(solution)/shard_map/ppermute | solution.py:454
  34.4 15.1 %collective-permute-start.6 = (bf16[4,208,384]{2,1,0:T(8,128)(2,1)S(1)}, bf16[4,208,384]{2,1,0:T(8,128)(2,1)S(1)}, u32[]{:S(2)}, u32[]{:S(2)}) collective-permute-start(bf16[4,208,384]{2,1,0:T(8,128)(2,1)S(1)} %pad_maximum_fusion.refs_0_), channel_id=1, source_target_pairs={{0,4},{1,3},{2,6},{3,1},{4,0},{5,7},{6,2},{7,5},{8,12},{9,11},{10,... | collective-permute-start | bytes 1916936 | tf_op jit(solution)/shard_map/ppermute | solution.py:454
  49.4 11.7 %copy-start.16 = (bf16[4,208,384]{2,1,0:T(8,128)(2,1)}, bf16[4,208,384]{2,1,0:T(8,128)(2,1)S(1)}, u32[]{:S(2)}) copy-start(bf16[4,208,384]{2,1,0:T(8,128)(2,1)S(1)} %collective-permute-done.6.refs_2_) | copy-start | bytes 1916932
  49.4 13.6 %collective-permute-start.7 = (bf16[4,208,384]{2,1,0:T(8,128)(2,1)}, bf16[4,208,384]{2,1,0:T(8,128)(2,1)}, u32[]{:S(2)}, u32[]{:S(2)}) collective-permute-start(bf16[4,208,384]{2,1,0:T(8,128)(2,1)} %collective-permute-done.5.refs_1_), channel_id=1, source_target_pairs={{0,4},{1,3},{2,6},{3,1},{4,0},{5,7},{6,2},{7,5},{8,12},{9,11},{10,... | collective-permute-start | bytes 1916936 | tf_op jit(solution)/shard_map/ppermute | solution.py:454
  50.6 12.5 %collective-permute-start.8 = (bf16[4,208,384]{2,1,0:T(8,128)(2,1)S(1)}, bf16[4,208,384]{2,1,0:T(8,128)(2,1)}, u32[]{:S(2)}, u32[]{:S(2)}) collective-permute-start(bf16[4,208,384]{2,1,0:T(8,128)(2,1)S(1)} %pad_maximum_fusion.refs_0_), channel_id=1, source_target_pairs={{0,1},{1,0},{2,3},{3,2},{4,5},{5,4},{6,7},{7,6},{8,9},{9,8},{10,11... | collective-permute-start | bytes 1916936 | tf_op jit(solution)/shard_map/ppermute | solution.py:454
  61.1 27.3 %collective-permute-start.13 = (bf16[4,192,768]{2,1,0:T(8,128)(2,1)}, bf16[4,192,768]{2,1,0:T(8,128)(2,1)S(1)}, u32[]{:S(2)}, u32[]{:S(2)}) collective-permute-start(bf16[4,192,768]{2,1,0:T(8,128)(2,1)} %bitcast.55), channel_id=1, source_target_pairs={{0,4},{1,5},{2,6},{3,7},{4,0},{5,1},{6,2},{7,3},{8,12},{9,13},{10,... | collective-permute-start | bytes 3538952 | tf_op jit(solution)/shard_map/ppermute | solution.py:454
  62.6 2.4 collective-permute-start.9
  62.6 3.3 collective-permute-start.10
  63.1 3.7 collective-permute-start.11
  63.1 24.6 %collective-permute-start.12 = (bf16[400,768]{1,0:T(8,128)(2,1)S(1)}, bf16[400,768]{1,0:T(8,128)(2,1)S(1)}, u32[]{:S(2)}, u32[]{:S(2)}) collective-permute-start(bf16[400,768]{1,0:T(8,128)(2,1)S(1)} %copy-done), channel_id=1, source_target_pairs={{0,2},{1,3},{2,0},{3,1},{4,6},{5,7},{6,4},{7,5},{8,10},{9,11},{10,... | collective-permute-start | bytes 1843208 | tf_op jit(solution)/shard_map/ppermute | solution.py:454
  65.0 27.4 %collective-permute-start.15 = (bf16[400,768]{1,0:T(8,128)(2,1)S(1)}, bf16[400,768]{1,0:T(8,128)(2,1)S(1)}, u32[]{:S(2)}, u32[]{:S(2)}) collective-permute-start(bf16[400,768]{1,0:T(8,128)(2,1)S(1)} %copy-done), channel_id=1, source_target_pairs={{0,1},{1,0},{2,3},{3,2},{4,5},{5,4},{6,7},{7,6},{8,9},{9,8},{10,11... | collective-permute-start | bytes 1843208 | tf_op jit(solution)/shard_map/ppermute | solution.py:454
  87.7 27.7 %copy-start.2 = (bf16[400,768]{1,0:T(8,128)(2,1)}, bf16[400,768]{1,0:T(8,128)(2,1)S(1)}, u32[]{:S(2)}) copy-start(bf16[400,768]{1,0:T(8,128)(2,1)S(1)} %collective-permute-done.12.refs_5_.g_a_ref) | copy-start | bytes 1843204
  89.4 26.4 %copy-start.1 = (bf16[400,768]{1,0:T(8,128)(2,1)S(1)}, bf16[400,768]{1,0:T(8,128)(2,1)}, u32[]{:S(2)}) copy-start(bf16[400,768]{1,0:T(8,128)(2,1)} %get-tuple-element.233.h_a_ref.refs_0_.refs_3_) | copy-start | bytes 1843204
  89.4 3.0 collective-permute-start.14
  89.5 16.6 %collective-permute-start.16 = (bf16[400,768]{1,0:T(8,128)(2,1)}, bf16[400,768]{1,0:T(8,128)(2,1)}, u32[]{:S(2)}, u32[]{:S(2)}) collective-permute-start(bf16[400,768]{1,0:T(8,128)(2,1)} %get-tuple-element.233.h_a_ref.refs_0_.refs_3_), channel_id=1, source_target_pairs={{0,2},{1,3},{2,0},{3,1},{4,6},{5,7},{6,4},{7,5},{8,10},{9,11},{10,... | collective-permute-start | bytes 1843208 | tf_op jit(solution)/shard_map/ppermute | solution.py:454
  90.9 16.1 %collective-permute-start.17 = (bf16[400,768]{1,0:T(8,128)(2,1)S(1)}, bf16[400,768]{1,0:T(8,128)(2,1)}, u32[]{:S(2)}, u32[]{:S(2)}) collective-permute-start(bf16[400,768]{1,0:T(8,128)(2,1)S(1)} %copy-done), channel_id=1, source_target_pairs={{0,4},{1,5},{2,6},{3,7},{4,0},{5,1},{6,2},{7,3},{8,12},{9,13},{10,... | collective-permute-start | bytes 1843208 | tf_op jit(solution)/shard_map/ppermute | solution.py:454
  113.9 38.6 %collective-permute-start.21 = (bf16[4,400,768]{2,1,0:T(8,128)(2,1)}, bf16[4,400,768]{2,1,0:T(8,128)(2,1)}, u32[]{:S(2)}, u32[]{:S(2)}) collective-permute-start(bf16[4,400,768]{2,1,0:T(8,128)(2,1)} %bitcast.66), channel_id=1, source_target_pairs={{0,2},{1,5},{2,0},{3,7},{4,6},{5,1},{6,4},{7,3},{8,10},{9,13},{10,... | collective-permute-start | bytes 7372808 | tf_op jit(solution)/shard_map/ppermute | solution.py:454
  115.4 2.9 collective-permute-start.19
  115.4 3.1 collective-permute-start.18
  115.9 27.9 %collective-permute-start.20 = (bf16[400,768]{1,0:T(8,128)(2,1)S(1)}, bf16[400,768]{1,0:T(8,128)(2,1)S(1)}, u32[]{:S(2)}, u32[]{:S(2)}) collective-permute-start(bf16[400,768]{1,0:T(8,128)(2,1)S(1)} %copy-done.1), channel_id=1, source_target_pairs={{0,4},{1,3},{2,6},{3,1},{4,0},{5,7},{6,2},{7,5},{8,12},{9,11},{10,... | collective-permute-start | bytes 1843208 | tf_op jit(solution)/shard_map/ppermute | solution.py:454
  117.4 128.5 %all-gather.19.cloned.1.call-start = ((), (), s32[]{:S(2)}) async-start(), calls=%async_computation.3 | async-start | bytes 3072000 | tf_op jit(solution)/shard_map/all_gather | solution.py:1554
  117.4 61.8 %collective-permute-start.23 = (bf16[4,400,768]{2,1,0:T(8,128)(2,1)}, bf16[4,400,768]{2,1,0:T(8,128)(2,1)}, u32[]{:S(2)}, u32[]{:S(2)}) collective-permute-start(bf16[4,400,768]{2,1,0:T(8,128)(2,1)} %bitcast.67), channel_id=1, source_target_pairs={{0,1},{1,0},{2,3},{3,2},{4,5},{5,4},{6,7},{7,6},{8,9},{9,8},{10,11... | collective-permute-start | bytes 7372808 | tf_op jit(solution)/shard_map/ppermute | solution.py:454
  152.5 30.2 %collective-permute-start.22 = (bf16[4,400,768]{2,1,0:T(8,128)(2,1)}, bf16[4,400,768]{2,1,0:T(8,128)(2,1)S(1)}, u32[]{:S(2)}, u32[]{:S(2)}) collective-permute-start(bf16[4,400,768]{2,1,0:T(8,128)(2,1)} %collective-permute-done.21.refs_5_.refs_6_), channel_id=1, source_target_pairs={{0,4},{1,3},{2,6},{3,1},{4,0},{5,7},{6,2},{7,5},{8,12},{9,11},{10,... | collective-permute-start | bytes 7372808 | tf_op jit(solution)/shard_map/ppermute | solution.py:454
  154.0 28.6 %collective-permute-start.24 = (bf16[4,400,768]{2,1,0:T(8,128)(2,1)}, bf16[4,400,768]{2,1,0:T(8,128)(2,1)}, u32[]{:S(2)}, u32[]{:S(2)}) collective-permute-start(bf16[4,400,768]{2,1,0:T(8,128)(2,1)} %collective-permute-done.21.refs_5_.refs_6_), channel_id=1, source_target_pairs={{0,1},{1,0},{2,3},{3,2},{4,5},{5,4},{6,7},{7,6},{8,9},{9,8},{10,11... | collective-permute-start | bytes 7372808 | tf_op jit(solution)/shard_map/ppermute | solution.py:454
  182.7 67.3 %copy-start.4 = (bf16[4,400,768]{2,1,0:T(8,128)(2,1)}, bf16[4,400,768]{2,1,0:T(8,128)(2,1)S(1)}, u32[]{:S(2)}) copy-start(bf16[4,400,768]{2,1,0:T(8,128)(2,1)S(1)} %collective-permute-done.22.refs_9_.refs_5_) | copy-start | bytes 7372804
  182.7 2.3 collective-permute-start.25
  187.0 5.0 %collective-permute-start.26 = (bf16[4,400,768]{2,1,0:T(8,128)(2,1)}, bf16[4,400,768]{2,1,0:T(8,128)(2,1)}, u32[]{:S(2)}, u32[]{:S(2)}) collective-permute-start(bf16[4,400,768]{2,1,0:T(8,128)(2,1)} %bitcast.33.refs_0_), channel_id=1, source_target_pairs={{0,1},{1,0},{2,3},{3,2},{4,5},{5,4},{6,7},{7,6},{8,9},{9,8},{10,11... | collective-permute-start | bytes 7372808 | tf_op jit(solution)/shard_map/ppermute | solution.py:454
  189.1 102.2 %all-gather.21.cloned.1.call-start = ((), (), s32[]{:S(2)}) async-start(), calls=%async_computation.4 | async-start | bytes 3072000 | tf_op jit(solution)/shard_map/all_gather | solution.py:1580
  189.2 15.6 %collective-permute-start.27 = (bf16[400,768]{1,0:T(8,128)(2,1)}, bf16[400,768]{1,0:T(8,128)(2,1)S(1)}, u32[]{:S(2)}, u32[]{:S(2)}) collective-permute-start(bf16[400,768]{1,0:T(8,128)(2,1)} %get-tuple-element.276), channel_id=1, source_target_pairs={{0,1},{1,0},{2,3},{3,2},{4,5},{5,4},{6,7},{7,6},{8,9},{9,8},{10,11... | collective-permute-start | bytes 1843208 | tf_op jit(solution)/shard_map/ppermute | solution.py:454
  189.2 16.6 %collective-permute-start.28 = (bf16[400,768]{1,0:T(8,128)(2,1)}, bf16[400,768]{1,0:T(8,128)(2,1)}, u32[]{:S(2)}, u32[]{:S(2)}) collective-permute-start(bf16[400,768]{1,0:T(8,128)(2,1)} %add_convert_fusion.2), channel_id=1, source_target_pairs={{0,2},{1,3},{2,0},{3,1},{4,6},{5,7},{6,4},{7,5},{8,10},{9,11},{10,... | collective-permute-start | bytes 1843208 | tf_op jit(solution)/shard_map/ppermute | solution.py:454
  210.9 6.9 %collective-permute-start.29 = (bf16[128,768]{1,0:T(8,128)(2,1)}, bf16[128,768]{1,0:T(8,128)(2,1)S(1)}, u32[]{:S(2)}, u32[]{:S(2)}) collective-permute-start(bf16[128,768]{1,0:T(8,128)(2,1)} %get-tuple-element.284), channel_id=1, source_target_pairs={{0,4},{1,5},{2,6},{3,7},{4,0},{5,1},{6,2},{7,3},{8,12},{9,13},{10,... | collective-permute-start | bytes 589832 | tf_op jit(solution)/shard_map/ppermute | solution.py:454
  217.7 30.2 %collective-permute-start.30 = (bf16[4,400,768]{2,1,0:T(8,128)(2,1)}, bf16[4,400,768]{2,1,0:T(8,128)(2,1)}, u32[]{:S(2)}, u32[]{:S(2)}) collective-permute-start(bf16[4,400,768]{2,1,0:T(8,128)(2,1)} %bitcast.33.refs_0_), channel_id=1, source_target_pairs={{0,2},{1,5},{2,0},{3,7},{4,6},{5,1},{6,4},{7,3},{8,10},{9,13},{10,... | collective-permute-start | bytes 7372808 | tf_op jit(solution)/shard_map/ppermute | solution.py:454
  219.2 159.0 %all-gather.23.cloned.1.call-start = ((), (), s32[]{:S(2)}) async-start(), calls=%async_computation.5 | async-start | bytes 2654208 | tf_op jit(solution)/shard_map/all_gather | solution.py:1647
  247.9 43.4 %collective-permute-start.32 = (bf16[4,208,1536]{2,1,0:T(8,128)(2,1)}, bf16[4,208,1536]{2,1,0:T(8,128)(2,1)}, u32[]{:S(2)}, u32[]{:S(2)}) collective-permute-start(bf16[4,208,1536]{2,1,0:T(8,128)(2,1)} %get-tuple-element.302), channel_id=1, source_target_pairs={{0,1},{1,0},{2,3},{3,2},{4,5},{5,4},{6,7},{7,6},{8,9},{9,8},{10,11... | collective-permute-start | bytes 7667720 | tf_op jit(solution)/shard_map/ppermute | solution.py:454
  247.9 12.2 %collective-permute-start.31 = (bf16[4,400,768]{2,1,0:T(8,128)(2,1)}, bf16[4,400,768]{2,1,0:T(8,128)(2,1)}, u32[]{:S(2)}, u32[]{:S(2)}) collective-permute-start(bf16[4,400,768]{2,1,0:T(8,128)(2,1)} %collective-permute-done.30.refs_1_.refs_0_), channel_id=1, source_target_pairs={{0,1},{1,0},{2,3},{3,2},{4,5},{5,4},{6,7},{7,6},{8,9},{9,8},{10,11... | collective-permute-start | bytes 7372808 | tf_op jit(solution)/shard_map/ppermute | solution.py:454
  248.5 42.9 %collective-permute-start.33 = (bf16[4,400,768]{2,1,0:T(8,128)(2,1)}, bf16[4,400,768]{2,1,0:T(8,128)(2,1)}, u32[]{:S(2)}, u32[]{:S(2)}) collective-permute-start(bf16[4,400,768]{2,1,0:T(8,128)(2,1)} %collective-permute-done.30.refs_1_.refs_0_), channel_id=1, source_target_pairs={{0,4},{1,3},{2,6},{3,1},{4,0},{5,7},{6,2},{7,5},{8,12},{9,11},{10,... | collective-permute-start | bytes 7372808 | tf_op jit(solution)/shard_map/ppermute | solution.py:454
  249.9 41.4 %collective-permute-start.34 = (bf16[4,400,768]{2,1,0:T(8,128)(2,1)}, bf16[4,400,768]{2,1,0:T(8,128)(2,1)}, u32[]{:S(2)}, u32[]{:S(2)}) collective-permute-start(bf16[4,400,768]{2,1,0:T(8,128)(2,1)} %bitcast.60), channel_id=1, source_target_pairs={{0,1},{1,0},{2,3},{3,2},{4,5},{5,4},{6,7},{7,6},{8,9},{9,8},{10,11... | collective-permute-start | bytes 7372808 | tf_op jit(solution)/shard_map/ppermute | solution.py:454
  249.9 41.4 %collective-permute-start.35 = (bf16[4,400,768]{2,1,0:T(8,128)(2,1)S(1)}, bf16[4,400,768]{2,1,0:T(8,128)(2,1)}, u32[]{:S(2)}, u32[]{:S(2)}) collective-permute-start(bf16[4,400,768]{2,1,0:T(8,128)(2,1)S(1)} %collective-permute-done.22.refs_9_.refs_5_), channel_id=1, source_target_pairs={{0,1},{1,0},{2,3},{3,2},{4,5},{5,4},{6,7},{7,6},{8,9},{9,8},{10,11... | collective-permute-start | bytes 7372808 | tf_op jit(solution)/shard_map/ppermute | solution.py:454
  291.4 7.7 %collective-permute-start.36 = (bf16[4,400,768]{2,1,0:T(8,128)(2,1)}, bf16[4,400,768]{2,1,0:T(8,128)(2,1)S(1)}, u32[]{:S(2)}, u32[]{:S(2)}) collective-permute-start(bf16[4,400,768]{2,1,0:T(8,128)(2,1)} %bitcast.63), channel_id=1, source_target_pairs={{0,1},{1,0},{2,3},{3,2},{4,5},{5,4},{6,7},{7,6},{8,9},{9,8},{10,11... | collective-permute-start | bytes 7372808 | tf_op jit(solution)/shard_map/ppermute | solution.py:454
  291.5 8.5 %collective-permute-start.37 = (bf16[4,400,768]{2,1,0:T(8,128)(2,1)}, bf16[4,400,768]{2,1,0:T(8,128)(2,1)}, u32[]{:S(2)}, u32[]{:S(2)}) collective-permute-start(bf16[4,400,768]{2,1,0:T(8,128)(2,1)} %collective-permute-done.33.refs_3_.refs_1_), channel_id=1, source_target_pairs={{0,1},{1,0},{2,3},{3,2},{4,5},{5,4},{6,7},{7,6},{8,9},{9,8},{10,11... | collective-permute-start | bytes 7372808 | tf_op jit(solution)/shard_map/ppermute | solution.py:454
  300.0 33.2 %collective-permute-start.38 = (bf16[4,208,384]{2,1,0:T(8,128)(2,1)}, bf16[4,208,384]{2,1,0:T(8,128)(2,1)}, u32[]{:S(2)}, u32[]{:S(2)}) collective-permute-start(bf16[4,208,384]{2,1,0:T(8,128)(2,1)} %get-tuple-element.327), channel_id=1, source_target_pairs={{0,2},{1,3},{2,0},{3,1},{4,6},{5,7},{6,4},{7,5},{8,10},{9,11},{10,... | collective-permute-start | bytes 1916936 | tf_op jit(solution)/shard_map/ppermute | solution.py:454
  301.4 31.8 %collective-permute-start.39 = (bf16[4,208,384]{2,1,0:T(8,128)(2,1)}, bf16[4,208,384]{2,1,0:T(8,128)(2,1)}, u32[]{:S(2)}, u32[]{:S(2)}) collective-permute-start(bf16[4,208,384]{2,1,0:T(8,128)(2,1)} %broadcast_select_fusion.2), channel_id=1, source_target_pairs={{0,4},{1,5},{2,6},{3,7},{4,0},{5,1},{6,2},{7,3},{8,12},{9,13},{10,... | collective-permute-start | bytes 1916936 | tf_op jit(solution)/shard_map/ppermute | solution.py:454
  302.9 30.3 %collective-permute-start.40 = (bf16[4,208,384]{2,1,0:T(8,128)(2,1)}, bf16[4,208,384]{2,1,0:T(8,128)(2,1)}, u32[]{:S(2)}, u32[]{:S(2)}) collective-permute-start(bf16[4,208,384]{2,1,0:T(8,128)(2,1)} %get-tuple-element.329), channel_id=1, source_target_pairs={{0,6},{1,7},{2,4},{3,5},{4,2},{5,3},{6,0},{7,1},{8,14},{9,15},{10,... | collective-permute-start | bytes 1916936 | tf_op jit(solution)/shard_map/ppermute | solution.py:454
  334.2 5.2 %collective-permute-start.41 = (bf16[384,768]{1,0:T(8,128)(2,1)}, bf16[384,768]{1,0:T(8,128)(2,1)}, u32[]{:S(2)}, u32[]{:S(2)}) collective-permute-start(bf16[384,768]{1,0:T(8,128)(2,1)} %get-tuple-element.339), channel_id=1, source_target_pairs={{0,1},{1,0},{2,3},{3,2},{4,5},{5,4},{6,7},{7,6},{8,9},{9,8},{10,11... | collective-permute-start | bytes 1769480 | tf_op jit(solution)/shard_map/ppermute | solution.py:454
  334.3 6.3 %collective-permute-start.42 = (bf16[384,768]{1,0:T(8,128)(2,1)}, bf16[384,768]{1,0:T(8,128)(2,1)S(1)}, u32[]{:S(2)}, u32[]{:S(2)}) collective-permute-start(bf16[384,768]{1,0:T(8,128)(2,1)} %get-tuple-element.340), channel_id=1, source_target_pairs={{0,1},{1,0},{2,3},{3,2},{4,5},{5,4},{6,7},{7,6},{8,9},{9,8},{10,11... | collective-permute-start | bytes 1769480 | tf_op jit(solution)/shard_map/ppermute | solution.py:454
  340.6 37.5 %collective-permute-start.46 = (bf16[384,768]{1,0:T(8,128)(2,1)S(1)}, bf16[384,768]{1,0:T(8,128)(2,1)S(1)}, u32[]{:S(2)}, u32[]{:S(2)}) collective-permute-start(bf16[384,768]{1,0:T(8,128)(2,1)S(1)} %add_convert_fusion.4), channel_id=1, source_target_pairs={{0,2},{1,3},{2,0},{3,1},{4,6},{5,7},{6,4},{7,5},{8,10},{9,11},{10,... | collective-permute-start | bytes 1769480 | tf_op jit(solution)/shard_map/ppermute | solution.py:454
  342.2 35.9 %collective-permute-start.43 = (bf16[208,384]{1,0:T(8,128)(2,1)S(1)}, bf16[208,384]{1,0:T(8,128)(2,1)S(1)}, u32[]{:S(2)}, u32[]{:S(2)}) collective-permute-start(bf16[208,384]{1,0:T(8,128)(2,1)S(1)} %get-tuple-element.356), channel_id=1, source_target_pairs={{0,8},{1,9},{2,10},{3,11},{4,12},{5,13},{6,14},{7,15},{8,16},{9,17... | collective-permute-start | bytes 479240 | tf_op jit(solution)/shard_map/ppermute | solution.py:454
  342.2 35.9 %collective-permute-start.44 = (bf16[208,384]{1,0:T(8,128)(2,1)S(1)}, bf16[208,384]{1,0:T(8,128)(2,1)S(1)}, u32[]{:S(2)}, u32[]{:S(2)}) collective-permute-start(bf16[208,384]{1,0:T(8,128)(2,1)S(1)} %get-tuple-element.357), channel_id=1, source_target_pairs={{0,16},{1,17},{2,18},{3,19},{4,20},{5,21},{6,22},{7,23},{8,24},{9,... | collective-permute-start | bytes 479240 | tf_op jit(solution)/shard_map/ppermute | solution.py:454
  344.1 34.0 %collective-permute-start.45 = (bf16[208,384]{1,0:T(8,128)(2,1)S(1)}, bf16[208,384]{1,0:T(8,128)(2,1)S(1)}, u32[]{:S(2)}, u32[]{:S(2)}) collective-permute-start(bf16[208,384]{1,0:T(8,128)(2,1)S(1)} %get-tuple-element.358), channel_id=1, source_target_pairs={{0,24},{1,25},{2,26},{3,27},{4,28},{5,29},{6,30},{7,31},{8,0},{9,1... | collective-permute-start | bytes 479240 | tf_op jit(solution)/shard_map/ppermute | solution.py:454
  378.3 8.9 %collective-permute-start.47 = (bf16[208,384]{1,0:T(8,128)(2,1)S(1)}, bf16[208,384]{1,0:T(8,128)(2,1)S(1)}, u32[]{:S(2)}, u32[]{:S(2)}) collective-permute-start(bf16[208,384]{1,0:T(8,128)(2,1)S(1)} %add_convert_fusion.5), channel_id=1, source_target_pairs={{0,2},{1,3},{2,0},{3,1},{4,6},{5,7},{6,4},{7,5},{8,10},{9,11},{10,... | collective-permute-start | bytes 479240 | tf_op jit(solution)/shard_map/ppermute | solution.py:454
  379.0 8.1 %collective-permute-start.48 = (bf16[208,384]{1,0:T(8,128)(2,1)S(1)}, bf16[208,384]{1,0:T(8,128)(2,1)S(1)}, u32[]{:S(2)}, u32[]{:S(2)}) collective-permute-start(bf16[208,384]{1,0:T(8,128)(2,1)S(1)} %add_convert_fusion.5), channel_id=1, source_target_pairs={{0,4},{1,5},{2,6},{3,7},{4,0},{5,1},{6,2},{7,3},{8,12},{9,13},{10,... | collective-permute-start | bytes 479240 | tf_op jit(solution)/shard_map/ppermute | solution.py:454
  380.5 7.3 %collective-permute-start.49 = (bf16[208,384]{1,0:T(8,128)(2,1)S(1)}, bf16[208,384]{1,0:T(8,128)(2,1)S(1)}, u32[]{:S(2)}, u32[]{:S(2)}) collective-permute-start(bf16[208,384]{1,0:T(8,128)(2,1)S(1)} %add_convert_fusion.5), channel_id=1, source_target_pairs={{0,6},{1,7},{2,4},{3,5},{4,2},{5,3},{6,0},{7,1},{8,14},{9,15},{10,... | collective-permute-start | bytes 479240 | tf_op jit(solution)/shard_map/ppermute | solution.py:454
  388.2 2.1 collective-permute-start.50
  (27 other events, 111.2 us)
Sparse Core Ops, SparseCore 0:
  28.9 32.0 all-gather.12
  62.6 51.2 all-gather.14
  117.5 49.3 all-gather.16
  189.2 49.7 all-gather.18
  240.4 50.8 all-gather.20
  340.8 31.1 all-gather.22

commit v5 on v4

--- a/solution.py
+++ b/solution.py
@@ -496,71 +496,87 @@
     base_ref,
     *refs,
 ):
-    h_refs, g_refs = refs[:blocks], refs[blocks : 2 * blocks]
-    refs = refs[2 * blocks :]
+    block_refs, refs = refs[: 2 * blocks], refs[2 * blocks :]
     more_refs, refs = refs[:more], refs[more:]
     wg_ref, wu_ref, wd_ref = refs[:3]
-    moe_refs, dx_refs, refs = refs[3 : 3 + blocks], refs[3 + blocks : 3 + 2 * blocks], refs[3 + 2 * blocks :]
+    results, refs = refs[3 : 3 + 2 * blocks], refs[3 + 2 * blocks :]
     (
         rank_sc,
         prob_sc,
         x_sc,
-        gd_sc,
         gate_sc,
         y_sc,
         acc_sc,
         dgate_sc,
-        ysel_sc,
-        dsel_sc,
+        sel_sc,
         drp_sc,
-    ) = refs[:11]
+        in_sc,
+        out_sc,
+        in_sems,
+        out_sems,
+    ) = refs[:13]
     e = pl.program_id(0)
     f = pl.program_id(1)
     experts = pl.num_programs(0)
     base = base_ref[0]
     copies = [
         pltpu.make_async_copy(source, into, refs[-1].at[i])
-        for i, (source, into) in enumerate(zip(more_refs, refs[11:]))
+        for i, (source, into) in enumerate(zip(more_refs, refs[13:]))
+    ]
+
+    arrivals = [
+        pltpu.make_async_copy(
+            block_refs[side * blocks + b],
+            in_sc.at[b, :, side * D : (side + 1) * D],
+            in_sems.at[side, b],
+        )
+        for b in range(blocks)
+        for side in range(2)
     ]
 
     @pl.when((e == 0) & (f == 0))
     def _():
-        for one in copies:
+        for one in arrivals + copies:
             one.start()
+        drp_sc[...] = jnp.zeros_like(drp_sc)
+        count = x_sc.shape[0]
+        rows = []
         for b in range(blocks):
-            rank_sc[b] = g_refs[b][TOK_DEV:, :TOK_DEV].astype(F32)
-            prob_sc[b] = h_refs[b][TOK_DEV:, :TOK_DEV].astype(F32) + h_refs[b][
-                TOK_DEV:, TOK_DEV:
+            for one in arrivals[2 * b : 2 * b + 2]:
+                one.wait()
+            rank_sc[b] = in_sc[b, TOK_DEV:, D : D + TOK_DEV].astype(F32)
+            prob_sc[b] = in_sc[b, TOK_DEV:, :TOK_DEV].astype(F32) + in_sc[
+                b, TOK_DEV:, TOK_DEV:D
             ].astype(F32)
-        drp_sc[...] = jnp.zeros_like(drp_sc)
+            hots = []
+            for i in range(count):
+                hot = one_hot_rows(rank_sc[b, pl.ds(base + i, 1), :])
+                gate_sc[i, b * SLOT : (b + 1) * SLOT, :] = jnp.sum(
+                    hot * prob_sc[b, pl.ds(base + i, 1), :], -1, keepdims=True
+                )
+                hots.append(hot)
+            hot = jnp.concatenate(hots, 0).astype(BF)
+            rows.append(jnp.dot(hot, in_sc[b, :TOK_DEV, :], preferred_element_type=F32))
+            if b % 2:
+                span = slice((b - 1) * SLOT, (b + 1) * SLOT)
+                for i in range(count):
+                    of = slice(i * SLOT, (i + 1) * SLOT)
+                    x_sc[i, span, :] = jnp.concatenate([v[of] for v in rows[-2:]], 0).astype(BF)
 
     @pl.when(f == 0)
     def _():
-        for pair in range(blocks // 2):
-            rows_x, rows_g = [], []
-            for b in (2 * pair, 2 * pair + 1):
-                hot = one_hot_rows(rank_sc[b, pl.ds(base + e, 1), :])
-                gate_sc[b * SLOT : (b + 1) * SLOT, :] = jnp.sum(
-                    hot * prob_sc[b, pl.ds(base + e, 1), :], -1, keepdims=True
-                )
-                hot = hot.astype(BF)
-                rows_x.append(jnp.dot(hot, h_refs[b][:TOK_DEV, :], preferred_element_type=F32))
-                rows_g.append(jnp.dot(hot, g_refs[b][:TOK_DEV, :], preferred_element_type=F32))
-            span = slice(pair * 2 * SLOT, (pair + 1) * 2 * SLOT)
-            x_sc[span, :] = jnp.concatenate(rows_x, 0).astype(BF)
-            gd_sc[span, :] = jnp.concatenate(rows_g, 0).astype(BF)
         y_sc[...] = jnp.zeros_like(y_sc)
         acc_sc[...] = jnp.zeros_like(acc_sc)
         dgate_sc[...] = jnp.zeros_like(dgate_sc)
 
-    rows = x_sc[...]
+    rows = x_sc[e, :, :D]
     gate_pre = jnp.dot(rows, wg_ref[0], preferred_element_type=F32)
     up_pre = jnp.dot(rows, wu_ref[0], preferred_element_type=F32)
-    back = contract(gd_sc[...], wd_ref[0], 1, 1)
+    back = contract(x_sc[e, :, D:], wd_ref[0], 1, 1)
     swish, slope = swish_parts(gate_pre)
     inner = (swish * up_pre).astype(BF)
     dgate_sc[...] += jnp.sum(back * inner.astype(F32), -1, keepdims=True)
-    back = back * gate_sc[...]
+    back = back * gate_sc[e]
     dgate_pre = (back * up_pre * slope).astype(BF)
     dup_pre = (back * swish).astype(BF)
     y_sc[...] += jnp.dot(inner, wd_ref[0], preferred_element_type=F32)
@@ -571,8 +587,8 @@
         for b in range(blocks):
             span = slice(b * SLOT, (b + 1) * SLOT)
             into = pl.ds(pl.multiple_of(e * SLOT, 8), SLOT)
-            ysel_sc[b, into, :] = y_sc[span, :] * gate_sc[span, :]
-            dsel_sc[b, into, :] = acc_sc[span, :]
+            sel_sc[b, into, :D] = y_sc[span, :] * gate_sc[e, span, :]
+            sel_sc[b, into, D:] = acc_sc[span, :]
             hot = one_hot_rows(rank_sc[b, pl.ds(base + e, 1), :])
             drp_sc[b, pl.ds(base + e, 1), :] = jnp.sum(hot * dgate_sc[span, :], 0, keepdims=True)
 
@@ -580,38 +596,47 @@
     def _():
         for one in copies:
             one.wait()
+        leaving = []
         for b in range(blocks):
             side, at = divmod(b, blocks // 2)
-            moe_out, dx_out = moe_refs[b], dx_refs[b]
+            moe_out, dx_out = out_sc.at[0, b], out_sc.at[1, b]
             hot = jnp.concatenate(
                 [
                     one_hot_rows(rank_sc[b, pl.ds(base + i, 1), :])
-                    for i in range(ysel_sc.shape[1] // SLOT)
+                    for i in range(x_sc.shape[0])
                 ],
                 0,
             ).astype(BF)
-            moe = contract(hot, ysel_sc[b].astype(BF), 0, 0)
-            dx = contract(hot, dsel_sc[b].astype(BF), 0, 0)
+            both = contract(hot, sel_sc[b].astype(BF), 0, 0)
+            moe, dx = both[:, :D], both[:, D:]
             drp = drp_sc[b]
             if more:
-                shared = refs[11 + 2 * at : 13 + 2 * at]
-                moe_before, dx_before = refs[15 + b], refs[15 + blocks + b]
-                moe = moe + shared[0][side] + moe_before[...].astype(F32)
-                dx = dx + shared[1][side] + dx_before[:TOK_DEV, :].astype(F32)
+                shared = refs[13 + 2 * at : 15 + 2 * at]
+                moe_before, dx_before = refs[17 + b], refs[17 + blocks + b]
+                moe = moe + shared[0][side].astype(F32) + moe_before[...].astype(F32)
+                dx = dx + shared[1][side].astype(F32) + dx_before[:TOK_DEV, :].astype(F32)
                 drp = drp + dx_before[TOK_DEV:, :TOK_DEV].astype(F32)
                 drp = drp + dx_before[TOK_DEV:, TOK_DEV:].astype(F32)
-            moe_out[...] = moe.astype(BF)
+            moe_out[:TOK_DEV, :] = moe.astype(BF)
             dx_out[:TOK_DEV, :] = dx.astype(BF)
             high = drp.astype(BF)
             dx_out[TOK_DEV:, :TOK_DEV] = high
             dx_out[TOK_DEV:, TOK_DEV:] = (drp - high.astype(F32)).astype(BF)
+            sent = (
+                pltpu.make_async_copy(moe_out.at[:TOK_DEV], results[b], out_sems.at[0, b]),
+                pltpu.make_async_copy(dx_out, results[blocks + b], out_sems.at[1, b]),
+            )
+            for one in sent:
+                one.start()
+            leaving += sent
+        for one in leaving:
+            one.wait()
 
 
 def group_experts(base, first, experts, h_group, g_group, more, w_gate, w_up, w_down):
     blocks = len(h_group)
     ff = w_gate.shape[2]
     tile = 512
-    whole = lambda *shape: pl.BlockSpec(shape, lambda e, f, s: (0,) * len(shape))
     results = [(TOK_DEV, D)] * blocks + [(ROWS, D)] * blocks
     return pl.pallas_call(
         functools.partial(group_kernel, blocks, len(more)),
@@ -619,26 +644,27 @@
         grid_spec=pltpu.PrefetchScalarGridSpec(
             num_scalar_prefetch=1,
             grid=(experts, ff // tile),
-            in_specs=[whole(ROWS, D)] * (2 * blocks)
-            + [pl.BlockSpec(memory_space=pl.ANY)] * len(more)
+            in_specs=[pl.BlockSpec(memory_space=pl.ANY)] * (2 * blocks + len(more))
             + [
                 pl.BlockSpec((1, D, tile), lambda e, f, s: (first + e, 0, f)),
                 pl.BlockSpec((1, D, tile), lambda e, f, s: (first + e, 0, f)),
                 pl.BlockSpec((1, tile, D), lambda e, f, s: (first + e, f, 0)),
             ],
-            out_specs=[whole(*s) for s in results],
+            out_specs=[pl.BlockSpec(memory_space=pltpu.HBM)] * len(results),
             scratch_shapes=[
                 pltpu.VMEM((blocks, EXPERTS, TOK_DEV), F32),
                 pltpu.VMEM((blocks, EXPERTS, TOK_DEV), F32),
-                pltpu.VMEM((blocks * SLOT, D), BF),
-                pltpu.VMEM((blocks * SLOT, D), BF),
-                pltpu.VMEM((blocks * SLOT, 1), F32),
+                pltpu.VMEM((experts, blocks * SLOT, 2 * D), BF),
+                pltpu.VMEM((experts, blocks * SLOT, 1), F32),
                 pltpu.VMEM((blocks * SLOT, D), F32),
                 pltpu.VMEM((blocks * SLOT, D), F32),
                 pltpu.VMEM((blocks * SLOT, 1), F32),
-                pltpu.VMEM((blocks, experts * SLOT, D), F32),
-                pltpu.VMEM((blocks, experts * SLOT, D), F32),
+                pltpu.VMEM((blocks, experts * SLOT, 2 * D), F32),
                 pltpu.VMEM((blocks, EXPERTS, TOK_DEV), F32),
+                pltpu.VMEM((blocks, ROWS, 2 * D), BF),
+                pltpu.VMEM((2, blocks, ROWS, D), BF),
+                pltpu.SemaphoreType.DMA((2, blocks)),
+                pltpu.SemaphoreType.DMA((2, blocks)),
             ]
             + [pltpu.VMEM(v.shape, v.dtype) for v in more]
             + [pltpu.SemaphoreType.DMA((max(1, len(more)),))],
@@ -649,7 +675,7 @@
     )(base, *h_group, *g_group, *more, w_gate, w_up, w_down)
 
 
-def shared_kernel(h_a_ref, h_b_ref, g_a_ref, g_b_ref, w_a_ref, w_b_ref, out_ref, dh_ref, h_sc, g_sc):
+def shared_kernel(h_a_ref, h_b_ref, g_a_ref, g_b_ref, w_a_ref, w_b_ref, out_ref, dh_ref, h_sc, g_sc, out_sc, dh_sc):
     for k, (h_ref, g_ref) in enumerate(((h_a_ref, g_a_ref), (h_b_ref, g_b_ref))):
         h_sc[k * TOK_DEV : (k + 1) * TOK_DEV, :] = h_ref[:TOK_DEV, :]
         g_sc[k * TOK_DEV : (k + 1) * TOK_DEV, :] = g_ref[:TOK_DEV, :]
@@ -667,14 +693,16 @@
         dgate_pre = (back * up_pre * slope).astype(BF)
         dup_pre = (back * swish).astype(BF)
         dh = contract(dgate_pre, w_gate, 1, 1) + contract(dup_pre, w_up, 1, 1)
-        for b in range(2):
-            rows = slice(b * TOK_DEV, (b + 1) * TOK_DEV)
-            out_ref[b] = out[rows] if k == 0 else out_ref[b] + out[rows]
-            dh_ref[b] = dh[rows] if k == 0 else dh_ref[b] + dh[rows]
+        if k == 0:
+            out_sc[...], dh_sc[...] = out, dh
+    for b in range(2):
+        rows = slice(b * TOK_DEV, (b + 1) * TOK_DEV)
+        out_ref[b] = (out_sc[rows, :] + out[rows]).astype(BF)
+        dh_ref[b] = (dh_sc[rows, :] + dh[rows]).astype(BF)
 
 
 def shared_rows(h_pair, g_pair, w_own, w_far):
-    rows = jax.ShapeDtypeStruct((2, TOK_DEV, D), F32)
+    rows = jax.ShapeDtypeStruct((2, TOK_DEV, D), BF)
     vmem = pl.BlockSpec(memory_space=pltpu.VMEM)
     return pl.pallas_call(
         shared_kernel,
@@ -684,6 +712,8 @@
         scratch_shapes=[
             pltpu.VMEM((2 * TOK_DEV, D), BF),
             pltpu.VMEM((2 * TOK_DEV, D), BF),
+            pltpu.VMEM((2 * TOK_DEV, D), F32),
+            pltpu.VMEM((2 * TOK_DEV, D), F32),
         ],
         compiler_params=pltpu.CompilerParams(vmem_limit_bytes=VMEM_LIMIT),
         cost_estimate=microseconds(8),
@@ -695,17 +725,29 @@
     per = h_parts[0].shape[0]
     copies = []
     for i in range(len(h_parts)):
-        into = pl.ds(i * per, per)
-        copies.append(
-            (
-                pltpu.make_async_copy(h_parts[i], h_buf.at[into], sems.at[0, i]),
-                pltpu.make_async_copy(g_parts[i], g_buf.at[into], sems.at[1, i]),
+        for k in range(per // 2):
+            at, into = pl.ds(2 * k, 2), pl.ds(i * per + 2 * k, 2)
+            number = i * (per // 2) + k
+            copies.append(
+                (
+                    pltpu.make_async_copy(h_parts[i].at[at], h_buf.at[into], sems.at[0, number]),
+                    pltpu.make_async_copy(g_parts[i].at[at], g_buf.at[into], sems.at[1, number]),
+                )
             )
-        )
     for pair in copies:
         for one in pair:
             one.start()
     return copies
+
+
+def each_pair(copies, work):
+    done = 0
+    for upto in [1, 2] + list(range(4, len(copies) + 1, 2)):
+        for pair in copies[done:upto]:
+            for one in pair:
+                one.wait()
+        lax.fori_loop(done, upto, work, 0, unroll=True)
+        done = upto
 
 
 def expert_slice_kernel(parts, more, pos_ref, *refs):
@@ -713,12 +755,12 @@
     weights = refs[2 * parts : 2 * parts + 3]
     refs = refs[2 * parts + 3 :]
     sums, refs = refs[: 3 * more], refs[3 * more :]
-    og_ref, ou_ref, od_ref, h_buf, g_buf, x_sc, gd_sc, rank_sc, prob_sc = refs[:9]
-    wg_ref, wu_ref, wd_ref, sems, w_sems = refs[9:]
+    outs, (buf, x_sc, gd_sc, rank_sc, prob_sc) = refs[:3], refs[3:8]
+    wg_ref, wu_ref, wd_ref, og_ref, ou_ref, od_ref, sems, w_sems, out_sems = refs[8:]
     base = pos_ref[0]
     experts, _, width = wg_ref.shape
     per = h_parts[0].shape[0]
-    copies = start_parts(h_parts, g_parts, h_buf, g_buf, sems)
+    copies = start_parts(h_parts, g_parts, buf.at[:, :, :D], buf.at[:, :, D:], sems)
     cols = pl.ds(pl.multiple_of(pos_ref[1] * width, width), width)
     loads = [
         pltpu.make_async_copy(weights[0].at[:, :, cols], wg_ref, w_sems.at[0]),
@@ -733,12 +775,12 @@
         one.start()
 
     def dispatch(pair, carry):
-        both_x, both_g = [], []
+        both = []
         for k in range(2):
             b = 2 * pair + k
-            rank_sc[k] = g_buf[b, TOK_DEV:, :TOK_DEV].astype(F32)
-            prob_sc[k] = h_buf[b, TOK_DEV:, :TOK_DEV].astype(F32) + h_buf[
-                b, TOK_DEV:, TOK_DEV:
+            rank_sc[k] = buf[b, TOK_DEV:, D : D + TOK_DEV].astype(F32)
+            prob_sc[k] = buf[b, TOK_DEV:, :TOK_DEV].astype(F32) + buf[
+                b, TOK_DEV:, TOK_DEV:D
             ].astype(F32)
             hots, gates = [], []
             for i in range(experts):
@@ -748,22 +790,16 @@
                 )
                 hots.append(hot)
             hot = jnp.concatenate(hots, 0).astype(BF)
-            both_x.append(jnp.dot(hot, h_buf[b, :TOK_DEV, :], preferred_element_type=F32))
-            both_g.append(
-                jnp.dot(hot, g_buf[b, :TOK_DEV, :], preferred_element_type=F32)
-                * jnp.concatenate(gates, 0)
-            )
+            rows = jnp.dot(hot, buf[b, :TOK_DEV, :], preferred_element_type=F32)
+            both.append((rows[:, :D], rows[:, D:] * jnp.concatenate(gates, 0)))
         into = pl.ds(pl.multiple_of(pair * 2 * SLOT, 2 * SLOT), 2 * SLOT)
         for i in range(experts):
             span = slice(i * SLOT, (i + 1) * SLOT)
-            x_sc[i, into, :] = jnp.concatenate([v[span] for v in both_x], 0).astype(BF)
-            gd_sc[i, into, :] = jnp.concatenate([v[span] for v in both_g], 0).astype(BF)
+            x_sc[i, into, :] = jnp.concatenate([v[0][span] for v in both], 0).astype(BF)
+            gd_sc[i, into, :] = jnp.concatenate([v[1][span] for v in both], 0).astype(BF)
         return carry
 
-    for i in range(parts):
-        for one in copies[i]:
-            one.wait()
-        lax.fori_loop(i * per // 2, (i + 1) * per // 2, dispatch, 0)
+    each_pair(copies, dispatch)
     for one in loads:
         one.wait()
 
@@ -785,9 +821,14 @@
             od_ref[i] += add_d
         else:
             og_ref[i], ou_ref[i], od_ref[i] = add_g, add_u, add_d
+        for k, source in enumerate((og_ref, ou_ref, od_ref)):
+            pltpu.make_async_copy(source.at[i], outs[k].at[i], out_sems.at[k, i]).start()
         return carry
 
-    lax.fori_loop(0, experts, products, 0)
+    lax.fori_loop(0, experts, products, 0, unroll=2 if experts % 2 == 0 else 1)
+    for i in range(experts):
+        for k, source in enumerate((og_ref, ou_ref, od_ref)):
+            pltpu.make_async_copy(source.at[i], outs[k].at[i], out_sems.at[k, i]).wait()
 
 
 def expert_slice_grads(pos, h_parts, g_parts, w_gate, w_up, w_down, width, sums=()):
@@ -795,26 +836,26 @@
     experts = w_gate.shape[0]
     blocks = parts * per
     shapes = ((experts, D, width), (experts, D, width), (experts, width, D))
-    vmem = pl.BlockSpec(memory_space=pltpu.VMEM)
     anywhere = pl.BlockSpec(memory_space=pl.ANY)
     return pl.pallas_call(
         functools.partial(expert_slice_kernel, parts, len(sums) // 3),
         out_shape=tuple(jax.ShapeDtypeStruct(s, F32) for s in shapes),
         in_specs=[pl.BlockSpec(memory_space=pltpu.SMEM)]
         + [anywhere] * (2 * parts + 3 + len(sums)),
-        out_specs=(vmem,) * 3,
+        out_specs=(pl.BlockSpec(memory_space=pltpu.HBM),) * 3,
         scratch_shapes=[
-            pltpu.VMEM((blocks, ROWS, D), BF),
-            pltpu.VMEM((blocks, ROWS, D), BF),
+            pltpu.VMEM((blocks, ROWS, 2 * D), BF),
             pltpu.VMEM((experts, blocks * SLOT, D), BF),
             pltpu.VMEM((experts, blocks * SLOT, D), BF),
             pltpu.VMEM((2, EXPERTS, TOK_DEV), F32),
             pltpu.VMEM((2, EXPERTS, TOK_DEV), F32),
         ]
         + [pltpu.VMEM(s, BF) for s in shapes]
+        + [pltpu.VMEM(s, F32) for s in shapes]
         + [
-            pltpu.SemaphoreType.DMA((2, parts)),
+            pltpu.SemaphoreType.DMA((2, blocks // 2)),
             pltpu.SemaphoreType.DMA((6,)),
+            pltpu.SemaphoreType.DMA((3, experts)),
         ],
         compiler_params=pltpu.CompilerParams(vmem_limit_bytes=VMEM_LIMIT),
         cost_estimate=microseconds(31),
@@ -827,6 +868,8 @@
     w_ref = refs[2 * parts]
     refs = refs[2 * parts + 1 :]
     sums, refs = refs[: 3 * more], refs[3 * more :]
+    if more:
+        mine_ref, refs = refs[0], refs[1:]
     og_ref, ou_ref, od_ref, h_buf, g_buf, inner_sc, wg_ref, wu_ref, wd_ref, sems = refs
     per = h_parts[0].shape[0]
     copies = start_parts(h_parts, g_parts, h_buf, g_buf, sems)
@@ -857,37 +900,41 @@
         od_ref[...] += contract(inner_sc[:, lanes], grads, 0, 0)
         return carry
 
-    for i in range(parts):
-        for one in copies[i]:
-            one.wait()
-        lax.fori_loop(i * per // 2, (i + 1) * per // 2, products, 0)
+    each_pair(copies, products)
+    if more:
+        rows = pl.ds(pl.multiple_of(pos_ref[2], 64), D // 4)
+        mine_ref[:, :256] = og_ref[rows, :].astype(BF)
+        mine_ref[:, 256:512] = ou_ref[rows, :].astype(BF)
+        down = od_ref[pl.ds(pl.multiple_of(pos_ref[3], 64), 64), :].astype(BF)
+        for i in range(3):
+            mine_ref[64 * i : 64 * (i + 1), 512:] = down[:, 256 * i : 256 * (i + 1)]
 
 
 def shared_slice_grads(pos, h_parts, g_parts, weights, sums=()):
     parts, per = len(h_parts), h_parts[0].shape[0]
     blocks = parts * per
     width = 256
+    shapes = ((256, width), (256, width), (128, D))
     vmem = pl.BlockSpec(memory_space=pltpu.VMEM)
     anywhere = pl.BlockSpec(memory_space=pl.ANY)
     return pl.pallas_call(
         functools.partial(shared_slice_kernel, parts, len(sums) // 3),
-        out_shape=(
-            jax.ShapeDtypeStruct((256, width), F32),
-            jax.ShapeDtypeStruct((256, width), F32),
-            jax.ShapeDtypeStruct((128, D), F32),
-        ),
+        out_shape=jax.ShapeDtypeStruct((D // 4, D), BF)
+        if sums
+        else tuple(jax.ShapeDtypeStruct(s, F32) for s in shapes),
         in_specs=[pl.BlockSpec(memory_space=pltpu.SMEM)]
         + [anywhere] * (2 * parts)
         + [vmem] * (1 + len(sums)),
-        out_specs=(vmem,) * 3,
-        scratch_shapes=[
+        out_specs=vmem if sums else (vmem,) * 3,
+        scratch_shapes=[pltpu.VMEM(s, F32) for s in (shapes if sums else ())]
+        + [
             pltpu.VMEM((blocks, ROWS, D), BF),
             pltpu.VMEM((blocks, ROWS, D), BF),
             pltpu.VMEM((2 * TOK_DEV, width), BF),
             pltpu.VMEM((D, width), BF),
             pltpu.VMEM((D, width), BF),
             pltpu.VMEM((width, D), BF),
-            pltpu.SemaphoreType.DMA((2, parts)),
+            pltpu.SemaphoreType.DMA((2, blocks // 2)),
         ],
         compiler_params=pltpu.CompilerParams(vmem_limit_bytes=VMEM_LIMIT),
         cost_estimate=microseconds(20),
@@ -927,10 +974,14 @@
     return value * cos + partner * sin
 
 
-def causal_mask(rows):
-    row = lax.broadcasted_iota(jnp.int32, (rows, rows), 0)
-    col = lax.broadcasted_iota(jnp.int32, (rows, rows), 1)
+def causal_mask(rows, heads):
+    row = lax.broadcasted_iota(jnp.int32, (heads * rows, rows), 0) % rows
+    col = lax.broadcasted_iota(jnp.int32, (heads * rows, rows), 1)
     return row, col
+
+
+def stacked(value, masks):
+    return jnp.concatenate([value * mask for mask in masks], 0)
 
 
 def unit_rms(value):
@@ -961,16 +1012,22 @@
         router_ref,
         cos_ref,
         sin_ref,
+        *outs,
+        h2_ref,
         w_ref,
         q_ref,
         k_ref,
         v_ref,
         o_ref,
         x1_ref,
-        h2_ref,
         h_sc,
         sems,
+        out_sems,
     ) = refs[8:]
+    kept = (w_ref, q_ref, k_ref, v_ref, o_ref, x1_ref)
+    leaving = [
+        pltpu.make_async_copy(kept[i], outs[i], out_sems.at[i]) for i in range(len(kept))
+    ]
     copies = []
     for part in range(8):
         for slot in range(4):
@@ -989,6 +1046,7 @@
     h_sc[TOK_DEV:, :] = (far * unit_rms(far) * gain1_ref[...]).astype(BF)
     for one in copies:
         one.wait()
+    leaving[0].start()
     for i in range(6):
         out_ref = (q_ref, k_ref, v_ref)[i // 2]
         product = jnp.dot(h_sc[...], w_ref[i], preferred_element_type=F32)
@@ -1000,12 +1058,14 @@
                 if i < 4:
                     value = turned(value, cos_ref[...], sin_ref[...])
                 out_ref[rows, at : at + 128] = value.astype(BF)
+        if i % 2:
+            leaving[1 + i // 2].start()
     masks = lane_halves()
-    row, col = causal_mask(PROMPT)
+    row, col = causal_mask(PROMPT, 2)
     prompt_ok = col <= row
-    row, col = causal_mask(CONT * CLEN)
+    row, col = causal_mask(CONT * CLEN, 2)
     cont_ok = (row // CLEN == col // CLEN) & (col <= row)
-    row = lax.broadcasted_iota(jnp.int32, (CONT * CLEN, 1), 0)
+    row = lax.broadcasted_iota(jnp.int32, (2 * CONT * CLEN, 1), 0) % (CONT * CLEN)
     reads_far = jnp.where(row < CLEN, place_ref[12], place_ref[13]).astype(F32)
     own_c = slice(PROMPT, TOK_DEV)
     far_p = slice(TOK_DEV, TOK_DEV + PROMPT)
@@ -1015,32 +1075,31 @@
         q_p, k_p, v_p = q_ref[:PROMPT, cols], k_ref[:PROMPT, cols], v_ref[:PROMPT, cols]
         q_c, k_c, v_c = q_ref[own_c, cols], k_ref[own_c, cols], v_ref[own_c, cols]
         k_f, v_f = k_ref[far_p, cols], v_ref[far_p, cols]
-        out_p, out_c = [], []
-        for mask in masks:
-            score = jnp.where(prompt_ok, 0.125 * contract(q_p * mask, k_p, 1, 1), -1e30)
-            out_p.append(
-                jnp.dot(softmax_of(score).astype(BF), v_p, preferred_element_type=F32)
-            )
-            query = q_c * mask
-            near, far = contract(query, k_p, 1, 1), contract(query, k_f, 1, 1)
-            first = 0.125 * jnp.where(reads_far > 0.5, far, near)
-            second = jnp.where(cont_ok, 0.125 * contract(query, k_c, 1, 1), -1e30)
-            first, second = softmax_of(first, second)
-            out_c.append(
-                jnp.dot((first * (1.0 - reads_far)).astype(BF), v_p, preferred_element_type=F32)
-                + jnp.dot((first * reads_far).astype(BF), v_f, preferred_element_type=F32)
-                + jnp.dot(second.astype(BF), v_c, preferred_element_type=F32)
-            )
-        o_ref[:PROMPT, cols] = pick_lanes(*out_p).astype(BF)
-        o_ref[own_c, cols] = pick_lanes(*out_c).astype(BF)
+        score = 0.125 * contract(stacked(q_p, masks), k_p, 1, 1)
+        prob = softmax_of(jnp.where(prompt_ok, score, -1e30)).astype(BF)
+        out = jnp.dot(prob, v_p, preferred_element_type=F32)
+        o_ref[:PROMPT, cols] = pick_lanes(out[:PROMPT], out[PROMPT:]).astype(BF)
+        query = stacked(q_c, masks)
+        near, far = contract(query, k_p, 1, 1), contract(query, k_f, 1, 1)
+        first = 0.125 * jnp.where(reads_far > 0.5, far, near)
+        second = jnp.where(cont_ok, 0.125 * contract(query, k_c, 1, 1), -1e30)
+        first, second = softmax_of(first, second)
+        out = (
+            jnp.dot((first * (1.0 - reads_far)).astype(BF), v_p, preferred_element_type=F32)
+            + jnp.dot((first * reads_far).astype(BF), v_f, preferred_element_type=F32)
+            + jnp.dot(second.astype(BF), v_c, preferred_element_type=F32)
+        )
+        o_ref[own_c, cols] = pick_lanes(out[: CONT * CLEN], out[CONT * CLEN :]).astype(BF)
         return carry
 
-    lax.fori_loop(0, HEADS // 2, heads, 0)
+    lax.fori_loop(0, HEADS // 2, heads, 0, unroll=3)
+    leaving[4].start()
     for i in range(2):
         cols = slice(384 * i, 384 * (i + 1))
         x1_ref[:, cols] = own_ref[:TOK_DEV, cols].astype(F32) + jnp.dot(
             o_ref[...], w_ref[6 + i], preferred_element_type=F32
         )
+    leaving[5].start()
     resid = x1_ref[...]
     hidden = (resid * unit_rms(resid) * gain2_ref[...]).astype(BF)
     h2_ref[:TOK_DEV, :] = hidden
@@ -1050,29 +1109,33 @@
     high = probs.astype(BF)
     h2_ref[TOK_DEV:, :TOK_DEV] = high
     h2_ref[TOK_DEV:, TOK_DEV:] = (probs - high.astype(F32)).astype(BF)
+    for one in leaving:
+        one.wait()
 
 
 def attention_forward(place, w_parts, h1, own, far, gain1, gain2, router_t, cos, sin):
     vmem = pl.BlockSpec(memory_space=pltpu.VMEM)
-    shape = jax.ShapeDtypeStruct
+    hbm = pl.BlockSpec(memory_space=pltpu.HBM)
+    kept = (
+        ((8, D, 384), BF),
+        ((2 * TOK_DEV, D), BF),
+        ((2 * TOK_DEV, D), BF),
+        ((2 * TOK_DEV, D), BF),
+        ((TOK_DEV, D), BF),
+        ((TOK_DEV, D), F32),
+    )
     return pl.pallas_call(
         attention_kernel,
-        out_shape=(
-            shape((8, D, 384), BF),
-            shape((2 * TOK_DEV, D), BF),
-            shape((2 * TOK_DEV, D), BF),
-            shape((2 * TOK_DEV, D), BF),
-            shape((TOK_DEV, D), BF),
-            shape((TOK_DEV, D), F32),
-            shape((ROWS, D), BF),
-        ),
+        out_shape=tuple(jax.ShapeDtypeStruct(*s) for s in kept + (((ROWS, D), BF),)),
         in_specs=[pl.BlockSpec(memory_space=pltpu.SMEM)]
         + [pl.BlockSpec(memory_space=pl.ANY)] * 8
         + [vmem] * 8,
-        out_specs=(vmem,) * 7,
-        scratch_shapes=[
+        out_specs=(hbm,) * len(kept) + (vmem,),
+        scratch_shapes=[pltpu.VMEM(*s) for s in kept]
+        + [
             pltpu.VMEM((2 * TOK_DEV, D), BF),
             pltpu.SemaphoreType.DMA((8, 4)),
+            pltpu.SemaphoreType.DMA((len(kept),)),
         ],
         compiler_params=pltpu.CompilerParams(vmem_limit_bytes=VMEM_LIMIT),
         cost_estimate=microseconds(20),
@@ -1161,48 +1224,59 @@
 
 def attention_back_kernel(
     flags_ref,
-    q_ref,
-    k_ref,
-    v_ref,
-    do_ref,
-    do_far_ref,
-    h1_ref,
-    w_ref,
-    own_ref,
-    gain1_ref,
-    cos_ref,
-    sin_ref,
-    dx1_ref,
-    gwo_ref,
-    grouter_ref,
-    ggain2_ref,
-    gtok_ref,
-    keep_ref,
-    send_ref,
-    dq_sc,
-    dk_sc,
-    dv_sc,
-    low_sc,
+    *refs,
 ):
+    sources = refs[:9]
+    do_far_ref, gain1_ref, cos_ref, sin_ref, grouter_ref, ggain2_ref = refs[9:15]
+    gtok_ref, keep_ref, send_ref = refs[15:18]
+    arrived = refs[18:27]
+    q_ref, k_ref, v_ref, do_ref, h1_ref, w_ref, own_ref, dx1_ref, gwo_ref = arrived
+    dq_sc, dk_sc, dv_sc, low_sc, product_sc, ext_sc, in_sems, out_sems = refs[27:]
+    copies = [
+        pltpu.make_async_copy(
+            sources[i].at[:6] if i == 5 else sources[i], arrived[i], in_sems.at[i]
+        )
+        for i in range(9)
+    ]
+    for one in copies:
+        one.start()
+
+    def put(number, source):
+        cols = slice((number % 2) * D, (number % 2 + 1) * D)
+        copy = lambda out: pltpu.make_async_copy(
+            source, out.at[:, : D // 4, cols], out_sems.at[number]
+        )
+
+        @pl.when(flags_ref[4] == number // 2)
+        def _():
+            copy(keep_ref).start()
+
+        @pl.when(flags_ref[4] != number // 2)
+        def _():
+            copy(send_ref).start()
+
+        return copy(keep_ref)
+
+    for one in copies[:4]:
+        one.wait()
     masks = lane_halves()
-    row, col = causal_mask(PROMPT)
+    row, col = causal_mask(PROMPT, 2)
     prompt_ok = col <= row
     cont_ok = (row // CLEN == col // CLEN) & (col <= row)
-    row = lax.broadcasted_iota(jnp.int32, (4 * CLEN, 1), 0) // CLEN
+    row = lax.broadcasted_iota(jnp.int32, (8 * CLEN, 1), 0) // CLEN % 4
     near = jnp.where(
         row < 2,
         jnp.where(row == 0, flags_ref[0], flags_ref[1]),
         jnp.where(row == 2, flags_ref[2], flags_ref[3]),
     ).astype(F32)
+    own_rows = row < 2
     own_c = slice(PROMPT, TOK_DEV)
     far_p = slice(TOK_DEV, TOK_DEV + PROMPT)
     far_c = slice(TOK_DEV + PROMPT, 2 * TOK_DEV)
     cont = CONT * CLEN
 
-    def either(own_near, far_own):
-        return jnp.concatenate(
-            [jnp.where(near[:cont] > 0.5, own_near[:cont], far_own), own_near[cont:]], 0
-        )
+    def either(own, other):
+        return jnp.where((near > 0.5) | ~own_rows, own, other)
 
     def heads(pair, carry):
         cols = pl.ds(pl.multiple_of(pair * 128, 128), 128)
@@ -1216,62 +1290,60 @@
         do_4 = jnp.concatenate([do_c, do_far_ref[:, cols]], 0)
         q_all = jnp.concatenate([q_p, q_4], 0)
         do_all = jnp.concatenate([do_p, do_4], 0)
-        dq_p, dq_c, dk_p, dk_c, dv_p, dv_c = [], [], [], [], [], []
-        for mask in masks:
-            score = jnp.where(prompt_ok, 0.125 * contract(q_p * mask, k_p, 1, 1), -1e30)
-            prob = softmax_of(score)
-            dprob = contract(do_p * mask, v_p, 1, 1)
-            ds = (prob * (dprob - jnp.sum(prob * dprob, -1, keepdims=True))).astype(BF)
-            query, grad = q_4 * mask, do_4 * mask
-            first = 0.125 * either(
-                contract(query, k_p, 1, 1), contract(query[:cont], k_f, 1, 1)
-            )
-            second = jnp.where(cont_ok, 0.125 * contract(query, k_4, 1, 1), -1e30)
-            first, second = softmax_of(first, second)
-            dfirst = either(contract(grad, v_p, 1, 1), contract(grad[:cont], v_f, 1, 1))
-            dsecond = contract(grad, v_4, 1, 1)
-            mean = jnp.sum(first * dfirst, -1, keepdims=True) + jnp.sum(
-                second * dsecond, -1, keepdims=True
-            )
-            ds1 = first * (dfirst - mean)
-            ds2 = (second * (dsecond - mean)).astype(BF)[:cont, :cont]
-            ds_near = (ds1 * near).astype(BF)
-            ds_far = (ds1 * (1.0 - near)).astype(BF)[:cont]
-            p_near = (first * near).astype(BF)
-            p_own = second.astype(BF)[:cont, :cont]
-            dq_p.append(jnp.dot(ds, k_p, preferred_element_type=F32))
-            dq_c.append(
-                jnp.dot(ds_near[:cont], k_p, preferred_element_type=F32)
-                + jnp.dot(ds_far, k_f, preferred_element_type=F32)
-                + jnp.dot(ds2, k_c, preferred_element_type=F32)
-            )
-            dk_p.append(contract(jnp.concatenate([ds, ds_near], 0), q_all, 0, 0))
-            dv_p.append(contract(jnp.concatenate([prob.astype(BF), p_near], 0), do_all, 0, 0))
-            dk_c.append(contract(ds2, q_c, 0, 0))
-            dv_c.append(contract(p_own, do_c, 0, 0))
-        for out, prompt_part, cont_part in (
-            (dq_sc, dq_p, dq_c),
-            (dk_sc, dk_p, dk_c),
-            (dv_sc, dv_p, dv_c),
+        rows = 4 * CLEN
+        query, grad = stacked(q_p, masks), stacked(do_p, masks)
+        score = jnp.where(prompt_ok, 0.125 * contract(query, k_p, 1, 1), -1e30)
+        prob = softmax_of(score)
+        dprob = contract(grad, v_p, 1, 1)
+        ds = (prob * (dprob - jnp.sum(prob * dprob, -1, keepdims=True))).astype(BF)
+        prob = prob.astype(BF)
+        query, grad = stacked(q_4, masks), stacked(do_4, masks)
+        first = 0.125 * either(contract(query, k_p, 1, 1), contract(query, k_f, 1, 1))
+        second = jnp.where(cont_ok, 0.125 * contract(query, k_4, 1, 1), -1e30)
+        first, second = softmax_of(first, second)
+        dfirst = either(contract(grad, v_p, 1, 1), contract(grad, v_f, 1, 1))
+        dsecond = contract(grad, v_4, 1, 1)
+        mean = jnp.sum(first * dfirst, -1, keepdims=True) + jnp.sum(
+            second * dsecond, -1, keepdims=True
+        )
+        ds1 = first * (dfirst - mean)
+        ds2 = (second * (dsecond - mean)).astype(BF)
+        ds_near = (ds1 * near).astype(BF)
+        ds_far = (ds1 * (1.0 - near)).astype(BF)
+        p_near = (first * near).astype(BF)
+        p_own = second.astype(BF)
+        out = jnp.dot(ds, k_p, preferred_element_type=F32)
+        dq_sc[:PROMPT, cols] = pick_lanes(out[:PROMPT], out[PROMPT:])
+        out = (
+            jnp.dot(ds_near, k_p, preferred_element_type=F32)
+            + jnp.dot(ds_far, k_f, preferred_element_type=F32)
+            + jnp.dot(ds2, k_4, preferred_element_type=F32)
+        )
+        dq_sc[own_c, cols] = pick_lanes(out[:cont], out[rows : rows + cont])
+        for out, left, left_own, right, own in (
+            (dk_sc, (ds, ds_near), ds2, q_all, q_c),
+            (dv_sc, (prob, p_near), p_own, do_all, do_c),
         ):
-            out[:PROMPT, cols] = pick_lanes(*prompt_part)
-            out[own_c, cols] = pick_lanes(*cont_part)
+            parts = [
+                contract(
+                    jnp.concatenate([part[h * rows : (h + 1) * rows] for part in left], 0),
+                    right,
+                    0,
+                    0,
+                )
+                for h in range(2)
+            ]
+            out[:PROMPT, cols] = pick_lanes(*parts)
+            parts = [
+                contract(left_own[h * rows : h * rows + cont, :cont], own, 0, 0) for h in range(2)
+            ]
+            out[own_c, cols] = pick_lanes(*parts)
         return carry
 
-    lax.fori_loop(0, HEADS // 2, heads, 0)
-
-    def put(owner, at, product):
-        for z in range(4):
-            rows = product[z * (D // 4) : (z + 1) * (D // 4), :]
-
-            @pl.when(flags_ref[4] == owner)
-            def _():
-                keep_ref[z, : D // 4, at : at + D] = rows
-
-            @pl.when(flags_ref[4] != owner)
-            def _():
-                send_ref[z, : D // 4, at : at + D] = rows
-
+    lax.fori_loop(0, HEADS // 2, heads, 0, unroll=3)
+    for one in copies[4:]:
+        one.wait()
+    leaving = [put(3, gwo_ref)]
     dh1 = None
     for i, source in enumerate((dq_sc, dk_sc, dv_sc)):
         for slab in range(6):
@@ -1282,81 +1354,67 @@
             low_sc[:, cols] = value.astype(BF)
         grads = low_sc[...]
         product = contract(h1_ref[...], grads, 0, 0).astype(BF)
-        put(i // 2, (i % 2) * D, product)
+        product_sc[i] = product.reshape(4, D // 4, D)
+        leaving.append(put(i, product_sc.at[i]))
         for half in range(2):
             part = contract(grads[:, 384 * half : 384 * (half + 1)], w_ref[2 * i + half], 1, 1)
             dh1 = part if dh1 is None else dh1 + part
-    put(1, D, gwo_ref[...])
-    inputs = own_ref[:TOK_DEV, :].astype(F32)
+    inputs = own_ref[...].astype(F32)
     scale = unit_rms(inputs)
     normed = inputs * scale
     ggain1 = jnp.sum(dh1 * normed, 0, keepdims=True)
     gains = jnp.concatenate([ggain1, ggain2_ref[...], jnp.zeros((EXT - 2, D), F32)], 0)
-    keep_ref[:, D // 4 :, :] = jnp.zeros((4, EXT, 2 * D), BF)
-    send_ref[:, D // 4 :, :] = jnp.zeros((4, EXT, 2 * D), BF)
+    ext_sc[...] = jnp.zeros_like(ext_sc)
     for z in range(4):
         cols = slice(z * (D // 4), (z + 1) * (D // 4))
         extras = jnp.concatenate([grouter_ref[:, cols], gains[:, cols]], 1).astype(BF)
-
-        @pl.when(flags_ref[4] == 0)
-        def _():
-            keep_ref[z, D // 4 :, : 2 * (D // 4)] = extras
-
-        @pl.when(flags_ref[4] != 0)
-        def _():
-            send_ref[z, D // 4 :, : 2 * (D // 4)] = extras
-
+        ext_sc[0, z, :, : 2 * (D // 4)] = extras
+    for k, out in enumerate((keep_ref, send_ref)):
+        which = flags_ref[4] if k == 0 else 1 - flags_ref[4]
+        leaving.append(
+            pltpu.make_async_copy(ext_sc.at[which], out.at[:, D // 4 :, :], out_sems.at[4 + k])
+        )
+        leaving[-1].start()
     dnormed = dh1 * gain1_ref[...]
     gtok_ref[...] = (
         scale * (dnormed - normed * jnp.mean(dnormed * normed, -1, keepdims=True)) + dx1_ref[...]
     )
+    for one in leaving:
+        one.wait()
 
 
 def attention_backward(
     flags, q, k, v, do, do_far, h1, w_all, own, gain1, cos, sin, dx1, gwo, grouter, ggain2
 ):
     shape = jax.ShapeDtypeStruct
-    whole = lambda *dims: pl.BlockSpec(dims, lambda i: (0,) * len(dims))
-    rows = whole(TOK_DEV, D)
-    both = whole(2 * TOK_DEV, D)
+    vmem = pl.BlockSpec(memory_space=pltpu.VMEM)
+    anywhere = pl.BlockSpec(memory_space=pl.ANY)
+    hbm = pl.BlockSpec(memory_space=pltpu.HBM)
     packed = (4, D // 4 + EXT, 2 * D)
+    late = (q, k, v, do, h1, w_all, own, dx1, gwo.reshape(4, D // 4, D))
     return pl.pallas_call(
         attention_back_kernel,
-        grid=(1,),
-        out_shape=(
-            shape((TOK_DEV, D), F32),
-            shape(packed, BF),
-            shape(packed, BF),
-        ),
-        in_specs=[
-            pl.BlockSpec(memory_space=pltpu.SMEM),
-            both,
-            both,
-            both,
-            rows,
-            whole(TOK_DEV - PROMPT, D),
-            rows,
-            whole(6, D, 384),
-            rows,
-            whole(1, D),
-            whole(TOK_DEV, 128),
-            whole(TOK_DEV, 128),
-            rows,
-            whole(D, D),
-            whole(EXPERTS, D),
-            whole(1, D),
-        ],
-        out_specs=(rows, whole(*packed), whole(*packed)),
+        out_shape=(shape((TOK_DEV, D), F32), shape(packed, BF), shape(packed, BF)),
+        in_specs=[pl.BlockSpec(memory_space=pltpu.SMEM)]
+        + [anywhere] * 9
+        + [vmem] * 6,
+        out_specs=(vmem, hbm, hbm),
         scratch_shapes=[
-            pltpu.VMEM((TOK_DEV, D), F32),
-            pltpu.VMEM((TOK_DEV, D), F32),
-            pltpu.VMEM((TOK_DEV, D), F32),
+            pltpu.VMEM((6,) + v.shape[1:] if i == 5 else v.shape, v.dtype)
+            for i, v in enumerate(late)
+        ]
+        + [pltpu.VMEM((TOK_DEV, D), F32)] * 3
+        + [
             pltpu.VMEM((TOK_DEV, D), BF),
+            pltpu.VMEM((3, 4, D // 4, D), BF),
+            pltpu.VMEM((2, 4, EXT, 2 * D), BF),
+            pltpu.SemaphoreType.DMA((9,)),
+            pltpu.SemaphoreType.DMA((6,)),
         ],
         compiler_params=pltpu.CompilerParams(vmem_limit_bytes=VMEM_LIMIT),
         cost_estimate=microseconds(23),
         name="attention_backward",
-    )(flags, q, k, v, do, do_far, h1, w_all, own, gain1, cos, sin, dx1, gwo, grouter, ggain2)
+    )(flags, *late, do_far, gain1, cos, sin, grouter, ggain2)
 
 
 def after(value, *earlier):
@@ -1437,6 +1495,11 @@
         return jnp.where(row == 0, left, right)
 
     return [pick(x, y), pick(1 - x, y), pick(x, 1 - y), pick(1 - x, 1 - y)]
+
+
+def canonical(slots, z):
+    order = [slots[0], slots[3], slots[2], slots[1]]
+    return lax.dynamic_slice_in_dim(jnp.stack(order + order), lax.rem(4 - z, 4), 4, 0)
 
 
 def lane_tables():
@@ -1480,15 +1543,17 @@
     dense = jnp.concatenate([dense, jnp.concatenate([router_weight.T, gains], 1)], 0)
     dense_z = [over_z(dense, step) for step in (1, 2, 3)]
 
+    units = lambda w: lax.dynamic_index_in_dim(
+        w.reshape(shard, 4, 8, 64), plane, 2, keepdims=False
+    ).reshape(shard, 256)
+    down = lax.dynamic_slice_in_dim(shared_down, plane * 64, 64, 0)
+    down = jnp.concatenate([down[:, 256 * i : 256 * (i + 1)] for i in range(3)], 0)
+    shared = jnp.concatenate([units(shared_gate), units(shared_up), down], 1)
     far = over_y(tokens)
     ids = jnp.broadcast_to(prompt_ids.astype(BF)[:, None], (CONT, 128))
     far_ids = over_y(ids)
     dense = jnp.stack([dense] + after(dense_z, far, far_ids))
-    slots = dense[:, shard:, :]
-    slots = jnp.stack([slots[0], slots[3], slots[2], slots[1]])
-    small = lax.dynamic_slice_in_dim(
-        jnp.concatenate([slots, slots], 0), lax.rem(4 - z, 4), 4, 0
-    )
+    small = canonical([dense[i, shard:, :] for i in range(4)], z)
     router_t = small[:, :, :shard].transpose(1, 0, 2).reshape(EXPERTS, D)
     gain1 = small[:, 0, shard:].reshape(1, D).astype(F32)
     gain2 = small[:, 1, shard:].reshape(1, D).astype(F32)
@@ -1517,17 +1582,10 @@
     g_x = over_x(g_near)
     g_group = [g_block, g_x, over_core(g_near), over_core(g_x)]
 
-    units = lambda w: lax.dynamic_index_in_dim(
-        w.reshape(shard, 4, 8, 64), plane, 2, keepdims=False
-    ).reshape(shard, 256)
-    down = lax.dynamic_slice_in_dim(shared_down, plane * 64, 64, 0)
-    down = jnp.concatenate([down[:, 256 * i : 256 * (i + 1)] for i in range(3)], 0)
-    shared = jnp.concatenate([units(shared_gate), units(shared_up), down], 1)
+    g_column = lax.all_gather(after(g_block, dense), "dp", axis=0, tiled=False)
+
     shared = lax.all_gather(after(shared, dense), "dp", axis=0, tiled=False)
     shared_far = over_y(after(shared, h1))
-
-    g_column = lax.all_gather(after(g_block, dense), "dp", axis=0, tiled=False)
-
     place = after(place, shared)
     flags = jnp.concatenate([prompt_ids == y, far_ids[:, 0].astype(jnp.int32) == y, core[None] != 0]).astype(jnp.int32)
     w_all, q, k, v, o, x1, h_block = attention_forward(
@@ -1545,13 +1603,14 @@
     more, (h_x, g_y) = beside(more, (h_x, over_y(after(g_block, h_block))))
     h_far, g_far = [h_x, over_core(h_x)], [g_x, g_group[3]]
     h_group = [h_near[0], h_far[0], h_near[1], h_far[1]]
+    g_second = jnp.where(core == 0, g_y, g_x)
+    h_group, g_second = after((h_group, g_second))
     part = group_experts(base[None], 0, 2, h_group, g_group, (), *experts_w)
     (part, h_far), h_b = beside((part, h_far), over_b(after(h_block, h_x)))
     g_first = over_a(after(g_column, h_x))
     more = more + shared_rows(h_far, g_far, shared, shared_far)
     more, g_first = beside(more, g_first)
-    g_second = jnp.where(core == 0, g_y, g_x)
-    g_second = lax.all_gather(after(g_second, h_x), "dp", axis=0, tiled=False)
+    g_second = lax.all_gather(g_second, "dp", axis=0, tiled=False)
     results = group_experts(
         base[None] + 2, 2, 2, h_group, g_group, (*more, *part), *experts_w
     )
@@ -1565,7 +1624,7 @@
     h_column = after(h_column, dx_x)
     h_core = [over_core(h_column)]
     window = jnp.array([0, 1, 3, 4], jnp.int32)[z]
-    s_pos = jnp.stack([window, (z // 2).astype(jnp.int32)])
+    s_pos = jnp.stack([window, z // 2, z * 192 - window * 128, (z % 2) * 64]).astype(jnp.int32)
     e_pos = jnp.stack([base, (z * 2 + y).astype(jnp.int32)])
     s_sums = shared_slice_grads(
         s_pos, [h_column, h_core[0]], [g_column, g_core[0]], shared
@@ -1575,7 +1634,7 @@
         dx, h_block, x1, cotangent, gain2, router_t, w_all
     )
     gwo = inner_rows(o, dx1.astype(BF)).astype(BF)
-    gwo, do_far = beside(gwo, over_y(do_c))
+    gwo, (do_far, g_second) = beside(gwo, (over_y(do_c), g_second))
     h_first = over_a(after(h_column, do_far))
     h_second = lax.all_gather(after(h_b, do_far), "dp", axis=0, tiled=False)
     grad_inputs, keep, send = attention_backward(
@@ -1596,8 +1655,9 @@
         grad_router_t,
         grad_gain2,
     )
-    (grad_inputs, keep, send), (h_first, g_second) = beside(
-        (grad_inputs, keep, send), (h_first, g_second)
+    (grad_inputs, keep, send), (h_first, g_far) = beside(
+        (grad_inputs, keep, send),
+        (h_first, [over_core(after(part, do_far)) for part in (g_second, g_third)]),
     )
     h_core.append(over_core(h_first))
     h_third = over_b(after(h_first, keep))
@@ -1606,19 +1666,18 @@
     e_sums = expert_slice_grads(e_pos, h_parts, g_parts, *experts_w, 256)
     (e_sums, keep), (send, h_second, h_third, g_far) = beside(
         (e_sums, keep),
-        (over_core(send), h_second, h_third, [over_core(after(v, keep)) for v in (g_second, g_third)]),
+        (over_core(send), h_second, h_third, g_far),
     )
     h_far = [over_core(h_second), over_core(h_third)]
     h_parts, g_parts = [h_second, h_third] + h_far, [g_second, g_third] + g_far
     pieces = plane_pieces(pair_sum(keep, send), x, y)
     h_parts, pieces = after((h_parts, pieces))
-    s_sums = shared_slice_grads(
+    mine = shared_slice_grads(
         s_pos, [h_first, h_core[1], *h_parts], [g_first, g_core[1], *g_parts], shared, s_sums
     )
-    (s_sums, pieces), there = beside(
-        (s_sums, pieces), [over(piece) for over, piece in zip(OTHERS, pieces[1:])]
-    )
-    s_gate, s_up, s_down = s_sums
+    (mine, pieces), there = beside(
+        (mine, pieces), [over(piece) for over, piece in zip(OTHERS, pieces[1:])]
+    )
     z_own = pieces[0].astype(F32)
     for piece in there:
         z_own = z_own + piece.astype(F32)
@@ -1627,20 +1686,10 @@
         lax.dynamic_index_in_dim(z_own, lax.rem(z + step, 4), 0, keepdims=False)
         for step in (0, 1, 2, 3)
     ]
-    moe = after(moe, s_gate)
+    moe = after(moe, mine)
     moe_x = pair_sum(moe[1], over_core(moe[3]))
     moe_core = over_core(moe[2])
 
-    lead = z * 192 - window * 128
-    s_down = lax.dynamic_slice_in_dim(s_down, (z % 2) * 64, 64, 0)
-    mine = jnp.concatenate(
-        [
-            lax.dynamic_slice_in_dim(s_gate, lead, 192, 0),
-            lax.dynamic_slice_in_dim(s_up, lead, 192, 0),
-            jnp.concatenate([s_down[:, 256 * i : 256 * (i + 1)] for i in range(3)], 0),
-        ],
-        1,
-    ).astype(BF)
     mine, z_parts, moe_x, moe_core, h_parts, g_parts = after(
         (mine, z_parts, moe_x, moe_core, h_parts, g_parts)
     )

time: 404 us -> 392 us (0.970)
  Pallas kernels: 228 us -> 205 us
  waiting for transfers between devices: 65.5 us -> 76.6 us
    pallas_call x2, Pallas kernels: 46.3 us -> 37.8 us  [the longest x1 20.7 us: attention_backward(): pl.pallas_call(attention_back_kernel, out_shape=(shape((TOK_DEV, D), F32)...]
    all_gather x1, waiting for transfers between devices: 0.01 us -> 7.81 us  [tuned_body(): g_second = lax.all_gather(g_second, 'dp', axis=0, tiled=False)]
    pallas_call x2, Pallas kernels: 62.4 us -> 55.1 us  [expert_slice_grads(): pl.pallas_call(functools.partial(expert_slice_kernel, parts, len(sums) //...]
  transfers between devices with their start and end apart: 57 -> 57, of which waited for: 25 -> 22; matrix products, arithmetic and copies ran while one was open for 9% -> 8% of each run, Pallas kernels for 57% -> 53%
where the time goes in v5:
time: 392 us; the launch traced here: 386 us
  Pallas kernels  205 us (52%)
  waiting for transfers between devices  76.6 us (20%)
  starting transfers between devices  45.6 us (12%)
  other arithmetic  20.5 us (5%)
  between operations  17.1 us (4%)
  local copies, waits for them, and re-layouts  17 us (4%)
    pallas_call x2, Pallas kernels, expert_slice_grads(): pl.pallas_call(functools.partial(expert_slice_kernel, parts, len(sums) //...  55.1 us
    ppermute x51, waiting for transfers between devices, moved(): return lax.ppermute(value, AXES, pairs)  51.2 us
    pallas_call x2, Pallas kernels, group_experts(): pl.pallas_call(functools.partial(group_kernel, blocks, len(more)), out_sh...  47.4 us
    ppermute x51, starting transfers between devices, moved(): return lax.ppermute(value, AXES, pairs)  45.4 us
    pallas_call x2, Pallas kernels, shared_slice_grads(): pl.pallas_call(functools.partial(shared_slice_kernel, parts, len(sums) //...  38.2 us
    pallas_call x1, Pallas kernels, attention_backward(): pl.pallas_call(attention_back_kernel, out_shape=(shape((TOK_DEV, D), F32)...  20.7 us
    pallas_call x1, Pallas kernels, attention_forward(): pl.pallas_call(attention_kernel, out_shape=tuple((jax.ShapeDtypeStruct(*s...  17.1 us
    pallas_call x2, Pallas kernels, shared_rows(): pl.pallas_call(shared_kernel, out_shape=(rows, rows), in_specs=[vmem] * 6...  15.5 us
  transfers between devices with their start and end apart: 57, of which 22 were waited for; matrix products, arithmetic and copies ran while one was open for 8% of the time, Pallas kernels for 53%

profile of v5, /device:TPU:0, one launch (start us, length us, event | category | flops | bytes accessed | tf_op | source)
XLA Modules:
  0.0 385.6 jit_solution(17578496609379564171)
XLA Ops:
  7.3 3.0 collective-permute-start.3
  12.2 1.6 collective-permute-start
  13.8 2.6 collective-permute-start.1
  16.4 1.3 collective-permute-start.2
  21.9 2.8 collective-permute-done.4
  24.7 2.1 collective-permute-done.1
  26.8 1.1 pad_maximum_fusion.refs_0_
  32.6 1.5 collective-permute-start.5
  38.2 2.2 norm_rows.1.refs_8_.refs_4_
  40.4 8.8 %collective-permute-done.5.refs_1_ = bf16[4,208,384]{2,1,0:T(8,128)(2,1)} collective-permute-done((bf16[4,208,384]{2,1,0:T(8,128)(2,1)S(1)}, bf16[4,208,384]{2,1,0:T(8,128)(2,1)}, u32[]{:S(2)}, u32[]{:S(2)}) %collective-permute-start.5) | collective-permute-done | bytes 639008 | tf_op jit(solution)/shard_map/ppermute | solution.py:454
  49.1 1.1 collective-permute-start.7
  50.3 10.4 %all-gather.13.cloned.1.call-done = bf16[768,768]{1,0:T(8,128)(2,1)} async-done(((bf16[192,768]{1,0:T(8,128)(2,1)}), bf16[768,768]{1,0:T(8,128)(2,1)}) %all-gather.13.cloned.1.call-update) | async-done | bytes 1179664 | tf_op jit(solution)/shard_map/all_gather | solution.py:1587
  60.7 1.9 collective-permute-start.13
  63.2 1.5 collective-permute-start.12
  66.9 17.1 %attention_forward.1 = (bf16[8,768,384]{2,1,0:T(8,128)(2,1)}, bf16[768,768]{1,0:T(8,128)(2,1)}, bf16[768,768]{1,0:T(8,128)(2,1)}, bf16[768,768]{1,0:T(8,128)(2,1...) custom-call(s32[14]{0:T(128)} %stack.109.place_ref, bf16[4,208,384]{2,1,0:T(8,128)(2,1)} %copy-done.11, ...), custom_call_target="tpu_custom_call" | custom-call | bytes 8000000 | tf_op jit(solution)/shard_map/attention_forward/pallas_call | solution.py:1127
  84.1 4.4 %collective-permute-done.13.w_b_ref = bf16[4,192,768]{2,1,0:T(8,128)(2,1)S(1)} collective-permute-done((bf16[4,192,768]{2,1,0:T(8,128)(2,1)}, bf16[4,192,768]{2,1,0:T(8,128)(2,1)S(1)}, u32[]{:S(2)}, u32[]{:S(2)}) %collective-permute-start.13) | collective-permute-done | bytes 1179680 | tf_op jit(solution)/shard_map/ppermute | solution.py:454
  89.4 1.5 collective-permute-start.16
  90.9 1.6 collective-permute-start.17
  94.2 7.6 %shared_rows.2 = (bf16[2,384,768]{2,1,0:T(8,128)(2,1)}, bf16[2,384,768]{2,1,0:T(8,128)(2,1)}) custom-call(bf16[400,768]{1,0:T(8,128)(2,1)} %get-tuple-element.239.h_a_ref.refs_0_.refs_3_, bf16[400,768]{1,0:T(8,128)(2,1)} %copy-done.6, bf16[400,768]{1,0:T(8,128)(2,1)} %fusion.2.g_a_ref.refs_4_, bf16[400,768]{1,0:T(8,128)(2,1)} %copy-done.5, ...), custom_call_target="tpu_custom_call" | custom-call | bytes 3200000 | tf_op jit(solution)/shard_map/shared_rows/pallas_call | solution.py:707
  101.8 4.2 %collective-permute-done.16.refs_1_.h_a_ref = bf16[400,768]{1,0:T(8,128)(2,1)} collective-permute-done((bf16[400,768]{1,0:T(8,128)(2,1)}, bf16[400,768]{1,0:T(8,128)(2,1)}, u32[]{:S(2)}, u32[]{:S(2)}) %collective-permute-start.16) | collective-permute-done | bytes 614432 | tf_op jit(solution)/shard_map/ppermute | solution.py:454
  107.0 7.0 %all-gather.15.cloned.1.call-done = bf16[1600,768]{1,0:T(8,128)(2,1)} async-done(((bf16[400,768]{1,0:T(8,128)(2,1)}), bf16[1600,768]{1,0:T(8,128)(2,1)}) %all-gather.15.cloned.1.call-update) | async-done | bytes 2457616 | tf_op jit(solution)/shard_map/all_gather | solution.py:1585
  113.9 1.5 collective-permute-start.21
  116.1 1.5 collective-permute-start.20
  117.5 2.0 broadcast_select_fusion.9
  120.6 22.3 %group_experts.2 = (bf16[384,768]{1,0:T(8,128)(2,1)}, bf16[384,768]{1,0:T(8,128)(2,1)}, bf16[384,768]{1,0:T(8,128)(2,1)}, bf16[384,768]{1,0:T(8,128)(2,1)}, bf16...) custom-call(s32[1]{0:T(128)} %bitcast.28.base_ref, ...), custom_call_target="tpu_custom_call" | custom-call | bytes 8400000 | tf_op jit(solution)/shard_map/group_experts/pallas_call | solution.py:641
  142.9 7.9 %shared_rows.3 = (bf16[2,384,768]{2,1,0:T(8,128)(2,1)}, bf16[2,384,768]{2,1,0:T(8,128)(2,1)}) custom-call(bf16[400,768]{1,0:T(8,128)(2,1)} %collective-permute-done.16.refs_1_.h_a_ref, bf16[400,768]{1,0:T(8,128)(2,1)} %copy-done.7, bf16[400,768]{1,0:T(8,128)(2,1)} %copy-done.2, bf16[400,768]{1,0:T(8,128)(2,1)} %copy-done.8, bf16[4,192,768]{2,1,0:T(8,128)(2,1)} %bitcast.60, ...), custom_call_target="tpu_custom_call" | custom-call | bytes 3200000 | tf_op jit(solution)/shard_map/shared_rows/pallas_call | solution.py:707
  150.8 1.4 collective-permute-start.22
  152.3 25.1 %group_experts.3 = (bf16[384,768]{1,0:T(8,128)(2,1)}, bf16[384,768]{1,0:T(8,128)(2,1)}, bf16[384,768]{1,0:T(8,128)(2,1)}, bf16[384,768]{1,0:T(8,128)(2,1)}, bf16...) custom-call(s32[1]{0:T(128)S(6)} %add.117.base_ref, ...), custom_call_target="tpu_custom_call" | custom-call | bytes 8400000 | tf_op jit(solution)/shard_map/group_experts/pallas_call | solution.py:641
  177.4 3.5 collective-permute-done.22.refs_9_.refs_5_
  181.0 2.2 collective-permute-done.25
  183.2 1.2 add_convert_fusion.2
  185.0 1.4 collective-permute-start.28
  187.7 1.3 pad_add_fusion.pos_ref
  189.5 11.8 %shared_slice_grads.2 = (f32[256,256]{1,0:T(8,128)}, f32[256,256]{1,0:T(8,128)}, f32[128,768]{1,0:T(8,128)}) custom-call(s32[4]{0:T(128)} %pad_add_fusion.pos_ref, bf16[4,400,768]{2,1,0:T(8,128)(2,1)} %bitcast.74, bf16[4,400,768]{2,1,0:T(8,128)(2,1)} %collective-permute-done.26.refs_1_.refs_2_, bf16[4,400,768]{2,1,0:T(8,128)(2,1)} %bitcast.71, ...), custom_call_target="tpu_custom_call" | custom-call | bytes 8000000 | tf_op jit(solution)/shard_map/shared_slice_grads/pallas_call | solution.py:920
  201.4 5.1 %branch_backward.1 = (f32[384,768]{1,0:T(8,128)}, bf16[384,768]{1,0:T(8,128)(2,1)}, bf16[128,768]{1,0:T(8,128)(2,1)}, f32[16,768]{1,0:T(8,128)}, f32[1,768]{1,0:T(1,128)}) custom-call(bf16[400,768]{1,0:T(8,128)(2,1)} %get-tuple-element.283.refs_0_, bf16[400,768]{1,0:T(8,128)(2,1)} %collective-permute-done.27.refs_1_, ...), custom_call_target="tpu_custom_call" | custom-call | bytes 2400000 | tf_op jit(solution)/shard_map/branch_backward/pallas_call | solution.py:1191
  206.5 1.4 collective-permute-start.29
  207.9 3.1 convolution_convert_fusion
  211.0 7.8 %all-gather.19.cloned.1.call-done = bf16[1600,768]{1,0:T(8,128)(2,1)} async-done(((bf16[400,768]{1,0:T(8,128)(2,1)}), bf16[1600,768]{1,0:T(8,128)(2,1)}) %all-gather.19.cloned.1.call-update) | async-done | bytes 2457616 | tf_op jit(solution)/shard_map/all_gather | solution.py:1613
  218.8 1.5 collective-permute-start.30
  222.2 20.7 %attention_backward.1 = (f32[384,768]{1,0:T(8,128)}, bf16[4,208,1536]{2,1,0:T(8,128)(2,1)}, bf16[4,208,1536]{2,1,0:T(8,128)(2,1)}) custom-call(s32[5]{0:T(128)} %add_convert_fusion.6.flags_ref, bf16[768,768]{1,0:T(8,128)(2,1)} %get-tuple-element.271.refs_0_, bf16[768,768]{1,0:T(8,128)(2,1)} %get-tuple-element.272.refs_1_, ...), custom_call_target="tpu_custom_call" | custom-call | bytes 9200000 | tf_op jit(solution)/shard_map/attention_backward/pallas_call | solution.py:1395
  242.9 6.2 %collective-permute-done.30.refs_1_.refs_0_ = bf16[4,400,768]{2,1,0:T(8,128)(2,1)} collective-permute-done((bf16[4,400,768]{2,1,0:T(8,128)(2,1)}, bf16[4,400,768]{2,1,0:T(8,128)(2,1)}, u32[]{:S(2)}, u32[]{:S(2)}) %collective-permute-start.30) | collective-permute-done | bytes 2457632 | tf_op jit(solution)/shard_map/ppermute | solution.py:454
  249.6 1.5 collective-permute-start.35
  251.6 6.1 %collective-permute-done.33.refs_3_.refs_1_ = bf16[4,400,768]{2,1,0:T(8,128)(2,1)} collective-permute-done((bf16[4,400,768]{2,1,0:T(8,128)(2,1)}, bf16[4,400,768]{2,1,0:T(8,128)(2,1)}, u32[]{:S(2)}, u32[]{:S(2)}) %collective-permute-start.33) | collective-permute-done | bytes 2457632 | tf_op jit(solution)/shard_map/ppermute | solution.py:454
  257.7 26.8 %expert_slice_grads.2 = (f32[4,768,256]{2,1,0:T(8,128)}, f32[4,768,256]{2,1,0:T(8,128)}, f32[4,256,768]{2,1,0:T(8,128)}) custom-call(s32[2]{0:T(128)} %pad_add_fusion.1.pos_ref, bf16[4,400,768]{2,1,0:T(8,128)(2,1)} %bitcast.76, bf16[4,400,768]{2,1,0:T(8,128)(2,1)} %collective-permute-done.30.refs_1_.refs_0_, ...), custom_call_target="tpu_custom_call" | custom-call | bytes 12400000 | tf_op jit(solution)/shard_map/expert_slice_grads/pallas_call | solution.py:840
  285.1 3.4 add_convert_fusion
  289.5 1.3 broadcast_select_fusion.1
  290.8 1.1 collective-permute-done.36.refs_4_.refs_2_
  292.9 1.5 collective-permute-start.38
  294.4 1.5 collective-permute-start.39
  296.4 26.4 %shared_slice_grads.3 = bf16[192,768]{1,0:T(8,128)(2,1)} custom-call(s32[4]{0:T(128)} %pad_add_fusion.pos_ref, bf16[4,400,768]{2,1,0:T(8,128)(2,1)} %collective-permute-done.30.refs_1_.refs_0_, bf16[4,400,768]{2,1,0:T(8,128)(2,1)} %collective-permute-done.33.refs_3_.refs_1_, bf16[4,400,768]{2,1,0:T(8,128)(2,1)} %bitcast.67, bf16[4,400,768]{2,1,0:T(8,128)(2,1)} %copy-done.4, ...), custom_call_target="tpu_custom_call" | custom-call | bytes 8000000 | tf_op jit(solution)/shard_map/shared_slice_grads/pallas_call | solution.py:920
  322.8 1.7 collective-permute-done.39
  325.4 1.4 collective-permute-done.41
  326.8 1.2 add_convert_fusion.4
  328.1 1.3 collective-permute-start.46
  329.3 1.6 collective-permute-start.44
  331.0 2.7 collective-permute-start.45
  333.7 28.3 %expert_slice_grads.3 = (f32[4,768,256]{2,1,0:T(8,128)}, f32[4,768,256]{2,1,0:T(8,128)}, f32[4,256,768]{2,1,0:T(8,128)}) custom-call(s32[2]{0:T(128)} %pad_add_fusion.1.pos_ref, bf16[4,400,768]{2,1,0:T(8,128)(2,1)} %bitcast.68, bf16[4,400,768]{2,1,0:T(8,128)(2,1)} %copy-done.4, bf16[4,400,768]{2,1,0:T(8,128)(2,1)} %collective-permute-done.36.refs_4_.refs_2_, ...), custom_call_target="tpu_custom_call" | custom-call | bytes 12400000 | tf_op jit(solution)/shard_map/expert_slice_grads/pallas_call | solution.py:840
  363.2 1.5 collective-permute-start.48
  364.7 1.1 collective-permute-start.49
  365.8 4.2 %place_shared.1 = (f32[192,2048]{1,0:T(8,128)}, f32[192,2048]{1,0:T(8,128)}, f32[512,768]{1,0:T(8,128)}) custom-call(bf16[8,192,768]{2,1,0:T(8,128)(2,1)} %bitcast.78), custom_call_target="tpu_custom_call" | custom-call | bytes 1600000 | tf_op jit(solution)/shard_map/place_shared/pallas_call | solution.py:1466
  370.0 2.2 add_convert_fusion.3
  372.6 2.1 collective-permute-done.50
  376.1 1.1 fusion.15
  377.4 1.1 fusion.14
  (200 shorter events, 33.5 us)
Async XLA Ops:
  7.2 12.8 %copy-start.13 = (bf16[192,2048]{1,0:T(8,128)(2,1)S(1)}, bf16[192,2048]{1,0:T(8,128)(2,1)}, u32[]{:S(2)}) copy-start(bf16[192,2048]{1,0:T(8,128)(2,1)} %param.32) | copy-start | bytes 2359300
  7.2 53.5 %all-gather.13.cloned.1.call-start = ((), (), s32[]{:S(2)}) async-start(), calls=%async_computation | async-start | bytes 1474560 | tf_op jit(solution)/shard_map/all_gather | solution.py:1587
  7.3 19.5 %collective-permute-start.3 = (bf16[384,768]{1,0:T(8,128)(2,1)}, bf16[384,768]{1,0:T(8,128)(2,1)}, u32[]{:S(2)}, u32[]{:S(2)}) collective-permute-start(bf16[384,768]{1,0:T(8,128)(2,1)} %refs_6_.1), channel_id=1, source_target_pairs={{0,4},{1,5},{2,6},{3,7},{4,0},{5,1},{6,2},{7,3},{8,12},{9,13},{10,... | collective-permute-start | bytes 1769480 | tf_op jit(solution)/shard_map/ppermute | solution.py:454
  12.2 12.5 %collective-permute-start = (bf16[208,384]{1,0:T(8,128)(2,1)}, bf16[208,384]{1,0:T(8,128)(2,1)S(1)}, u32[]{:S(2)}, u32[]{:S(2)}) collective-permute-start(bf16[208,384]{1,0:T(8,128)(2,1)} %maximum_maximum_fusion.1), channel_id=1, source_target_pairs={{0,8},{1,9},{2,10},{3,11},{4,12},{5,13},{6,14},{7,15},{8,16},{9,17... | collective-permute-start | bytes 479240 | tf_op jit(solution)/shard_map/ppermute | solution.py:454
  13.8 13.0 %collective-permute-start.1 = (bf16[208,384]{1,0:T(8,128)(2,1)}, bf16[208,384]{1,0:T(8,128)(2,1)S(1)}, u32[]{:S(2)}, u32[]{:S(2)}) collective-permute-start(bf16[208,384]{1,0:T(8,128)(2,1)} %maximum_maximum_fusion.1), channel_id=1, source_target_pairs={{0,16},{1,17},{2,18},{3,19},{4,20},{5,21},{6,22},{7,23},{8,24},{9,... | collective-permute-start | bytes 479240 | tf_op jit(solution)/shard_map/ppermute | solution.py:454
  16.4 10.4 %collective-permute-start.2 = (bf16[208,384]{1,0:T(8,128)(2,1)}, bf16[208,384]{1,0:T(8,128)(2,1)}, u32[]{:S(2)}, u32[]{:S(2)}) collective-permute-start(bf16[208,384]{1,0:T(8,128)(2,1)} %maximum_maximum_fusion.1), channel_id=1, source_target_pairs={{0,24},{1,25},{2,26},{3,27},{4,28},{5,29},{6,30},{7,31},{8,0},{9,1... | collective-permute-start | bytes 479240 | tf_op jit(solution)/shard_map/ppermute | solution.py:454
  18.3 6.3 %collective-permute-start.4 = (bf16[2,128]{0,1:T(8,128)(2,1)}, bf16[2,128]{0,1:T(8,128)(2,1)}, u32[]{:S(2)}, u32[]{:S(2)}) collective-permute-start(bf16[2,128]{0,1:T(8,128)(2,1)} %broadcast_in_dim.30), channel_id=1, source_target_pairs={{0,4},{1,5},{2,6},{3,7},{4,0},{5,1},{6,2},{7,3},{8,12},{9,13},{10,... | collective-permute-start | bytes 1544 | tf_op jit(solution)/shard_map/ppermute | solution.py:454
  27.9 22.4 %copy-start.11 = (bf16[4,208,384]{2,1,0:T(8,128)(2,1)}, bf16[4,208,384]{2,1,0:T(8,128)(2,1)S(1)}, u32[]{:S(2)}) copy-start(bf16[4,208,384]{2,1,0:T(8,128)(2,1)S(1)} %pad_maximum_fusion.refs_0_) | copy-start | bytes 1916932
  28.8 85.1 %all-gather.15.cloned.1.call-start = ((), (), s32[]{:S(2)}) async-start(), calls=%async_computation.1 | async-start | bytes 3072000 | tf_op jit(solution)/shard_map/all_gather | solution.py:1585
  30.0 33.2 %copy-start = (bf16[400,768]{1,0:T(8,128)(2,1)S(1)}, bf16[400,768]{1,0:T(8,128)(2,1)}, u32[]{:S(2)}) copy-start(bf16[400,768]{1,0:T(8,128)(2,1)} %fusion.2.g_a_ref.refs_4_) | copy-start | bytes 1843204
  30.0 154.4 %all-gather.17.cloned.1.call-start = ((), (), s32[]{:S(2)}) async-start(), calls=%async_computation.2 | async-start | bytes 3072000 | tf_op jit(solution)/shard_map/all_gather | solution.py:1599
  32.6 16.5 %collective-permute-start.5 = (bf16[4,208,384]{2,1,0:T(8,128)(2,1)S(1)}, bf16[4,208,384]{2,1,0:T(8,128)(2,1)}, u32[]{:S(2)}, u32[]{:S(2)}) collective-permute-start(bf16[4,208,384]{2,1,0:T(8,128)(2,1)S(1)} %pad_maximum_fusion.refs_0_), channel_id=1, source_target_pairs={{0,2},{1,5},{2,0},{3,7},{4,6},{5,1},{6,4},{7,3},{8,10},{9,13},{10,... | collective-permute-start | bytes 1916936 | tf_op jit(solution)/shard_map/ppermute | solution.py:454
  34.1 15.1 %collective-permute-start.6 = (bf16[4,208,384]{2,1,0:T(8,128)(2,1)S(1)}, bf16[4,208,384]{2,1,0:T(8,128)(2,1)S(1)}, u32[]{:S(2)}, u32[]{:S(2)}) collective-permute-start(bf16[4,208,384]{2,1,0:T(8,128)(2,1)S(1)} %pad_maximum_fusion.refs_0_), channel_id=1, source_target_pairs={{0,4},{1,3},{2,6},{3,1},{4,0},{5,7},{6,2},{7,5},{8,12},{9,11},{10,... | collective-permute-start | bytes 1916936 | tf_op jit(solution)/shard_map/ppermute | solution.py:454
  49.1 11.6 %copy-start.15 = (bf16[4,208,384]{2,1,0:T(8,128)(2,1)}, bf16[4,208,384]{2,1,0:T(8,128)(2,1)S(1)}, u32[]{:S(2)}) copy-start(bf16[4,208,384]{2,1,0:T(8,128)(2,1)S(1)} %collective-permute-done.6.refs_2_) | copy-start | bytes 1916932
  49.1 14.0 %collective-permute-start.7 = (bf16[4,208,384]{2,1,0:T(8,128)(2,1)}, bf16[4,208,384]{2,1,0:T(8,128)(2,1)}, u32[]{:S(2)}, u32[]{:S(2)}) collective-permute-start(bf16[4,208,384]{2,1,0:T(8,128)(2,1)} %collective-permute-done.5.refs_1_), channel_id=1, source_target_pairs={{0,4},{1,3},{2,6},{3,1},{4,0},{5,7},{6,2},{7,5},{8,12},{9,11},{10,... | collective-permute-start | bytes 1916936 | tf_op jit(solution)/shard_map/ppermute | solution.py:454
  50.3 12.9 %collective-permute-start.8 = (bf16[4,208,384]{2,1,0:T(8,128)(2,1)S(1)}, bf16[4,208,384]{2,1,0:T(8,128)(2,1)}, u32[]{:S(2)}, u32[]{:S(2)}) collective-permute-start(bf16[4,208,384]{2,1,0:T(8,128)(2,1)S(1)} %pad_maximum_fusion.refs_0_), channel_id=1, source_target_pairs={{0,1},{1,0},{2,3},{3,2},{4,5},{5,4},{6,7},{7,6},{8,9},{9,8},{10,11... | collective-permute-start | bytes 1916936 | tf_op jit(solution)/shard_map/ppermute | solution.py:454
  60.7 27.7 %collective-permute-start.13 = (bf16[4,192,768]{2,1,0:T(8,128)(2,1)}, bf16[4,192,768]{2,1,0:T(8,128)(2,1)S(1)}, u32[]{:S(2)}, u32[]{:S(2)}) collective-permute-start(bf16[4,192,768]{2,1,0:T(8,128)(2,1)} %bitcast.58), channel_id=1, source_target_pairs={{0,4},{1,5},{2,6},{3,7},{4,0},{5,1},{6,2},{7,3},{8,12},{9,13},{10,... | collective-permute-start | bytes 3538952 | tf_op jit(solution)/shard_map/ppermute | solution.py:454
  62.6 2.4 collective-permute-start.9
  62.6 3.3 collective-permute-start.10
  63.1 3.7 collective-permute-start.11
  63.2 20.9 %collective-permute-start.12 = (bf16[400,768]{1,0:T(8,128)(2,1)S(1)}, bf16[400,768]{1,0:T(8,128)(2,1)S(1)}, u32[]{:S(2)}, u32[]{:S(2)}) collective-permute-start(bf16[400,768]{1,0:T(8,128)(2,1)S(1)} %copy-done), channel_id=1, source_target_pairs={{0,2},{1,3},{2,0},{3,1},{4,6},{5,7},{6,4},{7,5},{8,10},{9,11},{10,... | collective-permute-start | bytes 1843208 | tf_op jit(solution)/shard_map/ppermute | solution.py:454
  65.1 27.4 %collective-permute-start.15 = (bf16[400,768]{1,0:T(8,128)(2,1)S(1)}, bf16[400,768]{1,0:T(8,128)(2,1)S(1)}, u32[]{:S(2)}, u32[]{:S(2)}) collective-permute-start(bf16[400,768]{1,0:T(8,128)(2,1)S(1)} %copy-done), channel_id=1, source_target_pairs={{0,1},{1,0},{2,3},{3,2},{4,5},{5,4},{6,7},{7,6},{8,9},{9,8},{10,11... | collective-permute-start | bytes 1843208 | tf_op jit(solution)/shard_map/ppermute | solution.py:454
  84.0 33.5 %copy-start.2 = (bf16[400,768]{1,0:T(8,128)(2,1)}, bf16[400,768]{1,0:T(8,128)(2,1)S(1)}, u32[]{:S(2)}) copy-start(bf16[400,768]{1,0:T(8,128)(2,1)S(1)} %collective-permute-done.12.refs_5_.g_a_ref) | copy-start | bytes 1843204
  89.4 26.6 %copy-start.1 = (bf16[400,768]{1,0:T(8,128)(2,1)S(1)}, bf16[400,768]{1,0:T(8,128)(2,1)}, u32[]{:S(2)}) copy-start(bf16[400,768]{1,0:T(8,128)(2,1)} %get-tuple-element.239.h_a_ref.refs_0_.refs_3_) | copy-start | bytes 1843204
  89.4 3.0 collective-permute-start.14
  89.4 16.6 %collective-permute-start.16 = (bf16[400,768]{1,0:T(8,128)(2,1)}, bf16[400,768]{1,0:T(8,128)(2,1)}, u32[]{:S(2)}, u32[]{:S(2)}) collective-permute-start(bf16[400,768]{1,0:T(8,128)(2,1)} %get-tuple-element.239.h_a_ref.refs_0_.refs_3_), channel_id=1, source_target_pairs={{0,2},{1,3},{2,0},{3,1},{4,6},{5,7},{6,4},{7,5},{8,10},{9,11},{10,... | collective-permute-start | bytes 1843208 | tf_op jit(solution)/shard_map/ppermute | solution.py:454
  90.9 16.1 %collective-permute-start.17 = (bf16[400,768]{1,0:T(8,128)(2,1)S(1)}, bf16[400,768]{1,0:T(8,128)(2,1)}, u32[]{:S(2)}, u32[]{:S(2)}) collective-permute-start(bf16[400,768]{1,0:T(8,128)(2,1)S(1)} %copy-done), channel_id=1, source_target_pairs={{0,4},{1,5},{2,6},{3,7},{4,0},{5,1},{6,2},{7,3},{8,12},{9,13},{10,... | collective-permute-start | bytes 1843208 | tf_op jit(solution)/shard_map/ppermute | solution.py:454
  113.9 36.8 %collective-permute-start.21 = (bf16[4,400,768]{2,1,0:T(8,128)(2,1)}, bf16[4,400,768]{2,1,0:T(8,128)(2,1)}, u32[]{:S(2)}, u32[]{:S(2)}) collective-permute-start(bf16[4,400,768]{2,1,0:T(8,128)(2,1)} %bitcast.69), channel_id=1, source_target_pairs={{0,2},{1,5},{2,0},{3,7},{4,6},{5,1},{6,4},{7,3},{8,10},{9,13},{10,... | collective-permute-start | bytes 7372808 | tf_op jit(solution)/shard_map/ppermute | solution.py:454
  115.4 103.4 %all-gather.19.cloned.1.call-start = ((), (), s32[]{:S(2)}) async-start(), calls=%async_computation.3 | async-start | bytes 3072000 | tf_op jit(solution)/shard_map/all_gather | solution.py:1613
  115.5 4.1 %collective-permute-start.18 = (bf16[400,768]{1,0:T(8,128)(2,1)}, bf16[400,768]{1,0:T(8,128)(2,1)S(1)}, u32[]{:S(2)}, u32[]{:S(2)}) collective-permute-start(bf16[400,768]{1,0:T(8,128)(2,1)} %collective-permute-done.16.refs_1_.h_a_ref), channel_id=1, source_target_pairs={{0,1},{1,0},{2,3},{3,2},{4,5},{5,4},{6,7},{7,6},{8,9},{9,8},{10,11... | collective-permute-start | bytes 1843208 | tf_op jit(solution)/shard_map/ppermute | solution.py:454
  115.6 4.0 %collective-permute-start.19 = (bf16[400,768]{1,0:T(8,128)(2,1)S(1)}, bf16[400,768]{1,0:T(8,128)(2,1)S(1)}, u32[]{:S(2)}, u32[]{:S(2)}) collective-permute-start(bf16[400,768]{1,0:T(8,128)(2,1)S(1)} %collective-permute-done.12.refs_5_.g_a_ref), channel_id=1, source_target_pairs={{0,1},{1,0},{2,3},{3,2},{4,5},{5,4},{6,7},{7,6},{8,9},{9,8},{10,11... | collective-permute-start | bytes 1843208 | tf_op jit(solution)/shard_map/ppermute | solution.py:454
  116.1 26.8 %collective-permute-start.20 = (bf16[400,768]{1,0:T(8,128)(2,1)S(1)}, bf16[400,768]{1,0:T(8,128)(2,1)S(1)}, u32[]{:S(2)}, u32[]{:S(2)}) collective-permute-start(bf16[400,768]{1,0:T(8,128)(2,1)S(1)} %copy-done.1), channel_id=1, source_target_pairs={{0,4},{1,3},{2,6},{3,1},{4,0},{5,7},{6,2},{7,5},{8,12},{9,11},{10,... | collective-permute-start | bytes 1843208 | tf_op jit(solution)/shard_map/ppermute | solution.py:454
  119.5 57.9 %collective-permute-start.23 = (bf16[4,400,768]{2,1,0:T(8,128)(2,1)}, bf16[4,400,768]{2,1,0:T(8,128)(2,1)}, u32[]{:S(2)}, u32[]{:S(2)}) collective-permute-start(bf16[4,400,768]{2,1,0:T(8,128)(2,1)} %bitcast.70), channel_id=1, source_target_pairs={{0,1},{1,0},{2,3},{3,2},{4,5},{5,4},{6,7},{7,6},{8,9},{9,8},{10,11... | collective-permute-start | bytes 7372808 | tf_op jit(solution)/shard_map/ppermute | solution.py:454
  150.8 30.2 %collective-permute-start.22 = (bf16[4,400,768]{2,1,0:T(8,128)(2,1)}, bf16[4,400,768]{2,1,0:T(8,128)(2,1)S(1)}, u32[]{:S(2)}, u32[]{:S(2)}) collective-permute-start(bf16[4,400,768]{2,1,0:T(8,128)(2,1)} %collective-permute-done.21.refs_5_.refs_6_), channel_id=1, source_target_pairs={{0,4},{1,3},{2,6},{3,1},{4,0},{5,7},{6,2},{7,5},{8,12},{9,11},{10,... | collective-permute-start | bytes 7372808 | tf_op jit(solution)/shard_map/ppermute | solution.py:454
  152.2 28.7 %collective-permute-start.24 = (bf16[4,400,768]{2,1,0:T(8,128)(2,1)}, bf16[4,400,768]{2,1,0:T(8,128)(2,1)}, u32[]{:S(2)}, u32[]{:S(2)}) collective-permute-start(bf16[4,400,768]{2,1,0:T(8,128)(2,1)} %collective-permute-done.21.refs_5_.refs_6_), channel_id=1, source_target_pairs={{0,1},{1,0},{2,3},{3,2},{4,5},{5,4},{6,7},{7,6},{8,9},{9,8},{10,11... | collective-permute-start | bytes 7372808 | tf_op jit(solution)/shard_map/ppermute | solution.py:454
  152.2 132.3 %all-gather.21.cloned.1.call-start = ((), (), s32[]{:S(2)}) async-start(), calls=%async_computation.4 | async-start | bytes 3072000 | tf_op jit(solution)/shard_map/all_gather | solution.py:1639
  180.9 39.4 %copy-start.3 = (bf16[4,400,768]{2,1,0:T(8,128)(2,1)}, bf16[4,400,768]{2,1,0:T(8,128)(2,1)S(1)}, u32[]{:S(2)}) copy-start(bf16[4,400,768]{2,1,0:T(8,128)(2,1)S(1)} %collective-permute-done.22.refs_9_.refs_5_) | copy-start | bytes 7372804
  180.9 2.2 collective-permute-start.25
  184.4 5.1 %collective-permute-start.26 = (bf16[4,400,768]{2,1,0:T(8,128)(2,1)}, bf16[4,400,768]{2,1,0:T(8,128)(2,1)}, u32[]{:S(2)}, u32[]{:S(2)}) collective-permute-start(bf16[4,400,768]{2,1,0:T(8,128)(2,1)} %bitcast.73), channel_id=1, source_target_pairs={{0,1},{1,0},{2,3},{3,2},{4,5},{5,4},{6,7},{7,6},{8,9},{9,8},{10,11... | collective-permute-start | bytes 7372808 | tf_op jit(solution)/shard_map/ppermute | solution.py:454
  184.7 16.7 %collective-permute-start.27 = (bf16[400,768]{1,0:T(8,128)(2,1)}, bf16[400,768]{1,0:T(8,128)(2,1)}, u32[]{:S(2)}, u32[]{:S(2)}) collective-permute-start(bf16[400,768]{1,0:T(8,128)(2,1)} %get-tuple-element.282), channel_id=1, source_target_pairs={{0,1},{1,0},{2,3},{3,2},{4,5},{5,4},{6,7},{7,6},{8,9},{9,8},{10,11... | collective-permute-start | bytes 1843208 | tf_op jit(solution)/shard_map/ppermute | solution.py:454
  185.0 16.4 %collective-permute-start.28 = (bf16[400,768]{1,0:T(8,128)(2,1)S(1)}, bf16[400,768]{1,0:T(8,128)(2,1)}, u32[]{:S(2)}, u32[]{:S(2)}) collective-permute-start(bf16[400,768]{1,0:T(8,128)(2,1)S(1)} %add_convert_fusion.2), channel_id=1, source_target_pairs={{0,2},{1,3},{2,0},{3,1},{4,6},{5,7},{6,4},{7,5},{8,10},{9,11},{10,... | collective-permute-start | bytes 1843208 | tf_op jit(solution)/shard_map/ppermute | solution.py:454
  206.5 12.4 %collective-permute-start.29 = (bf16[128,768]{1,0:T(8,128)(2,1)}, bf16[128,768]{1,0:T(8,128)(2,1)S(1)}, u32[]{:S(2)}, u32[]{:S(2)}) collective-permute-start(bf16[128,768]{1,0:T(8,128)(2,1)} %get-tuple-element.290), channel_id=1, source_target_pairs={{0,4},{1,5},{2,6},{3,7},{4,0},{5,1},{6,2},{7,3},{8,12},{9,13},{10,... | collective-permute-start | bytes 589832 | tf_op jit(solution)/shard_map/ppermute | solution.py:454
  218.8 30.2 %collective-permute-start.30 = (bf16[4,400,768]{2,1,0:T(8,128)(2,1)}, bf16[4,400,768]{2,1,0:T(8,128)(2,1)}, u32[]{:S(2)}, u32[]{:S(2)}) collective-permute-start(bf16[4,400,768]{2,1,0:T(8,128)(2,1)} %bitcast.75), channel_id=1, source_target_pairs={{0,2},{1,5},{2,0},{3,7},{4,6},{5,1},{6,4},{7,3},{8,10},{9,13},{10,... | collective-permute-start | bytes 7372808 | tf_op jit(solution)/shard_map/ppermute | solution.py:454
  220.3 28.7 %collective-permute-start.31 = (bf16[4,400,768]{2,1,0:T(8,128)(2,1)}, bf16[4,400,768]{2,1,0:T(8,128)(2,1)}, u32[]{:S(2)}, u32[]{:S(2)}) collective-permute-start(bf16[4,400,768]{2,1,0:T(8,128)(2,1)} %bitcast.63), channel_id=1, source_target_pairs={{0,1},{1,0},{2,3},{3,2},{4,5},{5,4},{6,7},{7,6},{8,9},{9,8},{10,11... | collective-permute-start | bytes 7372808 | tf_op jit(solution)/shard_map/ppermute | solution.py:454
  220.3 28.7 %collective-permute-start.32 = (bf16[4,400,768]{2,1,0:T(8,128)(2,1)S(1)}, bf16[4,400,768]{2,1,0:T(8,128)(2,1)}, u32[]{:S(2)}, u32[]{:S(2)}) collective-permute-start(bf16[4,400,768]{2,1,0:T(8,128)(2,1)S(1)} %collective-permute-done.22.refs_9_.refs_5_), channel_id=1, source_target_pairs={{0,1},{1,0},{2,3},{3,2},{4,5},{5,4},{6,7},{7,6},{8,9},{9,8},{10,11... | collective-permute-start | bytes 7372808 | tf_op jit(solution)/shard_map/ppermute | solution.py:454
  220.8 141.2 %all-gather.23.cloned.1.call-start = ((), (), s32[]{:S(2)}) async-start(), calls=%async_computation.5 | async-start | bytes 2654208 | tf_op jit(solution)/shard_map/all_gather | solution.py:1696
  249.0 35.5 %collective-permute-start.34 = (bf16[4,208,1536]{2,1,0:T(8,128)(2,1)}, bf16[4,208,1536]{2,1,0:T(8,128)(2,1)}, u32[]{:S(2)}, u32[]{:S(2)}) collective-permute-start(bf16[4,208,1536]{2,1,0:T(8,128)(2,1)} %get-tuple-element.311), channel_id=1, source_target_pairs={{0,1},{1,0},{2,3},{3,2},{4,5},{5,4},{6,7},{7,6},{8,9},{9,8},{10,11... | collective-permute-start | bytes 7667720 | tf_op jit(solution)/shard_map/ppermute | solution.py:454
  249.1 8.7 %collective-permute-start.33 = (bf16[4,400,768]{2,1,0:T(8,128)(2,1)}, bf16[4,400,768]{2,1,0:T(8,128)(2,1)}, u32[]{:S(2)}, u32[]{:S(2)}) collective-permute-start(bf16[4,400,768]{2,1,0:T(8,128)(2,1)} %collective-permute-done.30.refs_1_.refs_0_), channel_id=1, source_target_pairs={{0,1},{1,0},{2,3},{3,2},{4,5},{5,4},{6,7},{7,6},{8,9},{9,8},{10,11... | collective-permute-start | bytes 7372808 | tf_op jit(solution)/shard_map/ppermute | solution.py:454
  249.6 35.0 %collective-permute-start.35 = (bf16[4,400,768]{2,1,0:T(8,128)(2,1)}, bf16[4,400,768]{2,1,0:T(8,128)(2,1)S(1)}, u32[]{:S(2)}, u32[]{:S(2)}) collective-permute-start(bf16[4,400,768]{2,1,0:T(8,128)(2,1)} %collective-permute-done.30.refs_1_.refs_0_), channel_id=1, source_target_pairs={{0,4},{1,3},{2,6},{3,1},{4,0},{5,7},{6,2},{7,5},{8,12},{9,11},{10,... | collective-permute-start | bytes 7372808 | tf_op jit(solution)/shard_map/ppermute | solution.py:454
  284.6 7.4 %collective-permute-start.36 = (bf16[4,400,768]{2,1,0:T(8,128)(2,1)}, bf16[4,400,768]{2,1,0:T(8,128)(2,1)}, u32[]{:S(2)}, u32[]{:S(2)}) collective-permute-start(bf16[4,400,768]{2,1,0:T(8,128)(2,1)} %bitcast.66), channel_id=1, source_target_pairs={{0,1},{1,0},{2,3},{3,2},{4,5},{5,4},{6,7},{7,6},{8,9},{9,8},{10,11... | collective-permute-start | bytes 7372808 | tf_op jit(solution)/shard_map/ppermute | solution.py:454
  284.8 8.2 %collective-permute-start.37 = (bf16[4,400,768]{2,1,0:T(8,128)(2,1)S(1)}, bf16[4,400,768]{2,1,0:T(8,128)(2,1)}, u32[]{:S(2)}, u32[]{:S(2)}) collective-permute-start(bf16[4,400,768]{2,1,0:T(8,128)(2,1)S(1)} %collective-permute-done.35.refs_3_.refs_1_), channel_id=1, source_target_pairs={{0,1},{1,0},{2,3},{3,2},{4,5},{5,4},{6,7},{7,6},{8,9},{9,8},{10,11... | collective-permute-start | bytes 7372808 | tf_op jit(solution)/shard_map/ppermute | solution.py:454
  292.9 29.9 %collective-permute-start.38 = (bf16[4,208,384]{2,1,0:T(8,128)(2,1)}, bf16[4,208,384]{2,1,0:T(8,128)(2,1)S(1)}, u32[]{:S(2)}, u32[]{:S(2)}) collective-permute-start(bf16[4,208,384]{2,1,0:T(8,128)(2,1)} %get-tuple-element.331), channel_id=1, source_target_pairs={{0,2},{1,3},{2,0},{3,1},{4,6},{5,7},{6,4},{7,5},{8,10},{9,11},{10,... | collective-permute-start | bytes 1916936 | tf_op jit(solution)/shard_map/ppermute | solution.py:454
  294.4 30.0 %collective-permute-start.39 = (bf16[4,208,384]{2,1,0:T(8,128)(2,1)}, bf16[4,208,384]{2,1,0:T(8,128)(2,1)S(1)}, u32[]{:S(2)}, u32[]{:S(2)}) collective-permute-start(bf16[4,208,384]{2,1,0:T(8,128)(2,1)} %broadcast_select_fusion.2), channel_id=1, source_target_pairs={{0,4},{1,5},{2,6},{3,7},{4,0},{5,1},{6,2},{7,3},{8,12},{9,13},{10,... | collective-permute-start | bytes 1916936 | tf_op jit(solution)/shard_map/ppermute | solution.py:454
  295.9 28.6 %collective-permute-start.40 = (bf16[4,208,384]{2,1,0:T(8,128)(2,1)}, bf16[4,208,384]{2,1,0:T(8,128)(2,1)S(1)}, u32[]{:S(2)}, u32[]{:S(2)}) collective-permute-start(bf16[4,208,384]{2,1,0:T(8,128)(2,1)} %get-tuple-element.333), channel_id=1, source_target_pairs={{0,6},{1,7},{2,4},{3,5},{4,2},{5,3},{6,0},{7,1},{8,14},{9,15},{10,... | collective-permute-start | bytes 1916936 | tf_op jit(solution)/shard_map/ppermute | solution.py:454
  324.5 2.3 collective-permute-start.41
  324.5 3.6 collective-permute-start.42
  328.1 34.0 %collective-permute-start.46 = (bf16[384,768]{1,0:T(8,128)(2,1)S(1)}, bf16[384,768]{1,0:T(8,128)(2,1)S(1)}, u32[]{:S(2)}, u32[]{:S(2)}) collective-permute-start(bf16[384,768]{1,0:T(8,128)(2,1)S(1)} %add_convert_fusion.4), channel_id=1, source_target_pairs={{0,2},{1,3},{2,0},{3,1},{4,6},{5,7},{6,4},{7,5},{8,10},{9,11},{10,... | collective-permute-start | bytes 1769480 | tf_op jit(solution)/shard_map/ppermute | solution.py:454
  329.3 32.7 %collective-permute-start.43 = (bf16[208,384]{1,0:T(8,128)(2,1)S(1)}, bf16[208,384]{1,0:T(8,128)(2,1)S(1)}, u32[]{:S(2)}, u32[]{:S(2)}) collective-permute-start(bf16[208,384]{1,0:T(8,128)(2,1)S(1)} %get-tuple-element.358), channel_id=1, source_target_pairs={{0,8},{1,9},{2,10},{3,11},{4,12},{5,13},{6,14},{7,15},{8,16},{9,17... | collective-permute-start | bytes 479240 | tf_op jit(solution)/shard_map/ppermute | solution.py:454
  329.3 32.7 %collective-permute-start.44 = (bf16[208,384]{1,0:T(8,128)(2,1)S(1)}, bf16[208,384]{1,0:T(8,128)(2,1)S(1)}, u32[]{:S(2)}, u32[]{:S(2)}) collective-permute-start(bf16[208,384]{1,0:T(8,128)(2,1)S(1)} %get-tuple-element.359), channel_id=1, source_target_pairs={{0,16},{1,17},{2,18},{3,19},{4,20},{5,21},{6,22},{7,23},{8,24},{9,... | collective-permute-start | bytes 479240 | tf_op jit(solution)/shard_map/ppermute | solution.py:454
  331.0 31.0 %collective-permute-start.45 = (bf16[208,384]{1,0:T(8,128)(2,1)S(1)}, bf16[208,384]{1,0:T(8,128)(2,1)S(1)}, u32[]{:S(2)}, u32[]{:S(2)}) collective-permute-start(bf16[208,384]{1,0:T(8,128)(2,1)S(1)} %get-tuple-element.360), channel_id=1, source_target_pairs={{0,24},{1,25},{2,26},{3,27},{4,28},{5,29},{6,30},{7,31},{8,0},{9,1... | collective-permute-start | bytes 479240 | tf_op jit(solution)/shard_map/ppermute | solution.py:454
  362.2 9.9 %collective-permute-start.47 = (bf16[208,384]{1,0:T(8,128)(2,1)S(1)}, bf16[208,384]{1,0:T(8,128)(2,1)S(1)}, u32[]{:S(2)}, u32[]{:S(2)}) collective-permute-start(bf16[208,384]{1,0:T(8,128)(2,1)S(1)} %add_convert_fusion.5), channel_id=1, source_target_pairs={{0,2},{1,3},{2,0},{3,1},{4,6},{5,7},{6,4},{7,5},{8,10},{9,11},{10,... | collective-permute-start | bytes 479240 | tf_op jit(solution)/shard_map/ppermute | solution.py:454
  363.2 8.9 %collective-permute-start.48 = (bf16[208,384]{1,0:T(8,128)(2,1)S(1)}, bf16[208,384]{1,0:T(8,128)(2,1)S(1)}, u32[]{:S(2)}, u32[]{:S(2)}) collective-permute-start(bf16[208,384]{1,0:T(8,128)(2,1)S(1)} %add_convert_fusion.5), channel_id=1, source_target_pairs={{0,4},{1,5},{2,6},{3,7},{4,0},{5,1},{6,2},{7,3},{8,12},{9,13},{10,... | collective-permute-start | bytes 479240 | tf_op jit(solution)/shard_map/ppermute | solution.py:454
  364.7 7.4 %collective-permute-start.49 = (bf16[208,384]{1,0:T(8,128)(2,1)S(1)}, bf16[208,384]{1,0:T(8,128)(2,1)S(1)}, u32[]{:S(2)}, u32[]{:S(2)}) collective-permute-start(bf16[208,384]{1,0:T(8,128)(2,1)S(1)} %add_convert_fusion.5), channel_id=1, source_target_pairs={{0,6},{1,7},{2,4},{3,5},{4,2},{5,3},{6,0},{7,1},{8,14},{9,15},{10,... | collective-permute-start | bytes 479240 | tf_op jit(solution)/shard_map/ppermute | solution.py:454
  372.5 2.1 collective-permute-start.50
  (26 other events, 112.2 us)
Sparse Core Ops, SparseCore 0:
  28.9 31.6 all-gather.12
  62.3 51.6 all-gather.14
  115.6 50.8 all-gather.16
  167.9 50.8 all-gather.18
  220.9 50.1 all-gather.20
  328.2 30.0 all-gather.22

commit v6 on v5

--- a/solution.py
+++ b/solution.py
@@ -527,7 +527,7 @@
     arrivals = [
         pltpu.make_async_copy(
             block_refs[side * blocks + b],
-            in_sc.at[b, :, side * D : (side + 1) * D],
+            in_sc.at[b, : (ROWS, TOK_DEV)[side], side * D : (side + 1) * D],
             in_sems.at[side, b],
         )
         for b in range(blocks)
@@ -544,10 +544,8 @@
         for b in range(blocks):
             for one in arrivals[2 * b : 2 * b + 2]:
                 one.wait()
-            rank_sc[b] = in_sc[b, TOK_DEV:, D : D + TOK_DEV].astype(F32)
-            prob_sc[b] = in_sc[b, TOK_DEV:, :TOK_DEV].astype(F32) + in_sc[
-                b, TOK_DEV:, TOK_DEV:D
-            ].astype(F32)
+            rank_sc[b] = in_sc[b, TOK_DEV:, TOK_DEV:D].astype(F32)
+            prob_sc[b] = in_sc[b, TOK_DEV:, :TOK_DEV].astype(F32)
             hots = []
             for i in range(count):
                 hot = one_hot_rows(rank_sc[b, pl.ds(base + i, 1), :])
@@ -731,7 +729,9 @@
             copies.append(
                 (
                     pltpu.make_async_copy(h_parts[i].at[at], h_buf.at[into], sems.at[0, number]),
-                    pltpu.make_async_copy(g_parts[i].at[at], g_buf.at[into], sems.at[1, number]),
+                    pltpu.make_async_copy(
+                        g_parts[i].at[at, :TOK_DEV], g_buf.at[into, :TOK_DEV], sems.at[1, number]
+                    ),
                 )
             )
     for pair in copies:
@@ -778,10 +778,8 @@
         both = []
         for k in range(2):
             b = 2 * pair + k
-            rank_sc[k] = buf[b, TOK_DEV:, D : D + TOK_DEV].astype(F32)
-            prob_sc[k] = buf[b, TOK_DEV:, :TOK_DEV].astype(F32) + buf[
-                b, TOK_DEV:, TOK_DEV:D
-            ].astype(F32)
+            rank_sc[k] = buf[b, TOK_DEV:, TOK_DEV:D].astype(F32)
+            prob_sc[k] = buf[b, TOK_DEV:, :TOK_DEV].astype(F32)
             hots, gates = [], []
             for i in range(experts):
                 hot = one_hot_rows(rank_sc[k, pl.ds(base + i, 1), :])
@@ -1012,8 +1010,10 @@
         router_ref,
         cos_ref,
         sin_ref,
+        rank_ref,
         *outs,
         h2_ref,
+        probs_ref,
         w_ref,
         q_ref,
         k_ref,
@@ -1106,14 +1106,14 @@
     logits = contract(router_ref[...], hidden, 1, 1)
     logits = jnp.exp(logits - jnp.max(logits, 0, keepdims=True))
     probs = logits / jnp.sum(logits, 0, keepdims=True)
-    high = probs.astype(BF)
-    h2_ref[TOK_DEV:, :TOK_DEV] = high
-    h2_ref[TOK_DEV:, TOK_DEV:] = (probs - high.astype(F32)).astype(BF)
+    probs_ref[...] = probs
+    h2_ref[TOK_DEV:, :TOK_DEV] = probs.astype(BF)
+    h2_ref[TOK_DEV:, TOK_DEV:] = rank_ref[...]
     for one in leaving:
         one.wait()
 
 
-def attention_forward(place, w_parts, h1, own, far, gain1, gain2, router_t, cos, sin):
+def attention_forward(place, w_parts, h1, own, far, gain1, gain2, router_t, cos, sin, ranks):
     vmem = pl.BlockSpec(memory_space=pltpu.VMEM)
     hbm = pl.BlockSpec(memory_space=pltpu.HBM)
     kept = (
@@ -1126,11 +1126,14 @@
     )
     return pl.pallas_call(
         attention_kernel,
-        out_shape=tuple(jax.ShapeDtypeStruct(*s) for s in kept + (((ROWS, D), BF),)),
+        out_shape=tuple(
+            jax.ShapeDtypeStruct(*s)
+            for s in kept + (((ROWS, D), BF), ((EXPERTS, TOK_DEV), F32))
+        ),
         in_specs=[pl.BlockSpec(memory_space=pltpu.SMEM)]
         + [pl.BlockSpec(memory_space=pl.ANY)] * 8
-        + [vmem] * 8,
-        out_specs=(hbm,) * len(kept) + (vmem,),
+        + [vmem] * 9,
+        out_specs=(hbm,) * len(kept) + (vmem, vmem),
         scratch_shapes=[pltpu.VMEM(*s) for s in kept]
         + [
             pltpu.VMEM((2 * TOK_DEV, D), BF),
@@ -1140,13 +1143,14 @@
         compiler_params=pltpu.CompilerParams(vmem_limit_bytes=VMEM_LIMIT),
         cost_estimate=microseconds(20),
         name="attention_forward",
-    )(place, *w_parts, h1, own, far, gain1, gain2, router_t, cos, sin)
+    )(place, *w_parts, h1, own, far, gain1, gain2, router_t, cos, sin, ranks)
 
 
 def branch_kernel(*refs):
     dx_refs, refs = refs[:3], refs[3:]
     (
         h2_ref,
+        probs_ref,
         x1_ref,
         g_ref,
         gain2_ref,
@@ -1160,7 +1164,7 @@
     ) = refs
     dx = dx_refs[0][...].astype(F32) + dx_refs[1][...].astype(F32) + dx_refs[2][...].astype(F32)
     drp = dx[TOK_DEV:, :TOK_DEV] + dx[TOK_DEV:, TOK_DEV:]
-    probs = h2_ref[TOK_DEV:, :TOK_DEV].astype(F32) + h2_ref[TOK_DEV:, TOK_DEV:].astype(F32)
+    probs = probs_ref[...]
     dlogits = (probs * (drp - jnp.sum(probs * drp, 0, keepdims=True))).astype(BF)
     hidden = h2_ref[:TOK_DEV, :]
     grouter_ref[...] = jnp.dot(dlogits, hidden, preferred_element_type=F32)
@@ -1184,7 +1188,7 @@
     do_c_ref[...] = do_ref[PROMPT:, :]
 
 
-def branch_backward(dx, h_block, x1, grad, gain2, router_t, w_all):
+def branch_backward(dx, h_block, probs, x1, grad, gain2, router_t, w_all):
     shape = jax.ShapeDtypeStruct
     whole = lambda *dims: pl.BlockSpec(dims, lambda i: (0,) * len(dims))
     rows = whole(TOK_DEV, D)
@@ -1203,6 +1207,7 @@
             whole(ROWS, D),
             whole(ROWS, D),
             whole(ROWS, D),
+            whole(EXPERTS, TOK_DEV),
             rows,
             rows,
             whole(1, D),
@@ -1219,7 +1224,7 @@
         compiler_params=pltpu.CompilerParams(vmem_limit_bytes=VMEM_LIMIT),
         cost_estimate=microseconds(6),
         name="branch_backward",
-    )(*dx, h_block, x1, grad, gain2, router_t, w_all)
+    )(*dx, h_block, probs, x1, grad, gain2, router_t, w_all)
 
 
 def attention_back_kernel(
@@ -1577,7 +1582,7 @@
     before = (jnp.arange(TOK_DEV)[:, None] < jnp.arange(TOK_DEV)[None, :]).astype(BF)
     ranks = jnp.dot(member.astype(BF), before, preferred_element_type=F32)
     ranks = jnp.where(member, ranks, -1.0).astype(BF)
-    g_block = jnp.concatenate([cotangent, jnp.pad(ranks, ((0, 0), (0, D - TOK_DEV)))], 0)
+    g_block = cotangent
     g_near = after(g_block, h1)
     g_x = over_x(g_near)
     g_group = [g_block, g_x, over_core(g_near), over_core(g_x)]
@@ -1588,8 +1593,8 @@
     shared_far = over_y(after(shared, h1))
     place = after(place, shared)
     flags = jnp.concatenate([prompt_ids == y, far_ids[:, 0].astype(jnp.int32) == y, core[None] != 0]).astype(jnp.int32)
-    w_all, q, k, v, o, x1, h_block = attention_forward(
-        place, dense_parts, h1, tokens, far, gain1, gain2, router_t, cos, sin
+    w_all, q, k, v, o, x1, h_block, probs = attention_forward(
+        place, dense_parts, h1, tokens, far, gain1, gain2, router_t, cos, sin, ranks
     )
     (h_block, x1), (g_x, shared_far) = beside((h_block, x1), (g_x, shared_far))
     g_group = [g_block, g_x, over_core(g_block), over_core(g_x)]
@@ -1603,7 +1608,7 @@
     more, (h_x, g_y) = beside(more, (h_x, over_y(after(g_block, h_block))))
     h_far, g_far = [h_x, over_core(h_x)], [g_x, g_group[3]]
     h_group = [h_near[0], h_far[0], h_near[1], h_far[1]]
-    g_second = jnp.where(core == 0, g_y, g_x)
+    g_second = jnp.pad(jnp.where(core == 0, g_y, g_x), ((0, EXT), (0, 0)))
     h_group, g_second = after((h_group, g_second))
     part = group_experts(base[None], 0, 2, h_group, g_group, (), *experts_w)
     (part, h_far), h_b = beside((part, h_far), over_b(after(h_block, h_x)))
@@ -1631,7 +1636,7 @@
     )
     s_sums, dx = beside(s_sums, dx)
     dx1, do, do_c, grad_router_t, grad_gain2 = branch_backward(
-        dx, h_block, x1, cotangent, gain2, router_t, w_all
+        dx, h_block, probs, x1, cotangent, gain2, router_t, w_all
     )
     gwo = inner_rows(o, dx1.astype(BF)).astype(BF)
     gwo, (do_far, g_second) = beside(gwo, (over_y(do_c), g_second))

time: 392 us -> 390 us (level)
  local copies, waits for them, and re-layouts: 17 us -> 24.7 us
  waiting for transfers between devices: 76.6 us -> 71 us
    unnamed x78 -> x90, local copies, waits for them, and re-layouts: 7.24 us -> 13.3 us
    ppermute x51, waiting for transfers between devices: 51.2 us -> 46.1 us  [moved(): return lax.ppermute(value, AXES, pairs)]
  transfers between devices with their start and end apart: 57 -> 57, of which waited for: 22 -> 21; matrix products, arithmetic and copies ran while one was open for 8% -> 9% of each run, Pallas kernels for 53% -> 53%
where the time goes in v6:
time: 390 us; the launch traced here: 383 us
  Pallas kernels  204 us (52%)
  waiting for transfers between devices  71 us (18%)
  starting transfers between devices  43.1 us (11%)
  local copies, waits for them, and re-layouts  24.7 us (6%)
  other arithmetic  19 us (5%)
  between operations  17.1 us (4%)
  matrix products  3.9 us (1%)
    pallas_call x2, Pallas kernels, expert_slice_grads(): pl.pallas_call(functools.partial(expert_slice_kernel, parts, len(sums) //...  53.9 us
    pallas_call x2, Pallas kernels, group_experts(): pl.pallas_call(functools.partial(group_kernel, blocks, len(more)), out_sh...  47.2 us
    ppermute x51, waiting for transfers between devices, moved(): return lax.ppermute(value, AXES, pairs)  46.1 us
    ppermute x51, starting transfers between devices, moved(): return lax.ppermute(value, AXES, pairs)  42.9 us
    pallas_call x2, Pallas kernels, shared_slice_grads(): pl.pallas_call(functools.partial(shared_slice_kernel, parts, len(sums) //...  38.2 us
    pallas_call x1, Pallas kernels, attention_backward(): pl.pallas_call(attention_back_kernel, out_shape=(shape((TOK_DEV, D), F32)...  20.7 us
    pallas_call x1, Pallas kernels, attention_forward(): pl.pallas_call(attention_kernel, out_shape=tuple((jax.ShapeDtypeStruct(*s...  17.2 us
    pallas_call x2, Pallas kernels, shared_rows(): pl.pallas_call(shared_kernel, out_shape=(rows, rows), in_specs=[vmem] * 6...  15.4 us
  transfers between devices with their start and end apart: 57, of which 21 were waited for; matrix products, arithmetic and copies ran while one was open for 9% of the time, Pallas kernels for 53%

profile of v6, /device:TPU:0, one launch (start us, length us, event | category | flops | bytes accessed | tf_op | source)
XLA Modules:
  0.0 382.8 jit_solution(12725869014190217951)
XLA Ops:
  7.3 3.0 collective-permute-start.3
  10.3 1.0 fusion.5
  12.2 1.6 collective-permute-start
  13.8 2.6 collective-permute-start.1
  16.4 1.3 collective-permute-start.2
  22.9 1.8 collective-permute-done.4
  24.7 2.2 collective-permute-done.1
  26.9 1.2 pad_maximum_fusion.refs_0_
  31.7 1.5 collective-permute-start.5
  40.3 2.1 norm_rows.1.refs_8_.refs_4_
  42.4 5.8 %collective-permute-done.5.refs_1_ = bf16[4,208,384]{2,1,0:T(8,128)(2,1)S(1)} collective-permute-done((bf16[4,208,384]{2,1,0:T(8,128)(2,1)S(1)}, bf16[4,208,384]{2,1,0:T(8,128)(2,1)S(1)}, u32[]{:S(2)}, u32[]{:S(2)}) %collective-permute-start.5) | collective-permute-done | bytes 639008 | tf_op jit(solution)/shard_map/ppermute | solution.py:454
  48.2 1.2 collective-permute-start.7
  49.4 11.9 %all-gather.13.cloned.1.call-done = bf16[768,768]{1,0:T(8,128)(2,1)} async-done(((bf16[192,768]{1,0:T(8,128)(2,1)}), bf16[768,768]{1,0:T(8,128)(2,1)}) %all-gather.13.cloned.1.call-update) | async-done | bytes 1179664 | tf_op jit(solution)/shard_map/all_gather | solution.py:1592
  61.3 1.5 collective-permute-start.13
  63.3 1.5 collective-permute-start.12
  67.5 17.2 %attention_forward.1 = (bf16[8,768,384]{2,1,0:T(8,128)(2,1)}, bf16[768,768]{1,0:T(8,128)(2,1)}, bf16[768,768]{1,0:T(8,128)(2,1)}, bf16[768,768]{1,0:T(8,128)(2,1...) custom-call(s32[14]{0:T(128)} %stack.109.place_ref, ...), custom_call_target="tpu_custom_call" | custom-call | bytes 8000000 | tf_op jit(solution)/shard_map/attention_forward/pallas_call | solution.py:1127
  84.7 3.9 %collective-permute-done.13.w_b_ref = bf16[4,192,768]{2,1,0:T(8,128)(2,1)S(1)} collective-permute-done((bf16[4,192,768]{2,1,0:T(8,128)(2,1)}, bf16[4,192,768]{2,1,0:T(8,128)(2,1)S(1)}, u32[]{:S(2)}, u32[]{:S(2)}) %collective-permute-start.13) | collective-permute-done | bytes 1179680 | tf_op jit(solution)/shard_map/ppermute | solution.py:454
  89.6 1.5 collective-permute-start.16
  91.4 1.5 collective-permute-start.17
  94.8 7.6 %shared_rows.2 = (bf16[2,384,768]{2,1,0:T(8,128)(2,1)}, bf16[2,384,768]{2,1,0:T(8,128)(2,1)}) custom-call(bf16[400,768]{1,0:T(8,128)(2,1)} %get-tuple-element.240.h_a_ref.refs_0_.refs_3_, bf16[400,768]{1,0:T(8,128)(2,1)} %copy-done.7, bf16[384,768]{1,0:T(8,128)(2,1)} %refs_6_.2, bf16[384,768]{1,0:T(8,128)(2,1)} %copy-done.9, bf16[4,192,768]{2,1,0:T(8,128)(2,1)} %bitcast.59, ...), custom_call_target="tpu_custom_call" | custom-call | bytes 3200000 | tf_op jit(solution)/shard_map/shared_rows/pallas_call | solution.py:705
  102.4 4.6 %collective-permute-done.17 = bf16[384,768]{1,0:T(8,128)(2,1)} collective-permute-done((bf16[384,768]{1,0:T(8,128)(2,1)S(1)}, bf16[384,768]{1,0:T(8,128)(2,1)}, u32[]{:S(2)}, u32[]{:S(2)}) %collective-permute-start.17) | collective-permute-done | bytes 589856 | tf_op jit(solution)/shard_map/ppermute | solution.py:454
  107.0 5.5 %all-gather.15.cloned.1.call-done = bf16[1536,768]{1,0:T(8,128)(2,1)} async-done(((bf16[384,768]{1,0:T(8,128)(2,1)}), bf16[1536,768]{1,0:T(8,128)(2,1)}) %all-gather.15.cloned.1.call-update) | async-done | bytes 2359312 | tf_op jit(solution)/shard_map/all_gather | solution.py:1590
  112.5 1.5 collective-permute-start.21
  114.1 1.5 collective-permute-start.20
  116.2 1.1 broadcast_select_fusion.9
  119.3 22.2 %group_experts.2 = (bf16[384,768]{1,0:T(8,128)(2,1)}, bf16[384,768]{1,0:T(8,128)(2,1)}, bf16[384,768]{1,0:T(8,128)(2,1)}, bf16[384,768]{1,0:T(8,128)(2,1)}, bf16...) custom-call(s32[1]{0:T(128)} %bitcast.28.base_ref, ...), custom_call_target="tpu_custom_call" | custom-call | bytes 8400000 | tf_op jit(solution)/shard_map/group_experts/pallas_call | solution.py:639
  141.5 7.8 %shared_rows.3 = (bf16[2,384,768]{2,1,0:T(8,128)(2,1)}, bf16[2,384,768]{2,1,0:T(8,128)(2,1)}) custom-call(bf16[400,768]{1,0:T(8,128)(2,1)} %collective-permute-done.16.refs_1_.h_a_ref, bf16[400,768]{1,0:T(8,128)(2,1)} %copy-done.8, bf16[384,768]{1,0:T(8,128)(2,1)} %copy-done.6, bf16[384,768]{1,0:T(8,128)(2,1)} %copy-done.10, bf16[4,192,768]{2,1,0:T(8,128)(2,1)} %bitcast.60, ...), custom_call_target="tpu_custom_call" | custom-call | bytes 3200000 | tf_op jit(solution)/shard_map/shared_rows/pallas_call | solution.py:705
  150.3 25.0 %group_experts.3 = (bf16[384,768]{1,0:T(8,128)(2,1)}, bf16[384,768]{1,0:T(8,128)(2,1)}, bf16[384,768]{1,0:T(8,128)(2,1)}, bf16[384,768]{1,0:T(8,128)(2,1)}, bf16...) custom-call(s32[1]{0:T(128)S(6)} %add.117.base_ref, ...), custom_call_target="tpu_custom_call" | custom-call | bytes 8400000 | tf_op jit(solution)/shard_map/group_experts/pallas_call | solution.py:639
  175.3 3.1 collective-permute-done.22.refs_9_.refs_5_
  178.5 2.2 collective-permute-done.25
  180.7 1.2 add_convert_fusion.2
  184.2 1.3 pad_add_fusion.pos_ref
  185.5 2.3 collective-permute-done.26.refs_1_.refs_2_
  187.8 1.4 copy-done.4
  189.3 11.8 %shared_slice_grads.2 = (f32[256,256]{1,0:T(8,128)}, f32[256,256]{1,0:T(8,128)}, f32[128,768]{1,0:T(8,128)}) custom-call(s32[4]{0:T(128)} %pad_add_fusion.pos_ref, bf16[4,400,768]{2,1,0:T(8,128)(2,1)} %bitcast.36.refs_0_, bf16[4,400,768]{2,1,0:T(8,128)(2,1)} %copy-done.4, bf16[4,384,768]{2,1,0:T(8,128)(2,1)} %bitcast.71, ...), custom_call_target="tpu_custom_call" | custom-call | bytes 8000000 | tf_op jit(solution)/shard_map/shared_slice_grads/pallas_call | solution.py:918
  201.1 5.1 %branch_backward.1 = (f32[384,768]{1,0:T(8,128)}, bf16[384,768]{1,0:T(8,128)(2,1)}, bf16[128,768]{1,0:T(8,128)(2,1)}, f32[16,768]{1,0:T(8,128)}, f32[1,768]{1,0:T(1,128)}) custom-call(bf16[400,768]{1,0:T(8,128)(2,1)} %get-tuple-element.284.refs_0_, bf16[400,768]{1,0:T(8,128)(2,1)} %collective-permute-done.27.refs_1_, ...), custom_call_target="tpu_custom_call" | custom-call | bytes 2400000 | tf_op jit(solution)/shard_map/branch_backward/pallas_call | solution.py:1195
  207.0 3.1 convolution_convert_fusion
  210.1 7.3 %all-gather.19.cloned.1.call-done = bf16[1600,768]{1,0:T(8,128)(2,1)} async-done(((bf16[400,768]{1,0:T(8,128)(2,1)}), bf16[1600,768]{1,0:T(8,128)(2,1)}) %all-gather.19.cloned.1.call-update) | async-done | bytes 2457616 | tf_op jit(solution)/shard_map/all_gather | solution.py:1618
  217.4 1.5 collective-permute-start.30
  220.8 20.7 %attention_backward.1 = (f32[384,768]{1,0:T(8,128)}, bf16[4,208,1536]{2,1,0:T(8,128)(2,1)}, bf16[4,208,1536]{2,1,0:T(8,128)(2,1)}) custom-call(s32[5]{0:T(128)} %add_convert_fusion.6.flags_ref, bf16[768,768]{1,0:T(8,128)(2,1)} %get-tuple-element.272.refs_0_, bf16[768,768]{1,0:T(8,128)(2,1)} %get-tuple-element.273.refs_1_, ...), custom_call_target="tpu_custom_call" | custom-call | bytes 9200000 | tf_op jit(solution)/shard_map/attention_backward/pallas_call | solution.py:1400
  241.5 6.1 %collective-permute-done.30.refs_1_.refs_0_ = bf16[4,400,768]{2,1,0:T(8,128)(2,1)} collective-permute-done((bf16[4,400,768]{2,1,0:T(8,128)(2,1)}, bf16[4,400,768]{2,1,0:T(8,128)(2,1)}, u32[]{:S(2)}, u32[]{:S(2)}) %collective-permute-start.30) | collective-permute-done | bytes 2457632 | tf_op jit(solution)/shard_map/ppermute | solution.py:454
  248.1 1.5 collective-permute-start.35
  250.2 6.1 %collective-permute-done.33.refs_3_.refs_1_ = bf16[4,400,768]{2,1,0:T(8,128)(2,1)} collective-permute-done((bf16[4,400,768]{2,1,0:T(8,128)(2,1)}, bf16[4,400,768]{2,1,0:T(8,128)(2,1)}, u32[]{:S(2)}, u32[]{:S(2)}) %collective-permute-start.33) | collective-permute-done | bytes 2457632 | tf_op jit(solution)/shard_map/ppermute | solution.py:454
  256.3 26.8 %expert_slice_grads.2 = (f32[4,768,256]{2,1,0:T(8,128)}, f32[4,768,256]{2,1,0:T(8,128)}, f32[4,256,768]{2,1,0:T(8,128)}) custom-call(s32[2]{0:T(128)} %pad_add_fusion.1.pos_ref, bf16[4,400,768]{2,1,0:T(8,128)(2,1)} %bitcast.36.refs_0_, bf16[4,400,768]{2,1,0:T(8,128)(2,1)} %collective-permute-done.30.refs_1_.refs_0_, bf16[4,400,768]{2,1,0:T(8,128)(2,1)} %copy-done.4, ...), custom_call_target="tpu_custom_call" | custom-call | bytes 12400000 | tf_op jit(solution)/shard_map/expert_slice_grads/pallas_call | solution.py:838
  283.7 3.2 add_convert_fusion
  287.8 1.3 broadcast_select_fusion.1
  289.1 1.2 collective-permute-done.36.refs_4_.refs_2_
  290.3 1.4 collective-permute-done.37.refs_5_.refs_3_
  291.7 1.5 collective-permute-start.38
  293.2 1.5 collective-permute-start.39
  295.2 26.4 %shared_slice_grads.3 = bf16[192,768]{1,0:T(8,128)(2,1)} custom-call(s32[4]{0:T(128)} %pad_add_fusion.pos_ref, bf16[4,400,768]{2,1,0:T(8,128)(2,1)} %collective-permute-done.30.refs_1_.refs_0_, bf16[4,400,768]{2,1,0:T(8,128)(2,1)} %collective-permute-done.33.refs_3_.refs_1_, bf16[4,400,768]{2,1,0:T(8,128)(2,1)} %bitcast.67, ...), custom_call_target="tpu_custom_call" | custom-call | bytes 8000000 | tf_op jit(solution)/shard_map/shared_slice_grads/pallas_call | solution.py:918
  321.6 1.8 collective-permute-done.39
  323.9 1.8 add_convert_fusion.1
  326.9 1.3 collective-permute-start.46
  328.2 1.6 collective-permute-start.44
  329.8 2.7 collective-permute-start.45
  332.5 27.1 %expert_slice_grads.3 = (f32[4,768,256]{2,1,0:T(8,128)}, f32[4,768,256]{2,1,0:T(8,128)}, f32[4,256,768]{2,1,0:T(8,128)}) custom-call(s32[2]{0:T(128)} %pad_add_fusion.1.pos_ref, bf16[4,400,768]{2,1,0:T(8,128)(2,1)} %bitcast.68, bf16[4,400,768]{2,1,0:T(8,128)(2,1)} %collective-permute-done.35.refs_3_.refs_1_, bf16[4,400,768]{2,1,0:T(8,128)(2,1)} %copy-done.3, ...), custom_call_target="tpu_custom_call" | custom-call | bytes 12400000 | tf_op jit(solution)/shard_map/expert_slice_grads/pallas_call | solution.py:838
  360.8 1.5 collective-permute-start.48
  362.3 1.1 collective-permute-start.49
  363.4 4.2 %place_shared.1 = (f32[192,2048]{1,0:T(8,128)}, f32[192,2048]{1,0:T(8,128)}, f32[512,768]{1,0:T(8,128)}) custom-call(bf16[8,192,768]{2,1,0:T(8,128)(2,1)} %bitcast.74), custom_call_target="tpu_custom_call" | custom-call | bytes 1600000 | tf_op jit(solution)/shard_map/place_shared/pallas_call | solution.py:1471
  367.6 1.1 add_convert_fusion.3
  369.9 2.1 collective-permute-done.50
  373.4 1.1 fusion.13
  374.6 1.1 fusion.12
  (212 shorter events, 38.1 us)
Async XLA Ops:
  7.2 54.0 %all-gather.13.cloned.1.call-start = ((), (), s32[]{:S(2)}) async-start(), calls=%async_computation | async-start | bytes 1474560 | tf_op jit(solution)/shard_map/all_gather | solution.py:1592
  7.3 19.6 %collective-permute-start.3 = (bf16[384,768]{1,0:T(8,128)(2,1)}, bf16[384,768]{1,0:T(8,128)(2,1)}, u32[]{:S(2)}, u32[]{:S(2)}) collective-permute-start(bf16[384,768]{1,0:T(8,128)(2,1)} %refs_6_.3), channel_id=1, source_target_pairs={{0,4},{1,5},{2,6},{3,7},{4,0},{5,1},{6,2},{7,3},{8,12},{9,13},{10,... | collective-permute-start | bytes 1769480 | tf_op jit(solution)/shard_map/ppermute | solution.py:454
  12.2 12.5 %collective-permute-start = (bf16[208,384]{1,0:T(8,128)(2,1)}, bf16[208,384]{1,0:T(8,128)(2,1)}, u32[]{:S(2)}, u32[]{:S(2)}) collective-permute-start(bf16[208,384]{1,0:T(8,128)(2,1)} %maximum_maximum_fusion.1), channel_id=1, source_target_pairs={{0,8},{1,9},{2,10},{3,11},{4,12},{5,13},{6,14},{7,15},{8,16},{9,17... | collective-permute-start | bytes 479240 | tf_op jit(solution)/shard_map/ppermute | solution.py:454
  13.8 13.1 %collective-permute-start.1 = (bf16[208,384]{1,0:T(8,128)(2,1)}, bf16[208,384]{1,0:T(8,128)(2,1)}, u32[]{:S(2)}, u32[]{:S(2)}) collective-permute-start(bf16[208,384]{1,0:T(8,128)(2,1)} %maximum_maximum_fusion.1), channel_id=1, source_target_pairs={{0,16},{1,17},{2,18},{3,19},{4,20},{5,21},{6,22},{7,23},{8,24},{9,... | collective-permute-start | bytes 479240 | tf_op jit(solution)/shard_map/ppermute | solution.py:454
  16.4 10.5 %collective-permute-start.2 = (bf16[208,384]{1,0:T(8,128)(2,1)}, bf16[208,384]{1,0:T(8,128)(2,1)}, u32[]{:S(2)}, u32[]{:S(2)}) collective-permute-start(bf16[208,384]{1,0:T(8,128)(2,1)} %maximum_maximum_fusion.1), channel_id=1, source_target_pairs={{0,24},{1,25},{2,26},{3,27},{4,28},{5,29},{6,30},{7,31},{8,0},{9,1... | collective-permute-start | bytes 479240 | tf_op jit(solution)/shard_map/ppermute | solution.py:454
  18.4 6.3 %collective-permute-start.4 = (bf16[2,128]{0,1:T(8,128)(2,1)}, bf16[2,128]{0,1:T(8,128)(2,1)}, u32[]{:S(2)}, u32[]{:S(2)}) collective-permute-start(bf16[2,128]{0,1:T(8,128)(2,1)} %broadcast_in_dim.30), channel_id=1, source_target_pairs={{0,4},{1,5},{2,6},{3,7},{4,0},{5,1},{6,2},{7,3},{8,12},{9,13},{10,... | collective-permute-start | bytes 1544 | tf_op jit(solution)/shard_map/ppermute | solution.py:454
  28.1 21.3 %copy-start.13 = (bf16[4,208,384]{2,1,0:T(8,128)(2,1)}, bf16[4,208,384]{2,1,0:T(8,128)(2,1)S(1)}, u32[]{:S(2)}) copy-start(bf16[4,208,384]{2,1,0:T(8,128)(2,1)S(1)} %pad_maximum_fusion.refs_0_) | copy-start | bytes 1916932
  29.0 34.3 %copy-start.1 = (bf16[384,768]{1,0:T(8,128)(2,1)S(1)}, bf16[384,768]{1,0:T(8,128)(2,1)}, u32[]{:S(2)}) copy-start(bf16[384,768]{1,0:T(8,128)(2,1)} %refs_6_.2) | copy-start | bytes 1769476
  29.0 35.8 %copy-start.33 = (s32[384,2]{0,1:T(2,128)S(1)}, s32[384,2]{0,1:T(2,128)}, u32[]{:S(2)}) copy-start(s32[384,2]{0,1:T(2,128)} %param.22) | copy-start | bytes 9220
  29.0 83.5 %all-gather.15.cloned.1.call-start = ((), (), s32[]{:S(2)}) async-start(), calls=%async_computation.1 | async-start | bytes 2949120 | tf_op jit(solution)/shard_map/all_gather | solution.py:1590
  31.7 16.4 %collective-permute-start.5 = (bf16[4,208,384]{2,1,0:T(8,128)(2,1)S(1)}, bf16[4,208,384]{2,1,0:T(8,128)(2,1)S(1)}, u32[]{:S(2)}, u32[]{:S(2)}) collective-permute-start(bf16[4,208,384]{2,1,0:T(8,128)(2,1)S(1)} %pad_maximum_fusion.refs_0_), channel_id=1, source_target_pairs={{0,2},{1,5},{2,0},{3,7},{4,6},{5,1},{6,4},{7,3},{8,10},{9,13},{10,... | collective-permute-start | bytes 1916936 | tf_op jit(solution)/shard_map/ppermute | solution.py:454
  33.2 14.9 %collective-permute-start.6 = (bf16[4,208,384]{2,1,0:T(8,128)(2,1)S(1)}, bf16[4,208,384]{2,1,0:T(8,128)(2,1)S(1)}, u32[]{:S(2)}, u32[]{:S(2)}) collective-permute-start(bf16[4,208,384]{2,1,0:T(8,128)(2,1)S(1)} %pad_maximum_fusion.refs_0_), channel_id=1, source_target_pairs={{0,4},{1,3},{2,6},{3,1},{4,0},{5,7},{6,2},{7,5},{8,12},{9,11},{10,... | collective-permute-start | bytes 1916936 | tf_op jit(solution)/shard_map/ppermute | solution.py:454
  33.7 148.2 %all-gather.17.cloned.1.call-start = ((), (), s32[]{:S(2)}) async-start(), calls=%async_computation.2 | async-start | bytes 3072000 | tf_op jit(solution)/shard_map/all_gather | solution.py:1604
  48.1 19.3 %copy-start.16 = (bf16[4,208,384]{2,1,0:T(8,128)(2,1)}, bf16[4,208,384]{2,1,0:T(8,128)(2,1)S(1)}, u32[]{:S(2)}) copy-start(bf16[4,208,384]{2,1,0:T(8,128)(2,1)S(1)} %collective-permute-done.5.refs_1_) | copy-start | bytes 1916932
  48.2 15.2 %collective-permute-start.7 = (bf16[4,208,384]{2,1,0:T(8,128)(2,1)S(1)}, bf16[4,208,384]{2,1,0:T(8,128)(2,1)}, u32[]{:S(2)}, u32[]{:S(2)}) collective-permute-start(bf16[4,208,384]{2,1,0:T(8,128)(2,1)S(1)} %collective-permute-done.5.refs_1_), channel_id=1, source_target_pairs={{0,4},{1,3},{2,6},{3,1},{4,0},{5,7},{6,2},{7,5},{8,12},{9,11},{10,... | collective-permute-start | bytes 1916936 | tf_op jit(solution)/shard_map/ppermute | solution.py:454
  49.3 14.0 %collective-permute-start.8 = (bf16[4,208,384]{2,1,0:T(8,128)(2,1)S(1)}, bf16[4,208,384]{2,1,0:T(8,128)(2,1)}, u32[]{:S(2)}, u32[]{:S(2)}) collective-permute-start(bf16[4,208,384]{2,1,0:T(8,128)(2,1)S(1)} %pad_maximum_fusion.refs_0_), channel_id=1, source_target_pairs={{0,1},{1,0},{2,3},{3,2},{4,5},{5,4},{6,7},{7,6},{8,9},{9,8},{10,11... | collective-permute-start | bytes 1916936 | tf_op jit(solution)/shard_map/ppermute | solution.py:454
  61.3 27.3 %collective-permute-start.13 = (bf16[4,192,768]{2,1,0:T(8,128)(2,1)}, bf16[4,192,768]{2,1,0:T(8,128)(2,1)S(1)}, u32[]{:S(2)}, u32[]{:S(2)}) collective-permute-start(bf16[4,192,768]{2,1,0:T(8,128)(2,1)} %bitcast.58), channel_id=1, source_target_pairs={{0,4},{1,5},{2,6},{3,7},{4,0},{5,1},{6,2},{7,3},{8,12},{9,13},{10,... | collective-permute-start | bytes 3538952 | tf_op jit(solution)/shard_map/ppermute | solution.py:454
  62.8 3.0 collective-permute-start.9
  62.8 3.8 collective-permute-start.10
  63.3 4.1 %collective-permute-start.11 = (bf16[4,208,384]{2,1,0:T(8,128)(2,1)}, bf16[4,208,384]{2,1,0:T(8,128)(2,1)}, u32[]{:S(2)}, u32[]{:S(2)}) collective-permute-start(bf16[4,208,384]{2,1,0:T(8,128)(2,1)} %collective-permute-done.7.refs_3_), channel_id=1, source_target_pairs={{0,1},{1,0},{2,3},{3,2},{4,5},{5,4},{6,7},{7,6},{8,9},{9,8},{10,11... | collective-permute-start | bytes 1916936 | tf_op jit(solution)/shard_map/ppermute | solution.py:454
  63.3 21.3 %collective-permute-start.12 = (bf16[384,768]{1,0:T(8,128)(2,1)S(1)}, bf16[384,768]{1,0:T(8,128)(2,1)S(1)}, u32[]{:S(2)}, u32[]{:S(2)}) collective-permute-start(bf16[384,768]{1,0:T(8,128)(2,1)S(1)} %copy-done.1), channel_id=1, source_target_pairs={{0,2},{1,3},{2,0},{3,1},{4,6},{5,7},{6,4},{7,5},{8,10},{9,11},{10,... | collective-permute-start | bytes 1769480 | tf_op jit(solution)/shard_map/ppermute | solution.py:454
  84.7 31.5 %copy-start.6 = (bf16[384,768]{1,0:T(8,128)(2,1)}, bf16[384,768]{1,0:T(8,128)(2,1)S(1)}, u32[]{:S(2)}) copy-start(bf16[384,768]{1,0:T(8,128)(2,1)S(1)} %collective-permute-done.12.refs_5_.g_a_ref) | copy-start | bytes 1769476
  89.6 24.5 %copy-start = (bf16[400,768]{1,0:T(8,128)(2,1)S(1)}, bf16[400,768]{1,0:T(8,128)(2,1)}, u32[]{:S(2)}) copy-start(bf16[400,768]{1,0:T(8,128)(2,1)} %get-tuple-element.240.h_a_ref.refs_0_.refs_3_) | copy-start | bytes 1843204
  89.6 3.5 collective-permute-start.14
  89.6 17.4 %collective-permute-start.16 = (bf16[400,768]{1,0:T(8,128)(2,1)}, bf16[400,768]{1,0:T(8,128)(2,1)}, u32[]{:S(2)}, u32[]{:S(2)}) collective-permute-start(bf16[400,768]{1,0:T(8,128)(2,1)} %get-tuple-element.240.h_a_ref.refs_0_.refs_3_), channel_id=1, source_target_pairs={{0,2},{1,3},{2,0},{3,1},{4,6},{5,7},{6,4},{7,5},{8,10},{9,11},{10,... | collective-permute-start | bytes 1843208 | tf_op jit(solution)/shard_map/ppermute | solution.py:454
  91.1 2.0 collective-permute-start.15
  91.4 15.6 %collective-permute-start.17 = (bf16[384,768]{1,0:T(8,128)(2,1)S(1)}, bf16[384,768]{1,0:T(8,128)(2,1)}, u32[]{:S(2)}, u32[]{:S(2)}) collective-permute-start(bf16[384,768]{1,0:T(8,128)(2,1)S(1)} %copy-done.1), channel_id=1, source_target_pairs={{0,4},{1,5},{2,6},{3,7},{4,0},{5,1},{6,2},{7,3},{8,12},{9,13},{10,... | collective-permute-start | bytes 1769480 | tf_op jit(solution)/shard_map/ppermute | solution.py:454
  112.5 36.9 %collective-permute-start.21 = (bf16[4,384,768]{2,1,0:T(8,128)(2,1)}, bf16[4,384,768]{2,1,0:T(8,128)(2,1)}, u32[]{:S(2)}, u32[]{:S(2)}) collective-permute-start(bf16[4,384,768]{2,1,0:T(8,128)(2,1)} %bitcast.69), channel_id=1, source_target_pairs={{0,2},{1,5},{2,0},{3,7},{4,6},{5,1},{6,4},{7,3},{8,10},{9,13},{10,... | collective-permute-start | bytes 7077896 | tf_op jit(solution)/shard_map/ppermute | solution.py:454
  114.0 103.4 %all-gather.19.cloned.1.call-start = ((), (), s32[]{:S(2)}) async-start(), calls=%async_computation.3 | async-start | bytes 3072000 | tf_op jit(solution)/shard_map/all_gather | solution.py:1618
  114.0 4.2 %collective-permute-start.18 = (bf16[400,768]{1,0:T(8,128)(2,1)}, bf16[400,768]{1,0:T(8,128)(2,1)S(1)}, u32[]{:S(2)}, u32[]{:S(2)}) collective-permute-start(bf16[400,768]{1,0:T(8,128)(2,1)} %collective-permute-done.16.refs_1_.h_a_ref), channel_id=1, source_target_pairs={{0,1},{1,0},{2,3},{3,2},{4,5},{5,4},{6,7},{7,6},{8,9},{9,8},{10,11... | collective-permute-start | bytes 1843208 | tf_op jit(solution)/shard_map/ppermute | solution.py:454
  114.1 27.4 %collective-permute-start.20 = (bf16[400,768]{1,0:T(8,128)(2,1)S(1)}, bf16[400,768]{1,0:T(8,128)(2,1)S(1)}, u32[]{:S(2)}, u32[]{:S(2)}) collective-permute-start(bf16[400,768]{1,0:T(8,128)(2,1)S(1)} %copy-done), channel_id=1, source_target_pairs={{0,4},{1,3},{2,6},{3,1},{4,0},{5,7},{6,2},{7,5},{8,12},{9,11},{10,... | collective-permute-start | bytes 1843208 | tf_op jit(solution)/shard_map/ppermute | solution.py:454
  115.7 2.8 collective-permute-start.19
  115.7 59.7 %collective-permute-start.23 = (bf16[4,384,768]{2,1,0:T(8,128)(2,1)}, bf16[4,384,768]{2,1,0:T(8,128)(2,1)}, u32[]{:S(2)}, u32[]{:S(2)}) collective-permute-start(bf16[4,384,768]{2,1,0:T(8,128)(2,1)} %bitcast.70), channel_id=1, source_target_pairs={{0,1},{1,0},{2,3},{3,2},{4,5},{5,4},{6,7},{7,6},{8,9},{9,8},{10,11... | collective-permute-start | bytes 7077896 | tf_op jit(solution)/shard_map/ppermute | solution.py:454
  149.4 29.1 %collective-permute-start.22 = (bf16[4,384,768]{2,1,0:T(8,128)(2,1)}, bf16[4,384,768]{2,1,0:T(8,128)(2,1)S(1)}, u32[]{:S(2)}, u32[]{:S(2)}) collective-permute-start(bf16[4,384,768]{2,1,0:T(8,128)(2,1)} %collective-permute-done.21.refs_5_.refs_6_), channel_id=1, source_target_pairs={{0,4},{1,3},{2,6},{3,1},{4,0},{5,7},{6,2},{7,5},{8,12},{9,11},{10,... | collective-permute-start | bytes 7077896 | tf_op jit(solution)/shard_map/ppermute | solution.py:454
  150.2 28.3 %collective-permute-start.24 = (bf16[4,384,768]{2,1,0:T(8,128)(2,1)}, bf16[4,384,768]{2,1,0:T(8,128)(2,1)}, u32[]{:S(2)}, u32[]{:S(2)}) collective-permute-start(bf16[4,384,768]{2,1,0:T(8,128)(2,1)} %collective-permute-done.21.refs_5_.refs_6_), channel_id=1, source_target_pairs={{0,1},{1,0},{2,3},{3,2},{4,5},{5,4},{6,7},{7,6},{8,9},{9,8},{10,11... | collective-permute-start | bytes 7077896 | tf_op jit(solution)/shard_map/ppermute | solution.py:454
  150.2 132.9 %all-gather.21.cloned.1.call-start = ((), (), s32[]{:S(2)}) async-start(), calls=%async_computation.4 | async-start | bytes 3072000 | tf_op jit(solution)/shard_map/all_gather | solution.py:1644
  178.5 2.2 collective-permute-start.25
  182.0 5.8 %collective-permute-start.26 = (bf16[4,400,768]{2,1,0:T(8,128)(2,1)}, bf16[4,400,768]{2,1,0:T(8,128)(2,1)S(1)}, u32[]{:S(2)}, u32[]{:S(2)}) collective-permute-start(bf16[4,400,768]{2,1,0:T(8,128)(2,1)} %bitcast.36.refs_0_), channel_id=1, source_target_pairs={{0,1},{1,0},{2,3},{3,2},{4,5},{5,4},{6,7},{7,6},{8,9},{9,8},{10,11... | collective-permute-start | bytes 7372808 | tf_op jit(solution)/shard_map/ppermute | solution.py:454
  182.2 18.9 %collective-permute-start.27 = (bf16[400,768]{1,0:T(8,128)(2,1)}, bf16[400,768]{1,0:T(8,128)(2,1)}, u32[]{:S(2)}, u32[]{:S(2)}) collective-permute-start(bf16[400,768]{1,0:T(8,128)(2,1)} %get-tuple-element.283), channel_id=1, source_target_pairs={{0,1},{1,0},{2,3},{3,2},{4,5},{5,4},{6,7},{7,6},{8,9},{9,8},{10,11... | collective-permute-start | bytes 1843208 | tf_op jit(solution)/shard_map/ppermute | solution.py:454
  182.6 18.5 %collective-permute-start.28 = (bf16[400,768]{1,0:T(8,128)(2,1)S(1)}, bf16[400,768]{1,0:T(8,128)(2,1)}, u32[]{:S(2)}, u32[]{:S(2)}) collective-permute-start(bf16[400,768]{1,0:T(8,128)(2,1)S(1)} %add_convert_fusion.2), channel_id=1, source_target_pairs={{0,2},{1,3},{2,0},{3,1},{4,6},{5,7},{6,4},{7,5},{8,10},{9,11},{10,... | collective-permute-start | bytes 1843208 | tf_op jit(solution)/shard_map/ppermute | solution.py:454
  206.2 11.2 %collective-permute-start.29 = (bf16[128,768]{1,0:T(8,128)(2,1)}, bf16[128,768]{1,0:T(8,128)(2,1)S(1)}, u32[]{:S(2)}, u32[]{:S(2)}) collective-permute-start(bf16[128,768]{1,0:T(8,128)(2,1)} %get-tuple-element.292), channel_id=1, source_target_pairs={{0,4},{1,5},{2,6},{3,7},{4,0},{5,1},{6,2},{7,3},{8,12},{9,13},{10,... | collective-permute-start | bytes 589832 | tf_op jit(solution)/shard_map/ppermute | solution.py:454
  217.4 30.2 %collective-permute-start.30 = (bf16[4,400,768]{2,1,0:T(8,128)(2,1)}, bf16[4,400,768]{2,1,0:T(8,128)(2,1)}, u32[]{:S(2)}, u32[]{:S(2)}) collective-permute-start(bf16[4,400,768]{2,1,0:T(8,128)(2,1)} %bitcast.36.refs_0_), channel_id=1, source_target_pairs={{0,2},{1,5},{2,0},{3,7},{4,6},{5,1},{6,4},{7,3},{8,10},{9,13},{10,... | collective-permute-start | bytes 7372808 | tf_op jit(solution)/shard_map/ppermute | solution.py:454
  218.8 28.7 %collective-permute-start.31 = (bf16[4,400,768]{2,1,0:T(8,128)(2,1)}, bf16[4,400,768]{2,1,0:T(8,128)(2,1)S(1)}, u32[]{:S(2)}, u32[]{:S(2)}) collective-permute-start(bf16[4,400,768]{2,1,0:T(8,128)(2,1)} %bitcast.63), channel_id=1, source_target_pairs={{0,1},{1,0},{2,3},{3,2},{4,5},{5,4},{6,7},{7,6},{8,9},{9,8},{10,11... | collective-permute-start | bytes 7372808 | tf_op jit(solution)/shard_map/ppermute | solution.py:454
  218.8 22.7 %collective-permute-start.32 = (bf16[4,384,768]{2,1,0:T(8,128)(2,1)}, bf16[4,384,768]{2,1,0:T(8,128)(2,1)}, u32[]{:S(2)}, u32[]{:S(2)}) collective-permute-start(bf16[4,384,768]{2,1,0:T(8,128)(2,1)} %copy-done.5), channel_id=1, source_target_pairs={{0,1},{1,0},{2,3},{3,2},{4,5},{5,4},{6,7},{7,6},{8,9},{9,8},{10,11... | collective-permute-start | bytes 7077896 | tf_op jit(solution)/shard_map/ppermute | solution.py:454
  219.4 140.3 %all-gather.23.cloned.1.call-start = ((), (), s32[]{:S(2)}) async-start(), calls=%async_computation.5 | async-start | bytes 2654208 | tf_op jit(solution)/shard_map/all_gather | solution.py:1701
  247.6 35.4 %copy-start.2 = (bf16[4,400,768]{2,1,0:T(8,128)(2,1)}, bf16[4,400,768]{2,1,0:T(8,128)(2,1)S(1)}, u32[]{:S(2)}) copy-start(bf16[4,400,768]{2,1,0:T(8,128)(2,1)S(1)} %collective-permute-done.31.refs_10_.refs_6_) | copy-start | bytes 7372804
  247.6 35.5 %collective-permute-start.34 = (bf16[4,208,1536]{2,1,0:T(8,128)(2,1)}, bf16[4,208,1536]{2,1,0:T(8,128)(2,1)}, u32[]{:S(2)}, u32[]{:S(2)}) collective-permute-start(bf16[4,208,1536]{2,1,0:T(8,128)(2,1)} %get-tuple-element.313), channel_id=1, source_target_pairs={{0,1},{1,0},{2,3},{3,2},{4,5},{5,4},{6,7},{7,6},{8,9},{9,8},{10,11... | collective-permute-start | bytes 7667720 | tf_op jit(solution)/shard_map/ppermute | solution.py:454
  247.6 8.7 %collective-permute-start.33 = (bf16[4,400,768]{2,1,0:T(8,128)(2,1)}, bf16[4,400,768]{2,1,0:T(8,128)(2,1)}, u32[]{:S(2)}, u32[]{:S(2)}) collective-permute-start(bf16[4,400,768]{2,1,0:T(8,128)(2,1)} %collective-permute-done.30.refs_1_.refs_0_), channel_id=1, source_target_pairs={{0,1},{1,0},{2,3},{3,2},{4,5},{5,4},{6,7},{7,6},{8,9},{9,8},{10,11... | collective-permute-start | bytes 7372808 | tf_op jit(solution)/shard_map/ppermute | solution.py:454
  248.1 35.0 %collective-permute-start.35 = (bf16[4,400,768]{2,1,0:T(8,128)(2,1)}, bf16[4,400,768]{2,1,0:T(8,128)(2,1)}, u32[]{:S(2)}, u32[]{:S(2)}) collective-permute-start(bf16[4,400,768]{2,1,0:T(8,128)(2,1)} %collective-permute-done.30.refs_1_.refs_0_), channel_id=1, source_target_pairs={{0,4},{1,3},{2,6},{3,1},{4,0},{5,7},{6,2},{7,5},{8,12},{9,11},{10,... | collective-permute-start | bytes 7372808 | tf_op jit(solution)/shard_map/ppermute | solution.py:454
  283.1 7.2 %collective-permute-start.36 = (bf16[4,400,768]{2,1,0:T(8,128)(2,1)}, bf16[4,400,768]{2,1,0:T(8,128)(2,1)S(1)}, u32[]{:S(2)}, u32[]{:S(2)}) collective-permute-start(bf16[4,400,768]{2,1,0:T(8,128)(2,1)} %bitcast.66), channel_id=1, source_target_pairs={{0,1},{1,0},{2,3},{3,2},{4,5},{5,4},{6,7},{7,6},{8,9},{9,8},{10,11... | collective-permute-start | bytes 7372808 | tf_op jit(solution)/shard_map/ppermute | solution.py:454
  283.3 8.4 %collective-permute-start.37 = (bf16[4,400,768]{2,1,0:T(8,128)(2,1)}, bf16[4,400,768]{2,1,0:T(8,128)(2,1)}, u32[]{:S(2)}, u32[]{:S(2)}) collective-permute-start(bf16[4,400,768]{2,1,0:T(8,128)(2,1)} %collective-permute-done.35.refs_3_.refs_1_), channel_id=1, source_target_pairs={{0,1},{1,0},{2,3},{3,2},{4,5},{5,4},{6,7},{7,6},{8,9},{9,8},{10,11... | collective-permute-start | bytes 7372808 | tf_op jit(solution)/shard_map/ppermute | solution.py:454
  291.7 29.9 %collective-permute-start.38 = (bf16[4,208,384]{2,1,0:T(8,128)(2,1)}, bf16[4,208,384]{2,1,0:T(8,128)(2,1)}, u32[]{:S(2)}, u32[]{:S(2)}) collective-permute-start(bf16[4,208,384]{2,1,0:T(8,128)(2,1)} %get-tuple-element.333), channel_id=1, source_target_pairs={{0,2},{1,3},{2,0},{3,1},{4,6},{5,7},{6,4},{7,5},{8,10},{9,11},{10,... | collective-permute-start | bytes 1916936 | tf_op jit(solution)/shard_map/ppermute | solution.py:454
  293.2 30.2 %collective-permute-start.39 = (bf16[4,208,384]{2,1,0:T(8,128)(2,1)}, bf16[4,208,384]{2,1,0:T(8,128)(2,1)}, u32[]{:S(2)}, u32[]{:S(2)}) collective-permute-start(bf16[4,208,384]{2,1,0:T(8,128)(2,1)} %broadcast_select_fusion.2), channel_id=1, source_target_pairs={{0,4},{1,5},{2,6},{3,7},{4,0},{5,1},{6,2},{7,3},{8,12},{9,13},{10,... | collective-permute-start | bytes 1916936 | tf_op jit(solution)/shard_map/ppermute | solution.py:454
  294.7 28.7 %collective-permute-start.40 = (bf16[4,208,384]{2,1,0:T(8,128)(2,1)}, bf16[4,208,384]{2,1,0:T(8,128)(2,1)}, u32[]{:S(2)}, u32[]{:S(2)}) collective-permute-start(bf16[4,208,384]{2,1,0:T(8,128)(2,1)} %get-tuple-element.335), channel_id=1, source_target_pairs={{0,6},{1,7},{2,4},{3,5},{4,2},{5,3},{6,0},{7,1},{8,14},{9,15},{10,... | collective-permute-start | bytes 1916936 | tf_op jit(solution)/shard_map/ppermute | solution.py:454
  323.4 2.4 collective-permute-start.41
  323.4 3.5 collective-permute-start.42
  326.9 32.7 %collective-permute-start.46 = (bf16[384,768]{1,0:T(8,128)(2,1)S(1)}, bf16[384,768]{1,0:T(8,128)(2,1)S(1)}, u32[]{:S(2)}, u32[]{:S(2)}) collective-permute-start(bf16[384,768]{1,0:T(8,128)(2,1)S(1)} %add_convert_fusion.4), channel_id=1, source_target_pairs={{0,2},{1,3},{2,0},{3,1},{4,6},{5,7},{6,4},{7,5},{8,10},{9,11},{10,... | collective-permute-start | bytes 1769480 | tf_op jit(solution)/shard_map/ppermute | solution.py:454
  328.2 31.4 %collective-permute-start.43 = (bf16[208,384]{1,0:T(8,128)(2,1)S(1)}, bf16[208,384]{1,0:T(8,128)(2,1)S(1)}, u32[]{:S(2)}, u32[]{:S(2)}) collective-permute-start(bf16[208,384]{1,0:T(8,128)(2,1)S(1)} %get-tuple-element.360), channel_id=1, source_target_pairs={{0,8},{1,9},{2,10},{3,11},{4,12},{5,13},{6,14},{7,15},{8,16},{9,17... | collective-permute-start | bytes 479240 | tf_op jit(solution)/shard_map/ppermute | solution.py:454
  328.2 31.4 %collective-permute-start.44 = (bf16[208,384]{1,0:T(8,128)(2,1)S(1)}, bf16[208,384]{1,0:T(8,128)(2,1)S(1)}, u32[]{:S(2)}, u32[]{:S(2)}) collective-permute-start(bf16[208,384]{1,0:T(8,128)(2,1)S(1)} %get-tuple-element.361), channel_id=1, source_target_pairs={{0,16},{1,17},{2,18},{3,19},{4,20},{5,21},{6,22},{7,23},{8,24},{9,... | collective-permute-start | bytes 479240 | tf_op jit(solution)/shard_map/ppermute | solution.py:454
  329.8 29.8 %collective-permute-start.45 = (bf16[208,384]{1,0:T(8,128)(2,1)S(1)}, bf16[208,384]{1,0:T(8,128)(2,1)S(1)}, u32[]{:S(2)}, u32[]{:S(2)}) collective-permute-start(bf16[208,384]{1,0:T(8,128)(2,1)S(1)} %get-tuple-element.362), channel_id=1, source_target_pairs={{0,24},{1,25},{2,26},{3,27},{4,28},{5,29},{6,30},{7,31},{8,0},{9,1... | collective-permute-start | bytes 479240 | tf_op jit(solution)/shard_map/ppermute | solution.py:454
  359.8 8.9 %collective-permute-start.47 = (bf16[208,384]{1,0:T(8,128)(2,1)S(1)}, bf16[208,384]{1,0:T(8,128)(2,1)S(1)}, u32[]{:S(2)}, u32[]{:S(2)}) collective-permute-start(bf16[208,384]{1,0:T(8,128)(2,1)S(1)} %add_convert_fusion.5), channel_id=1, source_target_pairs={{0,2},{1,3},{2,0},{3,1},{4,6},{5,7},{6,4},{7,5},{8,10},{9,11},{10,... | collective-permute-start | bytes 479240 | tf_op jit(solution)/shard_map/ppermute | solution.py:454
  360.8 8.6 %collective-permute-start.48 = (bf16[208,384]{1,0:T(8,128)(2,1)S(1)}, bf16[208,384]{1,0:T(8,128)(2,1)S(1)}, u32[]{:S(2)}, u32[]{:S(2)}) collective-permute-start(bf16[208,384]{1,0:T(8,128)(2,1)S(1)} %add_convert_fusion.5), channel_id=1, source_target_pairs={{0,4},{1,5},{2,6},{3,7},{4,0},{5,1},{6,2},{7,3},{8,12},{9,13},{10,... | collective-permute-start | bytes 479240 | tf_op jit(solution)/shard_map/ppermute | solution.py:454
  362.3 7.1 %collective-permute-start.49 = (bf16[208,384]{1,0:T(8,128)(2,1)S(1)}, bf16[208,384]{1,0:T(8,128)(2,1)S(1)}, u32[]{:S(2)}, u32[]{:S(2)}) collective-permute-start(bf16[208,384]{1,0:T(8,128)(2,1)S(1)} %add_convert_fusion.5), channel_id=1, source_target_pairs={{0,6},{1,7},{2,4},{3,5},{4,2},{5,3},{6,0},{7,1},{8,14},{9,15},{10,... | collective-permute-start | bytes 479240 | tf_op jit(solution)/shard_map/ppermute | solution.py:454
  369.8 2.1 collective-permute-start.50
  (32 other events, 149.4 us)
Sparse Core Ops, SparseCore 0:
  29.2 32.0 all-gather.12
  62.9 49.5 all-gather.14
  114.1 50.8 all-gather.16
  166.4 50.8 all-gather.18
  219.5 50.1 all-gather.20
  327.0 30.0 all-gather.22

commit v7 on v6

--- a/solution.py
+++ b/solution.py
@@ -1589,7 +1589,7 @@
 
     g_column = lax.all_gather(after(g_block, dense), "dp", axis=0, tiled=False)
 
-    shared = lax.all_gather(after(shared, dense), "dp", axis=0, tiled=False)
+    shared = lax.all_gather(shared, "dp", axis=0, tiled=False)
     shared_far = over_y(after(shared, h1))
     place = after(place, shared)
     flags = jnp.concatenate([prompt_ids == y, far_ids[:, 0].astype(jnp.int32) == y, core[None] != 0]).astype(jnp.int32)

time: 390 us -> 397 us (1.018)
  waiting for transfers between devices: 71 us -> 87.6 us
    ppermute x51, waiting for transfers between devices: 46.1 us -> 70 us  [moved(): return lax.ppermute(value, AXES, pairs)]
    all_gather x1, waiting for transfers between devices: 11.9 us -> 0.01 us  [tuned_body(): shared = lax.all_gather(shared, 'dp', axis=0, tiled=False)]
    all_gather x1, waiting for transfers between devices: 7.28 us -> 17.4 us  [tuned_body(): g_second = lax.all_gather(g_second, 'dp', axis=0, tiled=False)]
    all_gather x1, waiting for transfers between devices: 5.51 us -> 0.01 us  [tuned_body(): g_column = lax.all_gather(after(g_block, dense), 'dp', axis=0, tiled=False)]
    unnamed x90 -> x84, local copies, waits for them, and re-layouts: 13.3 us -> 12.6 us
  transfers between devices with their start and end apart: 57 -> 57, of which waited for: 21 -> 19; matrix products, arithmetic and copies ran while one was open for 9% -> 6% of each run, Pallas kernels for 53% -> 52%
where the time goes in v7:
time: 397 us; the launch traced here: 390 us
  Pallas kernels  203 us (51%)
  waiting for transfers between devices  87.6 us (22%)
  starting transfers between devices  39.7 us (10%)
  local copies, waits for them, and re-layouts  22.7 us (6%)
  between operations  17.1 us (4%)
  other arithmetic  15.7 us (4%)
    ppermute x51, waiting for transfers between devices, moved(): return lax.ppermute(value, AXES, pairs)  70 us
    pallas_call x2, Pallas kernels, expert_slice_grads(): pl.pallas_call(functools.partial(expert_slice_kernel, parts, len(sums) //...  53.9 us
    pallas_call x2, Pallas kernels, group_experts(): pl.pallas_call(functools.partial(group_kernel, blocks, len(more)), out_sh...  47 us
    ppermute x51, starting transfers between devices, moved(): return lax.ppermute(value, AXES, pairs)  39.5 us
    pallas_call x2, Pallas kernels, shared_slice_grads(): pl.pallas_call(functools.partial(shared_slice_kernel, parts, len(sums) //...  38.2 us
    pallas_call x1, Pallas kernels, attention_backward(): pl.pallas_call(attention_back_kernel, out_shape=(shape((TOK_DEV, D), F32)...  20.7 us
    all_gather x1, waiting for transfers between devices, tuned_body(): g_second = lax.all_gather(g_second, 'dp', axis=0, tiled=False)  17.4 us
    pallas_call x1, Pallas kernels, attention_forward(): pl.pallas_call(attention_kernel, out_shape=tuple((jax.ShapeDtypeStruct(*s...  16.8 us
  transfers between devices with their start and end apart: 57, of which 19 were waited for; matrix products, arithmetic and copies ran while one was open for 6% of the time, Pallas kernels for 52%

profile of v7, /device:TPU:0, one launch (start us, length us, event | category | flops | bytes accessed | tf_op | source)
XLA Modules:
  0.0 390.1 jit_solution(11751896340093572784)
XLA Ops:
  9.7 1.4 copy.45
  11.8 1.1 maximum_maximum_fusion
  13.9 3.0 collective-permute-start.3
  17.2 1.6 collective-permute-start
  18.8 2.6 collective-permute-start.1
  21.4 1.3 collective-permute-start.2
  25.9 5.0 %collective-permute-done.4 = bf16[2,128]{0,1:T(8,128)(2,1)S(1)} collective-permute-done((bf16[2,128]{0,1:T(8,128)(2,1)S(1)}, bf16[2,128]{0,1:T(8,128)(2,1)S(1)}, u32[]{:S(2)}, u32[]{:S(2)}) %collective-permute-start.4) | collective-permute-done | bytes 544 | tf_op jit(solution)/shard_map/ppermute | solution.py:454
  30.9 6.7 %collective-permute-done.1 = bf16[208,384]{1,0:T(8,128)(2,1)S(1)} collective-permute-done((bf16[208,384]{1,0:T(8,128)(2,1)S(1)}, bf16[208,384]{1,0:T(8,128)(2,1)S(1)}, u32[]{:S(2)}, u32[]{:S(2)}) %collective-permute-start.1) | collective-permute-done | bytes 159776 | tf_op jit(solution)/shard_map/ppermute | solution.py:454
  38.5 1.5 collective-permute-start.5
  42.3 2.1 norm_rows.1.refs_8_.refs_4_
  44.4 10.2 %collective-permute-done.5.refs_1_ = bf16[4,208,384]{2,1,0:T(8,128)(2,1)S(1)} collective-permute-done((bf16[4,208,384]{2,1,0:T(8,128)(2,1)S(1)}, bf16[4,208,384]{2,1,0:T(8,128)(2,1)S(1)}, u32[]{:S(2)}, u32[]{:S(2)}) %collective-permute-start.5) | collective-permute-done | bytes 639008 | tf_op jit(solution)/shard_map/ppermute | solution.py:454
  55.5 1.3 collective-permute-start.13
  57.3 14.7 %collective-permute-done.7.refs_3_ = bf16[4,208,384]{2,1,0:T(8,128)(2,1)} collective-permute-done((bf16[4,208,384]{2,1,0:T(8,128)(2,1)S(1)}, bf16[4,208,384]{2,1,0:T(8,128)(2,1)}, u32[]{:S(2)}, u32[]{:S(2)}) %collective-permute-start.7) | collective-permute-done | bytes 639008 | tf_op jit(solution)/shard_map/ppermute | solution.py:454
  72.0 1.6 collective-permute-start.12
  76.1 16.8 %attention_forward.1 = (bf16[8,768,384]{2,1,0:T(8,128)(2,1)}, bf16[768,768]{1,0:T(8,128)(2,1)}, bf16[768,768]{1,0:T(8,128)(2,1)}, bf16[768,768]{1,0:T(8,128)(2,1...) custom-call(s32[14]{0:T(128)} %stack.109.place_ref, ...), custom_call_target="tpu_custom_call" | custom-call | bytes 8000000 | tf_op jit(solution)/shard_map/attention_forward/pallas_call | solution.py:1127
  93.0 1.0 copy-done.13
  94.8 2.1 collective-permute-done.15.g_b_ref.refs_6_
  98.6 7.6 %shared_rows.2 = (bf16[2,384,768]{2,1,0:T(8,128)(2,1)}, bf16[2,384,768]{2,1,0:T(8,128)(2,1)}) custom-call(bf16[400,768]{1,0:T(8,128)(2,1)} %get-tuple-element.238.h_a_ref.refs_0_.refs_3_, bf16[400,768]{1,0:T(8,128)(2,1)} %copy-done.7, bf16[384,768]{1,0:T(8,128)(2,1)} %refs_6_.2, bf16[384,768]{1,0:T(8,128)(2,1)} %copy-done.10, bf16[4,192,768]{2,1,0:T(8,128)(2,1)} %bitcast.59, ...), custom_call_target="tpu_custom_call" | custom-call | bytes 3200000 | tf_op jit(solution)/shard_map/shared_rows/pallas_call | solution.py:705
  106.1 4.5 %collective-permute-done.17 = bf16[384,768]{1,0:T(8,128)(2,1)} collective-permute-done((bf16[384,768]{1,0:T(8,128)(2,1)S(1)}, bf16[384,768]{1,0:T(8,128)(2,1)}, u32[]{:S(2)}, u32[]{:S(2)}) %collective-permute-start.17) | collective-permute-done | bytes 589856 | tf_op jit(solution)/shard_map/ppermute | solution.py:454
  110.6 1.5 collective-permute-start.21
  113.0 1.1 broadcast_select_fusion.9
  116.0 22.0 %group_experts.2 = (bf16[384,768]{1,0:T(8,128)(2,1)}, bf16[384,768]{1,0:T(8,128)(2,1)}, bf16[384,768]{1,0:T(8,128)(2,1)}, bf16[384,768]{1,0:T(8,128)(2,1)}, bf16...) custom-call(s32[1]{0:T(128)} %bitcast.28.base_ref, ...), custom_call_target="tpu_custom_call" | custom-call | bytes 8400000 | tf_op jit(solution)/shard_map/group_experts/pallas_call | solution.py:639
  138.0 7.8 %shared_rows.3 = (bf16[2,384,768]{2,1,0:T(8,128)(2,1)}, bf16[2,384,768]{2,1,0:T(8,128)(2,1)}) custom-call(bf16[400,768]{1,0:T(8,128)(2,1)} %collective-permute-done.16.refs_1_.h_a_ref, bf16[400,768]{1,0:T(8,128)(2,1)} %copy-done.8, bf16[384,768]{1,0:T(8,128)(2,1)} %copy-done.6, bf16[384,768]{1,0:T(8,128)(2,1)} %copy-done.11, bf16[4,192,768]{2,1,0:T(8,128)(2,1)} %bitcast.60, ...), custom_call_target="tpu_custom_call" | custom-call | bytes 3200000 | tf_op jit(solution)/shard_map/shared_rows/pallas_call | solution.py:705
  146.3 0.9 collective-permute-start.22
  147.8 25.1 %group_experts.3 = (bf16[384,768]{1,0:T(8,128)(2,1)}, bf16[384,768]{1,0:T(8,128)(2,1)}, bf16[384,768]{1,0:T(8,128)(2,1)}, bf16[384,768]{1,0:T(8,128)(2,1)}, bf16...) custom-call(s32[1]{0:T(128)S(6)} %add.117.base_ref, ...), custom_call_target="tpu_custom_call" | custom-call | bytes 8400000 | tf_op jit(solution)/shard_map/group_experts/pallas_call | solution.py:639
  172.9 2.5 collective-permute-done.22.refs_9_.refs_5_
  175.4 2.2 collective-permute-done.25
  177.7 1.2 add_convert_fusion.2
  179.5 1.5 collective-permute-start.28
  182.2 1.3 pad_add_fusion.pos_ref
  183.5 1.2 collective-permute-done.26.refs_1_.refs_2_
  184.7 1.4 copy-done.4
  186.2 11.8 %shared_slice_grads.2 = (f32[256,256]{1,0:T(8,128)}, f32[256,256]{1,0:T(8,128)}, f32[128,768]{1,0:T(8,128)}) custom-call(s32[4]{0:T(128)} %pad_add_fusion.pos_ref, bf16[4,400,768]{2,1,0:T(8,128)(2,1)} %bitcast.36.refs_0_, bf16[4,400,768]{2,1,0:T(8,128)(2,1)} %copy-done.4, bf16[4,384,768]{2,1,0:T(8,128)(2,1)} %bitcast.71, ...), custom_call_target="tpu_custom_call" | custom-call | bytes 8000000 | tf_op jit(solution)/shard_map/shared_slice_grads/pallas_call | solution.py:918
  198.1 5.1 %branch_backward.1 = (f32[384,768]{1,0:T(8,128)}, bf16[384,768]{1,0:T(8,128)(2,1)}, bf16[128,768]{1,0:T(8,128)(2,1)}, f32[16,768]{1,0:T(8,128)}, f32[1,768]{1,0:T(1,128)}) custom-call(bf16[400,768]{1,0:T(8,128)(2,1)} %get-tuple-element.282.refs_0_, bf16[400,768]{1,0:T(8,128)(2,1)} %collective-permute-done.27.refs_1_, ...), custom_call_target="tpu_custom_call" | custom-call | bytes 2400000 | tf_op jit(solution)/shard_map/branch_backward/pallas_call | solution.py:1195
  204.1 3.2 convolution_convert_fusion
  207.2 17.4 %all-gather.19.cloned.1.call-done = bf16[1600,768]{1,0:T(8,128)(2,1)} async-done(((bf16[400,768]{1,0:T(8,128)(2,1)}), bf16[1600,768]{1,0:T(8,128)(2,1)}) %all-gather.19.cloned.1.call-update) | async-done | bytes 2457616 | tf_op jit(solution)/shard_map/all_gather | solution.py:1618
  224.7 1.5 collective-permute-start.30
  227.3 20.7 %attention_backward.1 = (f32[384,768]{1,0:T(8,128)}, bf16[4,208,1536]{2,1,0:T(8,128)(2,1)}, bf16[4,208,1536]{2,1,0:T(8,128)(2,1)}) custom-call(s32[5]{0:T(128)} %add_convert_fusion.6.flags_ref, bf16[768,768]{1,0:T(8,128)(2,1)} %get-tuple-element.270.refs_0_, bf16[768,768]{1,0:T(8,128)(2,1)} %get-tuple-element.271.refs_1_, ...), custom_call_target="tpu_custom_call" | custom-call | bytes 9200000 | tf_op jit(solution)/shard_map/attention_backward/pallas_call | solution.py:1400
  248.0 6.9 %collective-permute-done.30.refs_1_.refs_0_ = bf16[4,400,768]{2,1,0:T(8,128)(2,1)} collective-permute-done((bf16[4,400,768]{2,1,0:T(8,128)(2,1)}, bf16[4,400,768]{2,1,0:T(8,128)(2,1)}, u32[]{:S(2)}, u32[]{:S(2)}) %collective-permute-start.30) | collective-permute-done | bytes 2457632 | tf_op jit(solution)/shard_map/ppermute | solution.py:454
  255.4 1.5 collective-permute-start.35
  257.4 6.1 %collective-permute-done.33.refs_3_.refs_1_ = bf16[4,400,768]{2,1,0:T(8,128)(2,1)} collective-permute-done((bf16[4,400,768]{2,1,0:T(8,128)(2,1)}, bf16[4,400,768]{2,1,0:T(8,128)(2,1)}, u32[]{:S(2)}, u32[]{:S(2)}) %collective-permute-start.33) | collective-permute-done | bytes 2457632 | tf_op jit(solution)/shard_map/ppermute | solution.py:454
  263.5 26.8 %expert_slice_grads.2 = (f32[4,768,256]{2,1,0:T(8,128)}, f32[4,768,256]{2,1,0:T(8,128)}, f32[4,256,768]{2,1,0:T(8,128)}) custom-call(s32[2]{0:T(128)} %pad_add_fusion.1.pos_ref, bf16[4,400,768]{2,1,0:T(8,128)(2,1)} %bitcast.36.refs_0_, bf16[4,400,768]{2,1,0:T(8,128)(2,1)} %collective-permute-done.30.refs_1_.refs_0_, bf16[4,400,768]{2,1,0:T(8,128)(2,1)} %copy-done.4, ...), custom_call_target="tpu_custom_call" | custom-call | bytes 12400000 | tf_op jit(solution)/shard_map/expert_slice_grads/pallas_call | solution.py:838
  290.9 3.2 add_convert_fusion
  294.1 1.0 broadcast_select_fusion.2
  295.1 1.3 broadcast_select_fusion.1
  296.4 1.1 collective-permute-done.36.refs_4_.refs_2_
  297.5 1.4 collective-permute-done.37.refs_5_.refs_3_
  299.0 1.5 collective-permute-start.38
  300.5 1.5 collective-permute-start.39
  302.5 26.4 %shared_slice_grads.3 = bf16[192,768]{1,0:T(8,128)(2,1)} custom-call(s32[4]{0:T(128)} %pad_add_fusion.pos_ref, bf16[4,400,768]{2,1,0:T(8,128)(2,1)} %collective-permute-done.30.refs_1_.refs_0_, bf16[4,400,768]{2,1,0:T(8,128)(2,1)} %collective-permute-done.33.refs_3_.refs_1_, bf16[4,400,768]{2,1,0:T(8,128)(2,1)} %bitcast.67, ...), custom_call_target="tpu_custom_call" | custom-call | bytes 8000000 | tf_op jit(solution)/shard_map/shared_slice_grads/pallas_call | solution.py:918
  328.8 1.8 collective-permute-done.39
  331.2 1.8 add_convert_fusion.1
  334.2 1.2 collective-permute-start.46
  335.5 1.7 collective-permute-start.44
  337.1 2.7 collective-permute-start.45
  339.8 27.1 %expert_slice_grads.3 = (f32[4,768,256]{2,1,0:T(8,128)}, f32[4,768,256]{2,1,0:T(8,128)}, f32[4,256,768]{2,1,0:T(8,128)}) custom-call(s32[2]{0:T(128)} %pad_add_fusion.1.pos_ref, bf16[4,400,768]{2,1,0:T(8,128)(2,1)} %bitcast.68, bf16[4,400,768]{2,1,0:T(8,128)(2,1)} %collective-permute-done.35.refs_3_.refs_1_, bf16[4,400,768]{2,1,0:T(8,128)(2,1)} %copy-done.3, ...), custom_call_target="tpu_custom_call" | custom-call | bytes 12400000 | tf_op jit(solution)/shard_map/expert_slice_grads/pallas_call | solution.py:838
  367.1 1.0 collective-permute-start.47
  368.1 1.5 collective-permute-start.48
  369.6 1.1 collective-permute-start.49
  370.6 4.2 %place_shared.1 = (f32[192,2048]{1,0:T(8,128)}, f32[192,2048]{1,0:T(8,128)}, f32[512,768]{1,0:T(8,128)}) custom-call(bf16[8,192,768]{2,1,0:T(8,128)(2,1)} %bitcast.74), custom_call_target="tpu_custom_call" | custom-call | bytes 1600000 | tf_op jit(solution)/shard_map/place_shared/pallas_call | solution.py:1471
  374.9 1.1 add_convert_fusion.3
  377.2 2.1 collective-permute-done.50
  380.7 1.1 fusion.13
  381.9 1.1 fusion.12
  (206 shorter events, 29.4 us)
Async XLA Ops:
  7.2 47.8 %all-gather.13.cloned.1.call-start = ((), (), s32[]{:S(2)}) async-start(), calls=%async_computation | async-start | bytes 1474560 | tf_op jit(solution)/shard_map/all_gather | solution.py:1592
  13.8 96.8 %all-gather.15.cloned.1.call-start = ((), (), s32[]{:S(2)}) async-start(), calls=%async_computation.1 | async-start | bytes 2949120 | tf_op jit(solution)/shard_map/all_gather | solution.py:1590
  13.9 23.8 %collective-permute-start.3 = (bf16[384,768]{1,0:T(8,128)(2,1)S(1)}, bf16[384,768]{1,0:T(8,128)(2,1)S(1)}, u32[]{:S(2)}, u32[]{:S(2)}) collective-permute-start(bf16[384,768]{1,0:T(8,128)(2,1)S(1)} %copy-done.9), channel_id=1, source_target_pairs={{0,4},{1,5},{2,6},{3,7},{4,0},{5,1},{6,2},{7,3},{8,12},{9,13},{10,... | collective-permute-start | bytes 1769480 | tf_op jit(solution)/shard_map/ppermute | solution.py:454
  17.2 13.7 %collective-permute-start = (bf16[208,384]{1,0:T(8,128)(2,1)S(1)}, bf16[208,384]{1,0:T(8,128)(2,1)S(1)}, u32[]{:S(2)}, u32[]{:S(2)}) collective-permute-start(bf16[208,384]{1,0:T(8,128)(2,1)S(1)} %maximum_maximum_fusion.1), channel_id=1, source_target_pairs={{0,8},{1,9},{2,10},{3,11},{4,12},{5,13},{6,14},{7,15},{8,16},{9,17... | collective-permute-start | bytes 479240 | tf_op jit(solution)/shard_map/ppermute | solution.py:454
  18.8 18.8 %collective-permute-start.1 = (bf16[208,384]{1,0:T(8,128)(2,1)S(1)}, bf16[208,384]{1,0:T(8,128)(2,1)S(1)}, u32[]{:S(2)}, u32[]{:S(2)}) collective-permute-start(bf16[208,384]{1,0:T(8,128)(2,1)S(1)} %maximum_maximum_fusion.1), channel_id=1, source_target_pairs={{0,16},{1,17},{2,18},{3,19},{4,20},{5,21},{6,22},{7,23},{8,24},{9,... | collective-permute-start | bytes 479240 | tf_op jit(solution)/shard_map/ppermute | solution.py:454
  21.4 16.2 %collective-permute-start.2 = (bf16[208,384]{1,0:T(8,128)(2,1)S(1)}, bf16[208,384]{1,0:T(8,128)(2,1)S(1)}, u32[]{:S(2)}, u32[]{:S(2)}) collective-permute-start(bf16[208,384]{1,0:T(8,128)(2,1)S(1)} %maximum_maximum_fusion.1), channel_id=1, source_target_pairs={{0,24},{1,25},{2,26},{3,27},{4,28},{5,29},{6,30},{7,31},{8,0},{9,1... | collective-permute-start | bytes 479240 | tf_op jit(solution)/shard_map/ppermute | solution.py:454
  22.8 8.2 %collective-permute-start.4 = (bf16[2,128]{0,1:T(8,128)(2,1)S(1)}, bf16[2,128]{0,1:T(8,128)(2,1)S(1)}, u32[]{:S(2)}, u32[]{:S(2)}) collective-permute-start(bf16[2,128]{0,1:T(8,128)(2,1)S(1)} %broadcast_in_dim.30), channel_id=1, source_target_pairs={{0,4},{1,5},{2,6},{3,7},{4,0},{5,1},{6,2},{7,3},{8,12},{9,13},{10,... | collective-permute-start | bytes 1544 | tf_op jit(solution)/shard_map/ppermute | solution.py:454
  38.5 33.6 %copy-start.14 = (bf16[4,208,384]{2,1,0:T(8,128)(2,1)}, bf16[4,208,384]{2,1,0:T(8,128)(2,1)S(1)}, u32[]{:S(2)}) copy-start(bf16[4,208,384]{2,1,0:T(8,128)(2,1)S(1)} %pad_maximum_fusion.refs_0_) | copy-start | bytes 1916932
  38.5 33.6 %copy-start.1 = (bf16[384,768]{1,0:T(8,128)(2,1)S(1)}, bf16[384,768]{1,0:T(8,128)(2,1)}, u32[]{:S(2)}) copy-start(bf16[384,768]{1,0:T(8,128)(2,1)} %refs_6_.2) | copy-start | bytes 1769476
  38.5 35.1 %copy-start.31 = (s32[384,2]{0,1:T(2,128)S(1)}, s32[384,2]{0,1:T(2,128)}, u32[]{:S(2)}) copy-start(s32[384,2]{0,1:T(2,128)} %param.22) | copy-start | bytes 9220
  38.5 16.2 %collective-permute-start.5 = (bf16[4,208,384]{2,1,0:T(8,128)(2,1)S(1)}, bf16[4,208,384]{2,1,0:T(8,128)(2,1)S(1)}, u32[]{:S(2)}, u32[]{:S(2)}) collective-permute-start(bf16[4,208,384]{2,1,0:T(8,128)(2,1)S(1)} %pad_maximum_fusion.refs_0_), channel_id=1, source_target_pairs={{0,2},{1,5},{2,0},{3,7},{4,6},{5,1},{6,4},{7,3},{8,10},{9,13},{10,... | collective-permute-start | bytes 1916936 | tf_op jit(solution)/shard_map/ppermute | solution.py:454
  40.0 14.7 %collective-permute-start.6 = (bf16[4,208,384]{2,1,0:T(8,128)(2,1)S(1)}, bf16[4,208,384]{2,1,0:T(8,128)(2,1)S(1)}, u32[]{:S(2)}, u32[]{:S(2)}) collective-permute-start(bf16[4,208,384]{2,1,0:T(8,128)(2,1)S(1)} %pad_maximum_fusion.refs_0_), channel_id=1, source_target_pairs={{0,4},{1,3},{2,6},{3,1},{4,0},{5,7},{6,2},{7,5},{8,12},{9,11},{10,... | collective-permute-start | bytes 1916936 | tf_op jit(solution)/shard_map/ppermute | solution.py:454
  40.0 138.9 %all-gather.17.cloned.1.call-start = ((), (), s32[]{:S(2)}) async-start(), calls=%async_computation.2 | async-start | bytes 3072000 | tf_op jit(solution)/shard_map/all_gather | solution.py:1604
  54.6 21.5 %copy-start.16 = (bf16[4,208,384]{2,1,0:T(8,128)(2,1)}, bf16[4,208,384]{2,1,0:T(8,128)(2,1)S(1)}, u32[]{:S(2)}) copy-start(bf16[4,208,384]{2,1,0:T(8,128)(2,1)S(1)} %collective-permute-done.5.refs_1_) | copy-start | bytes 1916932
  54.6 17.4 %collective-permute-start.7 = (bf16[4,208,384]{2,1,0:T(8,128)(2,1)S(1)}, bf16[4,208,384]{2,1,0:T(8,128)(2,1)}, u32[]{:S(2)}, u32[]{:S(2)}) collective-permute-start(bf16[4,208,384]{2,1,0:T(8,128)(2,1)S(1)} %collective-permute-done.5.refs_1_), channel_id=1, source_target_pairs={{0,4},{1,3},{2,6},{3,1},{4,0},{5,7},{6,2},{7,5},{8,12},{9,11},{10,... | collective-permute-start | bytes 1916936 | tf_op jit(solution)/shard_map/ppermute | solution.py:454
  54.8 17.2 %collective-permute-start.8 = (bf16[4,208,384]{2,1,0:T(8,128)(2,1)S(1)}, bf16[4,208,384]{2,1,0:T(8,128)(2,1)}, u32[]{:S(2)}, u32[]{:S(2)}) collective-permute-start(bf16[4,208,384]{2,1,0:T(8,128)(2,1)S(1)} %pad_maximum_fusion.refs_0_), channel_id=1, source_target_pairs={{0,1},{1,0},{2,3},{3,2},{4,5},{5,4},{6,7},{7,6},{8,9},{9,8},{10,11... | collective-permute-start | bytes 1916936 | tf_op jit(solution)/shard_map/ppermute | solution.py:454
  55.5 37.4 %collective-permute-start.13 = (bf16[4,192,768]{2,1,0:T(8,128)(2,1)}, bf16[4,192,768]{2,1,0:T(8,128)(2,1)S(1)}, u32[]{:S(2)}, u32[]{:S(2)}) collective-permute-start(bf16[4,192,768]{2,1,0:T(8,128)(2,1)} %bitcast.58), channel_id=1, source_target_pairs={{0,4},{1,5},{2,6},{3,7},{4,0},{5,1},{6,2},{7,3},{8,12},{9,13},{10,... | collective-permute-start | bytes 3538952 | tf_op jit(solution)/shard_map/ppermute | solution.py:454
  56.8 17.6 %collective-permute-start.9 = (bf16[4,208,384]{2,1,0:T(8,128)(2,1)S(1)}, bf16[4,208,384]{2,1,0:T(8,128)(2,1)S(1)}, u32[]{:S(2)}, u32[]{:S(2)}) collective-permute-start(bf16[4,208,384]{2,1,0:T(8,128)(2,1)S(1)} %collective-permute-done.5.refs_1_), channel_id=1, source_target_pairs={{0,1},{1,0},{2,3},{3,2},{4,5},{5,4},{6,7},{7,6},{8,9},{9,8},{10,11... | collective-permute-start | bytes 1916936 | tf_op jit(solution)/shard_map/ppermute | solution.py:454
  57.0 18.3 %collective-permute-start.10 = (bf16[4,208,384]{2,1,0:T(8,128)(2,1)}, bf16[4,208,384]{2,1,0:T(8,128)(2,1)S(1)}, u32[]{:S(2)}, u32[]{:S(2)}) collective-permute-start(bf16[4,208,384]{2,1,0:T(8,128)(2,1)} %copy-done.17), channel_id=1, source_target_pairs={{0,1},{1,0},{2,3},{3,2},{4,5},{5,4},{6,7},{7,6},{8,9},{9,8},{10,11... | collective-permute-start | bytes 1916936 | tf_op jit(solution)/shard_map/ppermute | solution.py:454
  72.0 4.1 %collective-permute-start.11 = (bf16[4,208,384]{2,1,0:T(8,128)(2,1)}, bf16[4,208,384]{2,1,0:T(8,128)(2,1)}, u32[]{:S(2)}, u32[]{:S(2)}) collective-permute-start(bf16[4,208,384]{2,1,0:T(8,128)(2,1)} %collective-permute-done.7.refs_3_), channel_id=1, source_target_pairs={{0,1},{1,0},{2,3},{3,2},{4,5},{5,4},{6,7},{7,6},{8,9},{9,8},{10,11... | collective-permute-start | bytes 1916936 | tf_op jit(solution)/shard_map/ppermute | solution.py:454
  72.0 20.9 %collective-permute-start.12 = (bf16[384,768]{1,0:T(8,128)(2,1)S(1)}, bf16[384,768]{1,0:T(8,128)(2,1)S(1)}, u32[]{:S(2)}, u32[]{:S(2)}) collective-permute-start(bf16[384,768]{1,0:T(8,128)(2,1)S(1)} %copy-done.1), channel_id=1, source_target_pairs={{0,2},{1,3},{2,0},{3,1},{4,6},{5,7},{6,4},{7,5},{8,10},{9,11},{10,... | collective-permute-start | bytes 1769480 | tf_op jit(solution)/shard_map/ppermute | solution.py:454
  92.9 20.1 %copy-start.6 = (bf16[384,768]{1,0:T(8,128)(2,1)}, bf16[384,768]{1,0:T(8,128)(2,1)S(1)}, u32[]{:S(2)}) copy-start(bf16[384,768]{1,0:T(8,128)(2,1)S(1)} %collective-permute-done.12.refs_5_.g_a_ref) | copy-start | bytes 1769476
  94.0 18.3 %copy-start = (bf16[400,768]{1,0:T(8,128)(2,1)S(1)}, bf16[400,768]{1,0:T(8,128)(2,1)}, u32[]{:S(2)}) copy-start(bf16[400,768]{1,0:T(8,128)(2,1)} %get-tuple-element.238.h_a_ref.refs_0_.refs_3_) | copy-start | bytes 1843204
  94.0 2.9 collective-permute-start.14
  94.2 16.4 %collective-permute-start.16 = (bf16[400,768]{1,0:T(8,128)(2,1)}, bf16[400,768]{1,0:T(8,128)(2,1)}, u32[]{:S(2)}, u32[]{:S(2)}) collective-permute-start(bf16[400,768]{1,0:T(8,128)(2,1)} %get-tuple-element.238.h_a_ref.refs_0_.refs_3_), channel_id=1, source_target_pairs={{0,2},{1,3},{2,0},{3,1},{4,6},{5,7},{6,4},{7,5},{8,10},{9,11},{10,... | collective-permute-start | bytes 1843208 | tf_op jit(solution)/shard_map/ppermute | solution.py:454
  94.7 2.1 collective-permute-start.15
  94.8 15.8 %collective-permute-start.17 = (bf16[384,768]{1,0:T(8,128)(2,1)S(1)}, bf16[384,768]{1,0:T(8,128)(2,1)}, u32[]{:S(2)}, u32[]{:S(2)}) collective-permute-start(bf16[384,768]{1,0:T(8,128)(2,1)S(1)} %copy-done.1), channel_id=1, source_target_pairs={{0,4},{1,5},{2,6},{3,7},{4,0},{5,1},{6,2},{7,3},{8,12},{9,13},{10,... | collective-permute-start | bytes 1769480 | tf_op jit(solution)/shard_map/ppermute | solution.py:454
  110.6 35.7 %collective-permute-start.21 = (bf16[4,384,768]{2,1,0:T(8,128)(2,1)}, bf16[4,384,768]{2,1,0:T(8,128)(2,1)}, u32[]{:S(2)}, u32[]{:S(2)}) collective-permute-start(bf16[4,384,768]{2,1,0:T(8,128)(2,1)} %bitcast.69), channel_id=1, source_target_pairs={{0,2},{1,5},{2,0},{3,7},{4,6},{5,1},{6,4},{7,3},{8,10},{9,13},{10,... | collective-permute-start | bytes 7077896 | tf_op jit(solution)/shard_map/ppermute | solution.py:454
  112.1 112.5 %all-gather.19.cloned.1.call-start = ((), (), s32[]{:S(2)}) async-start(), calls=%async_computation.3 | async-start | bytes 3072000 | tf_op jit(solution)/shard_map/all_gather | solution.py:1618
  112.2 2.8 collective-permute-start.18
  112.3 25.7 %collective-permute-start.20 = (bf16[400,768]{1,0:T(8,128)(2,1)S(1)}, bf16[400,768]{1,0:T(8,128)(2,1)S(1)}, u32[]{:S(2)}, u32[]{:S(2)}) collective-permute-start(bf16[400,768]{1,0:T(8,128)(2,1)S(1)} %copy-done), channel_id=1, source_target_pairs={{0,4},{1,3},{2,6},{3,1},{4,0},{5,7},{6,2},{7,5},{8,12},{9,11},{10,... | collective-permute-start | bytes 1843208 | tf_op jit(solution)/shard_map/ppermute | solution.py:454
  112.6 2.5 collective-permute-start.19
  115.0 57.9 %collective-permute-start.23 = (bf16[4,384,768]{2,1,0:T(8,128)(2,1)}, bf16[4,384,768]{2,1,0:T(8,128)(2,1)}, u32[]{:S(2)}, u32[]{:S(2)}) collective-permute-start(bf16[4,384,768]{2,1,0:T(8,128)(2,1)} %bitcast.70), channel_id=1, source_target_pairs={{0,1},{1,0},{2,3},{3,2},{4,5},{5,4},{6,7},{7,6},{8,9},{9,8},{10,11... | collective-permute-start | bytes 7077896 | tf_op jit(solution)/shard_map/ppermute | solution.py:454
  146.3 29.1 %collective-permute-start.22 = (bf16[4,384,768]{2,1,0:T(8,128)(2,1)}, bf16[4,384,768]{2,1,0:T(8,128)(2,1)S(1)}, u32[]{:S(2)}, u32[]{:S(2)}) collective-permute-start(bf16[4,384,768]{2,1,0:T(8,128)(2,1)} %collective-permute-done.21.refs_5_.refs_6_), channel_id=1, source_target_pairs={{0,4},{1,3},{2,6},{3,1},{4,0},{5,7},{6,2},{7,5},{8,12},{9,11},{10,... | collective-permute-start | bytes 7077896 | tf_op jit(solution)/shard_map/ppermute | solution.py:454
  147.3 28.1 %collective-permute-start.24 = (bf16[4,384,768]{2,1,0:T(8,128)(2,1)}, bf16[4,384,768]{2,1,0:T(8,128)(2,1)}, u32[]{:S(2)}, u32[]{:S(2)}) collective-permute-start(bf16[4,384,768]{2,1,0:T(8,128)(2,1)} %collective-permute-done.21.refs_5_.refs_6_), channel_id=1, source_target_pairs={{0,1},{1,0},{2,3},{3,2},{4,5},{5,4},{6,7},{7,6},{8,9},{9,8},{10,11... | collective-permute-start | bytes 7077896 | tf_op jit(solution)/shard_map/ppermute | solution.py:454
  147.7 142.6 %all-gather.21.cloned.1.call-start = ((), (), s32[]{:S(2)}) async-start(), calls=%async_computation.4 | async-start | bytes 3072000 | tf_op jit(solution)/shard_map/all_gather | solution.py:1644
  175.4 2.3 collective-permute-start.25
  178.9 5.8 %collective-permute-start.26 = (bf16[4,400,768]{2,1,0:T(8,128)(2,1)}, bf16[4,400,768]{2,1,0:T(8,128)(2,1)S(1)}, u32[]{:S(2)}, u32[]{:S(2)}) collective-permute-start(bf16[4,400,768]{2,1,0:T(8,128)(2,1)} %bitcast.36.refs_0_), channel_id=1, source_target_pairs={{0,1},{1,0},{2,3},{3,2},{4,5},{5,4},{6,7},{7,6},{8,9},{9,8},{10,11... | collective-permute-start | bytes 7372808 | tf_op jit(solution)/shard_map/ppermute | solution.py:454
  179.1 18.9 %collective-permute-start.27 = (bf16[400,768]{1,0:T(8,128)(2,1)}, bf16[400,768]{1,0:T(8,128)(2,1)}, u32[]{:S(2)}, u32[]{:S(2)}) collective-permute-start(bf16[400,768]{1,0:T(8,128)(2,1)} %get-tuple-element.281), channel_id=1, source_target_pairs={{0,1},{1,0},{2,3},{3,2},{4,5},{5,4},{6,7},{7,6},{8,9},{9,8},{10,11... | collective-permute-start | bytes 1843208 | tf_op jit(solution)/shard_map/ppermute | solution.py:454
  179.5 18.5 %collective-permute-start.28 = (bf16[400,768]{1,0:T(8,128)(2,1)S(1)}, bf16[400,768]{1,0:T(8,128)(2,1)}, u32[]{:S(2)}, u32[]{:S(2)}) collective-permute-start(bf16[400,768]{1,0:T(8,128)(2,1)S(1)} %add_convert_fusion.2), channel_id=1, source_target_pairs={{0,2},{1,3},{2,0},{3,1},{4,6},{5,7},{6,4},{7,5},{8,10},{9,11},{10,... | collective-permute-start | bytes 1843208 | tf_op jit(solution)/shard_map/ppermute | solution.py:454
  203.1 21.5 %collective-permute-start.29 = (bf16[128,768]{1,0:T(8,128)(2,1)}, bf16[128,768]{1,0:T(8,128)(2,1)S(1)}, u32[]{:S(2)}, u32[]{:S(2)}) collective-permute-start(bf16[128,768]{1,0:T(8,128)(2,1)} %get-tuple-element.290), channel_id=1, source_target_pairs={{0,4},{1,5},{2,6},{3,7},{4,0},{5,1},{6,2},{7,3},{8,12},{9,13},{10,... | collective-permute-start | bytes 589832 | tf_op jit(solution)/shard_map/ppermute | solution.py:454
  224.7 30.2 %collective-permute-start.30 = (bf16[4,400,768]{2,1,0:T(8,128)(2,1)}, bf16[4,400,768]{2,1,0:T(8,128)(2,1)}, u32[]{:S(2)}, u32[]{:S(2)}) collective-permute-start(bf16[4,400,768]{2,1,0:T(8,128)(2,1)} %bitcast.36.refs_0_), channel_id=1, source_target_pairs={{0,2},{1,5},{2,0},{3,7},{4,6},{5,1},{6,4},{7,3},{8,10},{9,13},{10,... | collective-permute-start | bytes 7372808 | tf_op jit(solution)/shard_map/ppermute | solution.py:454
  226.1 28.7 %collective-permute-start.31 = (bf16[4,400,768]{2,1,0:T(8,128)(2,1)}, bf16[4,400,768]{2,1,0:T(8,128)(2,1)S(1)}, u32[]{:S(2)}, u32[]{:S(2)}) collective-permute-start(bf16[4,400,768]{2,1,0:T(8,128)(2,1)} %bitcast.63), channel_id=1, source_target_pairs={{0,1},{1,0},{2,3},{3,2},{4,5},{5,4},{6,7},{7,6},{8,9},{9,8},{10,11... | collective-permute-start | bytes 7372808 | tf_op jit(solution)/shard_map/ppermute | solution.py:454
  226.1 21.9 %collective-permute-start.32 = (bf16[4,384,768]{2,1,0:T(8,128)(2,1)}, bf16[4,384,768]{2,1,0:T(8,128)(2,1)}, u32[]{:S(2)}, u32[]{:S(2)}) collective-permute-start(bf16[4,384,768]{2,1,0:T(8,128)(2,1)} %copy-done.5), channel_id=1, source_target_pairs={{0,1},{1,0},{2,3},{3,2},{4,5},{5,4},{6,7},{7,6},{8,9},{9,8},{10,11... | collective-permute-start | bytes 7077896 | tf_op jit(solution)/shard_map/ppermute | solution.py:454
  226.7 140.3 %all-gather.23.cloned.1.call-start = ((), (), s32[]{:S(2)}) async-start(), calls=%async_computation.5 | async-start | bytes 2654208 | tf_op jit(solution)/shard_map/all_gather | solution.py:1701
  254.9 35.4 %copy-start.2 = (bf16[4,400,768]{2,1,0:T(8,128)(2,1)}, bf16[4,400,768]{2,1,0:T(8,128)(2,1)S(1)}, u32[]{:S(2)}) copy-start(bf16[4,400,768]{2,1,0:T(8,128)(2,1)S(1)} %collective-permute-done.31.refs_10_.refs_6_) | copy-start | bytes 7372804
  254.9 35.5 %collective-permute-start.34 = (bf16[4,208,1536]{2,1,0:T(8,128)(2,1)}, bf16[4,208,1536]{2,1,0:T(8,128)(2,1)}, u32[]{:S(2)}, u32[]{:S(2)}) collective-permute-start(bf16[4,208,1536]{2,1,0:T(8,128)(2,1)} %get-tuple-element.311), channel_id=1, source_target_pairs={{0,1},{1,0},{2,3},{3,2},{4,5},{5,4},{6,7},{7,6},{8,9},{9,8},{10,11... | collective-permute-start | bytes 7667720 | tf_op jit(solution)/shard_map/ppermute | solution.py:454
  254.9 8.7 %collective-permute-start.33 = (bf16[4,400,768]{2,1,0:T(8,128)(2,1)}, bf16[4,400,768]{2,1,0:T(8,128)(2,1)}, u32[]{:S(2)}, u32[]{:S(2)}) collective-permute-start(bf16[4,400,768]{2,1,0:T(8,128)(2,1)} %collective-permute-done.30.refs_1_.refs_0_), channel_id=1, source_target_pairs={{0,1},{1,0},{2,3},{3,2},{4,5},{5,4},{6,7},{7,6},{8,9},{9,8},{10,11... | collective-permute-start | bytes 7372808 | tf_op jit(solution)/shard_map/ppermute | solution.py:454
  255.4 35.0 %collective-permute-start.35 = (bf16[4,400,768]{2,1,0:T(8,128)(2,1)}, bf16[4,400,768]{2,1,0:T(8,128)(2,1)}, u32[]{:S(2)}, u32[]{:S(2)}) collective-permute-start(bf16[4,400,768]{2,1,0:T(8,128)(2,1)} %collective-permute-done.30.refs_1_.refs_0_), channel_id=1, source_target_pairs={{0,4},{1,3},{2,6},{3,1},{4,0},{5,7},{6,2},{7,5},{8,12},{9,11},{10,... | collective-permute-start | bytes 7372808 | tf_op jit(solution)/shard_map/ppermute | solution.py:454
  290.4 7.1 %collective-permute-start.36 = (bf16[4,400,768]{2,1,0:T(8,128)(2,1)}, bf16[4,400,768]{2,1,0:T(8,128)(2,1)S(1)}, u32[]{:S(2)}, u32[]{:S(2)}) collective-permute-start(bf16[4,400,768]{2,1,0:T(8,128)(2,1)} %bitcast.66), channel_id=1, source_target_pairs={{0,1},{1,0},{2,3},{3,2},{4,5},{5,4},{6,7},{7,6},{8,9},{9,8},{10,11... | collective-permute-start | bytes 7372808 | tf_op jit(solution)/shard_map/ppermute | solution.py:454
  290.6 8.4 %collective-permute-start.37 = (bf16[4,400,768]{2,1,0:T(8,128)(2,1)}, bf16[4,400,768]{2,1,0:T(8,128)(2,1)}, u32[]{:S(2)}, u32[]{:S(2)}) collective-permute-start(bf16[4,400,768]{2,1,0:T(8,128)(2,1)} %collective-permute-done.35.refs_3_.refs_1_), channel_id=1, source_target_pairs={{0,1},{1,0},{2,3},{3,2},{4,5},{5,4},{6,7},{7,6},{8,9},{9,8},{10,11... | collective-permute-start | bytes 7372808 | tf_op jit(solution)/shard_map/ppermute | solution.py:454
  299.0 29.9 %collective-permute-start.38 = (bf16[4,208,384]{2,1,0:T(8,128)(2,1)}, bf16[4,208,384]{2,1,0:T(8,128)(2,1)}, u32[]{:S(2)}, u32[]{:S(2)}) collective-permute-start(bf16[4,208,384]{2,1,0:T(8,128)(2,1)} %get-tuple-element.331), channel_id=1, source_target_pairs={{0,2},{1,3},{2,0},{3,1},{4,6},{5,7},{6,4},{7,5},{8,10},{9,11},{10,... | collective-permute-start | bytes 1916936 | tf_op jit(solution)/shard_map/ppermute | solution.py:454
  300.5 30.2 %collective-permute-start.39 = (bf16[4,208,384]{2,1,0:T(8,128)(2,1)}, bf16[4,208,384]{2,1,0:T(8,128)(2,1)}, u32[]{:S(2)}, u32[]{:S(2)}) collective-permute-start(bf16[4,208,384]{2,1,0:T(8,128)(2,1)} %broadcast_select_fusion.2), channel_id=1, source_target_pairs={{0,4},{1,5},{2,6},{3,7},{4,0},{5,1},{6,2},{7,3},{8,12},{9,13},{10,... | collective-permute-start | bytes 1916936 | tf_op jit(solution)/shard_map/ppermute | solution.py:454
  302.0 28.7 %collective-permute-start.40 = (bf16[4,208,384]{2,1,0:T(8,128)(2,1)}, bf16[4,208,384]{2,1,0:T(8,128)(2,1)}, u32[]{:S(2)}, u32[]{:S(2)}) collective-permute-start(bf16[4,208,384]{2,1,0:T(8,128)(2,1)} %get-tuple-element.333), channel_id=1, source_target_pairs={{0,6},{1,7},{2,4},{3,5},{4,2},{5,3},{6,0},{7,1},{8,14},{9,15},{10,... | collective-permute-start | bytes 1916936 | tf_op jit(solution)/shard_map/ppermute | solution.py:454
  330.7 2.4 collective-permute-start.41
  330.7 3.5 collective-permute-start.42
  334.2 32.7 %collective-permute-start.46 = (bf16[384,768]{1,0:T(8,128)(2,1)S(1)}, bf16[384,768]{1,0:T(8,128)(2,1)S(1)}, u32[]{:S(2)}, u32[]{:S(2)}) collective-permute-start(bf16[384,768]{1,0:T(8,128)(2,1)S(1)} %add_convert_fusion.4), channel_id=1, source_target_pairs={{0,2},{1,3},{2,0},{3,1},{4,6},{5,7},{6,4},{7,5},{8,10},{9,11},{10,... | collective-permute-start | bytes 1769480 | tf_op jit(solution)/shard_map/ppermute | solution.py:454
  335.5 31.4 %collective-permute-start.43 = (bf16[208,384]{1,0:T(8,128)(2,1)S(1)}, bf16[208,384]{1,0:T(8,128)(2,1)S(1)}, u32[]{:S(2)}, u32[]{:S(2)}) collective-permute-start(bf16[208,384]{1,0:T(8,128)(2,1)S(1)} %get-tuple-element.358), channel_id=1, source_target_pairs={{0,8},{1,9},{2,10},{3,11},{4,12},{5,13},{6,14},{7,15},{8,16},{9,17... | collective-permute-start | bytes 479240 | tf_op jit(solution)/shard_map/ppermute | solution.py:454
  335.5 31.5 %collective-permute-start.44 = (bf16[208,384]{1,0:T(8,128)(2,1)S(1)}, bf16[208,384]{1,0:T(8,128)(2,1)S(1)}, u32[]{:S(2)}, u32[]{:S(2)}) collective-permute-start(bf16[208,384]{1,0:T(8,128)(2,1)S(1)} %get-tuple-element.359), channel_id=1, source_target_pairs={{0,16},{1,17},{2,18},{3,19},{4,20},{5,21},{6,22},{7,23},{8,24},{9,... | collective-permute-start | bytes 479240 | tf_op jit(solution)/shard_map/ppermute | solution.py:454
  337.1 29.8 %collective-permute-start.45 = (bf16[208,384]{1,0:T(8,128)(2,1)S(1)}, bf16[208,384]{1,0:T(8,128)(2,1)S(1)}, u32[]{:S(2)}, u32[]{:S(2)}) collective-permute-start(bf16[208,384]{1,0:T(8,128)(2,1)S(1)} %get-tuple-element.360), channel_id=1, source_target_pairs={{0,24},{1,25},{2,26},{3,27},{4,28},{5,29},{6,30},{7,31},{8,0},{9,1... | collective-permute-start | bytes 479240 | tf_op jit(solution)/shard_map/ppermute | solution.py:454
  367.1 8.9 %collective-permute-start.47 = (bf16[208,384]{1,0:T(8,128)(2,1)S(1)}, bf16[208,384]{1,0:T(8,128)(2,1)S(1)}, u32[]{:S(2)}, u32[]{:S(2)}) collective-permute-start(bf16[208,384]{1,0:T(8,128)(2,1)S(1)} %add_convert_fusion.5), channel_id=1, source_target_pairs={{0,2},{1,3},{2,0},{3,1},{4,6},{5,7},{6,4},{7,5},{8,10},{9,11},{10,... | collective-permute-start | bytes 479240 | tf_op jit(solution)/shard_map/ppermute | solution.py:454
  368.1 8.6 %collective-permute-start.48 = (bf16[208,384]{1,0:T(8,128)(2,1)S(1)}, bf16[208,384]{1,0:T(8,128)(2,1)S(1)}, u32[]{:S(2)}, u32[]{:S(2)}) collective-permute-start(bf16[208,384]{1,0:T(8,128)(2,1)S(1)} %add_convert_fusion.5), channel_id=1, source_target_pairs={{0,4},{1,5},{2,6},{3,7},{4,0},{5,1},{6,2},{7,3},{8,12},{9,13},{10,... | collective-permute-start | bytes 479240 | tf_op jit(solution)/shard_map/ppermute | solution.py:454
  369.6 7.1 %collective-permute-start.49 = (bf16[208,384]{1,0:T(8,128)(2,1)S(1)}, bf16[208,384]{1,0:T(8,128)(2,1)S(1)}, u32[]{:S(2)}, u32[]{:S(2)}) collective-permute-start(bf16[208,384]{1,0:T(8,128)(2,1)S(1)} %add_convert_fusion.5), channel_id=1, source_target_pairs={{0,6},{1,7},{2,4},{3,5},{4,2},{5,3},{6,0},{7,1},{8,14},{9,15},{10,... | collective-permute-start | bytes 479240 | tf_op jit(solution)/shard_map/ppermute | solution.py:454
  377.1 2.1 collective-permute-start.50
  (29 other events, 108.4 us)
Sparse Core Ops, SparseCore 0:
  13.9 40.1 all-gather.12
  55.7 48.9 all-gather.14
  112.3 59.9 all-gather.16
  173.7 50.8 all-gather.18
  226.8 50.1 all-gather.20
  334.3 30.0 all-gather.22
